TPU v7x, 32 devices: a whole 2x2x4 slice. The times are simulated.
32 devices in a mesh: seq: 16 (over z, y, core), head: 2 (over x).
Axes of the slice: x: 2, y: 2, z: 4, core: 2. Of those that a mesh axis runs over, the one named last changes fastest.
Arguments:
- query: bfloat16 [8192, 32, 128], P('seq', 'head'), may hold values from -6 to 6
- key: bfloat16 [8192, 16, 128], P('seq', 'head'), may hold values from -6 to 6
- value: bfloat16 [8192, 16, 128], P('seq', 'head'), may hold values from -6 to 6
- grad_out: bfloat16 [8192, 32, 128], P('seq', 'head'), may hold values from -25 to 25
- q_gain: float32 [128], replicated, may hold values from 0.1 to 1.9
- k_gain: float32 [128], replicated, may hold values from 0.1 to 1.9
Outputs:
- grad_query: bfloat16 [8192, 32, 128], P('seq', 'head')
- grad_key: bfloat16 [8192, 16, 128], P('seq', 'head')
- grad_value: bfloat16 [8192, 16, 128], P('seq', 'head')
- grad_q_gain: float32 [128], replicated
- grad_k_gain: float32 [128], replicated
All inputs are finite; a program needn't handle non-finite values.
Results may differ from a plain program's by a relative error of at most 0.0099.
Values may be sent and summed in bfloat16 or wider, within the bound.
No kernel may reach another device: no remote copies, remote signals or barrier semaphores. Data moves between devices by JAX's collectives and lax.ppermute only.
A program may use at most 128 MiB of HBM per device.

v0:
```python
import functools

import jax
import jax.numpy as jnp
from jax import lax
from jax.experimental import pallas as pl
from jax.experimental.pallas import tpu as pltpu
from jax.sharding import PartitionSpec as P

WINDOW = 1024
TILE = 128

score_scale = 168.0 ** (-0.5)
norm_eps = 1e-06
exp2_scale = score_scale * 1.4426950408889634

GROUPS = 3
HEAVY = pl.CostEstimate(flops=10**11, bytes_accessed=10**8, transcendentals=0)
LIGHT = pl.CostEstimate(flops=1000, bytes_accessed=1000, transcendentals=0)

NT = (((1,), (1,)), ((), ()))


def inverse_rms_of(as_float):
    return lax.rsqrt(jnp.mean(as_float * as_float, axis=-1, keepdims=True) + norm_eps)


def norm_back(d_normed, raw, inverse_rms, gain_vec):
    unit_rows = raw * inverse_rms
    d_unit = d_normed * gain_vec
    return inverse_rms * (
        d_unit - unit_rows * jnp.mean(d_unit * unit_rows, axis=-1, keepdims=True)
    )


def heads_kernel(
    shard_ref, q_ref, g_ref, own_ref, near_ref, far_ref, q_gain_ref, k_gain_ref,
    dq_ref, d_own_ref, d_near_ref, d_far_ref, gains_ref,
    k_low, k_low_t, values, q_low, probs_all, d_scores_all,
):
    rows = own_ref.shape[2]
    group = q_ref.shape[1] // rows
    lanes = TILE * group
    blocks = rows // TILE
    tiles = WINDOW // TILE
    q_gain, k_gain = q_gain_ref[...], k_gain_ref[...]
    far_ok = jnp.where(shard_ref[0] >= 2, 1.0, 0.0)
    near_ok = jnp.where(shard_ref[0] >= 1, 1.0, 0.0)
    key_refs = (far_ref, near_ref, own_ref)

    @pl.when(pl.program_id(0) == 0)
    def _():
        gains_ref[...] = jnp.zeros_like(gains_ref)

    for place, ref in enumerate(key_refs):
        raw = ref[0, 0].astype(jnp.float32)
        here = slice(place * rows, (place + 1) * rows)
        k_low[here, :] = (raw * inverse_rms_of(raw) * k_gain).astype(jnp.bfloat16)
        values[here, :] = ref[1, 0]
    k_low_t[...] = k_low[...].T
    raw_q = q_ref[0].astype(jnp.float32)
    q_low[...] = (raw_q * inverse_rms_of(raw_q) * q_gain).astype(jnp.bfloat16)

    key_ids = lax.broadcasted_iota(jnp.int32, (TILE, lanes), 0)
    token_ids = lax.broadcasted_iota(jnp.int32, (TILE, lanes), 1) // group
    late = key_ids <= token_ids
    edge_ok = jnp.where(late, 1.0, far_ok)
    q_gain_sum = jnp.zeros_like(q_gain)

    for block in range(blocks):
        span = slice(block * TILE, block * TILE + WINDOW + TILE)
        mine = slice(block * lanes, (block + 1) * lanes)
        scores = lax.dot_general(
            k_low[span, :], q_low[mine, :], NT, preferred_element_type=jnp.float32
        )
        scores = jnp.concatenate(
            [jnp.where(late, scores[WINDOW:], scores[:TILE]), scores[TILE:WINDOW]], axis=0
        )
        exp_scores = jnp.exp2(scores * exp2_scale)
        edge = exp_scores[:TILE] * edge_ok
        first_near = (blocks - block) * TILE
        first_own = first_near + rows
        total = jnp.sum(edge, axis=0, keepdims=True)
        for low, high, ok in (
            (TILE, first_near, far_ok),
            (first_near, min(first_own, WINDOW), near_ok),
            (first_own, WINDOW, None),
        ):
            if low < high:
                part = jnp.sum(exp_scores[low:high], axis=0, keepdims=True)
                total = total + (part if ok is None else part * ok)
        inverse = 1.0 / total
        probs = jnp.concatenate([edge, exp_scores[TILE:]], axis=0) * inverse
        d_probs = lax.dot_general(
            values[span, :], g_ref[0, mine, :], NT, preferred_element_type=jnp.float32
        )
        d_probs = jnp.concatenate(
            [jnp.where(late, d_probs[WINDOW:], d_probs[:TILE]), d_probs[TILE:WINDOW]], axis=0
        )
        offset = jnp.sum(probs * d_probs, axis=0, keepdims=True)
        d_scores = probs * (d_probs - offset)
        for whole, held in ((probs, probs_all), (d_scores, d_scores_all)):
            start = block * TILE
            held[start : start + TILE, mine] = jnp.where(late, 0.0, whole[:TILE]).astype(
                jnp.bfloat16
            )
            held[start + TILE : start + WINDOW, mine] = whole[TILE:].astype(jnp.bfloat16)
            held[start + WINDOW : start + WINDOW + TILE, mine] = jnp.where(
                late, whole[:TILE], 0.0
            ).astype(jnp.bfloat16)
        query_grad = score_scale * jnp.dot(
            k_low_t[:, span], d_scores_all[span, mine], preferred_element_type=jnp.float32
        ).T
        raw = q_ref[0, mine, :].astype(jnp.float32)
        inverse_rms = inverse_rms_of(raw)
        q_gain_sum = q_gain_sum + jnp.sum(query_grad * (raw * inverse_rms), axis=0, keepdims=True)
        dq_ref[0, mine, :] = norm_back(query_grad, raw, inverse_rms, q_gain).astype(dq_ref.dtype)

    pieces = [(tile, tile + 1, 0, tile + 1) for tile in range(blocks - 1)]
    pieces += [(blocks - 1, tiles + 1, 0, blocks)]
    pieces += [(tiles + block, tiles + block + 1, block, blocks) for block in range(1, blocks)]
    k_gain_sum = jnp.zeros_like(k_gain)
    for first, last, low, high in pieces:
        meets = slice(low * lanes, high * lanes)
        keys = slice(first * TILE, last * TILE)
        value_grad = jnp.dot(
            probs_all[keys, meets], g_ref[0, meets, :], preferred_element_type=jnp.float32
        )
        key_grad = score_scale * jnp.dot(
            d_scores_all[keys, meets], q_low[meets, :], preferred_element_type=jnp.float32
        )
        for place, (ref, out) in enumerate(
            zip(key_refs, (d_far_ref, d_near_ref, d_own_ref), strict=True)
        ):
            start = max(first * TILE, place * rows)
            stop = min(last * TILE, (place + 1) * rows)
            if start >= stop:
                continue
            inside = slice(start - place * rows, stop - place * rows)
            here = slice(start - first * TILE, stop - first * TILE)
            raw = ref[0, 0, inside, :].astype(jnp.float32)
            k_gain_sum = k_gain_sum + jnp.sum(
                key_grad[here] * (raw * inverse_rms_of(raw)), axis=0, keepdims=True
            )
            out[0, 0, inside, :] = key_grad[here].astype(out.dtype)
            out[1, 0, inside, :] = value_grad[here].astype(out.dtype)
    gains_ref[0:1, :] += q_gain_sum
    gains_ref[1:2, :] += k_gain_sum


def closed(shard_ref, own, returned, swapped, kind, head):
    keep = jnp.where(shard_ref[0] % 2 == 1, 0.0, 1.0)
    own, returned, swapped = (
        part[kind, head].astype(jnp.float32) for part in (own, returned, swapped)
    )
    return own + returned + keep * swapped


def close_kernel(shard_ref, own, returned, swapped, raw_ref, k_gain_ref, out):
    for head in range(own.shape[1]):
        grad = closed(shard_ref, own, returned, swapped, 0, head)
        raw = raw_ref[0, head].astype(jnp.float32)
        grad = norm_back(grad, raw, inverse_rms_of(raw), k_gain_ref[...])
        out[0, head] = grad.astype(out.dtype)
        out[1, head] = closed(shard_ref, own, returned, swapped, 1, head).astype(out.dtype)


def finish_kernel(shard_ref, own, returned, swapped, raw_ref, k_gain_ref, *rest):
    *done, key_out, value_out, by_token = rest
    before = [(part, head) for part in done for head in range(part.shape[1])]
    for kind, out in ((0, key_out), (1, value_out)):
        for place, (part, head) in enumerate(before):
            by_token[:, place, :] = part[kind, head].astype(jnp.float32)
        for head in range(own.shape[1]):
            grad = closed(shard_ref, own, returned, swapped, kind, head)
            if kind == 0:
                raw = raw_ref[0, head].astype(jnp.float32)
                grad = norm_back(grad, raw, inverse_rms_of(raw), k_gain_ref[...])
            by_token[:, len(before) + head, :] = grad
        out[...] = by_token[...].astype(out.dtype)


def later_kernel(*refs):
    pass


def later(array):
    anywhere = pl.BlockSpec(memory_space=pl.ANY)
    return pl.pallas_call(
        later_kernel,
        in_specs=[anywhere],
        out_specs=anywhere,
        out_shape=jax.ShapeDtypeStruct(array.shape, array.dtype),
        input_output_aliases={0: 0},
        cost_estimate=HEAVY,
    )(array)


def group_grads(shard, first, here, count, queries, grads, own, near, far, q_gain, k_gain):
    _, _, rows, width = own.shape
    query_rows = queries.shape[1]
    span = WINDOW + rows
    whole_q = pl.BlockSpec((1, query_rows, width), lambda head: (first + head, 0, 0))
    part = pl.BlockSpec((2, 1, rows, width), lambda head: (0, head, 0, 0))
    held = pl.BlockSpec((2, 1, rows, width), lambda head: (0, here + head, 0, 0))
    gain = pl.BlockSpec((1, width), lambda head: (0, 0))
    shape = (2, count, rows, width)
    return pl.pallas_call(
        heads_kernel,
        grid=(count,),
        in_specs=[
            pl.BlockSpec(memory_space=pltpu.SMEM), whole_q, whole_q, held, held, held, gain, gain,
        ],
        out_specs=[
            pl.BlockSpec((1, query_rows, width), lambda head: (head, 0, 0)),
            part,
            part,
            part,
            pl.BlockSpec((2, width), lambda head: (0, 0)),
        ],
        out_shape=[
            jax.ShapeDtypeStruct((count, query_rows, width), jnp.bfloat16),
            jax.ShapeDtypeStruct(shape, jnp.bfloat16),
            jax.ShapeDtypeStruct(shape, jnp.bfloat16),
            jax.ShapeDtypeStruct(shape, jnp.bfloat16),
            jax.ShapeDtypeStruct((2, width), jnp.float32),
        ],
        scratch_shapes=[
            pltpu.VMEM((span, width), jnp.bfloat16),
            pltpu.VMEM((width, span), jnp.bfloat16),
            pltpu.VMEM((span, width), jnp.bfloat16),
            pltpu.VMEM((query_rows, width), jnp.bfloat16),
            pltpu.VMEM((span, query_rows), jnp.bfloat16),
            pltpu.VMEM((span, query_rows), jnp.bfloat16),
        ],
        compiler_params=pltpu.CompilerParams(vmem_limit_bytes=60 * 1024 * 1024),
        cost_estimate=LIGHT,
    )(shard, queries, grads, own, near, far, q_gain, k_gain)


def close_group(shard, own, returned, swapped, raw, k_gain):
    smem, vmem = (pl.BlockSpec(memory_space=space) for space in (pltpu.SMEM, pltpu.VMEM))
    return pl.pallas_call(
        close_kernel,
        in_specs=[smem] + [vmem] * 5,
        out_specs=vmem,
        out_shape=jax.ShapeDtypeStruct(own.shape, jnp.bfloat16),
        cost_estimate=LIGHT,
    )(shard, own, returned, swapped, raw, k_gain)


def finish(shard, own, returned, swapped, raw, k_gain, done):
    _, count, rows, width = own.shape
    kv_dev = count + sum(part.shape[1] for part in done)
    shape = (rows, kv_dev, width)
    smem, vmem = (pl.BlockSpec(memory_space=space) for space in (pltpu.SMEM, pltpu.VMEM))
    return pl.pallas_call(
        finish_kernel,
        in_specs=[smem] + [vmem] * (5 + len(done)),
        out_specs=[vmem, vmem],
        out_shape=[jax.ShapeDtypeStruct(shape, jnp.bfloat16)] * 2,
        scratch_shapes=[pltpu.VMEM(shape, jnp.float32)],
        compiler_params=pltpu.CompilerParams(vmem_limit_bytes=40 * 1024 * 1024),
    )(shard, own, returned, swapped, raw, k_gain, *done)


def group_sizes(kv_dev):
    count = min(GROUPS, kv_dev)
    return [(kv_dev + count - 1 - place) // count for place in range(count)]


def summed(value, axis, step, stop=None):
    count = lax.axis_size(axis)
    assert count & (count - 1) == 0
    while step < (stop or count):
        pairs = [(source, source ^ step) for source in range(count)]
        value = value + lax.ppermute(value, axis, pairs)
        step *= 2
    return value


def per_device(query, key, value, grad_out, q_gain, k_gain):
    rows, heads, width = query.shape
    kv_dev = key.shape[1]
    group = heads // kv_dev
    count = lax.axis_size("seq")
    assert 2 * rows == WINDOW and rows % TILE == 0 and count % 2 == 0
    shard = lax.axis_index("seq")
    odd = shard % 2 == 1
    ahead = [(source, source + 2) for source in range(count - 2)]
    back = [(source + 2, source) for source in range(count - 2)]
    swap = [(source, source ^ 1) for source in range(count)]

    def by_head(array):
        split = array.reshape(rows, kv_dev, group, width)
        return jnp.transpose(split, (1, 0, 2, 3)).reshape(kv_dev, rows * group, width)

    sizes = group_sizes(kv_dev)
    starts = [sum(sizes[:place]) for place in range(len(sizes))]
    cuts = [(0, sizes[0])] + ([(sizes[0], kv_dev)] if len(sizes) > 1 else [])
    by_kind = lax.optimization_barrier([jnp.transpose(kind, (1, 0, 2)) for kind in (key, value)])
    owns = [jnp.stack([kind[low:high] for kind in by_kind]) for low, high in cuts]
    fars = [lax.ppermute(own, "seq", ahead) for own in owns]
    queries, grads = by_head(query), by_head(grad_out)
    scalar = shard.astype(jnp.int32).reshape(1)
    q_gain_2d, k_gain_2d = q_gain.reshape(1, width), k_gain.reshape(1, width)

    def split(d_own, d_near, d_far, raw):
        swapped = lax.ppermute(d_near, "seq", swap)
        from_pair = jnp.where(odd, swapped.astype(jnp.float32), 0.0)
        relayed = (d_far.astype(jnp.float32) + from_pair).astype(jnp.bfloat16)
        return relayed, (d_own, swapped, raw)

    def close(stays, returned):
        d_own, swapped, raw = stays
        return close_group(scalar, d_own, returned, swapped, raw, k_gain_2d)

    dq_parts, gains, kept, done = [], [], [], []
    grads_out = None
    for place, (first, size) in enumerate(zip(starts, sizes, strict=True)):
        if grads_out is not None:
            relayed, stays = split(*grads_out)
        if place < 2:
            own, far, start = owns[place], fars[place], cuts[place][0]
            if place:
                far, relayed = lax.optimization_barrier((later(far), relayed))
            else:
                far, queries, grads, *_ = lax.optimization_barrier(
                    (far, queries, grads, *owns[1:])
                )
            near = lax.ppermute(jnp.where(odd, far, own), "seq", swap)
        if grads_out is not None:
            if kept:
                before, returned = kept.pop()
                near, returned, relayed = lax.optimization_barrier((near, later(returned), relayed))
                done.append(close(before, returned))
            kept.append((stays, lax.ppermute(relayed, "seq", back)))
        here = slice(first - start, first - start + size)
        dq, *grads_out, gain = group_grads(
            scalar, first, first - start, size, queries, grads, own, near, far, q_gain_2d, k_gain_2d
        )
        grads_out.append(own[:1, here])
        dq_parts.append(dq)
        gains.append(gain)
    relayed, stays = split(*grads_out)
    gain_sum = sum(gains[1:], gains[0])
    if kept:
        before, returned = kept.pop()
        returned, gain_sum = lax.optimization_barrier((later(returned), gain_sum))
        done.append(close(before, returned))
    gain_sum = summed(gain_sum, "seq", 2)
    relayed, gain_sum = lax.optimization_barrier((relayed, gain_sum))
    returned = lax.ppermute(relayed, "seq", back)
    gain_sum = summed(gain_sum, "seq", 1, 2)
    gain_sum = summed(gain_sum, "head", 1)
    d_own, swapped, raw = stays
    grad_key, grad_value = finish(scalar, d_own, returned, swapped, raw, k_gain_2d, done)
    grad_query = jnp.concatenate(dq_parts).reshape(kv_dev, rows, group, width)
    grad_query = jnp.transpose(grad_query, (1, 0, 2, 3)).reshape(rows, heads, width)
    return (grad_query, grad_key, grad_value, gain_sum[0], gain_sum[1])


def solution(mesh):
    split, whole = P("seq", "head", None), P()
    return jax.shard_map(
        per_device,
        mesh=mesh,
        in_specs=(split, split, split, split, whole, whole),
        out_specs=(split, split, split, whole, whole),
        check_vma=False,
    )
```

profile of v0, /device:TPU:0, one launch (start us, length us, event | category | flops | bytes accessed | tf_op | source)
XLA Modules:
  0.0 139.6 jit_solution(2254767150913212714)
XLA Ops:
  0.6 1.9 %copy_bitcast_fusion = (bf16[8,512,128]{2,1,0:T(8,128)(2,1)S(1)}, bf16[8,512,128]{2,1,0:T(8,128)(2,1)S(1)}) fusion(bf16[512,8,128]{2,1,0:T(8,128)(2,1)} %param.8, bf16[512,8,128]{2,1,0:T(8,128)(2,1)} %param.7), kind=kLoop, calls=%fused_computation.5 | loop fusion | bytes 4194304 | tf_op jit(solution)/shard_map/transpose | solution.py:301
  3.7 5.8 %collective-permute-start = (bf16[2,3,512,128]{3,2,1,0:T(8,128)(2,1)}, bf16[2,3,512,128]{3,2,1,0:T(8,128)(2,1)}, u32[]{:S(2)}, u32[]{:S(2)}) collective-permute-start(bf16[2,3,512,128]{3,2,1,0:T(8,128)(2,1)} %pad_maximum_fusion.2.own_ref), channel_id=1, source_target_pairs={{0,4},{2,6},{4,8},{6,10},{8,12},{10,14},{12,16},{14,18},{16,20},{1... | collective-permute-start | bytes 2359304 | tf_op jit(solution)/shard_map/ppermute | solution.py:303
  10.7 2.6 %collective-permute-start.2 = (bf16[2,5,512,128]{3,2,1,0:T(8,128)(2,1)S(1)}, bf16[2,5,512,128]{3,2,1,0:T(8,128)(2,1)S(1)}, u32[]{:S(2)}, u32[]{:S(2)}) collective-permute-start(bf16[2,5,512,128]{3,2,1,0:T(8,128)(2,1)S(1)} %pad_maximum_fusion.1.own_ref), channel_id=1, source_target_pairs={{0,4},{2,6},{4,8},{6,10},{8,12},{10,14},{12,16},{14,18},{16,20},{1... | collective-permute-start | bytes 3932168 | tf_op jit(solution)/shard_map/ppermute | solution.py:303
  13.3 4.5 %copy.16 = bf16[512,8,2,128]{3,2,0,1:T(2,128)(2,1)} copy(bf16[512,8,2,128]{3,2,1,0:T(2,128)(2,1)} %bitcast.44) | data formatting | bytes 4194304 | tf_op jit(solution)/shard_map/reshape | solution.py:295
  17.8 3.0 %copy.17 = bf16[512,8,2,128]{3,2,0,1:T(2,128)(2,1)} copy(bf16[512,8,2,128]{3,2,1,0:T(2,128)(2,1)S(1)} %bitcast.45) | data formatting | bytes 4194304 | tf_op jit(solution)/shard_map/reshape | solution.py:295
  20.8 6.0 %collective-permute-done.far_ref = bf16[2,3,512,128]{3,2,1,0:T(8,128)(2,1)} collective-permute-done((bf16[2,3,512,128]{3,2,1,0:T(8,128)(2,1)}, bf16[2,3,512,128]{3,2,1,0:T(8,128)(2,1)}, u32[]{:S(2)}, u32[]{:S(2)}) %collective-permute-start) | collective-permute-done | bytes 786464 | tf_op jit(solution)/shard_map/ppermute | solution.py:303
  27.0 2.3 %collective-permute-done.1.near_ref = bf16[2,3,512,128]{3,2,1,0:T(8,128)(2,1)S(1)} collective-permute-done((bf16[2,3,512,128]{3,2,1,0:T(8,128)(2,1)S(1)}, bf16[2,3,512,128]{3,2,1,0:T(8,128)(2,1)S(1)}, u32[]{:S(2)}, u32[]{:S(2)}) %collective-permute-start.1) | collective-permute-done | bytes 786464 | tf_op jit(solution)/shard_map/ppermute | solution.py:331
  30.2 18.2 %shard_map.101 = (bf16[3,1024,128]{2,1,0:T(8,128)(2,1)}, bf16[2,3,512,128]{3,2,1,0:T(8,128)(2,1)}, bf16[2,3,512,128]{3,2,1,0:T(8,128)(2,1)}, bf16[2,3,512,128]{3,2,1,0:T(8,128)(2,1)}, f32[2,128]{1,0:T(2,128)}) custom-call(s32[1]{0:T(128)} %bitcast.shard_ref, bf16[8,1024,128]{2,1,0:T(8,128)(2,1)} %bitcast.37, bf16[8,1024,128]{2,1,0:T(8,128)(2,1)} %bitcast.40, ...), custom_call_target="tpu_custom_call" | custom-call | flops 1000 | bytes 1000 | tf_op jit(solution)/shard_map/pallas_call | solution.py:208
  48.5 5.1 %collective-permute-done.2.refs_0_ = bf16[2,5,512,128]{3,2,1,0:T(8,128)(2,1)S(1)} collective-permute-done((bf16[2,5,512,128]{3,2,1,0:T(8,128)(2,1)S(1)}, bf16[2,5,512,128]{3,2,1,0:T(8,128)(2,1)S(1)}, u32[]{:S(2)}, u32[]{:S(2)}) %collective-permute-start.2) | collective-permute-done | bytes 1310752 | tf_op jit(solution)/shard_map/ppermute | solution.py:303
  54.8 1.8 %add_convert_fusion.1 = bf16[2,3,512,128]{3,2,1,0:T(8,128)(2,1)S(1)} fusion(bf16[2,3,512,128]{3,2,1,0:T(8,128)(2,1)} %collective-permute-done.3.swapped, bf16[2,3,512,128]{3,2,1,0:T(8,128)(2,1)} %get-tuple-element.42, pred[]{:T(512)S(6)} %eq.5), kind=kLoop, calls=%fused_computation.2 | loop fusion | flops 1966080 | bytes 2359297 | tf_op jit(solution)/shard_map/convert_element_type | solution.py:311
  61.1 18.2 %shard_map.103 = (bf16[3,1024,128]{2,1,0:T(8,128)(2,1)}, bf16[2,3,512,128]{3,2,1,0:T(8,128)(2,1)}, bf16[2,3,512,128]{3,2,1,0:T(8,128)(2,1)}, bf16[2,3,512,128]{3,2,1,0:T(8,128)(2,1)}, f32[2,128]{1,0:T(2,128)}) custom-call(s32[1]{0:T(128)} %bitcast.shard_ref, bf16[8,1024,128]{2,1,0:T(8,128)(2,1)} %bitcast.38, bf16[8,1024,128]{2,1,0:T(8,128)(2,1)} %bitcast.41, ...), custom_call_target="tpu_custom_call" | custom-call | flops 1000 | bytes 1000 | tf_op jit(solution)/shard_map/pallas_call | solution.py:208
  79.6 2.2 %collective-permute-done.6.swapped = bf16[2,3,512,128]{3,2,1,0:T(8,128)(2,1)S(1)} collective-permute-done((bf16[2,3,512,128]{3,2,1,0:T(8,128)(2,1)}, bf16[2,3,512,128]{3,2,1,0:T(8,128)(2,1)S(1)}, u32[]{:S(2)}, u32[]{:S(2)}) %collective-permute-start.6) | collective-permute-done | bytes 786464 | tf_op jit(solution)/shard_map/ppermute | solution.py:309
  81.8 1.7 %add_convert_fusion = bf16[2,3,512,128]{3,2,1,0:T(8,128)(2,1)S(1)} fusion(bf16[2,3,512,128]{3,2,1,0:T(8,128)(2,1)S(1)} %collective-permute-done.6.swapped, bf16[2,3,512,128]{3,2,1,0:T(8,128)(2,1)} %get-tuple-element.47, pred[]{:T(512)S(6)} %eq.5), kind=kLoop, calls=%fused_computation.1 | loop fusion | flops 1966080 | bytes 2359297 | tf_op jit(solution)/shard_map/convert_element_type | solution.py:311
  84.8 12.9 %shard_map.105 = (bf16[2,1024,128]{2,1,0:T(8,128)(2,1)}, bf16[2,2,512,128]{3,2,1,0:T(8,128)(2,1)}, bf16[2,2,512,128]{3,2,1,0:T(8,128)(2,1)}, bf16[2,2,512,128]{3,2,1,0:T(8,128)(2,1)}, f32[2,128]{1,0:T(2,128)}) custom-call(s32[1]{0:T(128)} %bitcast.shard_ref, bf16[8,1024,128]{2,1,0:T(8,128)(2,1)} %bitcast.39, bf16[8,1024,128]{2,1,0:T(8,128)(2,1)} %bitcast.42, ...), custom_call_target="tpu_custom_call" | custom-call | flops 1000 | bytes 1000 | tf_op jit(solution)/shard_map/pallas_call | solution.py:208
  98.6 7.1 %collective-permute-done.8.refs_0_ = bf16[2,3,512,128]{3,2,1,0:T(8,128)(2,1)S(1)} collective-permute-done((bf16[2,3,512,128]{3,2,1,0:T(8,128)(2,1)S(1)}, bf16[2,3,512,128]{3,2,1,0:T(8,128)(2,1)S(1)}, u32[]{:S(2)}, u32[]{:S(2)}) %collective-permute-start.8) | collective-permute-done | bytes 786464 | tf_op jit(solution)/shard_map/ppermute | solution.py:337
  106.6 2.7 %collective-permute-start.9 = (f32[2,128]{1,0:T(2,128)S(1)}, f32[2,128]{1,0:T(2,128)S(1)}, u32[]{:S(2)}, u32[]{:S(2)}) collective-permute-start(f32[2,128]{1,0:T(2,128)S(1)} %add_add_fusion), channel_id=1, source_target_pairs={{0,4},{2,6},{4,0},{6,2},{8,12},{10,14},{12,8},{14,10},{16,20},{18,... | collective-permute-start | bytes 3080 | tf_op jit(solution)/shard_map/ppermute | solution.py:277
  109.3 1.5 %collective-permute-done.9 = f32[2,128]{1,0:T(2,128)S(1)} collective-permute-done((f32[2,128]{1,0:T(2,128)S(1)}, f32[2,128]{1,0:T(2,128)S(1)}, u32[]{:S(2)}, u32[]{:S(2)}) %collective-permute-start.9) | collective-permute-done | bytes 1056 | tf_op jit(solution)/shard_map/ppermute | solution.py:277
  110.9 2.1 %collective-permute-start.10 = (f32[2,128]{1,0:T(2,128)S(1)}, f32[2,128]{1,0:T(2,128)S(1)}, u32[]{:S(2)}, u32[]{:S(2)}) collective-permute-start(f32[2,128]{1,0:T(2,128)S(1)} %add.40), channel_id=1, source_target_pairs={{0,8},{2,10},{4,12},{6,14},{8,0},{10,2},{12,4},{14,6},{16,24},{18,... | collective-permute-start | bytes 3080 | tf_op jit(solution)/shard_map/ppermute | solution.py:277
  113.0 1.5 %collective-permute-done.10 = f32[2,128]{1,0:T(2,128)S(1)} collective-permute-done((f32[2,128]{1,0:T(2,128)S(1)}, f32[2,128]{1,0:T(2,128)S(1)}, u32[]{:S(2)}, u32[]{:S(2)}) %collective-permute-start.10) | collective-permute-done | bytes 1056 | tf_op jit(solution)/shard_map/ppermute | solution.py:277
  114.6 3.0 %collective-permute-start.11 = (f32[2,128]{1,0:T(2,128)S(1)}, f32[2,128]{1,0:T(2,128)S(1)}, u32[]{:S(2)}, u32[]{:S(2)}) collective-permute-start(f32[2,128]{1,0:T(2,128)S(1)} %add.41), channel_id=1, source_target_pairs={{0,16},{2,18},{4,20},{6,22},{8,24},{10,26},{12,28},{14,30},{16,0},... | collective-permute-start | bytes 3080 | tf_op jit(solution)/shard_map/ppermute | solution.py:277
  123.6 3.4 %shard_map.107.rest_0_ = bf16[2,3,512,128]{3,2,1,0:T(8,128)(2,1)} custom-call(s32[1]{0:T(128)} %bitcast.shard_ref, bf16[2,3,512,128]{3,2,1,0:T(8,128)(2,1)} %get-tuple-element.60.own, bf16[2,3,512,128]{3,2,1,0:T(8,128)(2,1)} %shard_map.104.returned, bf16[2,3,512,128]{3,2,1,0:T(8,128)(2,1)} %collective-permute-done.3.swapped, ...), custom_call_target="tpu_custom_call" | custom-call | flops 1000 | bytes 1000 | tf_op jit(solution)/shard_map/pallas_call | solution.py:243
  127.0 2.8 %copy.18 = bf16[512,8,2,128]{3,2,1,0:T(2,128)(2,1)} copy(bf16[512,8,2,128]{3,2,0,1:T(2,128)(2,1)S(1)} %bitcast.43) | data formatting | bytes 4194304 | tf_op jit(solution)/shard_map/transpose | solution.py:359
  129.8 3.5 %shard_map.108.rest_1_ = bf16[2,3,512,128]{3,2,1,0:T(8,128)(2,1)} custom-call(s32[1]{0:T(128)} %bitcast.shard_ref, bf16[2,3,512,128]{3,2,1,0:T(8,128)(2,1)} %get-tuple-element.62.own, bf16[2,3,512,128]{3,2,1,0:T(8,128)(2,1)} %shard_map.106.returned, bf16[2,3,512,128]{3,2,1,0:T(8,128)(2,1)} %copy-done.16, bf16[1,3,512,128]{3,2,1,0:T(8,128)(2,1)} %slice.33.raw_ref, ...), custom_call_target="tpu_custom_call" | custom-call | flops 1000 | bytes 1000 | tf_op jit(solution)/shard_map/pallas_call | solution.py:243
  135.0 4.7 %shard_map.109 = (bf16[512,8,128]{2,1,0:T(8,128)(2,1)}, bf16[512,8,128]{2,1,0:T(8,128)(2,1)}) custom-call(s32[1]{0:T(128)} %bitcast.shard_ref, bf16[2,2,512,128]{3,2,1,0:T(8,128)(2,1)S(1)} %copy-done.2, bf16[2,2,512,128]{3,2,1,0:T(8,128)(2,1)S(1)} %collective-permute-done.12.returned, bf16[2,2,512,128]{3,2,1,0:T(8,128)(2,1)S(1)} %collective-permute-done.7.swapped, ...), custom_call_target="tpu_custom_call" | custom-call | tf_op jit(solution)/shard_map/pallas_call | solution.py:257
  (92 shorter events, 20.2 us)
Async XLA Ops:
  3.7 23.1 %collective-permute-start = (bf16[2,3,512,128]{3,2,1,0:T(8,128)(2,1)}, bf16[2,3,512,128]{3,2,1,0:T(8,128)(2,1)}, u32[]{:S(2)}, u32[]{:S(2)}) collective-permute-start(bf16[2,3,512,128]{3,2,1,0:T(8,128)(2,1)} %pad_maximum_fusion.2.own_ref), channel_id=1, source_target_pairs={{0,4},{2,6},{4,8},{6,10},{8,12},{10,14},{12,16},{14,18},{16,20},{1... | collective-permute-start | bytes 2359304 | tf_op jit(solution)/shard_map/ppermute | solution.py:303
  9.5 47.0 %copy-start.7 = (bf16[1,5,512,128]{3,2,1,0:T(8,128)(2,1)}, bf16[1,5,512,128]{3,2,1,0:T(8,128)(2,1)S(1)}, u32[]{:S(2)}) copy-start(bf16[1,5,512,128]{3,2,1,0:T(8,128)(2,1)S(1)} %slice_bitcast_fusion.1) | copy-start | bytes 1966084
  10.7 43.0 %collective-permute-start.2 = (bf16[2,5,512,128]{3,2,1,0:T(8,128)(2,1)S(1)}, bf16[2,5,512,128]{3,2,1,0:T(8,128)(2,1)S(1)}, u32[]{:S(2)}, u32[]{:S(2)}) collective-permute-start(bf16[2,5,512,128]{3,2,1,0:T(8,128)(2,1)S(1)} %pad_maximum_fusion.1.own_ref), channel_id=1, source_target_pairs={{0,4},{2,6},{4,8},{6,10},{8,12},{10,14},{12,16},{14,18},{16,20},{1... | collective-permute-start | bytes 3932168 | tf_op jit(solution)/shard_map/ppermute | solution.py:303
  26.9 2.4 %collective-permute-start.1 = (bf16[2,3,512,128]{3,2,1,0:T(8,128)(2,1)S(1)}, bf16[2,3,512,128]{3,2,1,0:T(8,128)(2,1)S(1)}, u32[]{:S(2)}, u32[]{:S(2)}) collective-permute-start(bf16[2,3,512,128]{3,2,1,0:T(8,128)(2,1)S(1)} %broadcast_select_fusion.1), channel_id=1, source_target_pairs={{0,2},{2,0},{4,6},{6,4},{8,10},{10,8},{12,14},{14,12},{16,18},{18,... | collective-permute-start | bytes 2359304 | tf_op jit(solution)/shard_map/ppermute | solution.py:331
  48.4 6.4 %collective-permute-start.3 = (bf16[2,3,512,128]{3,2,1,0:T(8,128)(2,1)}, bf16[2,3,512,128]{3,2,1,0:T(8,128)(2,1)}, u32[]{:S(2)}, u32[]{:S(2)}) collective-permute-start(bf16[2,3,512,128]{3,2,1,0:T(8,128)(2,1)} %get-tuple-element.43), channel_id=1, source_target_pairs={{0,2},{2,0},{4,6},{6,4},{8,10},{10,8},{12,14},{14,12},{16,18},{18,... | collective-permute-start | bytes 2359304 | tf_op jit(solution)/shard_map/ppermute | solution.py:309
  56.9 3.1 %collective-permute-start.4 = (bf16[2,5,512,128]{3,2,1,0:T(8,128)(2,1)S(1)}, bf16[2,5,512,128]{3,2,1,0:T(8,128)(2,1)S(1)}, u32[]{:S(2)}, u32[]{:S(2)}) collective-permute-start(bf16[2,5,512,128]{3,2,1,0:T(8,128)(2,1)S(1)} %broadcast_select_fusion), channel_id=1, source_target_pairs={{0,2},{2,0},{4,6},{6,4},{8,10},{10,8},{12,14},{14,12},{16,18},{18,... | collective-permute-start | bytes 3932168 | tf_op jit(solution)/shard_map/ppermute | solution.py:331
  57.0 22.7 %collective-permute-start.5 = (bf16[2,3,512,128]{3,2,1,0:T(8,128)(2,1)S(1)}, bf16[2,3,512,128]{3,2,1,0:T(8,128)(2,1)}, u32[]{:S(2)}, u32[]{:S(2)}) collective-permute-start(bf16[2,3,512,128]{3,2,1,0:T(8,128)(2,1)S(1)} %add_convert_fusion.1), channel_id=1, source_target_pairs={{4,0},{6,2},{8,4},{10,6},{12,8},{14,10},{16,12},{18,14},{20,16},{2... | collective-permute-start | bytes 2359304 | tf_op jit(solution)/shard_map/ppermute | solution.py:337
  79.3 2.6 %collective-permute-start.6 = (bf16[2,3,512,128]{3,2,1,0:T(8,128)(2,1)}, bf16[2,3,512,128]{3,2,1,0:T(8,128)(2,1)S(1)}, u32[]{:S(2)}, u32[]{:S(2)}) collective-permute-start(bf16[2,3,512,128]{3,2,1,0:T(8,128)(2,1)} %get-tuple-element.48), channel_id=1, source_target_pairs={{0,2},{2,0},{4,6},{6,4},{8,10},{10,8},{12,14},{14,12},{16,18},{18,... | collective-permute-start | bytes 2359304 | tf_op jit(solution)/shard_map/ppermute | solution.py:309
  81.8 15.9 %copy-start.16 = (bf16[2,3,512,128]{3,2,1,0:T(8,128)(2,1)}, bf16[2,3,512,128]{3,2,1,0:T(8,128)(2,1)S(1)}, u32[]{:S(2)}) copy-start(bf16[2,3,512,128]{3,2,1,0:T(8,128)(2,1)S(1)} %collective-permute-done.6.swapped) | copy-start | bytes 2359300
  83.5 14.4 %copy-start.24 = (f32[2,128]{1,0:T(2,128)S(1)}, f32[2,128]{1,0:T(2,128)}, u32[]{:S(2)}) copy-start(f32[2,128]{1,0:T(2,128)} %get-tuple-element.55) | copy-start | bytes 3076
  83.5 14.4 %copy-start.25 = (f32[2,128]{1,0:T(2,128)S(1)}, f32[2,128]{1,0:T(2,128)}, u32[]{:S(2)}) copy-start(f32[2,128]{1,0:T(2,128)} %get-tuple-element.56) | copy-start | bytes 3076
  83.5 22.2 %collective-permute-start.8 = (bf16[2,3,512,128]{3,2,1,0:T(8,128)(2,1)S(1)}, bf16[2,3,512,128]{3,2,1,0:T(8,128)(2,1)S(1)}, u32[]{:S(2)}, u32[]{:S(2)}) collective-permute-start(bf16[2,3,512,128]{3,2,1,0:T(8,128)(2,1)S(1)} %add_convert_fusion), channel_id=1, source_target_pairs={{4,0},{6,2},{8,4},{10,6},{12,8},{14,10},{16,12},{18,14},{20,16},{2... | collective-permute-start | bytes 2359304 | tf_op jit(solution)/shard_map/ppermute | solution.py:337
  97.7 19.9 %collective-permute-start.7 = (bf16[2,2,512,128]{3,2,1,0:T(8,128)(2,1)}, bf16[2,2,512,128]{3,2,1,0:T(8,128)(2,1)S(1)}, u32[]{:S(2)}, u32[]{:S(2)}) collective-permute-start(bf16[2,2,512,128]{3,2,1,0:T(8,128)(2,1)} %get-tuple-element.53), channel_id=1, source_target_pairs={{0,2},{2,0},{4,6},{6,4},{8,10},{10,8},{12,14},{14,12},{16,18},{18,... | collective-permute-start | bytes 1572872 | tf_op jit(solution)/shard_map/ppermute | solution.py:309
  98.6 19.0 %copy-start.22 = (bf16[2,2,512,128]{3,2,1,0:T(8,128)(2,1)S(1)}, bf16[2,2,512,128]{3,2,1,0:T(8,128)(2,1)}, u32[]{:S(2)}) copy-start(bf16[2,2,512,128]{3,2,1,0:T(8,128)(2,1)} %get-tuple-element.52) | copy-start | bytes 1572868
  106.6 14.1 %copy-start.8 = (bf16[1,5,512,128]{3,2,1,0:T(8,128)(2,1)S(1)}, bf16[1,5,512,128]{3,2,1,0:T(8,128)(2,1)}, u32[]{:S(2)}) copy-start(bf16[1,5,512,128]{3,2,1,0:T(8,128)(2,1)} %copy-done.7) | copy-start | bytes 1966084
  106.6 16.7 %copy-start.18 = (bf16[3,1024,128]{2,1,0:T(8,128)(2,1)S(1)}, bf16[3,1024,128]{2,1,0:T(8,128)(2,1)}, u32[]{:S(2)}) copy-start(bf16[3,1024,128]{2,1,0:T(8,128)(2,1)} %get-tuple-element.41) | copy-start | bytes 2359300
  106.6 16.7 %copy-start.19 = (bf16[3,1024,128]{2,1,0:T(8,128)(2,1)S(1)}, bf16[3,1024,128]{2,1,0:T(8,128)(2,1)}, u32[]{:S(2)}) copy-start(bf16[3,1024,128]{2,1,0:T(8,128)(2,1)} %get-tuple-element.45) | copy-start | bytes 2359300
  106.6 16.7 %copy-start.23 = (bf16[2,1024,128]{2,1,0:T(8,128)(2,1)S(1)}, bf16[2,1024,128]{2,1,0:T(8,128)(2,1)}, u32[]{:S(2)}) copy-start(bf16[2,1024,128]{2,1,0:T(8,128)(2,1)} %get-tuple-element.50) | copy-start | bytes 1572868
  106.6 4.2 %collective-permute-start.9 = (f32[2,128]{1,0:T(2,128)S(1)}, f32[2,128]{1,0:T(2,128)S(1)}, u32[]{:S(2)}, u32[]{:S(2)}) collective-permute-start(f32[2,128]{1,0:T(2,128)S(1)} %add_add_fusion), channel_id=1, source_target_pairs={{0,4},{2,6},{4,0},{6,2},{8,12},{10,14},{12,8},{14,10},{16,20},{18,... | collective-permute-start | bytes 3080 | tf_op jit(solution)/shard_map/ppermute | solution.py:277
  110.9 3.7 %collective-permute-start.10 = (f32[2,128]{1,0:T(2,128)S(1)}, f32[2,128]{1,0:T(2,128)S(1)}, u32[]{:S(2)}, u32[]{:S(2)}) collective-permute-start(f32[2,128]{1,0:T(2,128)S(1)} %add.40), channel_id=1, source_target_pairs={{0,8},{2,10},{4,12},{6,14},{8,0},{10,2},{12,4},{14,6},{16,24},{18,... | collective-permute-start | bytes 3080 | tf_op jit(solution)/shard_map/ppermute | solution.py:277
  114.6 4.6 %collective-permute-start.11 = (f32[2,128]{1,0:T(2,128)S(1)}, f32[2,128]{1,0:T(2,128)S(1)}, u32[]{:S(2)}, u32[]{:S(2)}) collective-permute-start(f32[2,128]{1,0:T(2,128)S(1)} %add.41), channel_id=1, source_target_pairs={{0,16},{2,18},{4,20},{6,22},{8,24},{10,26},{12,28},{14,30},{16,0},... | collective-permute-start | bytes 3080 | tf_op jit(solution)/shard_map/ppermute | solution.py:277
  119.2 14.7 %collective-permute-start.12 = (bf16[2,2,512,128]{3,2,1,0:T(8,128)(2,1)}, bf16[2,2,512,128]{3,2,1,0:T(8,128)(2,1)S(1)}, u32[]{:S(2)}, u32[]{:S(2)}) collective-permute-start(bf16[2,2,512,128]{3,2,1,0:T(8,128)(2,1)} %add_convert_fusion.2), channel_id=1, source_target_pairs={{4,0},{6,2},{8,4},{10,6},{12,8},{14,10},{16,12},{18,14},{20,16},{2... | collective-permute-start | bytes 1572872 | tf_op jit(solution)/shard_map/ppermute | solution.py:353
  120.7 1.2 collective-permute-start.13
  121.9 11.4 %collective-permute-start.14 = (f32[2,128]{1,0:T(2,128)S(1)}, f32[2,128]{1,0:T(2,128)S(1)}, u32[]{:S(2)}, u32[]{:S(2)}) collective-permute-start(f32[2,128]{1,0:T(2,128)S(1)} %add.43), channel_id=1, source_target_pairs={{0,1},{1,0},{2,3},{3,2},{4,5},{5,4},{6,7},{7,6},{8,9},{9,8},{10,11... | collective-permute-start | bytes 3080 | tf_op jit(solution)/shard_map/ppermute | solution.py:277
  (17 other events, 65.4 us)
where the time goes:
time: 142 us; the launch traced here: 140 us
  Pallas kernels  60.8 us (43%)
  waiting for transfers between devices  28.4 us (20%)
  starting transfers between devices  22.8 us (16%)
  local copies, waits for them, and re-layouts  19.9 us (14%)
  other arithmetic  6.84 us (5%)
    pallas_call x3, Pallas kernels, group_grads(): pl.pallas_call(heads_kernel, grid=(count,), in_specs=[pl.BlockSpec(memory...  49.3 us
    ppermute x2, waiting for transfers between devices, per_device(): fars = [lax.ppermute(own, 'seq', ahead) for own in owns]  11.1 us
    ppermute x5, starting transfers between devices, summed(): value = value + lax.ppermute(value, axis, pairs)  9.43 us
    ppermute x2, starting transfers between devices, per_device(): fars = [lax.ppermute(own, 'seq', ahead) for own in owns]  8.38 us
    reshape x2, local copies, waits for them, and re-layouts, by_head(): split = array.reshape(rows, kv_dev, group, width)  7.46 us
    ppermute x2, waiting for transfers between devices, per_device(): kept.append((stays, lax.ppermute(relayed, 'seq', back)))  7.33 us
    pallas_call x2, Pallas kernels, close_group(): pl.pallas_call(close_kernel, in_specs=[smem] + [vmem] * 5, out_specs=vmem...  6.9 us
    unnamed x52, local copies, waits for them, and re-layouts  6.25 us
  transfers between devices with their start and end apart: 15, of which 11 were waited for; matrix products, arithmetic and copies ran while one was open for 10% of the time, Pallas kernels for 40%

commit v1 on v0

--- a/solution.py
+++ b/solution.py
@@ -180,20 +180,24 @@
         out[...] = by_token[...].astype(out.dtype)
 
 
-def later_kernel(*refs):
-    pass
-
-
-def later(array):
-    anywhere = pl.BlockSpec(memory_space=pl.ANY)
+def later_kernel(corner_ref, in_ref, out_ref):
+    if len(in_ref.shape) == 1:
+        out_ref[0] = in_ref[0]
+    else:
+        out_ref[...] = in_ref[...]
+
+
+def later(array, small):
+    vmem = pl.BlockSpec(memory_space=pltpu.VMEM)
+    held = pl.BlockSpec(memory_space=pltpu.SMEM if small.ndim == 1 else pltpu.VMEM)
     return pl.pallas_call(
         later_kernel,
-        in_specs=[anywhere],
-        out_specs=anywhere,
-        out_shape=jax.ShapeDtypeStruct(array.shape, array.dtype),
-        input_output_aliases={0: 0},
+        in_specs=[vmem, held],
+        out_specs=held,
+        out_shape=jax.ShapeDtypeStruct(small.shape, small.dtype),
+        compiler_params=pltpu.CompilerParams(vmem_limit_bytes=1024 * 1024),
         cost_estimate=HEAVY,
-    )(array)
+    )(array[0, 0, :16], small)
 
 
 def group_grads(shard, first, here, count, queries, grads, own, near, far, q_gain, k_gain):
@@ -233,7 +237,7 @@
             pltpu.VMEM((span, query_rows), jnp.bfloat16),
             pltpu.VMEM((span, query_rows), jnp.bfloat16),
         ],
-        compiler_params=pltpu.CompilerParams(vmem_limit_bytes=60 * 1024 * 1024),
+        compiler_params=pltpu.CompilerParams(vmem_limit_bytes=22 * 1024 * 1024),
         cost_estimate=LIGHT,
     )(shard, queries, grads, own, near, far, q_gain, k_gain)
 
@@ -245,6 +249,7 @@
         in_specs=[smem] + [vmem] * 5,
         out_specs=vmem,
         out_shape=jax.ShapeDtypeStruct(own.shape, jnp.bfloat16),
+        compiler_params=pltpu.CompilerParams(vmem_limit_bytes=12 * 1024 * 1024),
         cost_estimate=LIGHT,
     )(shard, own, returned, swapped, raw, k_gain)
 
@@ -260,7 +265,7 @@
         out_specs=[vmem, vmem],
         out_shape=[jax.ShapeDtypeStruct(shape, jnp.bfloat16)] * 2,
         scratch_shapes=[pltpu.VMEM(shape, jnp.float32)],
-        compiler_params=pltpu.CompilerParams(vmem_limit_bytes=40 * 1024 * 1024),
+        compiler_params=pltpu.CompilerParams(vmem_limit_bytes=20 * 1024 * 1024),
     )(shard, own, returned, swapped, raw, k_gain, *done)
 
 
@@ -269,14 +274,15 @@
     return [(kv_dev + count - 1 - place) // count for place in range(count)]
 
 
-def summed(value, axis, step, stop=None):
+def exchanged(value, axis, step):
+    pairs = [(source, source ^ step) for source in range(lax.axis_size(axis))]
+    return lax.ppermute(value, axis, pairs)
+
+
+def steps_of(axis):
     count = lax.axis_size(axis)
     assert count & (count - 1) == 0
-    while step < (stop or count):
-        pairs = [(source, source ^ step) for source in range(count)]
-        value = value + lax.ppermute(value, axis, pairs)
-        step *= 2
-    return value
+    return [(axis, 1 << place) for place in range(count.bit_length() - 1)]
 
 
 def per_device(query, key, value, grad_out, q_gain, k_gain):
@@ -323,21 +329,23 @@
         if place < 2:
             own, far, start = owns[place], fars[place], cuts[place][0]
             if place:
-                far, relayed = lax.optimization_barrier((later(far), relayed))
+                far, gains[0] = lax.optimization_barrier((far, gains[0]))
             else:
                 far, queries, grads, *_ = lax.optimization_barrier(
                     (far, queries, grads, *owns[1:])
                 )
             near = lax.ppermute(jnp.where(odd, far, own), "seq", swap)
+        scalar_now = scalar
         if grads_out is not None:
             if kept:
                 before, returned = kept.pop()
-                near, returned, relayed = lax.optimization_barrier((near, later(returned), relayed))
+                scalar_now = later(returned, scalar)
                 done.append(close(before, returned))
+            near, relayed, scalar_now = lax.optimization_barrier((near, relayed, scalar_now))
             kept.append((stays, lax.ppermute(relayed, "seq", back)))
         here = slice(first - start, first - start + size)
         dq, *grads_out, gain = group_grads(
-            scalar, first, first - start, size, queries, grads, own, near, far, q_gain_2d, k_gain_2d
+            scalar_now, first, first - start, size, queries, grads, own, near, far, q_gain_2d, k_gain_2d
         )
         grads_out.append(own[:1, here])
         dq_parts.append(dq)
@@ -346,17 +354,23 @@
     gain_sum = sum(gains[1:], gains[0])
     if kept:
         before, returned = kept.pop()
-        returned, gain_sum = lax.optimization_barrier((later(returned), gain_sum))
+        returned, done = lax.optimization_barrier((returned, done))
+        gain_sum = later(returned, gain_sum)
         done.append(close(before, returned))
-    gain_sum = summed(gain_sum, "seq", 2)
+    core, *chips = steps_of("seq")
+    gain_sum = gain_sum + exchanged(gain_sum, *chips[0])
     relayed, gain_sum = lax.optimization_barrier((relayed, gain_sum))
     returned = lax.ppermute(relayed, "seq", back)
-    gain_sum = summed(gain_sum, "seq", 1, 2)
-    gain_sum = summed(gain_sum, "head", 1)
+    grad_query = jnp.concatenate(dq_parts).reshape(kv_dev, rows, group, width)
+    grad_query = jnp.transpose(grad_query, (1, 0, 2, 3)).reshape(rows, heads, width)
+    *early, last = [core, *steps_of("head"), *chips[1:]]
+    for step in early:
+        gain_sum = gain_sum + exchanged(gain_sum, *step)
+    gain_sum, grad_query, done = lax.optimization_barrier((gain_sum, grad_query, done))
     d_own, swapped, raw = stays
     grad_key, grad_value = finish(scalar, d_own, returned, swapped, raw, k_gain_2d, done)
-    grad_query = jnp.concatenate(dq_parts).reshape(kv_dev, rows, group, width)
-    grad_query = jnp.transpose(grad_query, (1, 0, 2, 3)).reshape(rows, heads, width)
+    other, grad_key = lax.optimization_barrier((exchanged(gain_sum, *last), grad_key))
+    gain_sum = gain_sum + other
     return (grad_query, grad_key, grad_value, gain_sum[0], gain_sum[1])
 
 

time: 142 us -> 130 us (0.915); the launches traced: 140 us -> 130 us
  waiting for transfers between devices: 28.4 us -> 37.4 us
  Pallas kernels: 60.8 us -> 52.2 us
  local copies, waits for them, and re-layouts: 19.9 us -> 11.7 us
  other arithmetic: 6.84 us -> 2.37 us
  starting transfers between devices: 22.8 us -> 25 us
    pallas_call x2, Pallas kernels: 6.9 us -> 1.64 us  [close_group(): pl.pallas_call(close_kernel, in_specs=[smem] + [vmem] * 5, out_specs=vmem...]
    unnamed x52 -> x16, local copies, waits for them, and re-layouts: 6.25 us -> 1.64 us
    ppermute x2, waiting for transfers between devices: 7.33 us -> 11.7 us  [per_device(): kept.append((stays, lax.ppermute(relayed, 'seq', back)))]
    ppermute x2, waiting for transfers between devices: 11.1 us -> 15.1 us  [per_device(): fars = [lax.ppermute(own, 'seq', ahead) for own in owns]]
    pallas_call x3, Pallas kernels: 49.3 us -> 45.3 us  [group_grads(): pl.pallas_call(heads_kernel, grid=(count,), in_specs=[pl.BlockSpec(memory...]
    convert_element_type x3, other arithmetic: 4.44 us -> 0.69 us  [split(): relayed = (d_far.astype(jnp.float32) + from_pair).astype(jnp.bfloat16)]
    reshape x2, local copies, waits for them, and re-layouts: 7.46 us -> 4.62 us  [by_head(): split = array.reshape(rows, kv_dev, group, width)]
    ppermute x5, starting transfers between devices: 9.43 us -> 11.2 us  [exchanged(): return lax.ppermute(value, axis, pairs)]
  transfers between devices with their start and end apart: 15 -> 15, of which waited for: 11 -> 10; matrix products, arithmetic and copies ran while one was open for 10% -> 7% of each run, Pallas kernels for 40% -> 40%
where the time goes in v1:
time: 130 us
  Pallas kernels  52.2 us (40%)
  waiting for transfers between devices  37.4 us (29%)
  starting transfers between devices  25 us (19%)
  local copies, waits for them, and re-layouts  11.7 us (9%)
  other arithmetic  2.37 us (2%)
    pallas_call x3, Pallas kernels, group_grads(): pl.pallas_call(heads_kernel, grid=(count,), in_specs=[pl.BlockSpec(memory...  45.3 us
    ppermute x2, waiting for transfers between devices, per_device(): fars = [lax.ppermute(own, 'seq', ahead) for own in owns]  15.1 us
    ppermute x2, waiting for transfers between devices, per_device(): kept.append((stays, lax.ppermute(relayed, 'seq', back)))  11.7 us
    ppermute x5, starting transfers between devices, exchanged(): return lax.ppermute(value, axis, pairs)  11.2 us
    ppermute x2, starting transfers between devices, per_device(): fars = [lax.ppermute(own, 'seq', ahead) for own in owns]  8.38 us
    pallas_call x1, Pallas kernels, finish(): pl.pallas_call(finish_kernel, in_specs=[smem] + [vmem] * (5 + len(done)),...  4.7 us
    ppermute x5, waiting for transfers between devices, exchanged(): return lax.ppermute(value, axis, pairs)  4.7 us
    reshape x2, local copies, waits for them, and re-layouts, by_head(): split = array.reshape(rows, kv_dev, group, width)  4.62 us
  transfers between devices with their start and end apart: 15, of which 10 were waited for; matrix products, arithmetic and copies ran while one was open for 7% of the time, Pallas kernels for 40%

profile of v1, /device:TPU:0, one launch (start us, length us, event | category | flops | bytes accessed | tf_op | source)
XLA Modules:
  0.0 129.5 jit_solution(7383046350075565944)
XLA Ops:
  0.6 1.9 %copy_bitcast_fusion = (bf16[8,512,128]{2,1,0:T(8,128)(2,1)S(1)}, bf16[8,512,128]{2,1,0:T(8,128)(2,1)S(1)}) fusion(bf16[512,8,128]{2,1,0:T(8,128)(2,1)} %param.8, bf16[512,8,128]{2,1,0:T(8,128)(2,1)} %param.7), kind=kLoop, calls=%fused_computation.5 | loop fusion | bytes 4194304 | tf_op jit(solution)/shard_map/transpose | solution.py:307
  3.6 5.8 %collective-permute-start.1 = (bf16[2,3,512,128]{3,2,1,0:T(8,128)(2,1)}, bf16[2,3,512,128]{3,2,1,0:T(8,128)(2,1)}, u32[]{:S(2)}, u32[]{:S(2)}) collective-permute-start(bf16[2,3,512,128]{3,2,1,0:T(8,128)(2,1)} %pad_maximum_fusion.2.own_ref), channel_id=1, source_target_pairs={{0,4},{2,6},{4,8},{6,10},{8,12},{10,14},{12,16},{14,18},{16,20},{1... | collective-permute-start | bytes 2359304 | tf_op jit(solution)/shard_map/ppermute | solution.py:309
  11.2 2.6 %collective-permute-start = (bf16[2,5,512,128]{3,2,1,0:T(8,128)(2,1)S(1)}, bf16[2,5,512,128]{3,2,1,0:T(8,128)(2,1)S(1)}, u32[]{:S(2)}, u32[]{:S(2)}) collective-permute-start(bf16[2,5,512,128]{3,2,1,0:T(8,128)(2,1)S(1)} %pad_maximum_fusion.1.own_ref), channel_id=1, source_target_pairs={{0,4},{2,6},{4,8},{6,10},{8,12},{10,14},{12,16},{14,18},{16,20},{1... | collective-permute-start | bytes 3932168 | tf_op jit(solution)/shard_map/ppermute | solution.py:309
  13.8 3.2 %copy.14 = bf16[512,8,2,128]{3,2,0,1:T(2,128)(2,1)S(1)} copy(bf16[512,8,2,128]{3,2,1,0:T(2,128)(2,1)} %bitcast.51) | data formatting | bytes 4194304 | tf_op jit(solution)/shard_map/reshape | solution.py:301
  17.0 1.4 %copy.13 = bf16[512,8,2,128]{3,2,0,1:T(2,128)(2,1)S(1)} copy(bf16[512,8,2,128]{3,2,1,0:T(2,128)(2,1)S(1)} %bitcast.52) | data formatting | bytes 4194304 | tf_op jit(solution)/shard_map/reshape | solution.py:301
  18.5 8.2 %collective-permute-done.1.far_ref = bf16[2,3,512,128]{3,2,1,0:T(8,128)(2,1)} collective-permute-done((bf16[2,3,512,128]{3,2,1,0:T(8,128)(2,1)}, bf16[2,3,512,128]{3,2,1,0:T(8,128)(2,1)}, u32[]{:S(2)}, u32[]{:S(2)}) %collective-permute-start.1) | collective-permute-done | bytes 786464 | tf_op jit(solution)/shard_map/ppermute | solution.py:309
  26.9 2.3 %collective-permute-done.2.near_ref = bf16[2,3,512,128]{3,2,1,0:T(8,128)(2,1)S(1)} collective-permute-done((bf16[2,3,512,128]{3,2,1,0:T(8,128)(2,1)S(1)}, bf16[2,3,512,128]{3,2,1,0:T(8,128)(2,1)S(1)}, u32[]{:S(2)}, u32[]{:S(2)}) %collective-permute-start.2) | collective-permute-done | bytes 786464 | tf_op jit(solution)/shard_map/ppermute | solution.py:337
  29.2 17.4 %shard_map.101 = (bf16[3,1024,128]{2,1,0:T(8,128)(2,1)S(1)}, bf16[2,3,512,128]{3,2,1,0:T(8,128)(2,1)S(1)}, bf16[2,3,512,128]{3,2,1,0:T(8,128)(2,1)S(1)}, bf16[2,...) custom-call(s32[1]{0:T(128)} %bitcast.4.shard_ref.in_ref, bf16[8,1024,128]{2,1,0:T(8,128)(2,1)S(1)} %bitcast.38, ...), custom_call_target="tpu_custom_call" | custom-call | flops 1000 | bytes 1000 | tf_op jit(solution)/shard_map/pallas_call | solution.py:212
  46.6 6.9 %collective-permute-done.far_ref = bf16[2,5,512,128]{3,2,1,0:T(8,128)(2,1)S(1)} collective-permute-done((bf16[2,5,512,128]{3,2,1,0:T(8,128)(2,1)S(1)}, bf16[2,5,512,128]{3,2,1,0:T(8,128)(2,1)S(1)}, u32[]{:S(2)}, u32[]{:S(2)}) %collective-permute-start) | collective-permute-done | bytes 1310752 | tf_op jit(solution)/shard_map/ppermute | solution.py:309
  54.3 3.6 %collective-permute-done.4.swapped = bf16[2,3,512,128]{3,2,1,0:T(8,128)(2,1)S(1)} collective-permute-done((bf16[2,3,512,128]{3,2,1,0:T(8,128)(2,1)S(1)}, bf16[2,3,512,128]{3,2,1,0:T(8,128)(2,1)S(1)}, u32[]{:S(2)}, u32[]{:S(2)}) %collective-permute-start.4) | collective-permute-done | bytes 786464 | tf_op jit(solution)/shard_map/ppermute | solution.py:315
  58.2 1.5 %collective-permute-start.6 = (bf16[2,3,512,128]{3,2,1,0:T(8,128)(2,1)S(1)}, bf16[2,3,512,128]{3,2,1,0:T(8,128)(2,1)S(1)}, u32[]{:S(2)}, u32[]{:S(2)}) collective-permute-start(bf16[2,3,512,128]{3,2,1,0:T(8,128)(2,1)S(1)} %add_convert_fusion.1), channel_id=1, source_target_pairs={{4,0},{6,2},{8,4},{10,6},{12,8},{14,10},{16,12},{18,14},{20,16},{2... | collective-permute-start | bytes 2359304 | tf_op jit(solution)/shard_map/ppermute | solution.py:345
  59.7 16.4 %shard_map.102 = (bf16[3,1024,128]{2,1,0:T(8,128)(2,1)S(1)}, bf16[2,3,512,128]{3,2,1,0:T(8,128)(2,1)S(1)}, bf16[2,3,512,128]{3,2,1,0:T(8,128)(2,1)S(1)}, bf16[2,...) custom-call(s32[1]{0:T(128)} %bitcast.4.shard_ref.in_ref, bf16[8,1024,128]{2,1,0:T(8,128)(2,1)S(1)} %bitcast.39, ...), custom_call_target="tpu_custom_call" | custom-call | flops 1000 | bytes 1000 | tf_op jit(solution)/shard_map/pallas_call | solution.py:212
  76.3 4.2 %collective-permute-done.6.returned = bf16[2,3,512,128]{3,2,1,0:T(8,128)(2,1)S(1)} collective-permute-done((bf16[2,3,512,128]{3,2,1,0:T(8,128)(2,1)S(1)}, bf16[2,3,512,128]{3,2,1,0:T(8,128)(2,1)S(1)}, u32[]{:S(2)}, u32[]{:S(2)}) %collective-permute-start.6) | collective-permute-done | bytes 786464 | tf_op jit(solution)/shard_map/ppermute | solution.py:345
  81.2 1.5 %collective-permute-start.8 = (bf16[2,3,512,128]{3,2,1,0:T(8,128)(2,1)S(1)}, bf16[2,3,512,128]{3,2,1,0:T(8,128)(2,1)S(1)}, u32[]{:S(2)}, u32[]{:S(2)}) collective-permute-start(bf16[2,3,512,128]{3,2,1,0:T(8,128)(2,1)S(1)} %add_convert_fusion), channel_id=1, source_target_pairs={{4,0},{6,2},{8,4},{10,6},{12,8},{14,10},{16,12},{18,14},{20,16},{2... | collective-permute-start | bytes 2359304 | tf_op jit(solution)/shard_map/ppermute | solution.py:345
  82.8 11.6 %shard_map.104 = (bf16[2,1024,128]{2,1,0:T(8,128)(2,1)S(1)}, bf16[2,2,512,128]{3,2,1,0:T(8,128)(2,1)S(1)}, bf16[2,2,512,128]{3,2,1,0:T(8,128)(2,1)S(1)}, bf16[2,...) custom-call(s32[1]{0:T(128)} %shard_map.103.shard_ref, bf16[8,1024,128]{2,1,0:T(8,128)(2,1)S(1)} %bitcast.40, ...), custom_call_target="tpu_custom_call" | custom-call | flops 1000 | bytes 1000 | tf_op jit(solution)/shard_map/pallas_call | solution.py:212
  95.3 7.5 %collective-permute-done.8.returned = bf16[2,3,512,128]{3,2,1,0:T(8,128)(2,1)S(1)} collective-permute-done((bf16[2,3,512,128]{3,2,1,0:T(8,128)(2,1)S(1)}, bf16[2,3,512,128]{3,2,1,0:T(8,128)(2,1)S(1)}, u32[]{:S(2)}, u32[]{:S(2)}) %collective-permute-start.8) | collective-permute-done | bytes 786464 | tf_op jit(solution)/shard_map/ppermute | solution.py:345
  102.8 2.6 %collective-permute-start.9 = (f32[2,128]{1,0:T(2,128)S(1)}, f32[2,128]{1,0:T(2,128)S(1)}, u32[]{:S(2)}, u32[]{:S(2)}) collective-permute-start(f32[2,128]{1,0:T(2,128)S(1)} %shard_map.106), channel_id=1, source_target_pairs={{0,4},{2,6},{4,0},{6,2},{8,12},{10,14},{12,8},{14,10},{16,20},{18,... | collective-permute-start | bytes 3080 | tf_op jit(solution)/shard_map/ppermute | solution.py:279
  107.0 1.5 %collective-permute-start.14 = (bf16[2,2,512,128]{3,2,1,0:T(8,128)(2,1)S(1)}, bf16[2,2,512,128]{3,2,1,0:T(8,128)(2,1)S(1)}, u32[]{:S(2)}, u32[]{:S(2)}) collective-permute-start(bf16[2,2,512,128]{3,2,1,0:T(8,128)(2,1)S(1)} %add_convert_fusion.2), channel_id=1, source_target_pairs={{4,0},{6,2},{8,4},{10,6},{12,8},{14,10},{16,12},{18,14},{20,16},{2... | collective-permute-start | bytes 1572872 | tf_op jit(solution)/shard_map/ppermute | solution.py:363
  109.7 1.5 %collective-permute-start.11 = (f32[2,128]{1,0:T(2,128)S(1)}, f32[2,128]{1,0:T(2,128)S(1)}, u32[]{:S(2)}, u32[]{:S(2)}) collective-permute-start(f32[2,128]{1,0:T(2,128)S(1)} %add.41), channel_id=1, source_target_pairs={{0,1},{1,0},{2,3},{3,2},{4,5},{5,4},{6,7},{7,6},{8,9},{9,8},{10,11... | collective-permute-start | bytes 3080 | tf_op jit(solution)/shard_map/ppermute | solution.py:279
  111.3 2.0 %collective-permute-done.11 = f32[2,128]{1,0:T(2,128)S(1)} collective-permute-done((f32[2,128]{1,0:T(2,128)S(1)}, f32[2,128]{1,0:T(2,128)S(1)}, u32[]{:S(2)}, u32[]{:S(2)}) %collective-permute-start.11) | collective-permute-done | bytes 1056 | tf_op jit(solution)/shard_map/ppermute | solution.py:279
  113.3 4.1 %collective-permute-start.12 = (f32[2,128]{1,0:T(2,128)S(1)}, f32[2,128]{1,0:T(2,128)S(1)}, u32[]{:S(2)}, u32[]{:S(2)}) collective-permute-start(f32[2,128]{1,0:T(2,128)S(1)} %add.42), channel_id=1, source_target_pairs={{0,8},{2,10},{4,12},{6,14},{8,0},{10,2},{12,4},{14,6},{16,24},{18,... | collective-permute-start | bytes 3080 | tf_op jit(solution)/shard_map/ppermute | solution.py:279
  117.6 2.8 %copy.15 = bf16[512,8,2,128]{3,2,1,0:T(2,128)(2,1)} copy(bf16[512,8,2,128]{3,2,0,1:T(2,128)(2,1)S(1)} %bitcast.50) | data formatting | bytes 4194304 | tf_op jit(solution)/shard_map/transpose | solution.py:365
  121.4 2.9 %collective-permute-start.13 = (f32[2,128]{1,0:T(2,128)S(1)}, f32[2,128]{1,0:T(2,128)S(1)}, u32[]{:S(2)}, u32[]{:S(2)}) collective-permute-start(f32[2,128]{1,0:T(2,128)S(1)} %add.43), channel_id=1, source_target_pairs={{0,16},{2,18},{4,20},{6,22},{8,24},{10,26},{12,28},{14,30},{16,0},... | collective-permute-start | bytes 3080 | tf_op jit(solution)/shard_map/ppermute | solution.py:279
  124.3 4.7 %shard_map.108 = (bf16[512,8,128]{2,1,0:T(8,128)(2,1)}, bf16[512,8,128]{2,1,0:T(8,128)(2,1)}) custom-call(s32[1]{0:T(128)} %bitcast.4.shard_ref.in_ref, bf16[2,2,512,128]{3,2,1,0:T(8,128)(2,1)S(1)} %get-tuple-element.77.own, bf16[2,2,512,128]{3,2,1,0:T(8,128)(2,1)S(1)} %collective-permute-done.14.returned, ...), custom_call_target="tpu_custom_call" | custom-call | tf_op jit(solution)/shard_map/pallas_call | solution.py:262
  (57 shorter events, 10.5 us)
Async XLA Ops:
  3.6 23.1 %collective-permute-start.1 = (bf16[2,3,512,128]{3,2,1,0:T(8,128)(2,1)}, bf16[2,3,512,128]{3,2,1,0:T(8,128)(2,1)}, u32[]{:S(2)}, u32[]{:S(2)}) collective-permute-start(bf16[2,3,512,128]{3,2,1,0:T(8,128)(2,1)} %pad_maximum_fusion.2.own_ref), channel_id=1, source_target_pairs={{0,4},{2,6},{4,8},{6,10},{8,12},{10,14},{12,16},{14,18},{16,20},{1... | collective-permute-start | bytes 2359304 | tf_op jit(solution)/shard_map/ppermute | solution.py:309
  9.4 0.8 copy-start.2
  10.2 0.8 copy-start.5
  11.2 42.3 %collective-permute-start = (bf16[2,5,512,128]{3,2,1,0:T(8,128)(2,1)S(1)}, bf16[2,5,512,128]{3,2,1,0:T(8,128)(2,1)S(1)}, u32[]{:S(2)}, u32[]{:S(2)}) collective-permute-start(bf16[2,5,512,128]{3,2,1,0:T(8,128)(2,1)S(1)} %pad_maximum_fusion.1.own_ref), channel_id=1, source_target_pairs={{0,4},{2,6},{4,8},{6,10},{8,12},{10,14},{12,16},{14,18},{16,20},{1... | collective-permute-start | bytes 3932168 | tf_op jit(solution)/shard_map/ppermute | solution.py:309
  13.8 3.2 %copy-start.7 = (bf16[512,16,128]{2,1,0:T(8,128)(2,1)S(1)}, bf16[512,16,128]{2,1,0:T(8,128)(2,1)}, u32[]{:S(2)}) copy-start(bf16[512,16,128]{2,1,0:T(8,128)(2,1)} %param.6) | copy-start | bytes 6291460
  18.5 10.7 %copy-start = (f32[128]{0:T(128)S(1)}, f32[128]{0:T(128)}, u32[]{:S(2)}) copy-start(f32[128]{0:T(128)} %param.11) | copy-start | bytes 1540
  18.5 10.7 %copy-start.1 = (f32[128]{0:T(128)S(1)}, f32[128]{0:T(128)}, u32[]{:S(2)}) copy-start(f32[128]{0:T(128)} %param.10) | copy-start | bytes 1540
  26.9 2.3 %collective-permute-start.2 = (bf16[2,3,512,128]{3,2,1,0:T(8,128)(2,1)S(1)}, bf16[2,3,512,128]{3,2,1,0:T(8,128)(2,1)S(1)}, u32[]{:S(2)}, u32[]{:S(2)}) collective-permute-start(bf16[2,3,512,128]{3,2,1,0:T(8,128)(2,1)S(1)} %broadcast_select_fusion.1), channel_id=1, source_target_pairs={{0,2},{2,0},{4,6},{6,4},{8,10},{10,8},{12,14},{14,12},{16,18},{18,... | collective-permute-start | bytes 2359304 | tf_op jit(solution)/shard_map/ppermute | solution.py:337
  29.2 24.3 %copy-start.3 = (bf16[1,5,512,128]{3,2,1,0:T(8,128)(2,1)S(1)}, bf16[1,5,512,128]{3,2,1,0:T(8,128)(2,1)}, u32[]{:S(2)}) copy-start(bf16[1,5,512,128]{3,2,1,0:T(8,128)(2,1)} %copy-done.2) | copy-start | bytes 1966084
  29.2 24.3 %copy-start.6 = (bf16[1,5,512,128]{3,2,1,0:T(8,128)(2,1)S(1)}, bf16[1,5,512,128]{3,2,1,0:T(8,128)(2,1)}, u32[]{:S(2)}) copy-start(bf16[1,5,512,128]{3,2,1,0:T(8,128)(2,1)} %copy-done.5) | copy-start | bytes 1966084
  53.7 4.5 %collective-permute-start.3 = (bf16[2,5,512,128]{3,2,1,0:T(8,128)(2,1)S(1)}, bf16[2,5,512,128]{3,2,1,0:T(8,128)(2,1)S(1)}, u32[]{:S(2)}, u32[]{:S(2)}) collective-permute-start(bf16[2,5,512,128]{3,2,1,0:T(8,128)(2,1)S(1)} %broadcast_select_fusion), channel_id=1, source_target_pairs={{0,2},{2,0},{4,6},{6,4},{8,10},{10,8},{12,14},{14,12},{16,18},{18,... | collective-permute-start | bytes 3932168 | tf_op jit(solution)/shard_map/ppermute | solution.py:337
  53.8 4.1 %collective-permute-start.4 = (bf16[2,3,512,128]{3,2,1,0:T(8,128)(2,1)S(1)}, bf16[2,3,512,128]{3,2,1,0:T(8,128)(2,1)S(1)}, u32[]{:S(2)}, u32[]{:S(2)}) collective-permute-start(bf16[2,3,512,128]{3,2,1,0:T(8,128)(2,1)S(1)} %get-tuple-element.53), channel_id=1, source_target_pairs={{0,2},{2,0},{4,6},{6,4},{8,10},{10,8},{12,14},{14,12},{16,18},{18,... | collective-permute-start | bytes 2359304 | tf_op jit(solution)/shard_map/ppermute | solution.py:315
  58.2 22.2 %collective-permute-start.6 = (bf16[2,3,512,128]{3,2,1,0:T(8,128)(2,1)S(1)}, bf16[2,3,512,128]{3,2,1,0:T(8,128)(2,1)S(1)}, u32[]{:S(2)}, u32[]{:S(2)}) collective-permute-start(bf16[2,3,512,128]{3,2,1,0:T(8,128)(2,1)S(1)} %add_convert_fusion.1), channel_id=1, source_target_pairs={{4,0},{6,2},{8,4},{10,6},{12,8},{14,10},{16,12},{18,14},{20,16},{2... | collective-permute-start | bytes 2359304 | tf_op jit(solution)/shard_map/ppermute | solution.py:345
  76.1 4.9 %collective-permute-start.5 = (bf16[2,3,512,128]{3,2,1,0:T(8,128)(2,1)S(1)}, bf16[2,3,512,128]{3,2,1,0:T(8,128)(2,1)S(1)}, u32[]{:S(2)}, u32[]{:S(2)}) collective-permute-start(bf16[2,3,512,128]{3,2,1,0:T(8,128)(2,1)S(1)} %get-tuple-element.57), channel_id=1, source_target_pairs={{0,2},{2,0},{4,6},{6,4},{8,10},{10,8},{12,14},{14,12},{16,18},{18,... | collective-permute-start | bytes 2359304 | tf_op jit(solution)/shard_map/ppermute | solution.py:315
  81.2 21.5 %collective-permute-start.8 = (bf16[2,3,512,128]{3,2,1,0:T(8,128)(2,1)S(1)}, bf16[2,3,512,128]{3,2,1,0:T(8,128)(2,1)S(1)}, u32[]{:S(2)}, u32[]{:S(2)}) collective-permute-start(bf16[2,3,512,128]{3,2,1,0:T(8,128)(2,1)S(1)} %add_convert_fusion), channel_id=1, source_target_pairs={{4,0},{6,2},{8,4},{10,6},{12,8},{14,10},{16,12},{18,14},{20,16},{2... | collective-permute-start | bytes 2359304 | tf_op jit(solution)/shard_map/ppermute | solution.py:345
  94.4 11.1 %collective-permute-start.7 = (bf16[2,2,512,128]{3,2,1,0:T(8,128)(2,1)S(1)}, bf16[2,2,512,128]{3,2,1,0:T(8,128)(2,1)S(1)}, u32[]{:S(2)}, u32[]{:S(2)}) collective-permute-start(bf16[2,2,512,128]{3,2,1,0:T(8,128)(2,1)S(1)} %get-tuple-element.62), channel_id=1, source_target_pairs={{0,2},{2,0},{4,6},{6,4},{8,10},{10,8},{12,14},{14,12},{16,18},{18,... | collective-permute-start | bytes 1572872 | tf_op jit(solution)/shard_map/ppermute | solution.py:315
  102.8 8.4 %copy-start.4 = (bf16[1,5,512,128]{3,2,1,0:T(8,128)(2,1)S(1)}, bf16[1,5,512,128]{3,2,1,0:T(8,128)(2,1)}, u32[]{:S(2)}) copy-start(bf16[1,5,512,128]{3,2,1,0:T(8,128)(2,1)} %copy-done.2) | copy-start | bytes 1966084
  102.8 4.2 %collective-permute-start.9 = (f32[2,128]{1,0:T(2,128)S(1)}, f32[2,128]{1,0:T(2,128)S(1)}, u32[]{:S(2)}, u32[]{:S(2)}) collective-permute-start(f32[2,128]{1,0:T(2,128)S(1)} %shard_map.106), channel_id=1, source_target_pairs={{0,4},{2,6},{4,0},{6,2},{8,12},{10,14},{12,8},{14,10},{16,20},{18,... | collective-permute-start | bytes 3080 | tf_op jit(solution)/shard_map/ppermute | solution.py:279
  107.0 17.3 %collective-permute-start.14 = (bf16[2,2,512,128]{3,2,1,0:T(8,128)(2,1)S(1)}, bf16[2,2,512,128]{3,2,1,0:T(8,128)(2,1)S(1)}, u32[]{:S(2)}, u32[]{:S(2)}) collective-permute-start(bf16[2,2,512,128]{3,2,1,0:T(8,128)(2,1)S(1)} %add_convert_fusion.2), channel_id=1, source_target_pairs={{4,0},{6,2},{8,4},{10,6},{12,8},{14,10},{16,12},{18,14},{20,16},{2... | collective-permute-start | bytes 1572872 | tf_op jit(solution)/shard_map/ppermute | solution.py:363
  108.5 1.2 collective-permute-start.10
  109.7 3.6 %collective-permute-start.11 = (f32[2,128]{1,0:T(2,128)S(1)}, f32[2,128]{1,0:T(2,128)S(1)}, u32[]{:S(2)}, u32[]{:S(2)}) collective-permute-start(f32[2,128]{1,0:T(2,128)S(1)} %add.41), channel_id=1, source_target_pairs={{0,1},{1,0},{2,3},{3,2},{4,5},{5,4},{6,7},{7,6},{8,9},{9,8},{10,11... | collective-permute-start | bytes 3080 | tf_op jit(solution)/shard_map/ppermute | solution.py:279
  113.3 8.1 %collective-permute-start.12 = (f32[2,128]{1,0:T(2,128)S(1)}, f32[2,128]{1,0:T(2,128)S(1)}, u32[]{:S(2)}, u32[]{:S(2)}) collective-permute-start(f32[2,128]{1,0:T(2,128)S(1)} %add.42), channel_id=1, source_target_pairs={{0,8},{2,10},{4,12},{6,14},{8,0},{10,2},{12,4},{14,6},{16,24},{18,... | collective-permute-start | bytes 3080 | tf_op jit(solution)/shard_map/ppermute | solution.py:279
  121.4 7.6 %collective-permute-start.13 = (f32[2,128]{1,0:T(2,128)S(1)}, f32[2,128]{1,0:T(2,128)S(1)}, u32[]{:S(2)}, u32[]{:S(2)}) collective-permute-start(f32[2,128]{1,0:T(2,128)S(1)} %add.43), channel_id=1, source_target_pairs={{0,16},{2,18},{4,20},{6,22},{8,24},{10,26},{12,28},{14,30},{16,0},... | collective-permute-start | bytes 3080 | tf_op jit(solution)/shard_map/ppermute | solution.py:279

commit v2 on v1

--- a/solution.py
+++ b/solution.py
@@ -178,6 +178,36 @@
                 grad = norm_back(grad, raw, inverse_rms_of(raw), k_gain_ref[...])
             by_token[:, len(before) + head, :] = grad
         out[...] = by_token[...].astype(out.dtype)
+
+
+def choose_kernel(shard_ref, far_ref, own_ref, out_ref):
+    odd = shard_ref[0] % 2 == 1
+
+    @pl.when(odd)
+    def _():
+        out_ref[...] = far_ref[...]
+
+    @pl.when(jnp.logical_not(odd))
+    def _():
+        out_ref[...] = own_ref[...]
+
+
+def relay_kernel(shard_ref, far_ref, swapped_ref, out_ref):
+    odd = jnp.where(shard_ref[0] % 2 == 1, 1.0, 0.0)
+    total = far_ref[...].astype(jnp.float32) + odd * swapped_ref[...].astype(jnp.float32)
+    out_ref[...] = total.astype(out_ref.dtype)
+
+
+def small_call(kernel, shard, *arrays):
+    smem, vmem = (pl.BlockSpec(memory_space=space) for space in (pltpu.SMEM, pltpu.VMEM))
+    return pl.pallas_call(
+        kernel,
+        in_specs=[smem] + [vmem] * len(arrays),
+        out_specs=vmem,
+        out_shape=jax.ShapeDtypeStruct(arrays[0].shape, arrays[0].dtype),
+        compiler_params=pltpu.CompilerParams(vmem_limit_bytes=12 * 1024 * 1024),
+        cost_estimate=LIGHT,
+    )(shard, *arrays)
 
 
 def later_kernel(corner_ref, in_ref, out_ref):
@@ -274,15 +304,19 @@
     return [(kv_dev + count - 1 - place) // count for place in range(count)]
 
 
-def exchanged(value, axis, step):
-    pairs = [(source, source ^ step) for source in range(lax.axis_size(axis))]
-    return lax.ppermute(value, axis, pairs)
-
-
-def steps_of(axis):
+def exchanged(value, axis, low, high):
     count = lax.axis_size(axis)
     assert count & (count - 1) == 0
-    return [(axis, 1 << place) for place in range(count.bit_length() - 1)]
+    return [
+        lax.ppermute(value, axis, [(source, source ^ (mask << low)) for source in range(count)])
+        for mask in range(1, 1 << max(high - low, 0))
+    ]
+
+
+def summed(value, axis, low, high):
+    for place in range(low, high):
+        value = value + exchanged(value, axis, place, place + 1)[0]
+    return value
 
 
 def per_device(query, key, value, grad_out, q_gain, k_gain):
@@ -292,7 +326,6 @@
     count = lax.axis_size("seq")
     assert 2 * rows == WINDOW and rows % TILE == 0 and count % 2 == 0
     shard = lax.axis_index("seq")
-    odd = shard % 2 == 1
     ahead = [(source, source + 2) for source in range(count - 2)]
     back = [(source + 2, source) for source in range(count - 2)]
     swap = [(source, source ^ 1) for source in range(count)]
@@ -313,8 +346,7 @@
 
     def split(d_own, d_near, d_far, raw):
         swapped = lax.ppermute(d_near, "seq", swap)
-        from_pair = jnp.where(odd, swapped.astype(jnp.float32), 0.0)
-        relayed = (d_far.astype(jnp.float32) + from_pair).astype(jnp.bfloat16)
+        relayed = small_call(relay_kernel, scalar, d_far, swapped)
         return relayed, (d_own, swapped, raw)
 
     def close(stays, returned):
@@ -330,11 +362,13 @@
             own, far, start = owns[place], fars[place], cuts[place][0]
             if place:
                 far, gains[0] = lax.optimization_barrier((far, gains[0]))
+                gains[0] = later(far, gains[0])
+                far, gains[0], relayed = lax.optimization_barrier((far, gains[0], relayed))
             else:
                 far, queries, grads, *_ = lax.optimization_barrier(
                     (far, queries, grads, *owns[1:])
                 )
-            near = lax.ppermute(jnp.where(odd, far, own), "seq", swap)
+            near = lax.ppermute(small_call(choose_kernel, scalar, far, own), "seq", swap)
         scalar_now = scalar
         if grads_out is not None:
             if kept:
@@ -357,20 +391,22 @@
         returned, done = lax.optimization_barrier((returned, done))
         gain_sum = later(returned, gain_sum)
         done.append(close(before, returned))
-    core, *chips = steps_of("seq")
-    gain_sum = gain_sum + exchanged(gain_sum, *chips[0])
-    relayed, gain_sum = lax.optimization_barrier((relayed, gain_sum))
     returned = lax.ppermute(relayed, "seq", back)
     grad_query = jnp.concatenate(dq_parts).reshape(kv_dev, rows, group, width)
     grad_query = jnp.transpose(grad_query, (1, 0, 2, 3)).reshape(rows, heads, width)
-    *early, last = [core, *steps_of("head"), *chips[1:]]
-    for step in early:
-        gain_sum = gain_sum + exchanged(gain_sum, *step)
+    seq_bits, head_bits = ((lax.axis_size(axis) - 1).bit_length() for axis in ("seq", "head"))
+    gain_sum = summed(gain_sum, "seq", 0, 1)
+    gain_sum = summed(gain_sum, "head", 0, head_bits)
+    gain_sum = summed(gain_sum, "seq", 1, seq_bits - 2)
     gain_sum, grad_query, done = lax.optimization_barrier((gain_sum, grad_query, done))
     d_own, swapped, raw = stays
     grad_key, grad_value = finish(scalar, d_own, returned, swapped, raw, k_gain_2d, done)
-    other, grad_key = lax.optimization_barrier((exchanged(gain_sum, *last), grad_key))
-    gain_sum = gain_sum + other
+    others, grad_key = lax.optimization_barrier(
+        (exchanged(gain_sum, "seq", max(seq_bits - 2, 1), seq_bits), grad_key)
+    )
+    gain_sum = (gain_sum + others[0]) + (others[1] + others[2]) if len(others) == 3 else sum(
+        others, gain_sum
+    )
     return (grad_query, grad_key, grad_value, gain_sum[0], gain_sum[1])
 
 

time: 130 us -> 123 us (0.946)
  waiting for transfers between devices: 37.4 us -> 33.5 us
  other arithmetic: 2.37 us -> 0.46 us
  starting transfers between devices: 25 us -> 23.1 us
  Pallas kernels: 52.2 us -> 54 us
    ppermute x3, waiting for transfers between devices: 3.65 us -> 1.05 us  [split(): swapped = lax.ppermute(d_near, 'seq', swap)]
    ppermute x2, waiting for transfers between devices: 11.7 us -> 9.22 us  [per_device(): kept.append((stays, lax.ppermute(relayed, 'seq', back)))]
    pallas_call x0 -> x5, Pallas kernels: none -> 1.91 us  [small_call(): pl.pallas_call(kernel, in_specs=[smem] + [vmem] * len(arrays), out_specs=...]
    ppermute x7 -> x8, waiting for transfers between devices: 6.97 us -> 8.58 us  [the longest x2 5.29 us: per_device(): lax.ppermute(small_call(choose_kernel, scalar, far, own), 'seq', swap)]
    ppermute x7 -> x8, starting transfers between devices: 11.3 us -> 9.83 us  [the longest x6 9.69 us: exchanged(): lax.ppermute(value, axis, [(source, source ^ mask << low) for source in r...]
  transfers between devices with their start and end apart: 15 -> 16, of which waited for: 10 -> 10; matrix products, arithmetic and copies ran while one was open for 7% -> 6% of each run, Pallas kernels for 40% -> 43%
where the time goes in v2:
time: 123 us
  Pallas kernels  54 us (44%)
  waiting for transfers between devices  33.5 us (27%)
  starting transfers between devices  23.1 us (19%)
  local copies, waits for them, and re-layouts  10.8 us (9%)
    pallas_call x3, Pallas kernels, group_grads(): pl.pallas_call(heads_kernel, grid=(count,), in_specs=[pl.BlockSpec(memory...  45.2 us
    ppermute x2, waiting for transfers between devices, per_device(): fars = [lax.ppermute(own, 'seq', ahead) for own in owns]  14.7 us
    ppermute x6, starting transfers between devices, exchanged(): lax.ppermute(value, axis, [(source, source ^ mask << low) for source in r...  9.69 us
    ppermute x2, waiting for transfers between devices, per_device(): kept.append((stays, lax.ppermute(relayed, 'seq', back)))  9.22 us
    ppermute x2, starting transfers between devices, per_device(): fars = [lax.ppermute(own, 'seq', ahead) for own in owns]  8.4 us
    ppermute x2, waiting for transfers between devices, per_device(): lax.ppermute(small_call(choose_kernel, scalar, far, own), 'seq', swap)  5.29 us
    pallas_call x1, Pallas kernels, finish(): pl.pallas_call(finish_kernel, in_specs=[smem] + [vmem] * (5 + len(done)),...  4.71 us
    reshape x2, local copies, waits for them, and re-layouts, by_head(): split = array.reshape(rows, kv_dev, group, width)  4.62 us
  transfers between devices with their start and end apart: 16, of which 10 were waited for; matrix products, arithmetic and copies ran while one was open for 6% of the time, Pallas kernels for 43%

profile of v2, /device:TPU:0, one launch (start us, length us, event | category | flops | bytes accessed | tf_op | source)
XLA Modules:
  0.0 122.8 jit_solution(2937267873715687449)
XLA Ops:
  0.6 1.9 %copy_bitcast_fusion = (bf16[8,512,128]{2,1,0:T(8,128)(2,1)S(1)}, bf16[8,512,128]{2,1,0:T(8,128)(2,1)S(1)}) fusion(bf16[512,8,128]{2,1,0:T(8,128)(2,1)} %param.8, bf16[512,8,128]{2,1,0:T(8,128)(2,1)} %param.7), kind=kLoop, calls=%fused_computation.2 | loop fusion | bytes 4194304 | tf_op jit(solution)/shard_map/transpose | solution.py:340
  2.7 5.8 %collective-permute-start.1 = (bf16[2,3,512,128]{3,2,1,0:T(8,128)(2,1)S(1)}, bf16[2,3,512,128]{3,2,1,0:T(8,128)(2,1)}, u32[]{:S(2)}, u32[]{:S(2)}) collective-permute-start(bf16[2,3,512,128]{3,2,1,0:T(8,128)(2,1)S(1)} %pad_maximum_fusion.2.own_ref), channel_id=1, source_target_pairs={{0,4},{2,6},{4,8},{6,10},{8,12},{10,14},{12,16},{14,18},{16,20},{1... | collective-permute-start | bytes 2359304 | tf_op jit(solution)/shard_map/ppermute | solution.py:342
  9.5 2.6 %collective-permute-start = (bf16[2,5,512,128]{3,2,1,0:T(8,128)(2,1)S(1)}, bf16[2,5,512,128]{3,2,1,0:T(8,128)(2,1)S(1)}, u32[]{:S(2)}, u32[]{:S(2)}) collective-permute-start(bf16[2,5,512,128]{3,2,1,0:T(8,128)(2,1)S(1)} %pad_maximum_fusion.1.own_ref), channel_id=1, source_target_pairs={{0,4},{2,6},{4,8},{6,10},{8,12},{10,14},{12,16},{14,18},{16,20},{1... | collective-permute-start | bytes 3932168 | tf_op jit(solution)/shard_map/ppermute | solution.py:342
  12.2 3.2 %copy.13 = bf16[512,8,2,128]{3,2,0,1:T(2,128)(2,1)S(1)} copy(bf16[512,8,2,128]{3,2,1,0:T(2,128)(2,1)} %bitcast.53) | data formatting | bytes 4194304 | tf_op jit(solution)/shard_map/reshape | solution.py:334
  15.4 1.4 %copy.14 = bf16[512,8,2,128]{3,2,0,1:T(2,128)(2,1)S(1)} copy(bf16[512,8,2,128]{3,2,1,0:T(2,128)(2,1)S(1)} %bitcast.54) | data formatting | bytes 4194304 | tf_op jit(solution)/shard_map/reshape | solution.py:334
  16.8 8.7 %collective-permute-done.1.far_ref = bf16[2,3,512,128]{3,2,1,0:T(8,128)(2,1)} collective-permute-done((bf16[2,3,512,128]{3,2,1,0:T(8,128)(2,1)S(1)}, bf16[2,3,512,128]{3,2,1,0:T(8,128)(2,1)}, u32[]{:S(2)}, u32[]{:S(2)}) %collective-permute-start.1) | collective-permute-done | bytes 786464 | tf_op jit(solution)/shard_map/ppermute | solution.py:342
  25.5 1.2 shard_map.101
  26.8 2.3 %collective-permute-done.2.near_ref = bf16[2,3,512,128]{3,2,1,0:T(8,128)(2,1)S(1)} collective-permute-done((bf16[2,3,512,128]{3,2,1,0:T(8,128)(2,1)S(1)}, bf16[2,3,512,128]{3,2,1,0:T(8,128)(2,1)S(1)}, u32[]{:S(2)}, u32[]{:S(2)}) %collective-permute-start.2) | collective-permute-done | bytes 786464 | tf_op jit(solution)/shard_map/ppermute | solution.py:371
  29.1 17.2 %shard_map.102 = (bf16[3,1024,128]{2,1,0:T(8,128)(2,1)S(1)}, bf16[2,3,512,128]{3,2,1,0:T(8,128)(2,1)S(1)}, bf16[2,3,512,128]{3,2,1,0:T(8,128)(2,1)S(1)}, bf16[2,...) custom-call(s32[1]{0:T(128)} %bitcast.shard_ref.in_ref, bf16[8,1024,128]{2,1,0:T(8,128)(2,1)S(1)} %bitcast.37, ...), custom_call_target="tpu_custom_call" | custom-call | flops 1000 | bytes 1000 | tf_op jit(solution)/shard_map/pallas_call | solution.py:242
  46.5 6.0 %collective-permute-done.far_ref = bf16[2,5,512,128]{3,2,1,0:T(8,128)(2,1)S(1)} collective-permute-done((bf16[2,5,512,128]{3,2,1,0:T(8,128)(2,1)S(1)}, bf16[2,5,512,128]{3,2,1,0:T(8,128)(2,1)S(1)}, u32[]{:S(2)}, u32[]{:S(2)}) %collective-permute-start) | collective-permute-done | bytes 1310752 | tf_op jit(solution)/shard_map/ppermute | solution.py:342
  52.9 3.0 %collective-permute-done.4.near_ref = bf16[2,5,512,128]{3,2,1,0:T(8,128)(2,1)S(1)} collective-permute-done((bf16[2,5,512,128]{3,2,1,0:T(8,128)(2,1)S(1)}, bf16[2,5,512,128]{3,2,1,0:T(8,128)(2,1)S(1)}, u32[]{:S(2)}, u32[]{:S(2)}) %collective-permute-start.4) | collective-permute-done | bytes 1310752 | tf_op jit(solution)/shard_map/ppermute | solution.py:371
  55.9 1.5 %collective-permute-start.6 = (bf16[2,3,512,128]{3,2,1,0:T(8,128)(2,1)S(1)}, bf16[2,3,512,128]{3,2,1,0:T(8,128)(2,1)S(1)}, u32[]{:S(2)}, u32[]{:S(2)}) collective-permute-start(bf16[2,3,512,128]{3,2,1,0:T(8,128)(2,1)S(1)} %shard_map.104), channel_id=1, source_target_pairs={{4,0},{6,2},{8,4},{10,6},{12,8},{14,10},{16,12},{18,14},{20,16},{2... | collective-permute-start | bytes 2359304 | tf_op jit(solution)/shard_map/ppermute | solution.py:379
  57.4 16.4 %shard_map.106 = (bf16[3,1024,128]{2,1,0:T(8,128)(2,1)S(1)}, bf16[2,3,512,128]{3,2,1,0:T(8,128)(2,1)S(1)}, bf16[2,3,512,128]{3,2,1,0:T(8,128)(2,1)S(1)}, bf16[2,...) custom-call(s32[1]{0:T(128)} %bitcast.shard_ref.in_ref, bf16[8,1024,128]{2,1,0:T(8,128)(2,1)S(1)} %bitcast.38, ...), custom_call_target="tpu_custom_call" | custom-call | flops 1000 | bytes 1000 | tf_op jit(solution)/shard_map/pallas_call | solution.py:242
  74.0 4.2 %collective-permute-done.6.returned = bf16[2,3,512,128]{3,2,1,0:T(8,128)(2,1)S(1)} collective-permute-done((bf16[2,3,512,128]{3,2,1,0:T(8,128)(2,1)S(1)}, bf16[2,3,512,128]{3,2,1,0:T(8,128)(2,1)S(1)}, u32[]{:S(2)}, u32[]{:S(2)}) %collective-permute-start.6) | collective-permute-done | bytes 786464 | tf_op jit(solution)/shard_map/ppermute | solution.py:379
  78.9 1.4 %collective-permute-start.7 = (bf16[2,3,512,128]{3,2,1,0:T(8,128)(2,1)S(1)}, bf16[2,3,512,128]{3,2,1,0:T(8,128)(2,1)S(1)}, u32[]{:S(2)}, u32[]{:S(2)}) collective-permute-start(bf16[2,3,512,128]{3,2,1,0:T(8,128)(2,1)S(1)} %shard_map.107), channel_id=1, source_target_pairs={{4,0},{6,2},{8,4},{10,6},{12,8},{14,10},{16,12},{18,14},{20,16},{2... | collective-permute-start | bytes 2359304 | tf_op jit(solution)/shard_map/ppermute | solution.py:379
  80.4 11.6 %shard_map.110 = (bf16[2,1024,128]{2,1,0:T(8,128)(2,1)S(1)}, bf16[2,2,512,128]{3,2,1,0:T(8,128)(2,1)S(1)}, bf16[2,2,512,128]{3,2,1,0:T(8,128)(2,1)S(1)}, bf16[2,...) custom-call(s32[1]{0:T(128)} %shard_map.108.shard_ref, bf16[8,1024,128]{2,1,0:T(8,128)(2,1)S(1)} %bitcast.39, ...), custom_call_target="tpu_custom_call" | custom-call | flops 1000 | bytes 1000 | tf_op jit(solution)/shard_map/pallas_call | solution.py:242
  94.1 1.5 %collective-permute-start.15 = (bf16[2,2,512,128]{3,2,1,0:T(8,128)(2,1)S(1)}, bf16[2,2,512,128]{3,2,1,0:T(8,128)(2,1)S(1)}, u32[]{:S(2)}, u32[]{:S(2)}) collective-permute-start(bf16[2,2,512,128]{3,2,1,0:T(8,128)(2,1)S(1)} %shard_map.113), channel_id=1, source_target_pairs={{4,0},{6,2},{8,4},{10,6},{12,8},{14,10},{16,12},{18,14},{20,16},{2... | collective-permute-start | bytes 1572872 | tf_op jit(solution)/shard_map/ppermute | solution.py:394
  95.6 5.1 %collective-permute-done.7.returned = bf16[2,3,512,128]{3,2,1,0:T(8,128)(2,1)S(1)} collective-permute-done((bf16[2,3,512,128]{3,2,1,0:T(8,128)(2,1)S(1)}, bf16[2,3,512,128]{3,2,1,0:T(8,128)(2,1)S(1)}, u32[]{:S(2)}, u32[]{:S(2)}) %collective-permute-start.7) | collective-permute-done | bytes 786464 | tf_op jit(solution)/shard_map/ppermute | solution.py:379
  101.8 1.5 %collective-permute-start.9 = (f32[2,128]{1,0:T(2,128)S(1)}, f32[2,128]{1,0:T(2,128)S(1)}, u32[]{:S(2)}, u32[]{:S(2)}) collective-permute-start(f32[2,128]{1,0:T(2,128)S(1)} %add.26), channel_id=1, source_target_pairs={{0,1},{1,0},{2,3},{3,2},{4,5},{5,4},{6,7},{7,6},{8,9},{9,8},{10,11... | collective-permute-start | bytes 3080 | tf_op jit(solution)/shard_map/ppermute | solution.py:311
  103.4 2.0 %collective-permute-done.9 = f32[2,128]{1,0:T(2,128)S(1)} collective-permute-done((f32[2,128]{1,0:T(2,128)S(1)}, f32[2,128]{1,0:T(2,128)S(1)}, u32[]{:S(2)}, u32[]{:S(2)}) %collective-permute-start.9) | collective-permute-done | bytes 1056 | tf_op jit(solution)/shard_map/ppermute | solution.py:311
  105.4 2.6 %collective-permute-start.10 = (f32[2,128]{1,0:T(2,128)S(1)}, f32[2,128]{1,0:T(2,128)S(1)}, u32[]{:S(2)}, u32[]{:S(2)}) collective-permute-start(f32[2,128]{1,0:T(2,128)S(1)} %add.27), channel_id=1, source_target_pairs={{0,4},{2,6},{4,0},{6,2},{8,12},{10,14},{12,8},{14,10},{16,20},{18,... | collective-permute-start | bytes 3080 | tf_op jit(solution)/shard_map/ppermute | solution.py:311
  108.2 2.8 %copy.15 = bf16[512,8,2,128]{3,2,1,0:T(2,128)(2,1)} copy(bf16[512,8,2,128]{3,2,0,1:T(2,128)(2,1)S(1)} %bitcast.52) | data formatting | bytes 4194304 | tf_op jit(solution)/shard_map/transpose | solution.py:396
  111.9 5.1 %collective-permute-start.13 = (f32[2,128]{1,0:T(2,128)S(1)}, f32[2,128]{1,0:T(2,128)S(1)}, u32[]{:S(2)}, u32[]{:S(2)}) collective-permute-start(f32[2,128]{1,0:T(2,128)S(1)} %add.28), channel_id=1, source_target_pairs={{0,24},{2,26},{4,28},{6,30},{8,16},{10,18},{12,20},{14,22},{16,8},... | collective-permute-start | bytes 3080 | tf_op jit(solution)/shard_map/ppermute | solution.py:311
  117.6 4.7 %shard_map.114 = (bf16[512,8,128]{2,1,0:T(8,128)(2,1)}, bf16[512,8,128]{2,1,0:T(8,128)(2,1)}) custom-call(s32[1]{0:T(128)} %bitcast.shard_ref.in_ref, bf16[2,2,512,128]{3,2,1,0:T(8,128)(2,1)S(1)} %get-tuple-element.80.own, bf16[2,2,512,128]{3,2,1,0:T(8,128)(2,1)S(1)} %collective-permute-done.15.returned, ...), custom_call_target="tpu_custom_call" | custom-call | tf_op jit(solution)/shard_map/pallas_call | solution.py:292
  (58 shorter events, 8.4 us)
Async XLA Ops:
  2.6 6.0 %copy-start = (bf16[1,3,512,128]{3,2,1,0:T(8,128)(2,1)}, bf16[1,3,512,128]{3,2,1,0:T(8,128)(2,1)S(1)}, u32[]{:S(2)}) copy-start(bf16[1,3,512,128]{3,2,1,0:T(8,128)(2,1)S(1)} %slice_bitcast_fusion.3.raw_ref) | copy-start | bytes 1179652
  2.7 22.8 %collective-permute-start.1 = (bf16[2,3,512,128]{3,2,1,0:T(8,128)(2,1)S(1)}, bf16[2,3,512,128]{3,2,1,0:T(8,128)(2,1)}, u32[]{:S(2)}, u32[]{:S(2)}) collective-permute-start(bf16[2,3,512,128]{3,2,1,0:T(8,128)(2,1)S(1)} %pad_maximum_fusion.2.own_ref), channel_id=1, source_target_pairs={{0,4},{2,6},{4,8},{6,10},{8,12},{10,14},{12,16},{14,18},{16,20},{1... | collective-permute-start | bytes 2359304 | tf_op jit(solution)/shard_map/ppermute | solution.py:342
  8.6 0.8 copy-start.4
  9.5 43.0 %collective-permute-start = (bf16[2,5,512,128]{3,2,1,0:T(8,128)(2,1)S(1)}, bf16[2,5,512,128]{3,2,1,0:T(8,128)(2,1)S(1)}, u32[]{:S(2)}, u32[]{:S(2)}) collective-permute-start(bf16[2,5,512,128]{3,2,1,0:T(8,128)(2,1)S(1)} %pad_maximum_fusion.1.own_ref), channel_id=1, source_target_pairs={{0,4},{2,6},{4,8},{6,10},{8,12},{10,14},{12,16},{14,18},{16,20},{1... | collective-permute-start | bytes 3932168 | tf_op jit(solution)/shard_map/ppermute | solution.py:342
  12.2 3.2 %copy-start.6 = (bf16[512,16,128]{2,1,0:T(8,128)(2,1)S(1)}, bf16[512,16,128]{2,1,0:T(8,128)(2,1)}, u32[]{:S(2)}) copy-start(bf16[512,16,128]{2,1,0:T(8,128)(2,1)} %param.9) | copy-start | bytes 6291460
  16.8 12.3 %copy-start.2 = (f32[128]{0:T(128)S(1)}, f32[128]{0:T(128)}, u32[]{:S(2)}) copy-start(f32[128]{0:T(128)} %param.11) | copy-start | bytes 1540
  16.8 12.3 %copy-start.3 = (f32[128]{0:T(128)S(1)}, f32[128]{0:T(128)}, u32[]{:S(2)}) copy-start(f32[128]{0:T(128)} %param.10) | copy-start | bytes 1540
  26.7 2.4 %collective-permute-start.2 = (bf16[2,3,512,128]{3,2,1,0:T(8,128)(2,1)S(1)}, bf16[2,3,512,128]{3,2,1,0:T(8,128)(2,1)S(1)}, u32[]{:S(2)}, u32[]{:S(2)}) collective-permute-start(bf16[2,3,512,128]{3,2,1,0:T(8,128)(2,1)S(1)} %shard_map.101), channel_id=1, source_target_pairs={{0,2},{2,0},{4,6},{6,4},{8,10},{10,8},{12,14},{14,12},{16,18},{18,... | collective-permute-start | bytes 2359304 | tf_op jit(solution)/shard_map/ppermute | solution.py:371
  46.3 6.2 %collective-permute-start.3 = (bf16[2,3,512,128]{3,2,1,0:T(8,128)(2,1)S(1)}, bf16[2,3,512,128]{3,2,1,0:T(8,128)(2,1)S(1)}, u32[]{:S(2)}, u32[]{:S(2)}) collective-permute-start(bf16[2,3,512,128]{3,2,1,0:T(8,128)(2,1)S(1)} %get-tuple-element.57), channel_id=1, source_target_pairs={{0,2},{2,0},{4,6},{6,4},{8,10},{10,8},{12,14},{14,12},{16,18},{18,... | collective-permute-start | bytes 2359304 | tf_op jit(solution)/shard_map/ppermute | solution.py:348
  52.8 3.1 %collective-permute-start.4 = (bf16[2,5,512,128]{3,2,1,0:T(8,128)(2,1)S(1)}, bf16[2,5,512,128]{3,2,1,0:T(8,128)(2,1)S(1)}, u32[]{:S(2)}, u32[]{:S(2)}) collective-permute-start(bf16[2,5,512,128]{3,2,1,0:T(8,128)(2,1)S(1)} %shard_map.105), channel_id=1, source_target_pairs={{0,2},{2,0},{4,6},{6,4},{8,10},{10,8},{12,14},{14,12},{16,18},{18,... | collective-permute-start | bytes 3932168 | tf_op jit(solution)/shard_map/ppermute | solution.py:371
  55.9 22.2 %collective-permute-start.6 = (bf16[2,3,512,128]{3,2,1,0:T(8,128)(2,1)S(1)}, bf16[2,3,512,128]{3,2,1,0:T(8,128)(2,1)S(1)}, u32[]{:S(2)}, u32[]{:S(2)}) collective-permute-start(bf16[2,3,512,128]{3,2,1,0:T(8,128)(2,1)S(1)} %shard_map.104), channel_id=1, source_target_pairs={{4,0},{6,2},{8,4},{10,6},{12,8},{14,10},{16,12},{18,14},{20,16},{2... | collective-permute-start | bytes 2359304 | tf_op jit(solution)/shard_map/ppermute | solution.py:379
  73.8 4.9 %collective-permute-start.5 = (bf16[2,3,512,128]{3,2,1,0:T(8,128)(2,1)S(1)}, bf16[2,3,512,128]{3,2,1,0:T(8,128)(2,1)S(1)}, u32[]{:S(2)}, u32[]{:S(2)}) collective-permute-start(bf16[2,3,512,128]{3,2,1,0:T(8,128)(2,1)S(1)} %get-tuple-element.63), channel_id=1, source_target_pairs={{0,2},{2,0},{4,6},{6,4},{8,10},{10,8},{12,14},{14,12},{16,18},{18,... | collective-permute-start | bytes 2359304 | tf_op jit(solution)/shard_map/ppermute | solution.py:348
  78.9 13.1 %copy-start.1 = (bf16[1,3,512,128]{3,2,1,0:T(8,128)(2,1)S(1)}, bf16[1,3,512,128]{3,2,1,0:T(8,128)(2,1)}, u32[]{:S(2)}) copy-start(bf16[1,3,512,128]{3,2,1,0:T(8,128)(2,1)} %copy-done) | copy-start | bytes 1179652
  78.9 21.8 %collective-permute-start.7 = (bf16[2,3,512,128]{3,2,1,0:T(8,128)(2,1)S(1)}, bf16[2,3,512,128]{3,2,1,0:T(8,128)(2,1)S(1)}, u32[]{:S(2)}, u32[]{:S(2)}) collective-permute-start(bf16[2,3,512,128]{3,2,1,0:T(8,128)(2,1)S(1)} %shard_map.107), channel_id=1, source_target_pairs={{4,0},{6,2},{8,4},{10,6},{12,8},{14,10},{16,12},{18,14},{20,16},{2... | collective-permute-start | bytes 2359304 | tf_op jit(solution)/shard_map/ppermute | solution.py:379
  92.0 2.0 %collective-permute-start.14 = (bf16[2,2,512,128]{3,2,1,0:T(8,128)(2,1)S(1)}, bf16[2,2,512,128]{3,2,1,0:T(8,128)(2,1)S(1)}, u32[]{:S(2)}, u32[]{:S(2)}) collective-permute-start(bf16[2,2,512,128]{3,2,1,0:T(8,128)(2,1)S(1)} %get-tuple-element.82), channel_id=1, source_target_pairs={{0,2},{2,0},{4,6},{6,4},{8,10},{10,8},{12,14},{14,12},{16,18},{18,... | collective-permute-start | bytes 1572872 | tf_op jit(solution)/shard_map/ppermute | solution.py:348
  94.1 23.5 %collective-permute-start.15 = (bf16[2,2,512,128]{3,2,1,0:T(8,128)(2,1)S(1)}, bf16[2,2,512,128]{3,2,1,0:T(8,128)(2,1)S(1)}, u32[]{:S(2)}, u32[]{:S(2)}) collective-permute-start(bf16[2,2,512,128]{3,2,1,0:T(8,128)(2,1)S(1)} %shard_map.113), channel_id=1, source_target_pairs={{4,0},{6,2},{8,4},{10,6},{12,8},{14,10},{16,12},{18,14},{20,16},{2... | collective-permute-start | bytes 1572872 | tf_op jit(solution)/shard_map/ppermute | solution.py:394
  100.7 2.6 %copy-start.5 = (bf16[1,5,512,128]{3,2,1,0:T(8,128)(2,1)S(1)}, bf16[1,5,512,128]{3,2,1,0:T(8,128)(2,1)}, u32[]{:S(2)}) copy-start(bf16[1,5,512,128]{3,2,1,0:T(8,128)(2,1)} %copy-done.4) | copy-start | bytes 1966084
  100.7 1.1 collective-permute-start.8
  101.8 3.6 %collective-permute-start.9 = (f32[2,128]{1,0:T(2,128)S(1)}, f32[2,128]{1,0:T(2,128)S(1)}, u32[]{:S(2)}, u32[]{:S(2)}) collective-permute-start(f32[2,128]{1,0:T(2,128)S(1)} %add.26), channel_id=1, source_target_pairs={{0,1},{1,0},{2,3},{3,2},{4,5},{5,4},{6,7},{7,6},{8,9},{9,8},{10,11... | collective-permute-start | bytes 3080 | tf_op jit(solution)/shard_map/ppermute | solution.py:311
  105.4 6.5 %collective-permute-start.10 = (f32[2,128]{1,0:T(2,128)S(1)}, f32[2,128]{1,0:T(2,128)S(1)}, u32[]{:S(2)}, u32[]{:S(2)}) collective-permute-start(f32[2,128]{1,0:T(2,128)S(1)} %add.27), channel_id=1, source_target_pairs={{0,4},{2,6},{4,0},{6,2},{8,12},{10,14},{12,8},{14,10},{16,20},{18,... | collective-permute-start | bytes 3080 | tf_op jit(solution)/shard_map/ppermute | solution.py:311
  111.9 10.4 %collective-permute-start.13 = (f32[2,128]{1,0:T(2,128)S(1)}, f32[2,128]{1,0:T(2,128)S(1)}, u32[]{:S(2)}, u32[]{:S(2)}) collective-permute-start(f32[2,128]{1,0:T(2,128)S(1)} %add.28), channel_id=1, source_target_pairs={{0,24},{2,26},{4,28},{6,30},{8,16},{10,18},{12,20},{14,22},{16,8},... | collective-permute-start | bytes 3080 | tf_op jit(solution)/shard_map/ppermute | solution.py:311
  117.0 5.3 %collective-permute-start.12 = (f32[2,128]{1,0:T(2,128)S(1)}, f32[2,128]{1,0:T(2,128)S(1)}, u32[]{:S(2)}, u32[]{:S(2)}) collective-permute-start(f32[2,128]{1,0:T(2,128)S(1)} %add.28), channel_id=1, source_target_pairs={{0,16},{2,18},{4,20},{6,22},{8,24},{10,26},{12,28},{14,30},{16,0},... | collective-permute-start | bytes 3080 | tf_op jit(solution)/shard_map/ppermute | solution.py:311
  117.0 5.3 %collective-permute-start.11 = (f32[2,128]{1,0:T(2,128)S(1)}, f32[2,128]{1,0:T(2,128)S(1)}, u32[]{:S(2)}, u32[]{:S(2)}) collective-permute-start(f32[2,128]{1,0:T(2,128)S(1)} %add.28), channel_id=1, source_target_pairs={{0,8},{2,10},{4,12},{6,14},{8,0},{10,2},{12,4},{14,6},{16,24},{18,... | collective-permute-start | bytes 3080 | tf_op jit(solution)/shard_map/ppermute | solution.py:311

commit v3 on v2

--- a/solution.py
+++ b/solution.py
@@ -36,7 +36,7 @@
 def heads_kernel(
     shard_ref, q_ref, g_ref, own_ref, near_ref, far_ref, q_gain_ref, k_gain_ref,
     dq_ref, d_own_ref, d_near_ref, d_far_ref, gains_ref,
-    k_low, k_low_t, values, q_low, probs_all, d_scores_all,
+    k_low, k_low_t, k_rms, values, q_low, q_rms, probs_all, d_scores_all,
 ):
     rows = own_ref.shape[2]
     group = q_ref.shape[1] // rows
@@ -55,11 +55,15 @@
     for place, ref in enumerate(key_refs):
         raw = ref[0, 0].astype(jnp.float32)
         here = slice(place * rows, (place + 1) * rows)
-        k_low[here, :] = (raw * inverse_rms_of(raw) * k_gain).astype(jnp.bfloat16)
+        inverse_rms = jnp.broadcast_to(inverse_rms_of(raw), raw.shape)
+        k_rms[here, :] = inverse_rms
+        k_low[here, :] = (raw * inverse_rms * k_gain).astype(jnp.bfloat16)
         values[here, :] = ref[1, 0]
     k_low_t[...] = k_low[...].T
     raw_q = q_ref[0].astype(jnp.float32)
-    q_low[...] = (raw_q * inverse_rms_of(raw_q) * q_gain).astype(jnp.bfloat16)
+    inverse_rms = jnp.broadcast_to(inverse_rms_of(raw_q), raw_q.shape)
+    q_rms[...] = inverse_rms
+    q_low[...] = (raw_q * inverse_rms * q_gain).astype(jnp.bfloat16)
 
     key_ids = lax.broadcasted_iota(jnp.int32, (TILE, lanes), 0)
     token_ids = lax.broadcasted_iota(jnp.int32, (TILE, lanes), 1) // group
@@ -112,7 +116,7 @@
             k_low_t[:, span], d_scores_all[span, mine], preferred_element_type=jnp.float32
         ).T
         raw = q_ref[0, mine, :].astype(jnp.float32)
-        inverse_rms = inverse_rms_of(raw)
+        inverse_rms = q_rms[mine, :]
         q_gain_sum = q_gain_sum + jnp.sum(query_grad * (raw * inverse_rms), axis=0, keepdims=True)
         dq_ref[0, mine, :] = norm_back(query_grad, raw, inverse_rms, q_gain).astype(dq_ref.dtype)
 
@@ -138,10 +142,8 @@
                 continue
             inside = slice(start - place * rows, stop - place * rows)
             here = slice(start - first * TILE, stop - first * TILE)
-            raw = ref[0, 0, inside, :].astype(jnp.float32)
-            k_gain_sum = k_gain_sum + jnp.sum(
-                key_grad[here] * (raw * inverse_rms_of(raw)), axis=0, keepdims=True
-            )
+            unit = ref[0, 0, inside, :].astype(jnp.float32) * k_rms[start:stop, :]
+            k_gain_sum = k_gain_sum + jnp.sum(key_grad[here] * unit, axis=0, keepdims=True)
             out[0, 0, inside, :] = key_grad[here].astype(out.dtype)
             out[1, 0, inside, :] = value_grad[here].astype(out.dtype)
     gains_ref[0:1, :] += q_gain_sum
@@ -167,17 +169,18 @@
 
 def finish_kernel(shard_ref, own, returned, swapped, raw_ref, k_gain_ref, *rest):
     *done, key_out, value_out, by_token = rest
+    rows, heads, _ = key_out.shape
     before = [(part, head) for part in done for head in range(part.shape[1])]
     for kind, out in ((0, key_out), (1, value_out)):
         for place, (part, head) in enumerate(before):
-            by_token[:, place, :] = part[kind, head].astype(jnp.float32)
+            by_token[pl.ds(place, rows, stride=heads), :] = part[kind, head].astype(jnp.float32)
         for head in range(own.shape[1]):
             grad = closed(shard_ref, own, returned, swapped, kind, head)
             if kind == 0:
                 raw = raw_ref[0, head].astype(jnp.float32)
                 grad = norm_back(grad, raw, inverse_rms_of(raw), k_gain_ref[...])
-            by_token[:, len(before) + head, :] = grad
-        out[...] = by_token[...].astype(out.dtype)
+            by_token[pl.ds(len(before) + head, rows, stride=heads), :] = grad
+        out[...] = by_token[...].reshape(out.shape).astype(out.dtype)
 
 
 def choose_kernel(shard_ref, far_ref, own_ref, out_ref):
@@ -262,8 +265,10 @@
         scratch_shapes=[
             pltpu.VMEM((span, width), jnp.bfloat16),
             pltpu.VMEM((width, span), jnp.bfloat16),
+            pltpu.VMEM((span, width), jnp.float32),
             pltpu.VMEM((span, width), jnp.bfloat16),
             pltpu.VMEM((query_rows, width), jnp.bfloat16),
+            pltpu.VMEM((query_rows, width), jnp.float32),
             pltpu.VMEM((span, query_rows), jnp.bfloat16),
             pltpu.VMEM((span, query_rows), jnp.bfloat16),
         ],
@@ -294,7 +299,7 @@
         in_specs=[smem] + [vmem] * (5 + len(done)),
         out_specs=[vmem, vmem],
         out_shape=[jax.ShapeDtypeStruct(shape, jnp.bfloat16)] * 2,
-        scratch_shapes=[pltpu.VMEM(shape, jnp.float32)],
+        scratch_shapes=[pltpu.VMEM((rows * kv_dev, width), jnp.float32)],
         compiler_params=pltpu.CompilerParams(vmem_limit_bytes=20 * 1024 * 1024),
     )(shard, own, returned, swapped, raw, k_gain, *done)
 

time: 123 us -> 122 us (level)
  Pallas kernels: 54 us -> 50.7 us
  waiting for transfers between devices: 33.5 us -> 36.4 us
    pallas_call x1, Pallas kernels: 4.71 us -> 2.58 us  [finish(): pl.pallas_call(finish_kernel, in_specs=[smem] + [vmem] * (5 + len(done)),...]
    ppermute x2, waiting for transfers between devices: 9.22 us -> 10.5 us  [per_device(): kept.append((stays, lax.ppermute(relayed, 'seq', back)))]
  transfers between devices with their start and end apart: 16 -> 16, of which waited for: 10 -> 10; matrix products, arithmetic and copies ran while one was open for 6% -> 6% of each run, Pallas kernels for 43% -> 41%
where the time goes in v3:
time: 122 us; the launch traced here: 121 us
  Pallas kernels  50.7 us (42%)
  waiting for transfers between devices  36.4 us (30%)
  starting transfers between devices  22.2 us (18%)
  local copies, waits for them, and re-layouts  10.8 us (9%)
    pallas_call x3, Pallas kernels, group_grads(): pl.pallas_call(heads_kernel, grid=(count,), in_specs=[pl.BlockSpec(memory...  44 us
    ppermute x2, waiting for transfers between devices, per_device(): fars = [lax.ppermute(own, 'seq', ahead) for own in owns]  15.1 us
    ppermute x2, waiting for transfers between devices, per_device(): kept.append((stays, lax.ppermute(relayed, 'seq', back)))  10.5 us
    ppermute x6, starting transfers between devices, exchanged(): lax.ppermute(value, axis, [(source, source ^ mask << low) for source in r...  8.76 us
    ppermute x2, starting transfers between devices, per_device(): fars = [lax.ppermute(own, 'seq', ahead) for own in owns]  8.4 us
    ppermute x2, waiting for transfers between devices, per_device(): lax.ppermute(small_call(choose_kernel, scalar, far, own), 'seq', swap)  5.29 us
    reshape x2, local copies, waits for them, and re-layouts, by_head(): split = array.reshape(rows, kv_dev, group, width)  4.62 us
    ppermute x6, waiting for transfers between devices, exchanged(): lax.ppermute(value, axis, [(source, source ^ mask << low) for source in r...  4.47 us
  transfers between devices with their start and end apart: 16, of which 10 were waited for; matrix products, arithmetic and copies ran while one was open for 6% of the time, Pallas kernels for 41%

profile of v3, /device:TPU:0, one launch (start us, length us, event | category | flops | bytes accessed | tf_op | source)
XLA Modules:
  0.0 121.5 jit_solution(11836320556745020063)
XLA Ops:
  0.6 1.9 %copy_bitcast_fusion = (bf16[8,512,128]{2,1,0:T(8,128)(2,1)S(1)}, bf16[8,512,128]{2,1,0:T(8,128)(2,1)S(1)}) fusion(bf16[512,8,128]{2,1,0:T(8,128)(2,1)} %param.8, bf16[512,8,128]{2,1,0:T(8,128)(2,1)} %param.7), kind=kLoop, calls=%fused_computation.2 | loop fusion | bytes 4194304 | tf_op jit(solution)/shard_map/transpose | solution.py:345
  2.7 5.8 %collective-permute-start.1 = (bf16[2,3,512,128]{3,2,1,0:T(8,128)(2,1)S(1)}, bf16[2,3,512,128]{3,2,1,0:T(8,128)(2,1)}, u32[]{:S(2)}, u32[]{:S(2)}) collective-permute-start(bf16[2,3,512,128]{3,2,1,0:T(8,128)(2,1)S(1)} %pad_maximum_fusion.2.own_ref), channel_id=1, source_target_pairs={{0,4},{2,6},{4,8},{6,10},{8,12},{10,14},{12,16},{14,18},{16,20},{1... | collective-permute-start | bytes 2359304 | tf_op jit(solution)/shard_map/ppermute | solution.py:347
  9.5 2.6 %collective-permute-start = (bf16[2,5,512,128]{3,2,1,0:T(8,128)(2,1)S(1)}, bf16[2,5,512,128]{3,2,1,0:T(8,128)(2,1)S(1)}, u32[]{:S(2)}, u32[]{:S(2)}) collective-permute-start(bf16[2,5,512,128]{3,2,1,0:T(8,128)(2,1)S(1)} %pad_maximum_fusion.1.own_ref), channel_id=1, source_target_pairs={{0,4},{2,6},{4,8},{6,10},{8,12},{10,14},{12,16},{14,18},{16,20},{1... | collective-permute-start | bytes 3932168 | tf_op jit(solution)/shard_map/ppermute | solution.py:347
  12.2 3.2 %copy.13 = bf16[512,8,2,128]{3,2,0,1:T(2,128)(2,1)S(1)} copy(bf16[512,8,2,128]{3,2,1,0:T(2,128)(2,1)} %bitcast.53) | data formatting | bytes 4194304 | tf_op jit(solution)/shard_map/reshape | solution.py:339
  15.4 1.4 %copy.14 = bf16[512,8,2,128]{3,2,0,1:T(2,128)(2,1)S(1)} copy(bf16[512,8,2,128]{3,2,1,0:T(2,128)(2,1)S(1)} %bitcast.54) | data formatting | bytes 4194304 | tf_op jit(solution)/shard_map/reshape | solution.py:339
  16.8 8.7 %collective-permute-done.1.far_ref = bf16[2,3,512,128]{3,2,1,0:T(8,128)(2,1)} collective-permute-done((bf16[2,3,512,128]{3,2,1,0:T(8,128)(2,1)S(1)}, bf16[2,3,512,128]{3,2,1,0:T(8,128)(2,1)}, u32[]{:S(2)}, u32[]{:S(2)}) %collective-permute-start.1) | collective-permute-done | bytes 786464 | tf_op jit(solution)/shard_map/ppermute | solution.py:347
  26.8 2.3 %collective-permute-done.2.near_ref = bf16[2,3,512,128]{3,2,1,0:T(8,128)(2,1)S(1)} collective-permute-done((bf16[2,3,512,128]{3,2,1,0:T(8,128)(2,1)S(1)}, bf16[2,3,512,128]{3,2,1,0:T(8,128)(2,1)S(1)}, u32[]{:S(2)}, u32[]{:S(2)}) %collective-permute-start.2) | collective-permute-done | bytes 786464 | tf_op jit(solution)/shard_map/ppermute | solution.py:376
  29.1 16.8 %shard_map.102 = (bf16[3,1024,128]{2,1,0:T(8,128)(2,1)S(1)}, bf16[2,3,512,128]{3,2,1,0:T(8,128)(2,1)S(1)}, bf16[2,3,512,128]{3,2,1,0:T(8,128)(2,1)S(1)}, bf16[2,...) custom-call(s32[1]{0:T(128)} %bitcast.shard_ref.in_ref, bf16[8,1024,128]{2,1,0:T(8,128)(2,1)S(1)} %bitcast.37, ...), custom_call_target="tpu_custom_call" | custom-call | flops 1000 | bytes 1000 | tf_op jit(solution)/shard_map/pallas_call | solution.py:245
  46.1 6.4 %collective-permute-done.far_ref = bf16[2,5,512,128]{3,2,1,0:T(8,128)(2,1)S(1)} collective-permute-done((bf16[2,5,512,128]{3,2,1,0:T(8,128)(2,1)S(1)}, bf16[2,5,512,128]{3,2,1,0:T(8,128)(2,1)S(1)}, u32[]{:S(2)}, u32[]{:S(2)}) %collective-permute-start) | collective-permute-done | bytes 1310752 | tf_op jit(solution)/shard_map/ppermute | solution.py:347
  52.9 3.0 %collective-permute-done.4.near_ref = bf16[2,5,512,128]{3,2,1,0:T(8,128)(2,1)S(1)} collective-permute-done((bf16[2,5,512,128]{3,2,1,0:T(8,128)(2,1)S(1)}, bf16[2,5,512,128]{3,2,1,0:T(8,128)(2,1)S(1)}, u32[]{:S(2)}, u32[]{:S(2)}) %collective-permute-start.4) | collective-permute-done | bytes 1310752 | tf_op jit(solution)/shard_map/ppermute | solution.py:376
  55.9 1.5 %collective-permute-start.6 = (bf16[2,3,512,128]{3,2,1,0:T(8,128)(2,1)S(1)}, bf16[2,3,512,128]{3,2,1,0:T(8,128)(2,1)S(1)}, u32[]{:S(2)}, u32[]{:S(2)}) collective-permute-start(bf16[2,3,512,128]{3,2,1,0:T(8,128)(2,1)S(1)} %shard_map.104), channel_id=1, source_target_pairs={{4,0},{6,2},{8,4},{10,6},{12,8},{14,10},{16,12},{18,14},{20,16},{2... | collective-permute-start | bytes 2359304 | tf_op jit(solution)/shard_map/ppermute | solution.py:384
  57.4 15.9 %shard_map.106 = (bf16[3,1024,128]{2,1,0:T(8,128)(2,1)S(1)}, bf16[2,3,512,128]{3,2,1,0:T(8,128)(2,1)S(1)}, bf16[2,3,512,128]{3,2,1,0:T(8,128)(2,1)S(1)}, bf16[2,...) custom-call(s32[1]{0:T(128)} %bitcast.shard_ref.in_ref, bf16[8,1024,128]{2,1,0:T(8,128)(2,1)S(1)} %bitcast.38, ...), custom_call_target="tpu_custom_call" | custom-call | flops 1000 | bytes 1000 | tf_op jit(solution)/shard_map/pallas_call | solution.py:245
  73.5 4.6 %collective-permute-done.6.returned = bf16[2,3,512,128]{3,2,1,0:T(8,128)(2,1)S(1)} collective-permute-done((bf16[2,3,512,128]{3,2,1,0:T(8,128)(2,1)S(1)}, bf16[2,3,512,128]{3,2,1,0:T(8,128)(2,1)S(1)}, u32[]{:S(2)}, u32[]{:S(2)}) %collective-permute-start.6) | collective-permute-done | bytes 786464 | tf_op jit(solution)/shard_map/ppermute | solution.py:384
  78.9 1.4 %collective-permute-start.7 = (bf16[2,3,512,128]{3,2,1,0:T(8,128)(2,1)S(1)}, bf16[2,3,512,128]{3,2,1,0:T(8,128)(2,1)S(1)}, u32[]{:S(2)}, u32[]{:S(2)}) collective-permute-start(bf16[2,3,512,128]{3,2,1,0:T(8,128)(2,1)S(1)} %shard_map.107), channel_id=1, source_target_pairs={{4,0},{6,2},{8,4},{10,6},{12,8},{14,10},{16,12},{18,14},{20,16},{2... | collective-permute-start | bytes 2359304 | tf_op jit(solution)/shard_map/ppermute | solution.py:384
  80.4 11.3 %shard_map.110 = (bf16[2,1024,128]{2,1,0:T(8,128)(2,1)S(1)}, bf16[2,2,512,128]{3,2,1,0:T(8,128)(2,1)S(1)}, bf16[2,2,512,128]{3,2,1,0:T(8,128)(2,1)S(1)}, bf16[2,...) custom-call(s32[1]{0:T(128)} %shard_map.108.shard_ref, bf16[8,1024,128]{2,1,0:T(8,128)(2,1)S(1)} %bitcast.39, ...), custom_call_target="tpu_custom_call" | custom-call | flops 1000 | bytes 1000 | tf_op jit(solution)/shard_map/pallas_call | solution.py:245
  93.8 1.5 %collective-permute-start.15 = (bf16[2,2,512,128]{3,2,1,0:T(8,128)(2,1)S(1)}, bf16[2,2,512,128]{3,2,1,0:T(8,128)(2,1)S(1)}, u32[]{:S(2)}, u32[]{:S(2)}) collective-permute-start(bf16[2,2,512,128]{3,2,1,0:T(8,128)(2,1)S(1)} %shard_map.113), channel_id=1, source_target_pairs={{4,0},{6,2},{8,4},{10,6},{12,8},{14,10},{16,12},{18,14},{20,16},{2... | collective-permute-start | bytes 1572872 | tf_op jit(solution)/shard_map/ppermute | solution.py:399
  95.3 5.9 %collective-permute-done.7.returned = bf16[2,3,512,128]{3,2,1,0:T(8,128)(2,1)S(1)} collective-permute-done((bf16[2,3,512,128]{3,2,1,0:T(8,128)(2,1)S(1)}, bf16[2,3,512,128]{3,2,1,0:T(8,128)(2,1)S(1)}, u32[]{:S(2)}, u32[]{:S(2)}) %collective-permute-start.7) | collective-permute-done | bytes 786464 | tf_op jit(solution)/shard_map/ppermute | solution.py:384
  102.3 1.5 %collective-permute-start.9 = (f32[2,128]{1,0:T(2,128)S(1)}, f32[2,128]{1,0:T(2,128)S(1)}, u32[]{:S(2)}, u32[]{:S(2)}) collective-permute-start(f32[2,128]{1,0:T(2,128)S(1)} %add.26), channel_id=1, source_target_pairs={{0,1},{1,0},{2,3},{3,2},{4,5},{5,4},{6,7},{7,6},{8,9},{9,8},{10,11... | collective-permute-start | bytes 3080 | tf_op jit(solution)/shard_map/ppermute | solution.py:316
  103.9 2.0 %collective-permute-done.9 = f32[2,128]{1,0:T(2,128)S(1)} collective-permute-done((f32[2,128]{1,0:T(2,128)S(1)}, f32[2,128]{1,0:T(2,128)S(1)}, u32[]{:S(2)}, u32[]{:S(2)}) %collective-permute-start.9) | collective-permute-done | bytes 1056 | tf_op jit(solution)/shard_map/ppermute | solution.py:316
  105.9 2.4 %collective-permute-start.10 = (f32[2,128]{1,0:T(2,128)S(1)}, f32[2,128]{1,0:T(2,128)S(1)}, u32[]{:S(2)}, u32[]{:S(2)}) collective-permute-start(f32[2,128]{1,0:T(2,128)S(1)} %add.27), channel_id=1, source_target_pairs={{0,4},{2,6},{4,0},{6,2},{8,12},{10,14},{12,8},{14,10},{16,20},{18,... | collective-permute-start | bytes 3080 | tf_op jit(solution)/shard_map/ppermute | solution.py:316
  108.5 2.8 %copy.15 = bf16[512,8,2,128]{3,2,1,0:T(2,128)(2,1)} copy(bf16[512,8,2,128]{3,2,0,1:T(2,128)(2,1)S(1)} %bitcast.52) | data formatting | bytes 4194304 | tf_op jit(solution)/shard_map/transpose | solution.py:401
  112.1 4.3 %collective-permute-start.13 = (f32[2,128]{1,0:T(2,128)S(1)}, f32[2,128]{1,0:T(2,128)S(1)}, u32[]{:S(2)}, u32[]{:S(2)}) collective-permute-start(f32[2,128]{1,0:T(2,128)S(1)} %add.28), channel_id=1, source_target_pairs={{0,24},{2,26},{4,28},{6,30},{8,16},{10,18},{12,20},{14,22},{16,8},... | collective-permute-start | bytes 3080 | tf_op jit(solution)/shard_map/ppermute | solution.py:316
  117.1 2.6 %shard_map.114 = (bf16[512,8,128]{2,1,0:T(8,128)(2,1)}, bf16[512,8,128]{2,1,0:T(8,128)(2,1)}) custom-call(s32[1]{0:T(128)} %bitcast.shard_ref.in_ref, bf16[2,2,512,128]{3,2,1,0:T(8,128)(2,1)S(1)} %get-tuple-element.80.own, bf16[2,2,512,128]{3,2,1,0:T(8,128)(2,1)S(1)} %collective-permute-done.15.returned, ...), custom_call_target="tpu_custom_call" | custom-call | tf_op jit(solution)/shard_map/pallas_call | solution.py:297
  119.7 1.3 %collective-permute-done.12 = f32[2,128]{1,0:T(2,128)S(1)} collective-permute-done((f32[2,128]{1,0:T(2,128)S(1)}, f32[2,128]{1,0:T(2,128)S(1)}, u32[]{:S(2)}, u32[]{:S(2)}) %collective-permute-start.12) | collective-permute-done | bytes 1056 | tf_op jit(solution)/shard_map/ppermute | solution.py:316
  (58 shorter events, 9.4 us)
Async XLA Ops:
  2.6 6.0 %copy-start = (bf16[1,3,512,128]{3,2,1,0:T(8,128)(2,1)}, bf16[1,3,512,128]{3,2,1,0:T(8,128)(2,1)S(1)}, u32[]{:S(2)}) copy-start(bf16[1,3,512,128]{3,2,1,0:T(8,128)(2,1)S(1)} %slice_bitcast_fusion.3.raw_ref) | copy-start | bytes 1179652
  2.7 22.8 %collective-permute-start.1 = (bf16[2,3,512,128]{3,2,1,0:T(8,128)(2,1)S(1)}, bf16[2,3,512,128]{3,2,1,0:T(8,128)(2,1)}, u32[]{:S(2)}, u32[]{:S(2)}) collective-permute-start(bf16[2,3,512,128]{3,2,1,0:T(8,128)(2,1)S(1)} %pad_maximum_fusion.2.own_ref), channel_id=1, source_target_pairs={{0,4},{2,6},{4,8},{6,10},{8,12},{10,14},{12,16},{14,18},{16,20},{1... | collective-permute-start | bytes 2359304 | tf_op jit(solution)/shard_map/ppermute | solution.py:347
  8.6 0.8 copy-start.4
  9.5 43.0 %collective-permute-start = (bf16[2,5,512,128]{3,2,1,0:T(8,128)(2,1)S(1)}, bf16[2,5,512,128]{3,2,1,0:T(8,128)(2,1)S(1)}, u32[]{:S(2)}, u32[]{:S(2)}) collective-permute-start(bf16[2,5,512,128]{3,2,1,0:T(8,128)(2,1)S(1)} %pad_maximum_fusion.1.own_ref), channel_id=1, source_target_pairs={{0,4},{2,6},{4,8},{6,10},{8,12},{10,14},{12,16},{14,18},{16,20},{1... | collective-permute-start | bytes 3932168 | tf_op jit(solution)/shard_map/ppermute | solution.py:347
  12.2 3.2 %copy-start.6 = (bf16[512,16,128]{2,1,0:T(8,128)(2,1)S(1)}, bf16[512,16,128]{2,1,0:T(8,128)(2,1)}, u32[]{:S(2)}) copy-start(bf16[512,16,128]{2,1,0:T(8,128)(2,1)} %param.9) | copy-start | bytes 6291460
  16.8 12.3 %copy-start.2 = (f32[128]{0:T(128)S(1)}, f32[128]{0:T(128)}, u32[]{:S(2)}) copy-start(f32[128]{0:T(128)} %param.11) | copy-start | bytes 1540
  16.8 12.3 %copy-start.3 = (f32[128]{0:T(128)S(1)}, f32[128]{0:T(128)}, u32[]{:S(2)}) copy-start(f32[128]{0:T(128)} %param.10) | copy-start | bytes 1540
  26.7 2.4 %collective-permute-start.2 = (bf16[2,3,512,128]{3,2,1,0:T(8,128)(2,1)S(1)}, bf16[2,3,512,128]{3,2,1,0:T(8,128)(2,1)S(1)}, u32[]{:S(2)}, u32[]{:S(2)}) collective-permute-start(bf16[2,3,512,128]{3,2,1,0:T(8,128)(2,1)S(1)} %shard_map.101), channel_id=1, source_target_pairs={{0,2},{2,0},{4,6},{6,4},{8,10},{10,8},{12,14},{14,12},{16,18},{18,... | collective-permute-start | bytes 2359304 | tf_op jit(solution)/shard_map/ppermute | solution.py:376
  45.9 6.6 %collective-permute-start.3 = (bf16[2,3,512,128]{3,2,1,0:T(8,128)(2,1)S(1)}, bf16[2,3,512,128]{3,2,1,0:T(8,128)(2,1)S(1)}, u32[]{:S(2)}, u32[]{:S(2)}) collective-permute-start(bf16[2,3,512,128]{3,2,1,0:T(8,128)(2,1)S(1)} %get-tuple-element.57), channel_id=1, source_target_pairs={{0,2},{2,0},{4,6},{6,4},{8,10},{10,8},{12,14},{14,12},{16,18},{18,... | collective-permute-start | bytes 2359304 | tf_op jit(solution)/shard_map/ppermute | solution.py:353
  52.8 3.1 %collective-permute-start.4 = (bf16[2,5,512,128]{3,2,1,0:T(8,128)(2,1)S(1)}, bf16[2,5,512,128]{3,2,1,0:T(8,128)(2,1)S(1)}, u32[]{:S(2)}, u32[]{:S(2)}) collective-permute-start(bf16[2,5,512,128]{3,2,1,0:T(8,128)(2,1)S(1)} %shard_map.105), channel_id=1, source_target_pairs={{0,2},{2,0},{4,6},{6,4},{8,10},{10,8},{12,14},{14,12},{16,18},{18,... | collective-permute-start | bytes 3932168 | tf_op jit(solution)/shard_map/ppermute | solution.py:376
  55.9 22.2 %collective-permute-start.6 = (bf16[2,3,512,128]{3,2,1,0:T(8,128)(2,1)S(1)}, bf16[2,3,512,128]{3,2,1,0:T(8,128)(2,1)S(1)}, u32[]{:S(2)}, u32[]{:S(2)}) collective-permute-start(bf16[2,3,512,128]{3,2,1,0:T(8,128)(2,1)S(1)} %shard_map.104), channel_id=1, source_target_pairs={{4,0},{6,2},{8,4},{10,6},{12,8},{14,10},{16,12},{18,14},{20,16},{2... | collective-permute-start | bytes 2359304 | tf_op jit(solution)/shard_map/ppermute | solution.py:384
  73.3 5.3 %collective-permute-start.5 = (bf16[2,3,512,128]{3,2,1,0:T(8,128)(2,1)S(1)}, bf16[2,3,512,128]{3,2,1,0:T(8,128)(2,1)S(1)}, u32[]{:S(2)}, u32[]{:S(2)}) collective-permute-start(bf16[2,3,512,128]{3,2,1,0:T(8,128)(2,1)S(1)} %get-tuple-element.63), channel_id=1, source_target_pairs={{0,2},{2,0},{4,6},{6,4},{8,10},{10,8},{12,14},{14,12},{16,18},{18,... | collective-permute-start | bytes 2359304 | tf_op jit(solution)/shard_map/ppermute | solution.py:353
  78.9 12.8 %copy-start.1 = (bf16[1,3,512,128]{3,2,1,0:T(8,128)(2,1)S(1)}, bf16[1,3,512,128]{3,2,1,0:T(8,128)(2,1)}, u32[]{:S(2)}) copy-start(bf16[1,3,512,128]{3,2,1,0:T(8,128)(2,1)} %copy-done) | copy-start | bytes 1179652
  78.9 22.3 %collective-permute-start.7 = (bf16[2,3,512,128]{3,2,1,0:T(8,128)(2,1)S(1)}, bf16[2,3,512,128]{3,2,1,0:T(8,128)(2,1)S(1)}, u32[]{:S(2)}, u32[]{:S(2)}) collective-permute-start(bf16[2,3,512,128]{3,2,1,0:T(8,128)(2,1)S(1)} %shard_map.107), channel_id=1, source_target_pairs={{4,0},{6,2},{8,4},{10,6},{12,8},{14,10},{16,12},{18,14},{20,16},{2... | collective-permute-start | bytes 2359304 | tf_op jit(solution)/shard_map/ppermute | solution.py:384
  91.7 2.0 %collective-permute-start.14 = (bf16[2,2,512,128]{3,2,1,0:T(8,128)(2,1)S(1)}, bf16[2,2,512,128]{3,2,1,0:T(8,128)(2,1)S(1)}, u32[]{:S(2)}, u32[]{:S(2)}) collective-permute-start(bf16[2,2,512,128]{3,2,1,0:T(8,128)(2,1)S(1)} %get-tuple-element.82), channel_id=1, source_target_pairs={{0,2},{2,0},{4,6},{6,4},{8,10},{10,8},{12,14},{14,12},{16,18},{18,... | collective-permute-start | bytes 1572872 | tf_op jit(solution)/shard_map/ppermute | solution.py:353
  93.8 23.3 %collective-permute-start.15 = (bf16[2,2,512,128]{3,2,1,0:T(8,128)(2,1)S(1)}, bf16[2,2,512,128]{3,2,1,0:T(8,128)(2,1)S(1)}, u32[]{:S(2)}, u32[]{:S(2)}) collective-permute-start(bf16[2,2,512,128]{3,2,1,0:T(8,128)(2,1)S(1)} %shard_map.113), channel_id=1, source_target_pairs={{4,0},{6,2},{8,4},{10,6},{12,8},{14,10},{16,12},{18,14},{20,16},{2... | collective-permute-start | bytes 1572872 | tf_op jit(solution)/shard_map/ppermute | solution.py:399
  101.2 2.6 %copy-start.5 = (bf16[1,5,512,128]{3,2,1,0:T(8,128)(2,1)S(1)}, bf16[1,5,512,128]{3,2,1,0:T(8,128)(2,1)}, u32[]{:S(2)}) copy-start(bf16[1,5,512,128]{3,2,1,0:T(8,128)(2,1)} %copy-done.4) | copy-start | bytes 1966084
  101.2 1.1 collective-permute-start.8
  102.3 3.6 %collective-permute-start.9 = (f32[2,128]{1,0:T(2,128)S(1)}, f32[2,128]{1,0:T(2,128)S(1)}, u32[]{:S(2)}, u32[]{:S(2)}) collective-permute-start(f32[2,128]{1,0:T(2,128)S(1)} %add.26), channel_id=1, source_target_pairs={{0,1},{1,0},{2,3},{3,2},{4,5},{5,4},{6,7},{7,6},{8,9},{9,8},{10,11... | collective-permute-start | bytes 3080 | tf_op jit(solution)/shard_map/ppermute | solution.py:316
  105.9 6.2 %collective-permute-start.10 = (f32[2,128]{1,0:T(2,128)S(1)}, f32[2,128]{1,0:T(2,128)S(1)}, u32[]{:S(2)}, u32[]{:S(2)}) collective-permute-start(f32[2,128]{1,0:T(2,128)S(1)} %add.27), channel_id=1, source_target_pairs={{0,4},{2,6},{4,0},{6,2},{8,12},{10,14},{12,8},{14,10},{16,20},{18,... | collective-permute-start | bytes 3080 | tf_op jit(solution)/shard_map/ppermute | solution.py:316
  112.1 7.5 %collective-permute-start.13 = (f32[2,128]{1,0:T(2,128)S(1)}, f32[2,128]{1,0:T(2,128)S(1)}, u32[]{:S(2)}, u32[]{:S(2)}) collective-permute-start(f32[2,128]{1,0:T(2,128)S(1)} %add.28), channel_id=1, source_target_pairs={{0,24},{2,26},{4,28},{6,30},{8,16},{10,18},{12,20},{14,22},{16,8},... | collective-permute-start | bytes 3080 | tf_op jit(solution)/shard_map/ppermute | solution.py:316
  116.5 4.5 %collective-permute-start.12 = (f32[2,128]{1,0:T(2,128)S(1)}, f32[2,128]{1,0:T(2,128)S(1)}, u32[]{:S(2)}, u32[]{:S(2)}) collective-permute-start(f32[2,128]{1,0:T(2,128)S(1)} %add.28), channel_id=1, source_target_pairs={{0,16},{2,18},{4,20},{6,22},{8,24},{10,26},{12,28},{14,30},{16,0},... | collective-permute-start | bytes 3080 | tf_op jit(solution)/shard_map/ppermute | solution.py:316
  116.5 4.5 %collective-permute-start.11 = (f32[2,128]{1,0:T(2,128)S(1)}, f32[2,128]{1,0:T(2,128)S(1)}, u32[]{:S(2)}, u32[]{:S(2)}) collective-permute-start(f32[2,128]{1,0:T(2,128)S(1)} %add.28), channel_id=1, source_target_pairs={{0,8},{2,10},{4,12},{6,14},{8,0},{10,2},{12,4},{14,6},{16,24},{18,... | collective-permute-start | bytes 3080 | tf_op jit(solution)/shard_map/ppermute | solution.py:316

commit v4 on v3

--- a/solution.py
+++ b/solution.py
@@ -33,10 +33,14 @@
     )
 
 
+def by_sublane(tile):
+    return jnp.sum(tile.reshape(-1, 8, tile.shape[1]), axis=0)
+
+
 def heads_kernel(
     shard_ref, q_ref, g_ref, own_ref, near_ref, far_ref, q_gain_ref, k_gain_ref,
     dq_ref, d_own_ref, d_near_ref, d_far_ref, gains_ref,
-    k_low, k_low_t, k_rms, values, q_low, q_rms, probs_all, d_scores_all,
+    k_low, k_low_t, k_rms, values, q_low, q_rms, g_low, exps, d_scores, d_probs_held,
 ):
     rows = own_ref.shape[2]
     group = q_ref.shape[1] // rows
@@ -72,48 +76,50 @@
     q_gain_sum = jnp.zeros_like(q_gain)
 
     for block in range(blocks):
-        span = slice(block * TILE, block * TILE + WINDOW + TILE)
+        start = block * TILE
+        span = slice(start, start + WINDOW + TILE)
         mine = slice(block * lanes, (block + 1) * lanes)
         scores = lax.dot_general(
             k_low[span, :], q_low[mine, :], NT, preferred_element_type=jnp.float32
         )
-        scores = jnp.concatenate(
-            [jnp.where(late, scores[WINDOW:], scores[:TILE]), scores[TILE:WINDOW]], axis=0
+        edge = jnp.where(late, scores[WINDOW:], scores[:TILE])
+        edge = jnp.exp2(edge * exp2_scale) * edge_ok
+        exps[start : start + TILE, mine] = jnp.where(late, 0.0, edge).astype(jnp.bfloat16)
+        exps[start + WINDOW : start + WINDOW + TILE, mine] = jnp.where(late, edge, 0.0).astype(
+            jnp.bfloat16
         )
-        exp_scores = jnp.exp2(scores * exp2_scale)
-        edge = exp_scores[:TILE] * edge_ok
-        first_near = (blocks - block) * TILE
-        first_own = first_near + rows
-        total = jnp.sum(edge, axis=0, keepdims=True)
-        for low, high, ok in (
-            (TILE, first_near, far_ok),
-            (first_near, min(first_own, WINDOW), near_ok),
-            (first_own, WINDOW, None),
-        ):
-            if low < high:
-                part = jnp.sum(exp_scores[low:high], axis=0, keepdims=True)
-                total = total + (part if ok is None else part * ok)
-        inverse = 1.0 / total
-        probs = jnp.concatenate([edge, exp_scores[TILE:]], axis=0) * inverse
-        d_probs = lax.dot_general(
-            values[span, :], g_ref[0, mine, :], NT, preferred_element_type=jnp.float32
-        )
-        d_probs = jnp.concatenate(
-            [jnp.where(late, d_probs[WINDOW:], d_probs[:TILE]), d_probs[TILE:WINDOW]], axis=0
-        )
-        offset = jnp.sum(probs * d_probs, axis=0, keepdims=True)
-        d_scores = probs * (d_probs - offset)
-        for whole, held in ((probs, probs_all), (d_scores, d_scores_all)):
-            start = block * TILE
-            held[start : start + TILE, mine] = jnp.where(late, 0.0, whole[:TILE]).astype(
-                jnp.bfloat16
-            )
-            held[start + TILE : start + WINDOW, mine] = whole[TILE:].astype(jnp.bfloat16)
-            held[start + WINDOW : start + WINDOW + TILE, mine] = jnp.where(
-                late, whole[:TILE], 0.0
-            ).astype(jnp.bfloat16)
+        totals = {"own": by_sublane(edge)}
+        for tile in range(1, tiles):
+            part = jnp.exp2(scores[tile * TILE : (tile + 1) * TILE] * exp2_scale)
+            at = start + tile * TILE
+            exps[at : at + TILE, mine] = part.astype(jnp.bfloat16)
+            place = ("far", "near", "own")[min(at // rows, 2)]
+            part = by_sublane(part)
+            totals[place] = totals[place] + part if place in totals else part
+        total = totals["own"]
+        if "far" in totals:
+            total = total + totals["far"] * far_ok
+        if "near" in totals:
+            total = total + totals["near"] * near_ok
+        inverse = 1.0 / jnp.sum(total, axis=0, keepdims=True)
+        scaled_t = (g_ref[0, mine, :].astype(jnp.float32).T * inverse).astype(jnp.bfloat16)
+        g_low[mine, :] = scaled_t.T
+        d_probs = jnp.dot(values[span, :], scaled_t, preferred_element_type=jnp.float32)
+        offset = None
+        for tile in range(tiles + 1):
+            at = start + tile * TILE
+            part = d_probs[tile * TILE : (tile + 1) * TILE]
+            d_probs_held[tile * TILE : (tile + 1) * TILE, :] = part
+            part = by_sublane(exps[at : at + TILE, mine].astype(jnp.float32) * part)
+            offset = part if offset is None else offset + part
+        offset = inverse * jnp.sum(offset, axis=0, keepdims=True)
+        for tile in range(tiles + 1):
+            at = start + tile * TILE
+            part = d_probs_held[tile * TILE : (tile + 1) * TILE, :] - offset
+            part = exps[at : at + TILE, mine].astype(jnp.float32) * part
+            d_scores[at : at + TILE, mine] = part.astype(jnp.bfloat16)
         query_grad = score_scale * jnp.dot(
-            k_low_t[:, span], d_scores_all[span, mine], preferred_element_type=jnp.float32
+            k_low_t[:, span], d_scores[span, mine], preferred_element_type=jnp.float32
         ).T
         raw = q_ref[0, mine, :].astype(jnp.float32)
         inverse_rms = q_rms[mine, :]
@@ -128,10 +134,10 @@
         meets = slice(low * lanes, high * lanes)
         keys = slice(first * TILE, last * TILE)
         value_grad = jnp.dot(
-            probs_all[keys, meets], g_ref[0, meets, :], preferred_element_type=jnp.float32
+            exps[keys, meets], g_low[meets, :], preferred_element_type=jnp.float32
         )
         key_grad = score_scale * jnp.dot(
-            d_scores_all[keys, meets], q_low[meets, :], preferred_element_type=jnp.float32
+            d_scores[keys, meets], q_low[meets, :], preferred_element_type=jnp.float32
         )
         for place, (ref, out) in enumerate(
             zip(key_refs, (d_far_ref, d_near_ref, d_own_ref), strict=True)
@@ -269,8 +275,10 @@
             pltpu.VMEM((span, width), jnp.bfloat16),
             pltpu.VMEM((query_rows, width), jnp.bfloat16),
             pltpu.VMEM((query_rows, width), jnp.float32),
+            pltpu.VMEM((query_rows, width), jnp.bfloat16),
             pltpu.VMEM((span, query_rows), jnp.bfloat16),
             pltpu.VMEM((span, query_rows), jnp.bfloat16),
+            pltpu.VMEM((WINDOW + TILE, TILE * query_rows // rows), jnp.float32),
         ],
         compiler_params=pltpu.CompilerParams(vmem_limit_bytes=22 * 1024 * 1024),
         cost_estimate=LIGHT,

time: 122 us -> 122 us (level)
  no operation moved by 1% of the time
where the time goes in v4:
time: 122 us; the launch traced here: 121 us
  Pallas kernels  50.6 us (41%)
  waiting for transfers between devices  36.4 us (30%)
  starting transfers between devices  22.2 us (18%)
  local copies, waits for them, and re-layouts  10.8 us (9%)
    pallas_call x3, Pallas kernels, group_grads(): pl.pallas_call(heads_kernel, grid=(count,), in_specs=[pl.BlockSpec(memory...  44 us
    ppermute x2, waiting for transfers between devices, per_device(): fars = [lax.ppermute(own, 'seq', ahead) for own in owns]  15.1 us
    ppermute x2, waiting for transfers between devices, per_device(): kept.append((stays, lax.ppermute(relayed, 'seq', back)))  10.5 us
    ppermute x6, starting transfers between devices, exchanged(): lax.ppermute(value, axis, [(source, source ^ mask << low) for source in r...  8.75 us
    ppermute x2, starting transfers between devices, per_device(): fars = [lax.ppermute(own, 'seq', ahead) for own in owns]  8.4 us
    ppermute x2, waiting for transfers between devices, per_device(): lax.ppermute(small_call(choose_kernel, scalar, far, own), 'seq', swap)  5.29 us
    reshape x2, local copies, waits for them, and re-layouts, by_head(): split = array.reshape(rows, kv_dev, group, width)  4.62 us
    ppermute x6, waiting for transfers between devices, exchanged(): lax.ppermute(value, axis, [(source, source ^ mask << low) for source in r...  4.47 us
  transfers between devices with their start and end apart: 16, of which 10 were waited for; matrix products, arithmetic and copies ran while one was open for 6% of the time, Pallas kernels for 41%

profile of v4, /device:TPU:0, one launch (start us, length us, event | category | flops | bytes accessed | tf_op | source)
XLA Modules:
  0.0 121.5 jit_solution(10133539878430101337)
XLA Ops:
  0.6 1.9 %copy_bitcast_fusion = (bf16[8,512,128]{2,1,0:T(8,128)(2,1)S(1)}, bf16[8,512,128]{2,1,0:T(8,128)(2,1)S(1)}) fusion(bf16[512,8,128]{2,1,0:T(8,128)(2,1)} %param.8, bf16[512,8,128]{2,1,0:T(8,128)(2,1)} %param.7), kind=kLoop, calls=%fused_computation.2 | loop fusion | bytes 4194304 | tf_op jit(solution)/shard_map/transpose | solution.py:353
  2.7 5.8 %collective-permute-start.1 = (bf16[2,3,512,128]{3,2,1,0:T(8,128)(2,1)S(1)}, bf16[2,3,512,128]{3,2,1,0:T(8,128)(2,1)}, u32[]{:S(2)}, u32[]{:S(2)}) collective-permute-start(bf16[2,3,512,128]{3,2,1,0:T(8,128)(2,1)S(1)} %pad_maximum_fusion.2.own_ref), channel_id=1, source_target_pairs={{0,4},{2,6},{4,8},{6,10},{8,12},{10,14},{12,16},{14,18},{16,20},{1... | collective-permute-start | bytes 2359304 | tf_op jit(solution)/shard_map/ppermute | solution.py:355
  9.5 2.6 %collective-permute-start = (bf16[2,5,512,128]{3,2,1,0:T(8,128)(2,1)S(1)}, bf16[2,5,512,128]{3,2,1,0:T(8,128)(2,1)S(1)}, u32[]{:S(2)}, u32[]{:S(2)}) collective-permute-start(bf16[2,5,512,128]{3,2,1,0:T(8,128)(2,1)S(1)} %pad_maximum_fusion.1.own_ref), channel_id=1, source_target_pairs={{0,4},{2,6},{4,8},{6,10},{8,12},{10,14},{12,16},{14,18},{16,20},{1... | collective-permute-start | bytes 3932168 | tf_op jit(solution)/shard_map/ppermute | solution.py:355
  12.2 3.2 %copy.13 = bf16[512,8,2,128]{3,2,0,1:T(2,128)(2,1)S(1)} copy(bf16[512,8,2,128]{3,2,1,0:T(2,128)(2,1)} %bitcast.53) | data formatting | bytes 4194304 | tf_op jit(solution)/shard_map/reshape | solution.py:347
  15.4 1.4 %copy.14 = bf16[512,8,2,128]{3,2,0,1:T(2,128)(2,1)S(1)} copy(bf16[512,8,2,128]{3,2,1,0:T(2,128)(2,1)S(1)} %bitcast.54) | data formatting | bytes 4194304 | tf_op jit(solution)/shard_map/reshape | solution.py:347
  16.8 8.7 %collective-permute-done.1.far_ref = bf16[2,3,512,128]{3,2,1,0:T(8,128)(2,1)} collective-permute-done((bf16[2,3,512,128]{3,2,1,0:T(8,128)(2,1)S(1)}, bf16[2,3,512,128]{3,2,1,0:T(8,128)(2,1)}, u32[]{:S(2)}, u32[]{:S(2)}) %collective-permute-start.1) | collective-permute-done | bytes 786464 | tf_op jit(solution)/shard_map/ppermute | solution.py:355
  26.8 2.3 %collective-permute-done.2.near_ref = bf16[2,3,512,128]{3,2,1,0:T(8,128)(2,1)S(1)} collective-permute-done((bf16[2,3,512,128]{3,2,1,0:T(8,128)(2,1)S(1)}, bf16[2,3,512,128]{3,2,1,0:T(8,128)(2,1)S(1)}, u32[]{:S(2)}, u32[]{:S(2)}) %collective-permute-start.2) | collective-permute-done | bytes 786464 | tf_op jit(solution)/shard_map/ppermute | solution.py:384
  29.1 16.8 %shard_map.102 = (bf16[3,1024,128]{2,1,0:T(8,128)(2,1)S(1)}, bf16[2,3,512,128]{3,2,1,0:T(8,128)(2,1)S(1)}, bf16[2,3,512,128]{3,2,1,0:T(8,128)(2,1)S(1)}, bf16[2,...) custom-call(s32[1]{0:T(128)} %bitcast.shard_ref.in_ref, bf16[8,1024,128]{2,1,0:T(8,128)(2,1)S(1)} %bitcast.37, ...), custom_call_target="tpu_custom_call" | custom-call | flops 1000 | bytes 1000 | tf_op jit(solution)/shard_map/pallas_call | solution.py:251
  46.0 6.4 %collective-permute-done.far_ref = bf16[2,5,512,128]{3,2,1,0:T(8,128)(2,1)S(1)} collective-permute-done((bf16[2,5,512,128]{3,2,1,0:T(8,128)(2,1)S(1)}, bf16[2,5,512,128]{3,2,1,0:T(8,128)(2,1)S(1)}, u32[]{:S(2)}, u32[]{:S(2)}) %collective-permute-start) | collective-permute-done | bytes 1310752 | tf_op jit(solution)/shard_map/ppermute | solution.py:355
  52.9 3.0 %collective-permute-done.4.near_ref = bf16[2,5,512,128]{3,2,1,0:T(8,128)(2,1)S(1)} collective-permute-done((bf16[2,5,512,128]{3,2,1,0:T(8,128)(2,1)S(1)}, bf16[2,5,512,128]{3,2,1,0:T(8,128)(2,1)S(1)}, u32[]{:S(2)}, u32[]{:S(2)}) %collective-permute-start.4) | collective-permute-done | bytes 1310752 | tf_op jit(solution)/shard_map/ppermute | solution.py:384
  55.9 1.5 %collective-permute-start.6 = (bf16[2,3,512,128]{3,2,1,0:T(8,128)(2,1)S(1)}, bf16[2,3,512,128]{3,2,1,0:T(8,128)(2,1)S(1)}, u32[]{:S(2)}, u32[]{:S(2)}) collective-permute-start(bf16[2,3,512,128]{3,2,1,0:T(8,128)(2,1)S(1)} %shard_map.104), channel_id=1, source_target_pairs={{4,0},{6,2},{8,4},{10,6},{12,8},{14,10},{16,12},{18,14},{20,16},{2... | collective-permute-start | bytes 2359304 | tf_op jit(solution)/shard_map/ppermute | solution.py:392
  57.4 15.9 %shard_map.106 = (bf16[3,1024,128]{2,1,0:T(8,128)(2,1)S(1)}, bf16[2,3,512,128]{3,2,1,0:T(8,128)(2,1)S(1)}, bf16[2,3,512,128]{3,2,1,0:T(8,128)(2,1)S(1)}, bf16[2,...) custom-call(s32[1]{0:T(128)} %bitcast.shard_ref.in_ref, bf16[8,1024,128]{2,1,0:T(8,128)(2,1)S(1)} %bitcast.38, ...), custom_call_target="tpu_custom_call" | custom-call | flops 1000 | bytes 1000 | tf_op jit(solution)/shard_map/pallas_call | solution.py:251
  73.5 4.6 %collective-permute-done.6.returned = bf16[2,3,512,128]{3,2,1,0:T(8,128)(2,1)S(1)} collective-permute-done((bf16[2,3,512,128]{3,2,1,0:T(8,128)(2,1)S(1)}, bf16[2,3,512,128]{3,2,1,0:T(8,128)(2,1)S(1)}, u32[]{:S(2)}, u32[]{:S(2)}) %collective-permute-start.6) | collective-permute-done | bytes 786464 | tf_op jit(solution)/shard_map/ppermute | solution.py:392
  78.9 1.4 %collective-permute-start.7 = (bf16[2,3,512,128]{3,2,1,0:T(8,128)(2,1)S(1)}, bf16[2,3,512,128]{3,2,1,0:T(8,128)(2,1)S(1)}, u32[]{:S(2)}, u32[]{:S(2)}) collective-permute-start(bf16[2,3,512,128]{3,2,1,0:T(8,128)(2,1)S(1)} %shard_map.107), channel_id=1, source_target_pairs={{4,0},{6,2},{8,4},{10,6},{12,8},{14,10},{16,12},{18,14},{20,16},{2... | collective-permute-start | bytes 2359304 | tf_op jit(solution)/shard_map/ppermute | solution.py:392
  80.4 11.3 %shard_map.110 = (bf16[2,1024,128]{2,1,0:T(8,128)(2,1)S(1)}, bf16[2,2,512,128]{3,2,1,0:T(8,128)(2,1)S(1)}, bf16[2,2,512,128]{3,2,1,0:T(8,128)(2,1)S(1)}, bf16[2,...) custom-call(s32[1]{0:T(128)} %shard_map.108.shard_ref, bf16[8,1024,128]{2,1,0:T(8,128)(2,1)S(1)} %bitcast.39, ...), custom_call_target="tpu_custom_call" | custom-call | flops 1000 | bytes 1000 | tf_op jit(solution)/shard_map/pallas_call | solution.py:251
  93.8 1.5 %collective-permute-start.15 = (bf16[2,2,512,128]{3,2,1,0:T(8,128)(2,1)S(1)}, bf16[2,2,512,128]{3,2,1,0:T(8,128)(2,1)S(1)}, u32[]{:S(2)}, u32[]{:S(2)}) collective-permute-start(bf16[2,2,512,128]{3,2,1,0:T(8,128)(2,1)S(1)} %shard_map.113), channel_id=1, source_target_pairs={{4,0},{6,2},{8,4},{10,6},{12,8},{14,10},{16,12},{18,14},{20,16},{2... | collective-permute-start | bytes 1572872 | tf_op jit(solution)/shard_map/ppermute | solution.py:407
  95.3 5.9 %collective-permute-done.7.returned = bf16[2,3,512,128]{3,2,1,0:T(8,128)(2,1)S(1)} collective-permute-done((bf16[2,3,512,128]{3,2,1,0:T(8,128)(2,1)S(1)}, bf16[2,3,512,128]{3,2,1,0:T(8,128)(2,1)S(1)}, u32[]{:S(2)}, u32[]{:S(2)}) %collective-permute-start.7) | collective-permute-done | bytes 786464 | tf_op jit(solution)/shard_map/ppermute | solution.py:392
  102.4 1.5 %collective-permute-start.9 = (f32[2,128]{1,0:T(2,128)S(1)}, f32[2,128]{1,0:T(2,128)S(1)}, u32[]{:S(2)}, u32[]{:S(2)}) collective-permute-start(f32[2,128]{1,0:T(2,128)S(1)} %add.26), channel_id=1, source_target_pairs={{0,1},{1,0},{2,3},{3,2},{4,5},{5,4},{6,7},{7,6},{8,9},{9,8},{10,11... | collective-permute-start | bytes 3080 | tf_op jit(solution)/shard_map/ppermute | solution.py:324
  103.9 2.0 %collective-permute-done.9 = f32[2,128]{1,0:T(2,128)S(1)} collective-permute-done((f32[2,128]{1,0:T(2,128)S(1)}, f32[2,128]{1,0:T(2,128)S(1)}, u32[]{:S(2)}, u32[]{:S(2)}) %collective-permute-start.9) | collective-permute-done | bytes 1056 | tf_op jit(solution)/shard_map/ppermute | solution.py:324
  105.9 2.4 %collective-permute-start.10 = (f32[2,128]{1,0:T(2,128)S(1)}, f32[2,128]{1,0:T(2,128)S(1)}, u32[]{:S(2)}, u32[]{:S(2)}) collective-permute-start(f32[2,128]{1,0:T(2,128)S(1)} %add.27), channel_id=1, source_target_pairs={{0,4},{2,6},{4,0},{6,2},{8,12},{10,14},{12,8},{14,10},{16,20},{18,... | collective-permute-start | bytes 3080 | tf_op jit(solution)/shard_map/ppermute | solution.py:324
  108.5 2.8 %copy.15 = bf16[512,8,2,128]{3,2,1,0:T(2,128)(2,1)} copy(bf16[512,8,2,128]{3,2,0,1:T(2,128)(2,1)S(1)} %bitcast.52) | data formatting | bytes 4194304 | tf_op jit(solution)/shard_map/transpose | solution.py:409
  112.1 4.3 %collective-permute-start.13 = (f32[2,128]{1,0:T(2,128)S(1)}, f32[2,128]{1,0:T(2,128)S(1)}, u32[]{:S(2)}, u32[]{:S(2)}) collective-permute-start(f32[2,128]{1,0:T(2,128)S(1)} %add.28), channel_id=1, source_target_pairs={{0,24},{2,26},{4,28},{6,30},{8,16},{10,18},{12,20},{14,22},{16,8},... | collective-permute-start | bytes 3080 | tf_op jit(solution)/shard_map/ppermute | solution.py:324
  117.1 2.6 %shard_map.114 = (bf16[512,8,128]{2,1,0:T(8,128)(2,1)}, bf16[512,8,128]{2,1,0:T(8,128)(2,1)}) custom-call(s32[1]{0:T(128)} %bitcast.shard_ref.in_ref, bf16[2,2,512,128]{3,2,1,0:T(8,128)(2,1)S(1)} %get-tuple-element.80.own, bf16[2,2,512,128]{3,2,1,0:T(8,128)(2,1)S(1)} %collective-permute-done.15.returned, ...), custom_call_target="tpu_custom_call" | custom-call | tf_op jit(solution)/shard_map/pallas_call | solution.py:305
  119.7 1.3 %collective-permute-done.12 = f32[2,128]{1,0:T(2,128)S(1)} collective-permute-done((f32[2,128]{1,0:T(2,128)S(1)}, f32[2,128]{1,0:T(2,128)S(1)}, u32[]{:S(2)}, u32[]{:S(2)}) %collective-permute-start.12) | collective-permute-done | bytes 1056 | tf_op jit(solution)/shard_map/ppermute | solution.py:324
  (58 shorter events, 9.4 us)
Async XLA Ops:
  2.6 6.0 %copy-start = (bf16[1,3,512,128]{3,2,1,0:T(8,128)(2,1)}, bf16[1,3,512,128]{3,2,1,0:T(8,128)(2,1)S(1)}, u32[]{:S(2)}) copy-start(bf16[1,3,512,128]{3,2,1,0:T(8,128)(2,1)S(1)} %slice_bitcast_fusion.3.raw_ref) | copy-start | bytes 1179652
  2.7 22.8 %collective-permute-start.1 = (bf16[2,3,512,128]{3,2,1,0:T(8,128)(2,1)S(1)}, bf16[2,3,512,128]{3,2,1,0:T(8,128)(2,1)}, u32[]{:S(2)}, u32[]{:S(2)}) collective-permute-start(bf16[2,3,512,128]{3,2,1,0:T(8,128)(2,1)S(1)} %pad_maximum_fusion.2.own_ref), channel_id=1, source_target_pairs={{0,4},{2,6},{4,8},{6,10},{8,12},{10,14},{12,16},{14,18},{16,20},{1... | collective-permute-start | bytes 2359304 | tf_op jit(solution)/shard_map/ppermute | solution.py:355
  8.6 0.8 copy-start.4
  9.5 43.0 %collective-permute-start = (bf16[2,5,512,128]{3,2,1,0:T(8,128)(2,1)S(1)}, bf16[2,5,512,128]{3,2,1,0:T(8,128)(2,1)S(1)}, u32[]{:S(2)}, u32[]{:S(2)}) collective-permute-start(bf16[2,5,512,128]{3,2,1,0:T(8,128)(2,1)S(1)} %pad_maximum_fusion.1.own_ref), channel_id=1, source_target_pairs={{0,4},{2,6},{4,8},{6,10},{8,12},{10,14},{12,16},{14,18},{16,20},{1... | collective-permute-start | bytes 3932168 | tf_op jit(solution)/shard_map/ppermute | solution.py:355
  12.2 3.2 %copy-start.6 = (bf16[512,16,128]{2,1,0:T(8,128)(2,1)S(1)}, bf16[512,16,128]{2,1,0:T(8,128)(2,1)}, u32[]{:S(2)}) copy-start(bf16[512,16,128]{2,1,0:T(8,128)(2,1)} %param.9) | copy-start | bytes 6291460
  16.8 12.3 %copy-start.2 = (f32[128]{0:T(128)S(1)}, f32[128]{0:T(128)}, u32[]{:S(2)}) copy-start(f32[128]{0:T(128)} %param.11) | copy-start | bytes 1540
  16.8 12.3 %copy-start.3 = (f32[128]{0:T(128)S(1)}, f32[128]{0:T(128)}, u32[]{:S(2)}) copy-start(f32[128]{0:T(128)} %param.10) | copy-start | bytes 1540
  26.7 2.4 %collective-permute-start.2 = (bf16[2,3,512,128]{3,2,1,0:T(8,128)(2,1)S(1)}, bf16[2,3,512,128]{3,2,1,0:T(8,128)(2,1)S(1)}, u32[]{:S(2)}, u32[]{:S(2)}) collective-permute-start(bf16[2,3,512,128]{3,2,1,0:T(8,128)(2,1)S(1)} %shard_map.101), channel_id=1, source_target_pairs={{0,2},{2,0},{4,6},{6,4},{8,10},{10,8},{12,14},{14,12},{16,18},{18,... | collective-permute-start | bytes 2359304 | tf_op jit(solution)/shard_map/ppermute | solution.py:384
  45.8 6.6 %collective-permute-start.3 = (bf16[2,3,512,128]{3,2,1,0:T(8,128)(2,1)S(1)}, bf16[2,3,512,128]{3,2,1,0:T(8,128)(2,1)S(1)}, u32[]{:S(2)}, u32[]{:S(2)}) collective-permute-start(bf16[2,3,512,128]{3,2,1,0:T(8,128)(2,1)S(1)} %get-tuple-element.57), channel_id=1, source_target_pairs={{0,2},{2,0},{4,6},{6,4},{8,10},{10,8},{12,14},{14,12},{16,18},{18,... | collective-permute-start | bytes 2359304 | tf_op jit(solution)/shard_map/ppermute | solution.py:361
  52.8 3.1 %collective-permute-start.4 = (bf16[2,5,512,128]{3,2,1,0:T(8,128)(2,1)S(1)}, bf16[2,5,512,128]{3,2,1,0:T(8,128)(2,1)S(1)}, u32[]{:S(2)}, u32[]{:S(2)}) collective-permute-start(bf16[2,5,512,128]{3,2,1,0:T(8,128)(2,1)S(1)} %shard_map.105), channel_id=1, source_target_pairs={{0,2},{2,0},{4,6},{6,4},{8,10},{10,8},{12,14},{14,12},{16,18},{18,... | collective-permute-start | bytes 3932168 | tf_op jit(solution)/shard_map/ppermute | solution.py:384
  55.9 22.2 %collective-permute-start.6 = (bf16[2,3,512,128]{3,2,1,0:T(8,128)(2,1)S(1)}, bf16[2,3,512,128]{3,2,1,0:T(8,128)(2,1)S(1)}, u32[]{:S(2)}, u32[]{:S(2)}) collective-permute-start(bf16[2,3,512,128]{3,2,1,0:T(8,128)(2,1)S(1)} %shard_map.104), channel_id=1, source_target_pairs={{4,0},{6,2},{8,4},{10,6},{12,8},{14,10},{16,12},{18,14},{20,16},{2... | collective-permute-start | bytes 2359304 | tf_op jit(solution)/shard_map/ppermute | solution.py:392
  73.3 5.3 %collective-permute-start.5 = (bf16[2,3,512,128]{3,2,1,0:T(8,128)(2,1)S(1)}, bf16[2,3,512,128]{3,2,1,0:T(8,128)(2,1)S(1)}, u32[]{:S(2)}, u32[]{:S(2)}) collective-permute-start(bf16[2,3,512,128]{3,2,1,0:T(8,128)(2,1)S(1)} %get-tuple-element.63), channel_id=1, source_target_pairs={{0,2},{2,0},{4,6},{6,4},{8,10},{10,8},{12,14},{14,12},{16,18},{18,... | collective-permute-start | bytes 2359304 | tf_op jit(solution)/shard_map/ppermute | solution.py:361
  78.9 12.8 %copy-start.1 = (bf16[1,3,512,128]{3,2,1,0:T(8,128)(2,1)S(1)}, bf16[1,3,512,128]{3,2,1,0:T(8,128)(2,1)}, u32[]{:S(2)}) copy-start(bf16[1,3,512,128]{3,2,1,0:T(8,128)(2,1)} %copy-done) | copy-start | bytes 1179652
  78.9 22.3 %collective-permute-start.7 = (bf16[2,3,512,128]{3,2,1,0:T(8,128)(2,1)S(1)}, bf16[2,3,512,128]{3,2,1,0:T(8,128)(2,1)S(1)}, u32[]{:S(2)}, u32[]{:S(2)}) collective-permute-start(bf16[2,3,512,128]{3,2,1,0:T(8,128)(2,1)S(1)} %shard_map.107), channel_id=1, source_target_pairs={{4,0},{6,2},{8,4},{10,6},{12,8},{14,10},{16,12},{18,14},{20,16},{2... | collective-permute-start | bytes 2359304 | tf_op jit(solution)/shard_map/ppermute | solution.py:392
  91.7 2.0 %collective-permute-start.14 = (bf16[2,2,512,128]{3,2,1,0:T(8,128)(2,1)S(1)}, bf16[2,2,512,128]{3,2,1,0:T(8,128)(2,1)S(1)}, u32[]{:S(2)}, u32[]{:S(2)}) collective-permute-start(bf16[2,2,512,128]{3,2,1,0:T(8,128)(2,1)S(1)} %get-tuple-element.82), channel_id=1, source_target_pairs={{0,2},{2,0},{4,6},{6,4},{8,10},{10,8},{12,14},{14,12},{16,18},{18,... | collective-permute-start | bytes 1572872 | tf_op jit(solution)/shard_map/ppermute | solution.py:361
  93.8 23.3 %collective-permute-start.15 = (bf16[2,2,512,128]{3,2,1,0:T(8,128)(2,1)S(1)}, bf16[2,2,512,128]{3,2,1,0:T(8,128)(2,1)S(1)}, u32[]{:S(2)}, u32[]{:S(2)}) collective-permute-start(bf16[2,2,512,128]{3,2,1,0:T(8,128)(2,1)S(1)} %shard_map.113), channel_id=1, source_target_pairs={{4,0},{6,2},{8,4},{10,6},{12,8},{14,10},{16,12},{18,14},{20,16},{2... | collective-permute-start | bytes 1572872 | tf_op jit(solution)/shard_map/ppermute | solution.py:407
  101.2 2.6 %copy-start.5 = (bf16[1,5,512,128]{3,2,1,0:T(8,128)(2,1)S(1)}, bf16[1,5,512,128]{3,2,1,0:T(8,128)(2,1)}, u32[]{:S(2)}) copy-start(bf16[1,5,512,128]{3,2,1,0:T(8,128)(2,1)} %copy-done.4) | copy-start | bytes 1966084
  101.2 1.1 collective-permute-start.8
  102.4 3.6 %collective-permute-start.9 = (f32[2,128]{1,0:T(2,128)S(1)}, f32[2,128]{1,0:T(2,128)S(1)}, u32[]{:S(2)}, u32[]{:S(2)}) collective-permute-start(f32[2,128]{1,0:T(2,128)S(1)} %add.26), channel_id=1, source_target_pairs={{0,1},{1,0},{2,3},{3,2},{4,5},{5,4},{6,7},{7,6},{8,9},{9,8},{10,11... | collective-permute-start | bytes 3080 | tf_op jit(solution)/shard_map/ppermute | solution.py:324
  105.9 6.2 %collective-permute-start.10 = (f32[2,128]{1,0:T(2,128)S(1)}, f32[2,128]{1,0:T(2,128)S(1)}, u32[]{:S(2)}, u32[]{:S(2)}) collective-permute-start(f32[2,128]{1,0:T(2,128)S(1)} %add.27), channel_id=1, source_target_pairs={{0,4},{2,6},{4,0},{6,2},{8,12},{10,14},{12,8},{14,10},{16,20},{18,... | collective-permute-start | bytes 3080 | tf_op jit(solution)/shard_map/ppermute | solution.py:324
  112.1 7.5 %collective-permute-start.13 = (f32[2,128]{1,0:T(2,128)S(1)}, f32[2,128]{1,0:T(2,128)S(1)}, u32[]{:S(2)}, u32[]{:S(2)}) collective-permute-start(f32[2,128]{1,0:T(2,128)S(1)} %add.28), channel_id=1, source_target_pairs={{0,24},{2,26},{4,28},{6,30},{8,16},{10,18},{12,20},{14,22},{16,8},... | collective-permute-start | bytes 3080 | tf_op jit(solution)/shard_map/ppermute | solution.py:324
  116.5 4.5 %collective-permute-start.12 = (f32[2,128]{1,0:T(2,128)S(1)}, f32[2,128]{1,0:T(2,128)S(1)}, u32[]{:S(2)}, u32[]{:S(2)}) collective-permute-start(f32[2,128]{1,0:T(2,128)S(1)} %add.28), channel_id=1, source_target_pairs={{0,16},{2,18},{4,20},{6,22},{8,24},{10,26},{12,28},{14,30},{16,0},... | collective-permute-start | bytes 3080 | tf_op jit(solution)/shard_map/ppermute | solution.py:324
  116.5 4.5 %collective-permute-start.11 = (f32[2,128]{1,0:T(2,128)S(1)}, f32[2,128]{1,0:T(2,128)S(1)}, u32[]{:S(2)}, u32[]{:S(2)}) collective-permute-start(f32[2,128]{1,0:T(2,128)S(1)} %add.28), channel_id=1, source_target_pairs={{0,8},{2,10},{4,12},{6,14},{8,0},{10,2},{12,4},{14,6},{16,24},{18,... | collective-permute-start | bytes 3080 | tf_op jit(solution)/shard_map/ppermute | solution.py:324

commit v5 on v3

--- a/solution.py
+++ b/solution.py
@@ -8,7 +8,7 @@
 from jax.sharding import PartitionSpec as P
 
 WINDOW = 1024
-TILE = 128
+TILE = 256
 
 score_scale = 168.0 ** (-0.5)
 norm_eps = 1e-06

time: 122 us -> 121 us (level)
  Pallas kernels: 50.7 us -> 47.5 us
  waiting for transfers between devices: 36.4 us -> 39.3 us
    pallas_call x3, Pallas kernels: 44 us -> 40.8 us  [group_grads(): pl.pallas_call(heads_kernel, grid=(count,), in_specs=[pl.BlockSpec(memory...]
    ppermute x2, waiting for transfers between devices: 10.5 us -> 13.3 us  [per_device(): kept.append((stays, lax.ppermute(relayed, 'seq', back)))]
  transfers between devices with their start and end apart: 16 -> 16, of which waited for: 10 -> 10; matrix products, arithmetic and copies ran while one was open for 6% -> 7% of each run, Pallas kernels for 41% -> 39%
where the time goes in v5:
time: 121 us
  Pallas kernels  47.5 us (39%)
  waiting for transfers between devices  39.3 us (32%)
  starting transfers between devices  21.7 us (18%)
  local copies, waits for them, and re-layouts  10.8 us (9%)
    pallas_call x3, Pallas kernels, group_grads(): pl.pallas_call(heads_kernel, grid=(count,), in_specs=[pl.BlockSpec(memory...  40.8 us
    ppermute x2, waiting for transfers between devices, per_device(): fars = [lax.ppermute(own, 'seq', ahead) for own in owns]  16.3 us
    ppermute x2, waiting for transfers between devices, per_device(): kept.append((stays, lax.ppermute(relayed, 'seq', back)))  13.3 us
    ppermute x2, starting transfers between devices, per_device(): fars = [lax.ppermute(own, 'seq', ahead) for own in owns]  8.4 us
    ppermute x6, starting transfers between devices, exchanged(): lax.ppermute(value, axis, [(source, source ^ mask << low) for source in r...  8.25 us
    ppermute x2, waiting for transfers between devices, per_device(): lax.ppermute(small_call(choose_kernel, scalar, far, own), 'seq', swap)  5.29 us
    reshape x2, local copies, waits for them, and re-layouts, by_head(): split = array.reshape(rows, kv_dev, group, width)  4.62 us
    ppermute x6, waiting for transfers between devices, exchanged(): lax.ppermute(value, axis, [(source, source ^ mask << low) for source in r...  3.39 us
  transfers between devices with their start and end apart: 16, of which 10 were waited for; matrix products, arithmetic and copies ran while one was open for 7% of the time, Pallas kernels for 39%

profile of v5, /device:TPU:0, one launch (start us, length us, event | category | flops | bytes accessed | tf_op | source)
XLA Modules:
  0.0 120.7 jit_solution(3145259897826810597)
XLA Ops:
  0.6 1.9 %copy_bitcast_fusion = (bf16[8,512,128]{2,1,0:T(8,128)(2,1)S(1)}, bf16[8,512,128]{2,1,0:T(8,128)(2,1)S(1)}) fusion(bf16[512,8,128]{2,1,0:T(8,128)(2,1)} %param.8, bf16[512,8,128]{2,1,0:T(8,128)(2,1)} %param.7), kind=kLoop, calls=%fused_computation.2 | loop fusion | bytes 4194304 | tf_op jit(solution)/shard_map/transpose | solution.py:345
  2.7 5.8 %collective-permute-start.1 = (bf16[2,3,512,128]{3,2,1,0:T(8,128)(2,1)S(1)}, bf16[2,3,512,128]{3,2,1,0:T(8,128)(2,1)}, u32[]{:S(2)}, u32[]{:S(2)}) collective-permute-start(bf16[2,3,512,128]{3,2,1,0:T(8,128)(2,1)S(1)} %pad_maximum_fusion.2.own_ref), channel_id=1, source_target_pairs={{0,4},{2,6},{4,8},{6,10},{8,12},{10,14},{12,16},{14,18},{16,20},{1... | collective-permute-start | bytes 2359304 | tf_op jit(solution)/shard_map/ppermute | solution.py:347
  9.5 2.6 %collective-permute-start = (bf16[2,5,512,128]{3,2,1,0:T(8,128)(2,1)S(1)}, bf16[2,5,512,128]{3,2,1,0:T(8,128)(2,1)S(1)}, u32[]{:S(2)}, u32[]{:S(2)}) collective-permute-start(bf16[2,5,512,128]{3,2,1,0:T(8,128)(2,1)S(1)} %pad_maximum_fusion.1.own_ref), channel_id=1, source_target_pairs={{0,4},{2,6},{4,8},{6,10},{8,12},{10,14},{12,16},{14,18},{16,20},{1... | collective-permute-start | bytes 3932168 | tf_op jit(solution)/shard_map/ppermute | solution.py:347
  12.2 3.2 %copy.13 = bf16[512,8,2,128]{3,2,0,1:T(2,128)(2,1)S(1)} copy(bf16[512,8,2,128]{3,2,1,0:T(2,128)(2,1)} %bitcast.53) | data formatting | bytes 4194304 | tf_op jit(solution)/shard_map/reshape | solution.py:339
  15.4 1.4 %copy.14 = bf16[512,8,2,128]{3,2,0,1:T(2,128)(2,1)S(1)} copy(bf16[512,8,2,128]{3,2,1,0:T(2,128)(2,1)S(1)} %bitcast.54) | data formatting | bytes 4194304 | tf_op jit(solution)/shard_map/reshape | solution.py:339
  16.8 8.7 %collective-permute-done.1.far_ref = bf16[2,3,512,128]{3,2,1,0:T(8,128)(2,1)} collective-permute-done((bf16[2,3,512,128]{3,2,1,0:T(8,128)(2,1)S(1)}, bf16[2,3,512,128]{3,2,1,0:T(8,128)(2,1)}, u32[]{:S(2)}, u32[]{:S(2)}) %collective-permute-start.1) | collective-permute-done | bytes 786464 | tf_op jit(solution)/shard_map/ppermute | solution.py:347
  26.8 2.3 %collective-permute-done.2.near_ref = bf16[2,3,512,128]{3,2,1,0:T(8,128)(2,1)S(1)} collective-permute-done((bf16[2,3,512,128]{3,2,1,0:T(8,128)(2,1)S(1)}, bf16[2,3,512,128]{3,2,1,0:T(8,128)(2,1)S(1)}, u32[]{:S(2)}, u32[]{:S(2)}) %collective-permute-start.2) | collective-permute-done | bytes 786464 | tf_op jit(solution)/shard_map/ppermute | solution.py:376
  29.1 15.6 %shard_map.102 = (bf16[3,1024,128]{2,1,0:T(8,128)(2,1)S(1)}, bf16[2,3,512,128]{3,2,1,0:T(8,128)(2,1)S(1)}, bf16[2,3,512,128]{3,2,1,0:T(8,128)(2,1)S(1)}, bf16[2,...) custom-call(s32[1]{0:T(128)} %bitcast.shard_ref.in_ref, bf16[8,1024,128]{2,1,0:T(8,128)(2,1)S(1)} %bitcast.37, ...), custom_call_target="tpu_custom_call" | custom-call | flops 1000 | bytes 1000 | tf_op jit(solution)/shard_map/pallas_call | solution.py:245
  44.9 7.6 %collective-permute-done.far_ref = bf16[2,5,512,128]{3,2,1,0:T(8,128)(2,1)S(1)} collective-permute-done((bf16[2,5,512,128]{3,2,1,0:T(8,128)(2,1)S(1)}, bf16[2,5,512,128]{3,2,1,0:T(8,128)(2,1)S(1)}, u32[]{:S(2)}, u32[]{:S(2)}) %collective-permute-start) | collective-permute-done | bytes 1310752 | tf_op jit(solution)/shard_map/ppermute | solution.py:347
  52.9 3.0 %collective-permute-done.4.near_ref = bf16[2,5,512,128]{3,2,1,0:T(8,128)(2,1)S(1)} collective-permute-done((bf16[2,5,512,128]{3,2,1,0:T(8,128)(2,1)S(1)}, bf16[2,5,512,128]{3,2,1,0:T(8,128)(2,1)S(1)}, u32[]{:S(2)}, u32[]{:S(2)}) %collective-permute-start.4) | collective-permute-done | bytes 1310752 | tf_op jit(solution)/shard_map/ppermute | solution.py:376
  55.9 1.5 %collective-permute-start.6 = (bf16[2,3,512,128]{3,2,1,0:T(8,128)(2,1)S(1)}, bf16[2,3,512,128]{3,2,1,0:T(8,128)(2,1)S(1)}, u32[]{:S(2)}, u32[]{:S(2)}) collective-permute-start(bf16[2,3,512,128]{3,2,1,0:T(8,128)(2,1)S(1)} %shard_map.104), channel_id=1, source_target_pairs={{4,0},{6,2},{8,4},{10,6},{12,8},{14,10},{16,12},{18,14},{20,16},{2... | collective-permute-start | bytes 2359304 | tf_op jit(solution)/shard_map/ppermute | solution.py:384
  57.4 14.7 %shard_map.106 = (bf16[3,1024,128]{2,1,0:T(8,128)(2,1)S(1)}, bf16[2,3,512,128]{3,2,1,0:T(8,128)(2,1)S(1)}, bf16[2,3,512,128]{3,2,1,0:T(8,128)(2,1)S(1)}, bf16[2,...) custom-call(s32[1]{0:T(128)} %bitcast.shard_ref.in_ref, bf16[8,1024,128]{2,1,0:T(8,128)(2,1)S(1)} %bitcast.38, ...), custom_call_target="tpu_custom_call" | custom-call | flops 1000 | bytes 1000 | tf_op jit(solution)/shard_map/pallas_call | solution.py:245
  72.4 5.8 %collective-permute-done.6.returned = bf16[2,3,512,128]{3,2,1,0:T(8,128)(2,1)S(1)} collective-permute-done((bf16[2,3,512,128]{3,2,1,0:T(8,128)(2,1)S(1)}, bf16[2,3,512,128]{3,2,1,0:T(8,128)(2,1)S(1)}, u32[]{:S(2)}, u32[]{:S(2)}) %collective-permute-start.6) | collective-permute-done | bytes 786464 | tf_op jit(solution)/shard_map/ppermute | solution.py:384
  78.9 1.4 %collective-permute-start.7 = (bf16[2,3,512,128]{3,2,1,0:T(8,128)(2,1)S(1)}, bf16[2,3,512,128]{3,2,1,0:T(8,128)(2,1)S(1)}, u32[]{:S(2)}, u32[]{:S(2)}) collective-permute-start(bf16[2,3,512,128]{3,2,1,0:T(8,128)(2,1)S(1)} %shard_map.107), channel_id=1, source_target_pairs={{4,0},{6,2},{8,4},{10,6},{12,8},{14,10},{16,12},{18,14},{20,16},{2... | collective-permute-start | bytes 2359304 | tf_op jit(solution)/shard_map/ppermute | solution.py:384
  80.4 10.5 %shard_map.110 = (bf16[2,1024,128]{2,1,0:T(8,128)(2,1)S(1)}, bf16[2,2,512,128]{3,2,1,0:T(8,128)(2,1)S(1)}, bf16[2,2,512,128]{3,2,1,0:T(8,128)(2,1)S(1)}, bf16[2,...) custom-call(s32[1]{0:T(128)} %shard_map.108.shard_ref, bf16[8,1024,128]{2,1,0:T(8,128)(2,1)S(1)} %bitcast.39, ...), custom_call_target="tpu_custom_call" | custom-call | flops 1000 | bytes 1000 | tf_op jit(solution)/shard_map/pallas_call | solution.py:245
  93.0 1.5 %collective-permute-start.15 = (bf16[2,2,512,128]{3,2,1,0:T(8,128)(2,1)S(1)}, bf16[2,2,512,128]{3,2,1,0:T(8,128)(2,1)S(1)}, u32[]{:S(2)}, u32[]{:S(2)}) collective-permute-start(bf16[2,2,512,128]{3,2,1,0:T(8,128)(2,1)S(1)} %shard_map.113), channel_id=1, source_target_pairs={{4,0},{6,2},{8,4},{10,6},{12,8},{14,10},{16,12},{18,14},{20,16},{2... | collective-permute-start | bytes 1572872 | tf_op jit(solution)/shard_map/ppermute | solution.py:399
  94.5 7.5 %collective-permute-done.7.returned = bf16[2,3,512,128]{3,2,1,0:T(8,128)(2,1)S(1)} collective-permute-done((bf16[2,3,512,128]{3,2,1,0:T(8,128)(2,1)S(1)}, bf16[2,3,512,128]{3,2,1,0:T(8,128)(2,1)S(1)}, u32[]{:S(2)}, u32[]{:S(2)}) %collective-permute-start.7) | collective-permute-done | bytes 786464 | tf_op jit(solution)/shard_map/ppermute | solution.py:384
  103.2 1.5 %collective-permute-start.9 = (f32[2,128]{1,0:T(2,128)S(1)}, f32[2,128]{1,0:T(2,128)S(1)}, u32[]{:S(2)}, u32[]{:S(2)}) collective-permute-start(f32[2,128]{1,0:T(2,128)S(1)} %add.26), channel_id=1, source_target_pairs={{0,1},{1,0},{2,3},{3,2},{4,5},{5,4},{6,7},{7,6},{8,9},{9,8},{10,11... | collective-permute-start | bytes 3080 | tf_op jit(solution)/shard_map/ppermute | solution.py:316
  104.7 2.0 %collective-permute-done.9 = f32[2,128]{1,0:T(2,128)S(1)} collective-permute-done((f32[2,128]{1,0:T(2,128)S(1)}, f32[2,128]{1,0:T(2,128)S(1)}, u32[]{:S(2)}, u32[]{:S(2)}) %collective-permute-start.9) | collective-permute-done | bytes 1056 | tf_op jit(solution)/shard_map/ppermute | solution.py:316
  106.8 2.3 %collective-permute-start.10 = (f32[2,128]{1,0:T(2,128)S(1)}, f32[2,128]{1,0:T(2,128)S(1)}, u32[]{:S(2)}, u32[]{:S(2)}) collective-permute-start(f32[2,128]{1,0:T(2,128)S(1)} %add.27), channel_id=1, source_target_pairs={{0,4},{2,6},{4,0},{6,2},{8,12},{10,14},{12,8},{14,10},{16,20},{18,... | collective-permute-start | bytes 3080 | tf_op jit(solution)/shard_map/ppermute | solution.py:316
  109.3 2.8 %copy.15 = bf16[512,8,2,128]{3,2,1,0:T(2,128)(2,1)} copy(bf16[512,8,2,128]{3,2,0,1:T(2,128)(2,1)S(1)} %bitcast.52) | data formatting | bytes 4194304 | tf_op jit(solution)/shard_map/transpose | solution.py:401
  112.9 2.8 %collective-permute-start.13 = (f32[2,128]{1,0:T(2,128)S(1)}, f32[2,128]{1,0:T(2,128)S(1)}, u32[]{:S(2)}, u32[]{:S(2)}) collective-permute-start(f32[2,128]{1,0:T(2,128)S(1)} %add.28), channel_id=1, source_target_pairs={{0,24},{2,26},{4,28},{6,30},{8,16},{10,18},{12,20},{14,22},{16,8},... | collective-permute-start | bytes 3080 | tf_op jit(solution)/shard_map/ppermute | solution.py:316
  115.8 1.6 %collective-permute-start.11 = (f32[2,128]{1,0:T(2,128)S(1)}, f32[2,128]{1,0:T(2,128)S(1)}, u32[]{:S(2)}, u32[]{:S(2)}) collective-permute-start(f32[2,128]{1,0:T(2,128)S(1)} %add.28), channel_id=1, source_target_pairs={{0,8},{2,10},{4,12},{6,14},{8,0},{10,2},{12,4},{14,6},{16,24},{18,... | collective-permute-start | bytes 3080 | tf_op jit(solution)/shard_map/ppermute | solution.py:316
  117.4 2.6 %shard_map.114 = (bf16[512,8,128]{2,1,0:T(8,128)(2,1)}, bf16[512,8,128]{2,1,0:T(8,128)(2,1)}) custom-call(s32[1]{0:T(128)} %bitcast.shard_ref.in_ref, bf16[2,2,512,128]{3,2,1,0:T(8,128)(2,1)S(1)} %get-tuple-element.80.own, bf16[2,2,512,128]{3,2,1,0:T(8,128)(2,1)S(1)} %collective-permute-done.15.returned, ...), custom_call_target="tpu_custom_call" | custom-call | tf_op jit(solution)/shard_map/pallas_call | solution.py:297
  (58 shorter events, 9.2 us)
Async XLA Ops:
  2.6 6.0 %copy-start = (bf16[1,3,512,128]{3,2,1,0:T(8,128)(2,1)}, bf16[1,3,512,128]{3,2,1,0:T(8,128)(2,1)S(1)}, u32[]{:S(2)}) copy-start(bf16[1,3,512,128]{3,2,1,0:T(8,128)(2,1)S(1)} %slice_bitcast_fusion.3.raw_ref) | copy-start | bytes 1179652
  2.7 22.8 %collective-permute-start.1 = (bf16[2,3,512,128]{3,2,1,0:T(8,128)(2,1)S(1)}, bf16[2,3,512,128]{3,2,1,0:T(8,128)(2,1)}, u32[]{:S(2)}, u32[]{:S(2)}) collective-permute-start(bf16[2,3,512,128]{3,2,1,0:T(8,128)(2,1)S(1)} %pad_maximum_fusion.2.own_ref), channel_id=1, source_target_pairs={{0,4},{2,6},{4,8},{6,10},{8,12},{10,14},{12,16},{14,18},{16,20},{1... | collective-permute-start | bytes 2359304 | tf_op jit(solution)/shard_map/ppermute | solution.py:347
  8.6 0.8 copy-start.4
  9.5 43.0 %collective-permute-start = (bf16[2,5,512,128]{3,2,1,0:T(8,128)(2,1)S(1)}, bf16[2,5,512,128]{3,2,1,0:T(8,128)(2,1)S(1)}, u32[]{:S(2)}, u32[]{:S(2)}) collective-permute-start(bf16[2,5,512,128]{3,2,1,0:T(8,128)(2,1)S(1)} %pad_maximum_fusion.1.own_ref), channel_id=1, source_target_pairs={{0,4},{2,6},{4,8},{6,10},{8,12},{10,14},{12,16},{14,18},{16,20},{1... | collective-permute-start | bytes 3932168 | tf_op jit(solution)/shard_map/ppermute | solution.py:347
  12.2 3.2 %copy-start.6 = (bf16[512,16,128]{2,1,0:T(8,128)(2,1)S(1)}, bf16[512,16,128]{2,1,0:T(8,128)(2,1)}, u32[]{:S(2)}) copy-start(bf16[512,16,128]{2,1,0:T(8,128)(2,1)} %param.9) | copy-start | bytes 6291460
  16.8 12.3 %copy-start.2 = (f32[128]{0:T(128)S(1)}, f32[128]{0:T(128)}, u32[]{:S(2)}) copy-start(f32[128]{0:T(128)} %param.11) | copy-start | bytes 1540
  16.8 12.3 %copy-start.3 = (f32[128]{0:T(128)S(1)}, f32[128]{0:T(128)}, u32[]{:S(2)}) copy-start(f32[128]{0:T(128)} %param.10) | copy-start | bytes 1540
  26.7 2.4 %collective-permute-start.2 = (bf16[2,3,512,128]{3,2,1,0:T(8,128)(2,1)S(1)}, bf16[2,3,512,128]{3,2,1,0:T(8,128)(2,1)S(1)}, u32[]{:S(2)}, u32[]{:S(2)}) collective-permute-start(bf16[2,3,512,128]{3,2,1,0:T(8,128)(2,1)S(1)} %shard_map.101), channel_id=1, source_target_pairs={{0,2},{2,0},{4,6},{6,4},{8,10},{10,8},{12,14},{14,12},{16,18},{18,... | collective-permute-start | bytes 2359304 | tf_op jit(solution)/shard_map/ppermute | solution.py:376
  44.7 7.8 %collective-permute-start.3 = (bf16[2,3,512,128]{3,2,1,0:T(8,128)(2,1)S(1)}, bf16[2,3,512,128]{3,2,1,0:T(8,128)(2,1)S(1)}, u32[]{:S(2)}, u32[]{:S(2)}) collective-permute-start(bf16[2,3,512,128]{3,2,1,0:T(8,128)(2,1)S(1)} %get-tuple-element.57), channel_id=1, source_target_pairs={{0,2},{2,0},{4,6},{6,4},{8,10},{10,8},{12,14},{14,12},{16,18},{18,... | collective-permute-start | bytes 2359304 | tf_op jit(solution)/shard_map/ppermute | solution.py:353
  52.8 3.1 %collective-permute-start.4 = (bf16[2,5,512,128]{3,2,1,0:T(8,128)(2,1)S(1)}, bf16[2,5,512,128]{3,2,1,0:T(8,128)(2,1)S(1)}, u32[]{:S(2)}, u32[]{:S(2)}) collective-permute-start(bf16[2,5,512,128]{3,2,1,0:T(8,128)(2,1)S(1)} %shard_map.105), channel_id=1, source_target_pairs={{0,2},{2,0},{4,6},{6,4},{8,10},{10,8},{12,14},{14,12},{16,18},{18,... | collective-permute-start | bytes 3932168 | tf_op jit(solution)/shard_map/ppermute | solution.py:376
  55.9 22.2 %collective-permute-start.6 = (bf16[2,3,512,128]{3,2,1,0:T(8,128)(2,1)S(1)}, bf16[2,3,512,128]{3,2,1,0:T(8,128)(2,1)S(1)}, u32[]{:S(2)}, u32[]{:S(2)}) collective-permute-start(bf16[2,3,512,128]{3,2,1,0:T(8,128)(2,1)S(1)} %shard_map.104), channel_id=1, source_target_pairs={{4,0},{6,2},{8,4},{10,6},{12,8},{14,10},{16,12},{18,14},{20,16},{2... | collective-permute-start | bytes 2359304 | tf_op jit(solution)/shard_map/ppermute | solution.py:384
  72.2 6.5 %collective-permute-start.5 = (bf16[2,3,512,128]{3,2,1,0:T(8,128)(2,1)S(1)}, bf16[2,3,512,128]{3,2,1,0:T(8,128)(2,1)S(1)}, u32[]{:S(2)}, u32[]{:S(2)}) collective-permute-start(bf16[2,3,512,128]{3,2,1,0:T(8,128)(2,1)S(1)} %get-tuple-element.63), channel_id=1, source_target_pairs={{0,2},{2,0},{4,6},{6,4},{8,10},{10,8},{12,14},{14,12},{16,18},{18,... | collective-permute-start | bytes 2359304 | tf_op jit(solution)/shard_map/ppermute | solution.py:353
  78.9 12.0 %copy-start.1 = (bf16[1,3,512,128]{3,2,1,0:T(8,128)(2,1)S(1)}, bf16[1,3,512,128]{3,2,1,0:T(8,128)(2,1)}, u32[]{:S(2)}) copy-start(bf16[1,3,512,128]{3,2,1,0:T(8,128)(2,1)} %copy-done) | copy-start | bytes 1179652
  78.9 23.1 %collective-permute-start.7 = (bf16[2,3,512,128]{3,2,1,0:T(8,128)(2,1)S(1)}, bf16[2,3,512,128]{3,2,1,0:T(8,128)(2,1)S(1)}, u32[]{:S(2)}, u32[]{:S(2)}) collective-permute-start(bf16[2,3,512,128]{3,2,1,0:T(8,128)(2,1)S(1)} %shard_map.107), channel_id=1, source_target_pairs={{4,0},{6,2},{8,4},{10,6},{12,8},{14,10},{16,12},{18,14},{20,16},{2... | collective-permute-start | bytes 2359304 | tf_op jit(solution)/shard_map/ppermute | solution.py:384
  90.9 2.0 %collective-permute-start.14 = (bf16[2,2,512,128]{3,2,1,0:T(8,128)(2,1)S(1)}, bf16[2,2,512,128]{3,2,1,0:T(8,128)(2,1)S(1)}, u32[]{:S(2)}, u32[]{:S(2)}) collective-permute-start(bf16[2,2,512,128]{3,2,1,0:T(8,128)(2,1)S(1)} %get-tuple-element.82), channel_id=1, source_target_pairs={{0,2},{2,0},{4,6},{6,4},{8,10},{10,8},{12,14},{14,12},{16,18},{18,... | collective-permute-start | bytes 1572872 | tf_op jit(solution)/shard_map/ppermute | solution.py:353
  93.0 24.4 %collective-permute-start.15 = (bf16[2,2,512,128]{3,2,1,0:T(8,128)(2,1)S(1)}, bf16[2,2,512,128]{3,2,1,0:T(8,128)(2,1)S(1)}, u32[]{:S(2)}, u32[]{:S(2)}) collective-permute-start(bf16[2,2,512,128]{3,2,1,0:T(8,128)(2,1)S(1)} %shard_map.113), channel_id=1, source_target_pairs={{4,0},{6,2},{8,4},{10,6},{12,8},{14,10},{16,12},{18,14},{20,16},{2... | collective-permute-start | bytes 1572872 | tf_op jit(solution)/shard_map/ppermute | solution.py:399
  102.0 2.6 %copy-start.5 = (bf16[1,5,512,128]{3,2,1,0:T(8,128)(2,1)S(1)}, bf16[1,5,512,128]{3,2,1,0:T(8,128)(2,1)}, u32[]{:S(2)}) copy-start(bf16[1,5,512,128]{3,2,1,0:T(8,128)(2,1)} %copy-done.4) | copy-start | bytes 1966084
  102.0 1.1 collective-permute-start.8
  103.2 3.6 %collective-permute-start.9 = (f32[2,128]{1,0:T(2,128)S(1)}, f32[2,128]{1,0:T(2,128)S(1)}, u32[]{:S(2)}, u32[]{:S(2)}) collective-permute-start(f32[2,128]{1,0:T(2,128)S(1)} %add.26), channel_id=1, source_target_pairs={{0,1},{1,0},{2,3},{3,2},{4,5},{5,4},{6,7},{7,6},{8,9},{9,8},{10,11... | collective-permute-start | bytes 3080 | tf_op jit(solution)/shard_map/ppermute | solution.py:316
  106.8 6.1 %collective-permute-start.10 = (f32[2,128]{1,0:T(2,128)S(1)}, f32[2,128]{1,0:T(2,128)S(1)}, u32[]{:S(2)}, u32[]{:S(2)}) collective-permute-start(f32[2,128]{1,0:T(2,128)S(1)} %add.27), channel_id=1, source_target_pairs={{0,4},{2,6},{4,0},{6,2},{8,12},{10,14},{12,8},{14,10},{16,20},{18,... | collective-permute-start | bytes 3080 | tf_op jit(solution)/shard_map/ppermute | solution.py:316
  112.9 7.1 %collective-permute-start.13 = (f32[2,128]{1,0:T(2,128)S(1)}, f32[2,128]{1,0:T(2,128)S(1)}, u32[]{:S(2)}, u32[]{:S(2)}) collective-permute-start(f32[2,128]{1,0:T(2,128)S(1)} %add.28), channel_id=1, source_target_pairs={{0,24},{2,26},{4,28},{6,30},{8,16},{10,18},{12,20},{14,22},{16,8},... | collective-permute-start | bytes 3080 | tf_op jit(solution)/shard_map/ppermute | solution.py:316
  115.7 4.5 %collective-permute-start.12 = (f32[2,128]{1,0:T(2,128)S(1)}, f32[2,128]{1,0:T(2,128)S(1)}, u32[]{:S(2)}, u32[]{:S(2)}) collective-permute-start(f32[2,128]{1,0:T(2,128)S(1)} %add.28), channel_id=1, source_target_pairs={{0,16},{2,18},{4,20},{6,22},{8,24},{10,26},{12,28},{14,30},{16,0},... | collective-permute-start | bytes 3080 | tf_op jit(solution)/shard_map/ppermute | solution.py:316
  115.8 4.4 %collective-permute-start.11 = (f32[2,128]{1,0:T(2,128)S(1)}, f32[2,128]{1,0:T(2,128)S(1)}, u32[]{:S(2)}, u32[]{:S(2)}) collective-permute-start(f32[2,128]{1,0:T(2,128)S(1)} %add.28), channel_id=1, source_target_pairs={{0,8},{2,10},{4,12},{6,14},{8,0},{10,2},{12,4},{14,6},{16,24},{18,... | collective-permute-start | bytes 3080 | tf_op jit(solution)/shard_map/ppermute | solution.py:316

commit v6 on v5

--- a/solution.py
+++ b/solution.py
@@ -34,7 +34,7 @@
 
 
 def heads_kernel(
-    shard_ref, q_ref, g_ref, own_ref, near_ref, far_ref, q_gain_ref, k_gain_ref,
+    shard_ref, q_ref, g_ref, own_ref, near_ref, far_ref, q_gain_ref, k_gain_ref, _,
     dq_ref, d_own_ref, d_near_ref, d_far_ref, gains_ref,
     k_low, k_low_t, k_rms, values, q_low, q_rms, probs_all, d_scores_all,
 ):
@@ -118,7 +118,8 @@
         raw = q_ref[0, mine, :].astype(jnp.float32)
         inverse_rms = q_rms[mine, :]
         q_gain_sum = q_gain_sum + jnp.sum(query_grad * (raw * inverse_rms), axis=0, keepdims=True)
-        dq_ref[0, mine, :] = norm_back(query_grad, raw, inverse_rms, q_gain).astype(dq_ref.dtype)
+        query_grad = norm_back(query_grad, raw, inverse_rms, q_gain).astype(dq_ref.dtype)
+        dq_ref[start : start + TILE, 0, :, :] = query_grad.reshape(TILE, group, -1)
 
     pieces = [(tile, tile + 1, 0, tile + 1) for tile in range(blocks - 1)]
     pieces += [(blocks - 1, tiles + 1, 0, blocks)]
@@ -233,10 +234,11 @@
     )(array[0, 0, :16], small)
 
 
-def group_grads(shard, first, here, count, queries, grads, own, near, far, q_gain, k_gain):
+def group_grads(shard, first, here, count, queries, grads, own, near, far, q_gain, k_gain, dq):
     _, _, rows, width = own.shape
     query_rows = queries.shape[1]
     span = WINDOW + rows
+    group = query_rows // rows
     whole_q = pl.BlockSpec((1, query_rows, width), lambda head: (first + head, 0, 0))
     part = pl.BlockSpec((2, 1, rows, width), lambda head: (0, head, 0, 0))
     held = pl.BlockSpec((2, 1, rows, width), lambda head: (0, here + head, 0, 0))
@@ -247,16 +249,17 @@
         grid=(count,),
         in_specs=[
             pl.BlockSpec(memory_space=pltpu.SMEM), whole_q, whole_q, held, held, held, gain, gain,
+            pl.BlockSpec(memory_space=pl.ANY),
         ],
         out_specs=[
-            pl.BlockSpec((1, query_rows, width), lambda head: (head, 0, 0)),
+            pl.BlockSpec((rows, 1, group, width), lambda head: (0, first + head, 0, 0)),
             part,
             part,
             part,
             pl.BlockSpec((2, width), lambda head: (0, 0)),
         ],
         out_shape=[
-            jax.ShapeDtypeStruct((count, query_rows, width), jnp.bfloat16),
+            jax.ShapeDtypeStruct(dq.shape, dq.dtype),
             jax.ShapeDtypeStruct(shape, jnp.bfloat16),
             jax.ShapeDtypeStruct(shape, jnp.bfloat16),
             jax.ShapeDtypeStruct(shape, jnp.bfloat16),
@@ -272,9 +275,10 @@
             pltpu.VMEM((span, query_rows), jnp.bfloat16),
             pltpu.VMEM((span, query_rows), jnp.bfloat16),
         ],
+        input_output_aliases={8: 0},
         compiler_params=pltpu.CompilerParams(vmem_limit_bytes=22 * 1024 * 1024),
         cost_estimate=LIGHT,
-    )(shard, queries, grads, own, near, far, q_gain, k_gain)
+    )(shard, queries, grads, own, near, far, q_gain, k_gain, dq)
 
 
 def close_group(shard, own, returned, swapped, raw, k_gain):
@@ -309,19 +313,19 @@
     return [(kv_dev + count - 1 - place) // count for place in range(count)]
 
 
-def exchanged(value, axis, low, high):
-    count = lax.axis_size(axis)
+def exchanged(value, *bits):
+    count = lax.axis_size(("seq", "head"))
     assert count & (count - 1) == 0
+    masks = [1 << bit for bit in bits]
+    masks += [sum(masks)] if len(masks) > 1 else []
     return [
-        lax.ppermute(value, axis, [(source, source ^ (mask << low)) for source in range(count)])
-        for mask in range(1, 1 << max(high - low, 0))
+        lax.ppermute(value, ("seq", "head"), [(source, source ^ mask) for source in range(count)])
+        for mask in masks
     ]
 
 
-def summed(value, axis, low, high):
-    for place in range(low, high):
-        value = value + exchanged(value, axis, place, place + 1)[0]
-    return value
+def summed(value, others):
+    return value + others[0] if len(others) == 1 else (value + others[0]) + (others[1] + others[2])
 
 
 def per_device(query, key, value, grad_out, q_gain, k_gain):
@@ -358,7 +362,8 @@
         d_own, swapped, raw = stays
         return close_group(scalar, d_own, returned, swapped, raw, k_gain_2d)
 
-    dq_parts, gains, kept, done = [], [], [], []
+    gains, kept, done = [], [], []
+    grad_query = jnp.zeros((rows, kv_dev, group, width), query.dtype)
     grads_out = None
     for place, (first, size) in enumerate(zip(starts, sizes, strict=True)):
         if grads_out is not None:
@@ -383,35 +388,36 @@
             near, relayed, scalar_now = lax.optimization_barrier((near, relayed, scalar_now))
             kept.append((stays, lax.ppermute(relayed, "seq", back)))
         here = slice(first - start, first - start + size)
-        dq, *grads_out, gain = group_grads(
-            scalar_now, first, first - start, size, queries, grads, own, near, far, q_gain_2d, k_gain_2d
+        grad_query, *grads_out, gain = group_grads(
+            scalar_now, first, first - start, size, queries, grads, own, near, far,
+            q_gain_2d, k_gain_2d, grad_query,
         )
         grads_out.append(own[:1, here])
-        dq_parts.append(dq)
         gains.append(gain)
     relayed, stays = split(*grads_out)
+    head_bits, seq_bits = ((lax.axis_size(axis) - 1).bit_length() for axis in ("head", "seq"))
+    assert head_bits and seq_bits > 3
+    chips = range(head_bits + 1, head_bits + seq_bits)
     gain_sum = sum(gains[1:], gains[0])
+    others = exchanged(gain_sum, chips[0])
     if kept:
         before, returned = kept.pop()
         returned, done = lax.optimization_barrier((returned, done))
         gain_sum = later(returned, gain_sum)
         done.append(close(before, returned))
+    gain_sum, others = lax.optimization_barrier((gain_sum, others))
+    gain_sum = summed(gain_sum, others)
     returned = lax.ppermute(relayed, "seq", back)
-    grad_query = jnp.concatenate(dq_parts).reshape(kv_dev, rows, group, width)
-    grad_query = jnp.transpose(grad_query, (1, 0, 2, 3)).reshape(rows, heads, width)
-    seq_bits, head_bits = ((lax.axis_size(axis) - 1).bit_length() for axis in ("seq", "head"))
-    gain_sum = summed(gain_sum, "seq", 0, 1)
-    gain_sum = summed(gain_sum, "head", 0, head_bits)
-    gain_sum = summed(gain_sum, "seq", 1, seq_bits - 2)
+    grad_query = grad_query.reshape(rows, heads, width)
+    exchanges = [(0, head_bits), *((bit,) for bit in range(1, head_bits))]
+    exchanges += [(bit,) for bit in chips[1:-2]]
+    for bits in exchanges:
+        gain_sum = summed(gain_sum, exchanged(gain_sum, *bits))
     gain_sum, grad_query, done = lax.optimization_barrier((gain_sum, grad_query, done))
     d_own, swapped, raw = stays
     grad_key, grad_value = finish(scalar, d_own, returned, swapped, raw, k_gain_2d, done)
-    others, grad_key = lax.optimization_barrier(
-        (exchanged(gain_sum, "seq", max(seq_bits - 2, 1), seq_bits), grad_key)
-    )
-    gain_sum = (gain_sum + others[0]) + (others[1] + others[2]) if len(others) == 3 else sum(
-        others, gain_sum
-    )
+    others, grad_key = lax.optimization_barrier((exchanged(gain_sum, *chips[-2:]), grad_key))
+    gain_sum = summed(gain_sum, others)
     return (grad_query, grad_key, grad_value, gain_sum[0], gain_sum[1])
 
 

time: 121 us -> 116 us (0.959)
  waiting for transfers between devices: 39.3 us -> 31.6 us
  Pallas kernels: 47.5 us -> 49.5 us
    ppermute x2, waiting for transfers between devices: 13.3 us -> 8.54 us  [per_device(): kept.append((stays, lax.ppermute(relayed, 'seq', back)))]
    ppermute x2, waiting for transfers between devices: 16.3 us -> 13.3 us  [per_device(): fars = [lax.ppermute(own, 'seq', ahead) for own in owns]]
    transpose x1 -> x0, local copies, waits for them, and re-layouts: 2.76 us -> none  [per_device(): jnp.transpose(grad_query, (1, 0, 2, 3)).reshape(rows, heads, width)]
    broadcast_in_dim x0 -> x1, local copies, waits for them, and re-layouts: none -> 2.4 us  [per_device(): grad_query = jnp.zeros((rows, kv_dev, group, width), query.dtype)]
    pallas_call x3, Pallas kernels: 40.8 us -> 42.8 us  [group_grads(): pl.pallas_call(heads_kernel, grid=(count,), in_specs=[pl.BlockSpec(memory...]
    ppermute x6 -> x7, starting transfers between devices: 8.25 us -> 9.86 us  [exchanged(): lax.ppermute(value, ('seq', 'head'), [(source, source ^ mask) for source...]
    ppermute x1, waiting for transfers between devices: 0.01 us -> 1.5 us  [per_device(): returned = lax.ppermute(relayed, 'seq', back)]
    ppermute x6 -> x7, waiting for transfers between devices: 3.39 us -> 2.95 us  [exchanged(): lax.ppermute(value, ('seq', 'head'), [(source, source ^ mask) for source...]
  transfers between devices with their start and end apart: 16 -> 17, of which waited for: 10 -> 10; matrix products, arithmetic and copies ran while one was open for 7% -> 6% of each run, Pallas kernels for 39% -> 42%
where the time goes in v6:
time: 116 us
  Pallas kernels  49.5 us (43%)
  waiting for transfers between devices  31.6 us (27%)
  starting transfers between devices  22.9 us (20%)
  local copies, waits for them, and re-layouts  10.5 us (9%)
    pallas_call x3, Pallas kernels, group_grads(): pl.pallas_call(heads_kernel, grid=(count,), in_specs=[pl.BlockSpec(memory...  42.8 us
    ppermute x2, waiting for transfers between devices, per_device(): fars = [lax.ppermute(own, 'seq', ahead) for own in owns]  13.3 us
    ppermute x7, starting transfers between devices, exchanged(): lax.ppermute(value, ('seq', 'head'), [(source, source ^ mask) for source...  9.86 us
    ppermute x2, waiting for transfers between devices, per_device(): kept.append((stays, lax.ppermute(relayed, 'seq', back)))  8.54 us
    ppermute x2, starting transfers between devices, per_device(): fars = [lax.ppermute(own, 'seq', ahead) for own in owns]  8.4 us
    ppermute x2, waiting for transfers between devices, per_device(): lax.ppermute(small_call(choose_kernel, scalar, far, own), 'seq', swap)  5.29 us
    reshape x2, local copies, waits for them, and re-layouts, by_head(): split = array.reshape(rows, kv_dev, group, width)  4.62 us
    ppermute x7, waiting for transfers between devices, exchanged(): lax.ppermute(value, ('seq', 'head'), [(source, source ^ mask) for source...  2.95 us
  transfers between devices with their start and end apart: 17, of which 10 were waited for; matrix products, arithmetic and copies ran while one was open for 6% of the time, Pallas kernels for 42%

profile of v6, /device:TPU:0, one launch (start us, length us, event | category | flops | bytes accessed | tf_op | source)
XLA Modules:
  0.0 115.6 jit_solution(17480702873174685046)
XLA Ops:
  0.6 1.9 %copy_bitcast_fusion = (bf16[8,512,128]{2,1,0:T(8,128)(2,1)S(1)}, bf16[8,512,128]{2,1,0:T(8,128)(2,1)S(1)}) fusion(bf16[512,8,128]{2,1,0:T(8,128)(2,1)} %param.8, bf16[512,8,128]{2,1,0:T(8,128)(2,1)} %param.7), kind=kLoop, calls=%fused_computation.1 | loop fusion | bytes 4194304 | tf_op jit(solution)/shard_map/transpose | solution.py:349
  2.7 5.8 %collective-permute-start.1 = (bf16[2,3,512,128]{3,2,1,0:T(8,128)(2,1)S(1)}, bf16[2,3,512,128]{3,2,1,0:T(8,128)(2,1)}, u32[]{:S(2)}, u32[]{:S(2)}) collective-permute-start(bf16[2,3,512,128]{3,2,1,0:T(8,128)(2,1)S(1)} %pad_maximum_fusion.1.own_ref), channel_id=1, source_target_pairs={{0,4},{2,6},{4,8},{6,10},{8,12},{10,14},{12,16},{14,18},{16,20},{1... | collective-permute-start | bytes 2359304 | tf_op jit(solution)/shard_map/ppermute | solution.py:351
  9.5 2.6 %collective-permute-start = (bf16[2,5,512,128]{3,2,1,0:T(8,128)(2,1)S(1)}, bf16[2,5,512,128]{3,2,1,0:T(8,128)(2,1)S(1)}, u32[]{:S(2)}, u32[]{:S(2)}) collective-permute-start(bf16[2,5,512,128]{3,2,1,0:T(8,128)(2,1)S(1)} %pad_maximum_fusion.own_ref), channel_id=1, source_target_pairs={{0,4},{2,6},{4,8},{6,10},{8,12},{10,14},{12,16},{14,18},{16,20},{1... | collective-permute-start | bytes 3932168 | tf_op jit(solution)/shard_map/ppermute | solution.py:351
  12.2 3.2 %copy.16 = bf16[512,8,2,128]{3,2,0,1:T(2,128)(2,1)S(1)} copy(bf16[512,8,2,128]{3,2,1,0:T(2,128)(2,1)} %bitcast.50) | data formatting | bytes 4194304 | tf_op jit(solution)/shard_map/reshape | solution.py:343
  15.4 1.4 %copy.17 = bf16[512,8,2,128]{3,2,0,1:T(2,128)(2,1)S(1)} copy(bf16[512,8,2,128]{3,2,1,0:T(2,128)(2,1)S(1)} %bitcast.51) | data formatting | bytes 4194304 | tf_op jit(solution)/shard_map/reshape | solution.py:343
  16.8 8.7 %collective-permute-done.1.far_ref = bf16[2,3,512,128]{3,2,1,0:T(8,128)(2,1)} collective-permute-done((bf16[2,3,512,128]{3,2,1,0:T(8,128)(2,1)S(1)}, bf16[2,3,512,128]{3,2,1,0:T(8,128)(2,1)}, u32[]{:S(2)}, u32[]{:S(2)}) %collective-permute-start.1) | collective-permute-done | bytes 786464 | tf_op jit(solution)/shard_map/ppermute | solution.py:351
  26.8 2.3 %collective-permute-done.2.near_ref = bf16[2,3,512,128]{3,2,1,0:T(8,128)(2,1)S(1)} collective-permute-done((bf16[2,3,512,128]{3,2,1,0:T(8,128)(2,1)S(1)}, bf16[2,3,512,128]{3,2,1,0:T(8,128)(2,1)S(1)}, u32[]{:S(2)}, u32[]{:S(2)}) %collective-permute-start.2) | collective-permute-done | bytes 786464 | tf_op jit(solution)/shard_map/ppermute | solution.py:381
  29.1 2.4 %broadcast_in_dim.3._ = bf16[512,8,2,128]{3,2,1,0:T(2,128)(2,1)} broadcast(bf16[]{:T(256)} %constant.7.clone.1), dimensions={} | broadcast | bytes 2097154 | tf_op jit(solution)/shard_map/broadcast_in_dim | solution.py:366
  31.5 16.3 %shard_map.102 = (bf16[512,8,2,128]{3,2,1,0:T(2,128)(2,1)}, bf16[2,3,512,128]{3,2,1,0:T(8,128)(2,1)S(1)}, bf16[2,3,512,128]{3,2,1,0:T(8,128)(2,1)S(1)}, bf16[2,3,512,128]{3,2,1,0:T(8,128)(2,1)S(1)}, f32[2,128]{1,0:T(2,128)S(1)}) custom-call(s32[1]{0:T(128)} %bitcast.shard_ref.in_ref, ...), custom_call_target="tpu_custom_call", output_to_operand_aliasing={{0}: (8, {})} | custom-call | flops 1000 | bytes 1000 | tf_op jit(solution)/shard_map/pallas_call | solution.py:247
  47.9 4.6 %collective-permute-done.far_ref = bf16[2,5,512,128]{3,2,1,0:T(8,128)(2,1)S(1)} collective-permute-done((bf16[2,5,512,128]{3,2,1,0:T(8,128)(2,1)S(1)}, bf16[2,5,512,128]{3,2,1,0:T(8,128)(2,1)S(1)}, u32[]{:S(2)}, u32[]{:S(2)}) %collective-permute-start) | collective-permute-done | bytes 1310752 | tf_op jit(solution)/shard_map/ppermute | solution.py:351
  52.9 3.0 %collective-permute-done.4.near_ref = bf16[2,5,512,128]{3,2,1,0:T(8,128)(2,1)S(1)} collective-permute-done((bf16[2,5,512,128]{3,2,1,0:T(8,128)(2,1)S(1)}, bf16[2,5,512,128]{3,2,1,0:T(8,128)(2,1)S(1)}, u32[]{:S(2)}, u32[]{:S(2)}) %collective-permute-start.4) | collective-permute-done | bytes 1310752 | tf_op jit(solution)/shard_map/ppermute | solution.py:381
  55.9 1.5 %collective-permute-start.6 = (bf16[2,3,512,128]{3,2,1,0:T(8,128)(2,1)S(1)}, bf16[2,3,512,128]{3,2,1,0:T(8,128)(2,1)S(1)}, u32[]{:S(2)}, u32[]{:S(2)}) collective-permute-start(bf16[2,3,512,128]{3,2,1,0:T(8,128)(2,1)S(1)} %shard_map.104), channel_id=1, source_target_pairs={{4,0},{6,2},{8,4},{10,6},{12,8},{14,10},{16,12},{18,14},{20,16},{2... | collective-permute-start | bytes 2359304 | tf_op jit(solution)/shard_map/ppermute | solution.py:389
  57.4 15.3 %shard_map.106 = (bf16[512,8,2,128]{3,2,1,0:T(2,128)(2,1)}, bf16[2,3,512,128]{3,2,1,0:T(8,128)(2,1)S(1)}, bf16[2,3,512,128]{3,2,1,0:T(8,128)(2,1)S(1)}, bf16[2,3,512,128]{3,2,1,0:T(8,128)(2,1)S(1)}, f32[2,128]{1,0:T(2,128)S(1)}) custom-call(s32[1]{0:T(128)} %bitcast.shard_ref.in_ref, ...), custom_call_target="tpu_custom_call", output_to_operand_aliasing={{0}: (8, {})} | custom-call | flops 1000 | bytes 1000 | tf_op jit(solution)/shard_map/pallas_call | solution.py:247
  72.9 5.3 %collective-permute-done.6.returned = bf16[2,3,512,128]{3,2,1,0:T(8,128)(2,1)S(1)} collective-permute-done((bf16[2,3,512,128]{3,2,1,0:T(8,128)(2,1)S(1)}, bf16[2,3,512,128]{3,2,1,0:T(8,128)(2,1)S(1)}, u32[]{:S(2)}, u32[]{:S(2)}) %collective-permute-start.6) | collective-permute-done | bytes 786464 | tf_op jit(solution)/shard_map/ppermute | solution.py:389
  78.9 1.3 %collective-permute-start.7 = (bf16[2,3,512,128]{3,2,1,0:T(8,128)(2,1)S(1)}, bf16[2,3,512,128]{3,2,1,0:T(8,128)(2,1)S(1)}, u32[]{:S(2)}, u32[]{:S(2)}) collective-permute-start(bf16[2,3,512,128]{3,2,1,0:T(8,128)(2,1)S(1)} %shard_map.107), channel_id=1, source_target_pairs={{4,0},{6,2},{8,4},{10,6},{12,8},{14,10},{16,12},{18,14},{20,16},{2... | collective-permute-start | bytes 2359304 | tf_op jit(solution)/shard_map/ppermute | solution.py:389
  80.2 11.2 %shard_map.110 = (bf16[512,8,2,128]{3,2,1,0:T(2,128)(2,1)}, bf16[2,2,512,128]{3,2,1,0:T(8,128)(2,1)S(1)}, bf16[2,2,512,128]{3,2,1,0:T(8,128)(2,1)S(1)}, bf16[2,2,512,128]{3,2,1,0:T(8,128)(2,1)S(1)}, f32[2,128]{1,0:T(2,128)S(1)}) custom-call(s32[1]{0:T(128)} %shard_map.108.shard_ref, ...), custom_call_target="tpu_custom_call", output_to_operand_aliasing={{0}: (8, {})} | custom-call | flops 1000 | bytes 1000 | tf_op jit(solution)/shard_map/pallas_call | solution.py:247
  91.4 3.3 %collective-permute-start.8 = (f32[2,128]{1,0:T(2,128)S(1)}, f32[2,128]{1,0:T(2,128)S(1)}, u32[]{:S(2)}, u32[]{:S(2)}) collective-permute-start(f32[2,128]{1,0:T(2,128)S(1)} %add_add_fusion.2.in_ref), channel_id=1, source_target_pairs={{0,4},{1,5},{2,6},{3,7},{4,0},{5,1},{6,2},{7,3},{8,12},{9,13},{10,... | collective-permute-start | bytes 3080 | tf_op jit(solution)/shard_map/ppermute | solution.py:322
  95.7 1.5 %collective-permute-start.16 = (bf16[2,2,512,128]{3,2,1,0:T(8,128)(2,1)S(1)}, bf16[2,2,512,128]{3,2,1,0:T(8,128)(2,1)S(1)}, u32[]{:S(2)}, u32[]{:S(2)}) collective-permute-start(bf16[2,2,512,128]{3,2,1,0:T(8,128)(2,1)S(1)} %shard_map.113), channel_id=1, source_target_pairs={{4,0},{6,2},{8,4},{10,6},{12,8},{14,10},{16,12},{18,14},{20,16},{2... | collective-permute-start | bytes 1572872 | tf_op jit(solution)/shard_map/ppermute | solution.py:410
  97.2 3.3 %collective-permute-done.7.returned = bf16[2,3,512,128]{3,2,1,0:T(8,128)(2,1)S(1)} collective-permute-done((bf16[2,3,512,128]{3,2,1,0:T(8,128)(2,1)S(1)}, bf16[2,3,512,128]{3,2,1,0:T(8,128)(2,1)S(1)}, u32[]{:S(2)}, u32[]{:S(2)}) %collective-permute-start.7) | collective-permute-done | bytes 786464 | tf_op jit(solution)/shard_map/ppermute | solution.py:389
  100.6 1.6 %collective-permute-start.10 = (f32[2,128]{1,0:T(2,128)S(1)}, f32[2,128]{1,0:T(2,128)S(1)}, u32[]{:S(2)}, u32[]{:S(2)}) collective-permute-start(f32[2,128]{1,0:T(2,128)S(1)} %add.29), channel_id=1, source_target_pairs={{0,2},{1,3},{2,0},{3,1},{4,6},{5,7},{6,4},{7,5},{8,10},{9,11},{10,... | collective-permute-start | bytes 3080 | tf_op jit(solution)/shard_map/ppermute | solution.py:322
  103.6 2.1 %collective-permute-done.9 = f32[2,128]{1,0:T(2,128)S(1)} collective-permute-done((f32[2,128]{1,0:T(2,128)S(1)}, f32[2,128]{1,0:T(2,128)S(1)}, u32[]{:S(2)}, u32[]{:S(2)}) %collective-permute-start.9) | collective-permute-done | bytes 1056 | tf_op jit(solution)/shard_map/ppermute | solution.py:322
  105.8 3.8 %collective-permute-start.14 = (f32[2,128]{1,0:T(2,128)S(1)}, f32[2,128]{1,0:T(2,128)S(1)}, u32[]{:S(2)}, u32[]{:S(2)}) collective-permute-start(f32[2,128]{1,0:T(2,128)S(1)} %add_add_fusion.1), channel_id=1, source_target_pairs={{0,24},{1,25},{2,26},{3,27},{4,28},{5,29},{6,30},{7,31},{8,16},{9,... | collective-permute-start | bytes 3080 | tf_op jit(solution)/shard_map/ppermute | solution.py:322
  110.2 1.5 %collective-permute-done.16.returned = bf16[2,2,512,128]{3,2,1,0:T(8,128)(2,1)S(1)} collective-permute-done((bf16[2,2,512,128]{3,2,1,0:T(8,128)(2,1)S(1)}, bf16[2,2,512,128]{3,2,1,0:T(8,128)(2,1)S(1)}, u32[]{:S(2)}, u32[]{:S(2)}) %collective-permute-start.16) | collective-permute-done | bytes 524320 | tf_op jit(solution)/shard_map/ppermute | solution.py:410
  111.7 2.6 %shard_map.114 = (bf16[512,8,128]{2,1,0:T(8,128)(2,1)}, bf16[512,8,128]{2,1,0:T(8,128)(2,1)}) custom-call(s32[1]{0:T(128)} %bitcast.shard_ref.in_ref, bf16[2,2,512,128]{3,2,1,0:T(8,128)(2,1)S(1)} %get-tuple-element.84.own, bf16[2,2,512,128]{3,2,1,0:T(8,128)(2,1)S(1)} %collective-permute-done.16.returned, ...), custom_call_target="tpu_custom_call" | custom-call | tf_op jit(solution)/shard_map/pallas_call | solution.py:301
  (58 shorter events, 8.3 us)
Async XLA Ops:
  2.6 6.0 %copy-start = (bf16[1,3,512,128]{3,2,1,0:T(8,128)(2,1)}, bf16[1,3,512,128]{3,2,1,0:T(8,128)(2,1)S(1)}, u32[]{:S(2)}) copy-start(bf16[1,3,512,128]{3,2,1,0:T(8,128)(2,1)S(1)} %slice_bitcast_fusion.3.raw_ref) | copy-start | bytes 1179652
  2.7 22.8 %collective-permute-start.1 = (bf16[2,3,512,128]{3,2,1,0:T(8,128)(2,1)S(1)}, bf16[2,3,512,128]{3,2,1,0:T(8,128)(2,1)}, u32[]{:S(2)}, u32[]{:S(2)}) collective-permute-start(bf16[2,3,512,128]{3,2,1,0:T(8,128)(2,1)S(1)} %pad_maximum_fusion.1.own_ref), channel_id=1, source_target_pairs={{0,4},{2,6},{4,8},{6,10},{8,12},{10,14},{12,16},{14,18},{16,20},{1... | collective-permute-start | bytes 2359304 | tf_op jit(solution)/shard_map/ppermute | solution.py:351
  8.6 0.8 copy-start.4
  9.5 43.0 %collective-permute-start = (bf16[2,5,512,128]{3,2,1,0:T(8,128)(2,1)S(1)}, bf16[2,5,512,128]{3,2,1,0:T(8,128)(2,1)S(1)}, u32[]{:S(2)}, u32[]{:S(2)}) collective-permute-start(bf16[2,5,512,128]{3,2,1,0:T(8,128)(2,1)S(1)} %pad_maximum_fusion.own_ref), channel_id=1, source_target_pairs={{0,4},{2,6},{4,8},{6,10},{8,12},{10,14},{12,16},{14,18},{16,20},{1... | collective-permute-start | bytes 3932168 | tf_op jit(solution)/shard_map/ppermute | solution.py:351
  12.2 3.2 %copy-start.6 = (bf16[512,16,128]{2,1,0:T(8,128)(2,1)S(1)}, bf16[512,16,128]{2,1,0:T(8,128)(2,1)}, u32[]{:S(2)}) copy-start(bf16[512,16,128]{2,1,0:T(8,128)(2,1)} %param.9) | copy-start | bytes 6291460
  25.5 6.0 %copy-start.2 = (f32[128]{0:T(128)S(1)}, f32[128]{0:T(128)}, u32[]{:S(2)}) copy-start(f32[128]{0:T(128)} %param.11) | copy-start | bytes 1540
  25.5 6.0 %copy-start.3 = (f32[128]{0:T(128)S(1)}, f32[128]{0:T(128)}, u32[]{:S(2)}) copy-start(f32[128]{0:T(128)} %param.10) | copy-start | bytes 1540
  26.8 2.4 %collective-permute-start.2 = (bf16[2,3,512,128]{3,2,1,0:T(8,128)(2,1)S(1)}, bf16[2,3,512,128]{3,2,1,0:T(8,128)(2,1)S(1)}, u32[]{:S(2)}, u32[]{:S(2)}) collective-permute-start(bf16[2,3,512,128]{3,2,1,0:T(8,128)(2,1)S(1)} %shard_map.101), channel_id=1, source_target_pairs={{0,2},{2,0},{4,6},{6,4},{8,10},{10,8},{12,14},{14,12},{16,18},{18,... | collective-permute-start | bytes 2359304 | tf_op jit(solution)/shard_map/ppermute | solution.py:381
  47.8 4.7 %collective-permute-start.3 = (bf16[2,3,512,128]{3,2,1,0:T(8,128)(2,1)S(1)}, bf16[2,3,512,128]{3,2,1,0:T(8,128)(2,1)S(1)}, u32[]{:S(2)}, u32[]{:S(2)}) collective-permute-start(bf16[2,3,512,128]{3,2,1,0:T(8,128)(2,1)S(1)} %get-tuple-element.59), channel_id=1, source_target_pairs={{0,2},{2,0},{4,6},{6,4},{8,10},{10,8},{12,14},{14,12},{16,18},{18,... | collective-permute-start | bytes 2359304 | tf_op jit(solution)/shard_map/ppermute | solution.py:357
  52.8 3.1 %collective-permute-start.4 = (bf16[2,5,512,128]{3,2,1,0:T(8,128)(2,1)S(1)}, bf16[2,5,512,128]{3,2,1,0:T(8,128)(2,1)S(1)}, u32[]{:S(2)}, u32[]{:S(2)}) collective-permute-start(bf16[2,5,512,128]{3,2,1,0:T(8,128)(2,1)S(1)} %shard_map.105), channel_id=1, source_target_pairs={{0,2},{2,0},{4,6},{6,4},{8,10},{10,8},{12,14},{14,12},{16,18},{18,... | collective-permute-start | bytes 3932168 | tf_op jit(solution)/shard_map/ppermute | solution.py:381
  55.9 22.2 %collective-permute-start.6 = (bf16[2,3,512,128]{3,2,1,0:T(8,128)(2,1)S(1)}, bf16[2,3,512,128]{3,2,1,0:T(8,128)(2,1)S(1)}, u32[]{:S(2)}, u32[]{:S(2)}) collective-permute-start(bf16[2,3,512,128]{3,2,1,0:T(8,128)(2,1)S(1)} %shard_map.104), channel_id=1, source_target_pairs={{4,0},{6,2},{8,4},{10,6},{12,8},{14,10},{16,12},{18,14},{20,16},{2... | collective-permute-start | bytes 2359304 | tf_op jit(solution)/shard_map/ppermute | solution.py:389
  72.7 5.9 %collective-permute-start.5 = (bf16[2,3,512,128]{3,2,1,0:T(8,128)(2,1)S(1)}, bf16[2,3,512,128]{3,2,1,0:T(8,128)(2,1)S(1)}, u32[]{:S(2)}, u32[]{:S(2)}) collective-permute-start(bf16[2,3,512,128]{3,2,1,0:T(8,128)(2,1)S(1)} %get-tuple-element.66), channel_id=1, source_target_pairs={{0,2},{2,0},{4,6},{6,4},{8,10},{10,8},{12,14},{14,12},{16,18},{18,... | collective-permute-start | bytes 2359304 | tf_op jit(solution)/shard_map/ppermute | solution.py:357
  78.9 21.6 %collective-permute-start.7 = (bf16[2,3,512,128]{3,2,1,0:T(8,128)(2,1)S(1)}, bf16[2,3,512,128]{3,2,1,0:T(8,128)(2,1)S(1)}, u32[]{:S(2)}, u32[]{:S(2)}) collective-permute-start(bf16[2,3,512,128]{3,2,1,0:T(8,128)(2,1)S(1)} %shard_map.107), channel_id=1, source_target_pairs={{4,0},{6,2},{8,4},{10,6},{12,8},{14,10},{16,12},{18,14},{20,16},{2... | collective-permute-start | bytes 2359304 | tf_op jit(solution)/shard_map/ppermute | solution.py:389
  80.2 14.5 %copy-start.1 = (bf16[1,3,512,128]{3,2,1,0:T(8,128)(2,1)S(1)}, bf16[1,3,512,128]{3,2,1,0:T(8,128)(2,1)}, u32[]{:S(2)}) copy-start(bf16[1,3,512,128]{3,2,1,0:T(8,128)(2,1)} %copy-done) | copy-start | bytes 1179652
  91.4 4.1 %collective-permute-start.15 = (bf16[2,2,512,128]{3,2,1,0:T(8,128)(2,1)S(1)}, bf16[2,2,512,128]{3,2,1,0:T(8,128)(2,1)S(1)}, u32[]{:S(2)}, u32[]{:S(2)}) collective-permute-start(bf16[2,2,512,128]{3,2,1,0:T(8,128)(2,1)S(1)} %get-tuple-element.86), channel_id=1, source_target_pairs={{0,2},{2,0},{4,6},{6,4},{8,10},{10,8},{12,14},{14,12},{16,18},{18,... | collective-permute-start | bytes 1572872 | tf_op jit(solution)/shard_map/ppermute | solution.py:357
  91.4 9.1 %collective-permute-start.8 = (f32[2,128]{1,0:T(2,128)S(1)}, f32[2,128]{1,0:T(2,128)S(1)}, u32[]{:S(2)}, u32[]{:S(2)}) collective-permute-start(f32[2,128]{1,0:T(2,128)S(1)} %add_add_fusion.2.in_ref), channel_id=1, source_target_pairs={{0,4},{1,5},{2,6},{3,7},{4,0},{5,1},{6,2},{7,3},{8,12},{9,13},{10,... | collective-permute-start | bytes 3080 | tf_op jit(solution)/shard_map/ppermute | solution.py:322
  95.7 16.0 %collective-permute-start.16 = (bf16[2,2,512,128]{3,2,1,0:T(8,128)(2,1)S(1)}, bf16[2,2,512,128]{3,2,1,0:T(8,128)(2,1)S(1)}, u32[]{:S(2)}, u32[]{:S(2)}) collective-permute-start(bf16[2,2,512,128]{3,2,1,0:T(8,128)(2,1)S(1)} %shard_map.113), channel_id=1, source_target_pairs={{4,0},{6,2},{8,4},{10,6},{12,8},{14,10},{16,12},{18,14},{20,16},{2... | collective-permute-start | bytes 1572872 | tf_op jit(solution)/shard_map/ppermute | solution.py:410
  100.5 2.2 %copy-start.5 = (bf16[1,5,512,128]{3,2,1,0:T(8,128)(2,1)S(1)}, bf16[1,5,512,128]{3,2,1,0:T(8,128)(2,1)}, u32[]{:S(2)}) copy-start(bf16[1,5,512,128]{3,2,1,0:T(8,128)(2,1)} %copy-done.4) | copy-start | bytes 1966084
  100.6 3.0 %collective-permute-start.11 = (f32[2,128]{1,0:T(2,128)S(1)}, f32[2,128]{1,0:T(2,128)S(1)}, u32[]{:S(2)}, u32[]{:S(2)}) collective-permute-start(f32[2,128]{1,0:T(2,128)S(1)} %add.29), channel_id=1, source_target_pairs={{0,3},{1,2},{2,1},{3,0},{4,7},{5,6},{6,5},{7,4},{8,11},{9,10},{10,... | collective-permute-start | bytes 3080 | tf_op jit(solution)/shard_map/ppermute | solution.py:322
  100.6 3.0 %collective-permute-start.10 = (f32[2,128]{1,0:T(2,128)S(1)}, f32[2,128]{1,0:T(2,128)S(1)}, u32[]{:S(2)}, u32[]{:S(2)}) collective-permute-start(f32[2,128]{1,0:T(2,128)S(1)} %add.29), channel_id=1, source_target_pairs={{0,2},{1,3},{2,0},{3,1},{4,6},{5,7},{6,4},{7,5},{8,10},{9,11},{10,... | collective-permute-start | bytes 3080 | tf_op jit(solution)/shard_map/ppermute | solution.py:322
  102.2 3.6 %collective-permute-start.9 = (f32[2,128]{1,0:T(2,128)S(1)}, f32[2,128]{1,0:T(2,128)S(1)}, u32[]{:S(2)}, u32[]{:S(2)}) collective-permute-start(f32[2,128]{1,0:T(2,128)S(1)} %add.29), channel_id=1, source_target_pairs={{0,1},{1,0},{2,3},{3,2},{4,5},{5,4},{6,7},{7,6},{8,9},{9,8},{10,11... | collective-permute-start | bytes 3080 | tf_op jit(solution)/shard_map/ppermute | solution.py:322
  105.8 9.3 %collective-permute-start.14 = (f32[2,128]{1,0:T(2,128)S(1)}, f32[2,128]{1,0:T(2,128)S(1)}, u32[]{:S(2)}, u32[]{:S(2)}) collective-permute-start(f32[2,128]{1,0:T(2,128)S(1)} %add_add_fusion.1), channel_id=1, source_target_pairs={{0,24},{1,25},{2,26},{3,27},{4,28},{5,29},{6,30},{7,31},{8,16},{9,... | collective-permute-start | bytes 3080 | tf_op jit(solution)/shard_map/ppermute | solution.py:322
  109.6 5.5 %collective-permute-start.13 = (f32[2,128]{1,0:T(2,128)S(1)}, f32[2,128]{1,0:T(2,128)S(1)}, u32[]{:S(2)}, u32[]{:S(2)}) collective-permute-start(f32[2,128]{1,0:T(2,128)S(1)} %add_add_fusion.1), channel_id=1, source_target_pairs={{0,16},{1,17},{2,18},{3,19},{4,20},{5,21},{6,22},{7,23},{8,24},{9,... | collective-permute-start | bytes 3080 | tf_op jit(solution)/shard_map/ppermute | solution.py:322
  109.6 5.5 %collective-permute-start.12 = (f32[2,128]{1,0:T(2,128)S(1)}, f32[2,128]{1,0:T(2,128)S(1)}, u32[]{:S(2)}, u32[]{:S(2)}) collective-permute-start(f32[2,128]{1,0:T(2,128)S(1)} %add_add_fusion.1), channel_id=1, source_target_pairs={{0,8},{1,9},{2,10},{3,11},{4,12},{5,13},{6,14},{7,15},{8,0},{9,1},... | collective-permute-start | bytes 3080 | tf_op jit(solution)/shard_map/ppermute | solution.py:322

commit v7 on v6

--- a/solution.py
+++ b/solution.py
@@ -35,7 +35,7 @@
 
 def heads_kernel(
     shard_ref, q_ref, g_ref, own_ref, near_ref, far_ref, q_gain_ref, k_gain_ref, _,
-    dq_ref, d_own_ref, d_near_ref, d_far_ref, gains_ref,
+    dq_ref, d_own_ref, d_near_k_ref, d_near_v_ref, d_far_ref, gains_ref,
     k_low, k_low_t, k_rms, values, q_low, q_rms, probs_all, d_scores_all,
 ):
     rows = own_ref.shape[2]
@@ -47,6 +47,11 @@
     far_ok = jnp.where(shard_ref[0] >= 2, 1.0, 0.0)
     near_ok = jnp.where(shard_ref[0] >= 1, 1.0, 0.0)
     key_refs = (far_ref, near_ref, own_ref)
+    grad_refs = (
+        (d_far_ref.at[0], d_far_ref.at[1]),
+        (d_near_k_ref, d_near_v_ref),
+        (d_own_ref.at[0], d_own_ref.at[1]),
+    )
 
     @pl.when(pl.program_id(0) == 0)
     def _():
@@ -134,9 +139,7 @@
         key_grad = score_scale * jnp.dot(
             d_scores_all[keys, meets], q_low[meets, :], preferred_element_type=jnp.float32
         )
-        for place, (ref, out) in enumerate(
-            zip(key_refs, (d_far_ref, d_near_ref, d_own_ref), strict=True)
-        ):
+        for place, (ref, outs) in enumerate(zip(key_refs, grad_refs, strict=True)):
             start = max(first * TILE, place * rows)
             stop = min(last * TILE, (place + 1) * rows)
             if start >= stop:
@@ -145,21 +148,20 @@
             here = slice(start - first * TILE, stop - first * TILE)
             unit = ref[0, 0, inside, :].astype(jnp.float32) * k_rms[start:stop, :]
             k_gain_sum = k_gain_sum + jnp.sum(key_grad[here] * unit, axis=0, keepdims=True)
-            out[0, 0, inside, :] = key_grad[here].astype(out.dtype)
-            out[1, 0, inside, :] = value_grad[here].astype(out.dtype)
+            outs[0][0, inside, :] = key_grad[here].astype(outs[0].dtype)
+            outs[1][0, inside, :] = value_grad[here].astype(outs[1].dtype)
     gains_ref[0:1, :] += q_gain_sum
     gains_ref[1:2, :] += k_gain_sum
 
 
 def closed(shard_ref, own, returned, swapped, kind, head):
     keep = jnp.where(shard_ref[0] % 2 == 1, 0.0, 1.0)
-    own, returned, swapped = (
-        part[kind, head].astype(jnp.float32) for part in (own, returned, swapped)
-    )
-    return own + returned + keep * swapped
-
-
-def close_kernel(shard_ref, own, returned, swapped, raw_ref, k_gain_ref, out):
+    own, returned = (part[kind, head].astype(jnp.float32) for part in (own, returned))
+    return own + returned + keep * swapped[kind][head].astype(jnp.float32)
+
+
+def close_kernel(shard_ref, own, returned, swapped_k, swapped_v, raw_ref, k_gain_ref, out):
+    swapped = (swapped_k, swapped_v)
     for head in range(own.shape[1]):
         grad = closed(shard_ref, own, returned, swapped, 0, head)
         raw = raw_ref[0, head].astype(jnp.float32)
@@ -168,7 +170,8 @@
         out[1, head] = closed(shard_ref, own, returned, swapped, 1, head).astype(out.dtype)
 
 
-def finish_kernel(shard_ref, own, returned, swapped, raw_ref, k_gain_ref, *rest):
+def finish_kernel(shard_ref, own, returned, swapped_k, swapped_v, raw_ref, k_gain_ref, *rest):
+    swapped = (swapped_k, swapped_v)
     *done, key_out, value_out, by_token = rest
     rows, heads, _ = key_out.shape
     before = [(part, head) for part in done for head in range(part.shape[1])]
@@ -196,10 +199,25 @@
         out_ref[...] = own_ref[...]
 
 
-def relay_kernel(shard_ref, far_ref, swapped_ref, out_ref):
+def relay_kernel(shard_ref, far_ref, swapped_k_ref, swapped_v_ref, out_ref):
     odd = jnp.where(shard_ref[0] % 2 == 1, 1.0, 0.0)
-    total = far_ref[...].astype(jnp.float32) + odd * swapped_ref[...].astype(jnp.float32)
-    out_ref[...] = total.astype(out_ref.dtype)
+    for kind, ref in enumerate((swapped_k_ref, swapped_v_ref)):
+        total = far_ref[kind].astype(jnp.float32) + odd * ref[...].astype(jnp.float32)
+        out_ref[kind] = total.astype(out_ref.dtype)
+
+
+def choose(shard, far, own, here, count):
+    _, _, rows, width = own.shape
+    held = pl.BlockSpec((2, 1, rows, width), lambda head: (0, here + head, 0, 0))
+    return pl.pallas_call(
+        choose_kernel,
+        grid=(count,),
+        in_specs=[pl.BlockSpec(memory_space=pltpu.SMEM), held, held],
+        out_specs=pl.BlockSpec((2, 1, rows, width), lambda head: (0, head, 0, 0)),
+        out_shape=jax.ShapeDtypeStruct((2, count, rows, width), own.dtype),
+        compiler_params=pltpu.CompilerParams(vmem_limit_bytes=8 * 1024 * 1024),
+        cost_estimate=LIGHT,
+    )(shard, far, own)
 
 
 def small_call(kernel, shard, *arrays):
@@ -221,7 +239,7 @@
         out_ref[...] = in_ref[...]
 
 
-def later(array, small):
+def later(array, small, cost=None):
     vmem = pl.BlockSpec(memory_space=pltpu.VMEM)
     held = pl.BlockSpec(memory_space=pltpu.SMEM if small.ndim == 1 else pltpu.VMEM)
     return pl.pallas_call(
@@ -230,7 +248,7 @@
         out_specs=held,
         out_shape=jax.ShapeDtypeStruct(small.shape, small.dtype),
         compiler_params=pltpu.CompilerParams(vmem_limit_bytes=1024 * 1024),
-        cost_estimate=HEAVY,
+        cost_estimate=cost or HEAVY,
     )(array[0, 0, :16], small)
 
 
@@ -242,26 +260,29 @@
     whole_q = pl.BlockSpec((1, query_rows, width), lambda head: (first + head, 0, 0))
     part = pl.BlockSpec((2, 1, rows, width), lambda head: (0, head, 0, 0))
     held = pl.BlockSpec((2, 1, rows, width), lambda head: (0, here + head, 0, 0))
+    half = pl.BlockSpec((1, rows, width), lambda head: (head, 0, 0))
     gain = pl.BlockSpec((1, width), lambda head: (0, 0))
     shape = (2, count, rows, width)
     return pl.pallas_call(
         heads_kernel,
         grid=(count,),
         in_specs=[
-            pl.BlockSpec(memory_space=pltpu.SMEM), whole_q, whole_q, held, held, held, gain, gain,
+            pl.BlockSpec(memory_space=pltpu.SMEM), whole_q, whole_q, held, part, held, gain, gain,
             pl.BlockSpec(memory_space=pl.ANY),
         ],
         out_specs=[
             pl.BlockSpec((rows, 1, group, width), lambda head: (0, first + head, 0, 0)),
             part,
-            part,
+            half,
+            half,
             part,
             pl.BlockSpec((2, width), lambda head: (0, 0)),
         ],
         out_shape=[
             jax.ShapeDtypeStruct(dq.shape, dq.dtype),
             jax.ShapeDtypeStruct(shape, jnp.bfloat16),
-            jax.ShapeDtypeStruct(shape, jnp.bfloat16),
+            jax.ShapeDtypeStruct(shape[1:], jnp.bfloat16),
+            jax.ShapeDtypeStruct(shape[1:], jnp.bfloat16),
             jax.ShapeDtypeStruct(shape, jnp.bfloat16),
             jax.ShapeDtypeStruct((2, width), jnp.float32),
         ],
@@ -285,12 +306,12 @@
     smem, vmem = (pl.BlockSpec(memory_space=space) for space in (pltpu.SMEM, pltpu.VMEM))
     return pl.pallas_call(
         close_kernel,
-        in_specs=[smem] + [vmem] * 5,
+        in_specs=[smem] + [vmem] * 6,
         out_specs=vmem,
         out_shape=jax.ShapeDtypeStruct(own.shape, jnp.bfloat16),
         compiler_params=pltpu.CompilerParams(vmem_limit_bytes=12 * 1024 * 1024),
         cost_estimate=LIGHT,
-    )(shard, own, returned, swapped, raw, k_gain)
+    )(shard, own, returned, *swapped, raw, k_gain)
 
 
 def finish(shard, own, returned, swapped, raw, k_gain, done):
@@ -300,12 +321,12 @@
     smem, vmem = (pl.BlockSpec(memory_space=space) for space in (pltpu.SMEM, pltpu.VMEM))
     return pl.pallas_call(
         finish_kernel,
-        in_specs=[smem] + [vmem] * (5 + len(done)),
+        in_specs=[smem] + [vmem] * (6 + len(done)),
         out_specs=[vmem, vmem],
         out_shape=[jax.ShapeDtypeStruct(shape, jnp.bfloat16)] * 2,
         scratch_shapes=[pltpu.VMEM((rows * kv_dev, width), jnp.float32)],
         compiler_params=pltpu.CompilerParams(vmem_limit_bytes=20 * 1024 * 1024),
-    )(shard, own, returned, swapped, raw, k_gain, *done)
+    )(shard, own, returned, *swapped, raw, k_gain, *done)
 
 
 def group_sizes(kv_dev):
@@ -353,9 +374,9 @@
     scalar = shard.astype(jnp.int32).reshape(1)
     q_gain_2d, k_gain_2d = q_gain.reshape(1, width), k_gain.reshape(1, width)
 
-    def split(d_own, d_near, d_far, raw):
-        swapped = lax.ppermute(d_near, "seq", swap)
-        relayed = small_call(relay_kernel, scalar, d_far, swapped)
+    def split(d_own, d_near_k, d_near_v, d_far, raw):
+        swapped = [lax.ppermute(half, "seq", swap) for half in (d_near_k, d_near_v)]
+        relayed = small_call(relay_kernel, scalar, d_far, *swapped)
         return relayed, (d_own, swapped, raw)
 
     def close(stays, returned):
@@ -378,14 +399,17 @@
                 far, queries, grads, *_ = lax.optimization_barrier(
                     (far, queries, grads, *owns[1:])
                 )
-            near = lax.ppermute(small_call(choose_kernel, scalar, far, own), "seq", swap)
+        elif place:
+            far, gains[-1] = lax.optimization_barrier((far, gains[-1]))
+        chosen = choose(scalar, far, own, first - start, size)
+        near = lax.ppermute(chosen, "seq", swap)
         scalar_now = scalar
         if grads_out is not None:
             if kept:
                 before, returned = kept.pop()
-                scalar_now = later(returned, scalar)
+                near, returned = lax.optimization_barrier((near, returned))
+                scalar_now = later(returned, scalar, LIGHT)
                 done.append(close(before, returned))
-            near, relayed, scalar_now = lax.optimization_barrier((near, relayed, scalar_now))
             kept.append((stays, lax.ppermute(relayed, "seq", back)))
         here = slice(first - start, first - start + size)
         grad_query, *grads_out, gain = group_grads(

time: 116 us -> 112 us (0.966)
  waiting for transfers between devices: 31.6 us -> 24.7 us
  starting transfers between devices: 22.9 us -> 24.9 us
  Pallas kernels: 49.5 us -> 50.7 us
    ppermute x2, waiting for transfers between devices: 8.54 us -> 3.82 us  [per_device(): kept.append((stays, lax.ppermute(relayed, 'seq', back)))]
    pallas_call x3 -> x6, Pallas kernels: 4.23 us -> 6.73 us  [the longest x3 2.6 us: choose(): pl.pallas_call(choose_kernel, grid=(count,), in_specs=[pl.BlockSpec(memor...]
    ppermute x5 -> x9, starting transfers between devices: 0.42 us -> 1.88 us  [the longest x6 1.53 us: split(): swapped = [lax.ppermute(half, 'seq', swap) for half in (d_near_k, d_near_v)]]
    pallas_call x5 -> x3, Pallas kernels: 1.94 us -> 0.63 us  [small_call(): pl.pallas_call(kernel, in_specs=[smem] + [vmem] * len(arrays), out_specs=...]
    ppermute x2, waiting for transfers between devices: 13.3 us -> 12.1 us  [per_device(): fars = [lax.ppermute(own, 'seq', ahead) for own in owns]]
    ppermute x5 -> x9, waiting for transfers between devices: 5.3 us -> 4.4 us  [the longest x3 3.07 us: per_device(): near = lax.ppermute(chosen, 'seq', swap)]
  transfers between devices with their start and end apart: 17 -> 21, of which waited for: 10 -> 13; matrix products, arithmetic and copies ran while one was open for 6% -> 7% of each run, Pallas kernels for 42% -> 45%
where the time goes in v7:
time: 112 us
  Pallas kernels  50.7 us (45%)
  starting transfers between devices  24.9 us (22%)
  waiting for transfers between devices  24.7 us (22%)
  local copies, waits for them, and re-layouts  10.5 us (9%)
    pallas_call x3, Pallas kernels, group_grads(): pl.pallas_call(heads_kernel, grid=(count,), in_specs=[pl.BlockSpec(memory...  42.8 us
    ppermute x2, waiting for transfers between devices, per_device(): fars = [lax.ppermute(own, 'seq', ahead) for own in owns]  12.1 us
    ppermute x7, starting transfers between devices, exchanged(): lax.ppermute(value, ('seq', 'head'), [(source, source ^ mask) for source...  10.4 us
    ppermute x2, starting transfers between devices, per_device(): fars = [lax.ppermute(own, 'seq', ahead) for own in owns]  8.4 us
    reshape x2, local copies, waits for them, and re-layouts, by_head(): split = array.reshape(rows, kv_dev, group, width)  4.62 us
    ppermute x7, waiting for transfers between devices, exchanged(): lax.ppermute(value, ('seq', 'head'), [(source, source ^ mask) for source...  4.03 us
    ppermute x2, waiting for transfers between devices, per_device(): kept.append((stays, lax.ppermute(relayed, 'seq', back)))  3.82 us
    ppermute x3, waiting for transfers between devices, per_device(): near = lax.ppermute(chosen, 'seq', swap)  3.07 us
  transfers between devices with their start and end apart: 21, of which 13 were waited for; matrix products, arithmetic and copies ran while one was open for 7% of the time, Pallas kernels for 45%

profile of v7, /device:TPU:0, one launch (start us, length us, event | category | flops | bytes accessed | tf_op | source)
XLA Modules:
  0.0 112.0 jit_solution(704620417361638430)
XLA Ops:
  0.6 1.9 %copy_bitcast_fusion = (bf16[8,512,128]{2,1,0:T(8,128)(2,1)S(1)}, bf16[8,512,128]{2,1,0:T(8,128)(2,1)S(1)}) fusion(bf16[512,8,128]{2,1,0:T(8,128)(2,1)} %param.8, bf16[512,8,128]{2,1,0:T(8,128)(2,1)} %param.7), kind=kLoop, calls=%fused_computation.1 | loop fusion | bytes 4194304 | tf_op jit(solution)/shard_map/transpose | solution.py:370
  2.7 5.8 %collective-permute-start = (bf16[2,3,512,128]{3,2,1,0:T(8,128)(2,1)S(1)}, bf16[2,3,512,128]{3,2,1,0:T(8,128)(2,1)}, u32[]{:S(2)}, u32[]{:S(2)}) collective-permute-start(bf16[2,3,512,128]{3,2,1,0:T(8,128)(2,1)S(1)} %pad_maximum_fusion.1.own_ref), channel_id=1, source_target_pairs={{0,4},{2,6},{4,8},{6,10},{8,12},{10,14},{12,16},{14,18},{16,20},{1... | collective-permute-start | bytes 2359304 | tf_op jit(solution)/shard_map/ppermute | solution.py:372
  9.5 2.6 %collective-permute-start.1 = (bf16[2,5,512,128]{3,2,1,0:T(8,128)(2,1)S(1)}, bf16[2,5,512,128]{3,2,1,0:T(8,128)(2,1)S(1)}, u32[]{:S(2)}, u32[]{:S(2)}) collective-permute-start(bf16[2,5,512,128]{3,2,1,0:T(8,128)(2,1)S(1)} %pad_maximum_fusion.own_ref), channel_id=1, source_target_pairs={{0,4},{2,6},{4,8},{6,10},{8,12},{10,14},{12,16},{14,18},{16,20},{1... | collective-permute-start | bytes 3932168 | tf_op jit(solution)/shard_map/ppermute | solution.py:372
  12.2 3.2 %copy.16 = bf16[512,8,2,128]{3,2,0,1:T(2,128)(2,1)S(1)} copy(bf16[512,8,2,128]{3,2,1,0:T(2,128)(2,1)} %bitcast.50) | data formatting | bytes 4194304 | tf_op jit(solution)/shard_map/reshape | solution.py:364
  15.4 1.4 %copy.17 = bf16[512,8,2,128]{3,2,0,1:T(2,128)(2,1)S(1)} copy(bf16[512,8,2,128]{3,2,1,0:T(2,128)(2,1)S(1)} %bitcast.51) | data formatting | bytes 4194304 | tf_op jit(solution)/shard_map/reshape | solution.py:364
  16.8 8.7 %collective-permute-done.far_ref = bf16[2,3,512,128]{3,2,1,0:T(8,128)(2,1)} collective-permute-done((bf16[2,3,512,128]{3,2,1,0:T(8,128)(2,1)S(1)}, bf16[2,3,512,128]{3,2,1,0:T(8,128)(2,1)}, u32[]{:S(2)}, u32[]{:S(2)}) %collective-permute-start) | collective-permute-done | bytes 786464 | tf_op jit(solution)/shard_map/ppermute | solution.py:372
  25.5 2.0 %shard_map.101 = bf16[2,3,512,128]{3,2,1,0:T(8,128)(2,1)S(1)} custom-call(s32[1]{0:T(128)} %bitcast.shard_ref.in_ref, bf16[2,3,512,128]{3,2,1,0:T(8,128)(2,1)} %collective-permute-done.far_ref, bf16[2,3,512,128]{3,2,1,0:T(8,128)(2,1)S(1)} %pad_maximum_fusion.1.own_ref), custom_call_target="tpu_custom_call" | custom-call | flops 1000 | bytes 1000 | tf_op jit(solution)/shard_map/pallas_call | solution.py:212
  27.7 2.3 %collective-permute-done.2.near_ref = bf16[2,3,512,128]{3,2,1,0:T(8,128)(2,1)S(1)} collective-permute-done((bf16[2,3,512,128]{3,2,1,0:T(8,128)(2,1)S(1)}, bf16[2,3,512,128]{3,2,1,0:T(8,128)(2,1)S(1)}, u32[]{:S(2)}, u32[]{:S(2)}) %collective-permute-start.2) | collective-permute-done | bytes 786464 | tf_op jit(solution)/shard_map/ppermute | solution.py:405
  29.9 2.4 %broadcast_in_dim.3._ = bf16[512,8,2,128]{3,2,1,0:T(2,128)(2,1)} broadcast(bf16[]{:T(256)} %constant.7.clone.1), dimensions={} | broadcast | bytes 2097154 | tf_op jit(solution)/shard_map/broadcast_in_dim | solution.py:387
  32.3 16.3 %shard_map.102 = (bf16[512,8,2,128]{3,2,1,0:T(2,128)(2,1)}, bf16[2,3,512,128]{3,2,1,0:T(8,128)(2,1)S(1)}, bf16[3,512,128]{2,1,0:T(8,128)(2,1)S(1)}, bf16[3,512,1...) custom-call(s32[1]{0:T(128)} %bitcast.shard_ref.in_ref, ...), custom_call_target="tpu_custom_call", output_to_operand_aliasing={{0}: (8, {})} | custom-call | flops 1000 | bytes 1000 | tf_op jit(solution)/shard_map/pallas_call | solution.py:266
  49.1 3.4 %collective-permute-done.1.far_ref = bf16[2,5,512,128]{3,2,1,0:T(8,128)(2,1)S(1)} collective-permute-done((bf16[2,5,512,128]{3,2,1,0:T(8,128)(2,1)S(1)}, bf16[2,5,512,128]{3,2,1,0:T(8,128)(2,1)S(1)}, u32[]{:S(2)}, u32[]{:S(2)}) %collective-permute-start.1) | collective-permute-done | bytes 1310752 | tf_op jit(solution)/shard_map/ppermute | solution.py:372
  53.2 1.5 %collective-permute-start.10 = (bf16[2,3,512,128]{3,2,1,0:T(8,128)(2,1)S(1)}, bf16[2,3,512,128]{3,2,1,0:T(8,128)(2,1)S(1)}, u32[]{:S(2)}, u32[]{:S(2)}) collective-permute-start(bf16[2,3,512,128]{3,2,1,0:T(8,128)(2,1)S(1)} %shard_map.104), channel_id=1, source_target_pairs={{4,0},{6,2},{8,4},{10,6},{12,8},{14,10},{16,12},{18,14},{20,16},{2... | collective-permute-start | bytes 2359304 | tf_op jit(solution)/shard_map/ppermute | solution.py:413
  55.4 15.4 %shard_map.106 = (bf16[512,8,2,128]{3,2,1,0:T(2,128)(2,1)}, bf16[2,3,512,128]{3,2,1,0:T(8,128)(2,1)S(1)}, bf16[3,512,128]{2,1,0:T(8,128)(2,1)S(1)}, bf16[3,512,1...) custom-call(s32[1]{0:T(128)} %bitcast.shard_ref.in_ref, ...), custom_call_target="tpu_custom_call", output_to_operand_aliasing={{0}: (8, {})} | custom-call | flops 1000 | bytes 1000 | tf_op jit(solution)/shard_map/pallas_call | solution.py:266
  73.4 1.3 %collective-permute-start.8 = (bf16[2,3,512,128]{3,2,1,0:T(8,128)(2,1)S(1)}, bf16[2,3,512,128]{3,2,1,0:T(8,128)(2,1)S(1)}, u32[]{:S(2)}, u32[]{:S(2)}) collective-permute-start(bf16[2,3,512,128]{3,2,1,0:T(8,128)(2,1)S(1)} %shard_map.107), channel_id=1, source_target_pairs={{4,0},{6,2},{8,4},{10,6},{12,8},{14,10},{16,12},{18,14},{20,16},{2... | collective-permute-start | bytes 2359304 | tf_op jit(solution)/shard_map/ppermute | solution.py:413
  74.7 1.1 collective-permute-done.10.returned
  76.3 11.2 %shard_map.111 = (bf16[512,8,2,128]{3,2,1,0:T(2,128)(2,1)}, bf16[2,2,512,128]{3,2,1,0:T(8,128)(2,1)S(1)}, bf16[2,512,128]{2,1,0:T(8,128)(2,1)S(1)}, bf16[2,512,1...) custom-call(s32[1]{0:T(128)} %shard_map.110.shard_ref, ...), custom_call_target="tpu_custom_call", output_to_operand_aliasing={{0}: (8, {})} | custom-call | flops 1000 | bytes 1000 | tf_op jit(solution)/shard_map/pallas_call | solution.py:266
  88.0 2.6 %collective-permute-start.11 = (f32[2,128]{1,0:T(2,128)S(1)}, f32[2,128]{1,0:T(2,128)S(1)}, u32[]{:S(2)}, u32[]{:S(2)}) collective-permute-start(f32[2,128]{1,0:T(2,128)S(1)} %add_add_fusion.2.in_ref), channel_id=1, source_target_pairs={{0,4},{1,5},{2,6},{3,7},{4,0},{5,1},{6,2},{7,3},{8,12},{9,13},{10,... | collective-permute-start | bytes 3080 | tf_op jit(solution)/shard_map/ppermute | solution.py:343
  91.6 1.5 %collective-permute-start.20 = (bf16[2,2,512,128]{3,2,1,0:T(8,128)(2,1)S(1)}, bf16[2,2,512,128]{3,2,1,0:T(8,128)(2,1)S(1)}, u32[]{:S(2)}, u32[]{:S(2)}) collective-permute-start(bf16[2,2,512,128]{3,2,1,0:T(8,128)(2,1)S(1)} %shard_map.114), channel_id=1, source_target_pairs={{4,0},{6,2},{8,4},{10,6},{12,8},{14,10},{16,12},{18,14},{20,16},{2... | collective-permute-start | bytes 1572872 | tf_op jit(solution)/shard_map/ppermute | solution.py:434
  93.1 2.8 %collective-permute-done.8.returned = bf16[2,3,512,128]{3,2,1,0:T(8,128)(2,1)S(1)} collective-permute-done((bf16[2,3,512,128]{3,2,1,0:T(8,128)(2,1)S(1)}, bf16[2,3,512,128]{3,2,1,0:T(8,128)(2,1)S(1)}, u32[]{:S(2)}, u32[]{:S(2)}) %collective-permute-start.8) | collective-permute-done | bytes 786464 | tf_op jit(solution)/shard_map/ppermute | solution.py:413
  95.9 0.9 collective-permute-start.14
  98.9 2.2 %collective-permute-done.12 = f32[2,128]{1,0:T(2,128)S(1)} collective-permute-done((f32[2,128]{1,0:T(2,128)S(1)}, f32[2,128]{1,0:T(2,128)S(1)}, u32[]{:S(2)}, u32[]{:S(2)}) %collective-permute-start.12) | collective-permute-done | bytes 1056 | tf_op jit(solution)/shard_map/ppermute | solution.py:343
  101.1 4.9 %collective-permute-start.17 = (f32[2,128]{1,0:T(2,128)S(1)}, f32[2,128]{1,0:T(2,128)S(1)}, u32[]{:S(2)}, u32[]{:S(2)}) collective-permute-start(f32[2,128]{1,0:T(2,128)S(1)} %add_add_fusion.1), channel_id=1, source_target_pairs={{0,24},{1,25},{2,26},{3,27},{4,28},{5,29},{6,30},{7,31},{8,16},{9,... | collective-permute-start | bytes 3080 | tf_op jit(solution)/shard_map/ppermute | solution.py:343
  107.1 2.6 %shard_map.115 = (bf16[512,8,128]{2,1,0:T(8,128)(2,1)}, bf16[512,8,128]{2,1,0:T(8,128)(2,1)}) custom-call(s32[1]{0:T(128)} %bitcast.shard_ref.in_ref, bf16[2,2,512,128]{3,2,1,0:T(8,128)(2,1)S(1)} %get-tuple-element.85.own, bf16[2,2,512,128]{3,2,1,0:T(8,128)(2,1)S(1)} %collective-permute-done.20.returned, ...), custom_call_target="tpu_custom_call" | custom-call | tf_op jit(solution)/shard_map/pallas_call | solution.py:322
  109.7 1.7 %collective-permute-done.17 = f32[2,128]{1,0:T(2,128)S(1)} collective-permute-done((f32[2,128]{1,0:T(2,128)S(1)}, f32[2,128]{1,0:T(2,128)S(1)}, u32[]{:S(2)}, u32[]{:S(2)}) %collective-permute-start.17) | collective-permute-done | bytes 1056 | tf_op jit(solution)/shard_map/ppermute | solution.py:343
  (67 shorter events, 11.4 us)
Async XLA Ops:
  2.7 22.8 %collective-permute-start = (bf16[2,3,512,128]{3,2,1,0:T(8,128)(2,1)S(1)}, bf16[2,3,512,128]{3,2,1,0:T(8,128)(2,1)}, u32[]{:S(2)}, u32[]{:S(2)}) collective-permute-start(bf16[2,3,512,128]{3,2,1,0:T(8,128)(2,1)S(1)} %pad_maximum_fusion.1.own_ref), channel_id=1, source_target_pairs={{0,4},{2,6},{4,8},{6,10},{8,12},{10,14},{12,16},{14,18},{16,20},{1... | collective-permute-start | bytes 2359304 | tf_op jit(solution)/shard_map/ppermute | solution.py:372
  9.5 42.9 %collective-permute-start.1 = (bf16[2,5,512,128]{3,2,1,0:T(8,128)(2,1)S(1)}, bf16[2,5,512,128]{3,2,1,0:T(8,128)(2,1)S(1)}, u32[]{:S(2)}, u32[]{:S(2)}) collective-permute-start(bf16[2,5,512,128]{3,2,1,0:T(8,128)(2,1)S(1)} %pad_maximum_fusion.own_ref), channel_id=1, source_target_pairs={{0,4},{2,6},{4,8},{6,10},{8,12},{10,14},{12,16},{14,18},{16,20},{1... | collective-permute-start | bytes 3932168 | tf_op jit(solution)/shard_map/ppermute | solution.py:372
  25.5 6.8 %copy-start.2 = (f32[128]{0:T(128)S(1)}, f32[128]{0:T(128)}, u32[]{:S(2)}) copy-start(f32[128]{0:T(128)} %param.11) | copy-start | bytes 1540
  25.5 6.8 %copy-start.3 = (f32[128]{0:T(128)S(1)}, f32[128]{0:T(128)}, u32[]{:S(2)}) copy-start(f32[128]{0:T(128)} %param.10) | copy-start | bytes 1540
  27.6 2.4 %collective-permute-start.2 = (bf16[2,3,512,128]{3,2,1,0:T(8,128)(2,1)S(1)}, bf16[2,3,512,128]{3,2,1,0:T(8,128)(2,1)S(1)}, u32[]{:S(2)}, u32[]{:S(2)}) collective-permute-start(bf16[2,3,512,128]{3,2,1,0:T(8,128)(2,1)S(1)} %shard_map.101), channel_id=1, source_target_pairs={{0,2},{2,0},{4,6},{6,4},{8,10},{10,8},{12,14},{14,12},{16,18},{18,... | collective-permute-start | bytes 2359304 | tf_op jit(solution)/shard_map/ppermute | solution.py:405
  48.6 3.9 %collective-permute-start.3 = (bf16[3,512,128]{2,1,0:T(8,128)(2,1)S(1)}, bf16[3,512,128]{2,1,0:T(8,128)(2,1)S(1)}, u32[]{:S(2)}, u32[]{:S(2)}) collective-permute-start(bf16[3,512,128]{2,1,0:T(8,128)(2,1)S(1)} %get-tuple-element.60), channel_id=1, source_target_pairs={{0,2},{2,0},{4,6},{6,4},{8,10},{10,8},{12,14},{14,12},{16,18},{18,... | collective-permute-start | bytes 1179656 | tf_op jit(solution)/shard_map/ppermute | solution.py:378
  48.7 3.7 %collective-permute-start.4 = (bf16[3,512,128]{2,1,0:T(8,128)(2,1)S(1)}, bf16[3,512,128]{2,1,0:T(8,128)(2,1)S(1)}, u32[]{:S(2)}, u32[]{:S(2)}) collective-permute-start(bf16[3,512,128]{2,1,0:T(8,128)(2,1)S(1)} %get-tuple-element.61), channel_id=1, source_target_pairs={{0,2},{2,0},{4,6},{6,4},{8,10},{10,8},{12,14},{14,12},{16,18},{18,... | collective-permute-start | bytes 1179656 | tf_op jit(solution)/shard_map/ppermute | solution.py:378
  53.1 2.4 %collective-permute-start.5 = (bf16[2,3,512,128]{3,2,1,0:T(8,128)(2,1)S(1)}, bf16[2,3,512,128]{3,2,1,0:T(8,128)(2,1)S(1)}, u32[]{:S(2)}, u32[]{:S(2)}) collective-permute-start(bf16[2,3,512,128]{3,2,1,0:T(8,128)(2,1)S(1)} %shard_map.105), channel_id=1, source_target_pairs={{0,2},{2,0},{4,6},{6,4},{8,10},{10,8},{12,14},{14,12},{16,18},{18,... | collective-permute-start | bytes 2359304 | tf_op jit(solution)/shard_map/ppermute | solution.py:405
  53.2 22.6 %collective-permute-start.10 = (bf16[2,3,512,128]{3,2,1,0:T(8,128)(2,1)S(1)}, bf16[2,3,512,128]{3,2,1,0:T(8,128)(2,1)S(1)}, u32[]{:S(2)}, u32[]{:S(2)}) collective-permute-start(bf16[2,3,512,128]{3,2,1,0:T(8,128)(2,1)S(1)} %shard_map.104), channel_id=1, source_target_pairs={{4,0},{6,2},{8,4},{10,6},{12,8},{14,10},{16,12},{18,14},{20,16},{2... | collective-permute-start | bytes 2359304 | tf_op jit(solution)/shard_map/ppermute | solution.py:413
  70.8 1.7 %collective-permute-start.6 = (bf16[3,512,128]{2,1,0:T(8,128)(2,1)S(1)}, bf16[3,512,128]{2,1,0:T(8,128)(2,1)S(1)}, u32[]{:S(2)}, u32[]{:S(2)}) collective-permute-start(bf16[3,512,128]{2,1,0:T(8,128)(2,1)S(1)} %get-tuple-element.65), channel_id=1, source_target_pairs={{0,2},{2,0},{4,6},{6,4},{8,10},{10,8},{12,14},{14,12},{16,18},{18,... | collective-permute-start | bytes 1179656 | tf_op jit(solution)/shard_map/ppermute | solution.py:378
  71.0 2.1 %collective-permute-start.7 = (bf16[3,512,128]{2,1,0:T(8,128)(2,1)S(1)}, bf16[3,512,128]{2,1,0:T(8,128)(2,1)S(1)}, u32[]{:S(2)}, u32[]{:S(2)}) collective-permute-start(bf16[3,512,128]{2,1,0:T(8,128)(2,1)S(1)} %get-tuple-element.66), channel_id=1, source_target_pairs={{0,2},{2,0},{4,6},{6,4},{8,10},{10,8},{12,14},{14,12},{16,18},{18,... | collective-permute-start | bytes 1179656 | tf_op jit(solution)/shard_map/ppermute | solution.py:378
  71.6 4.1 %collective-permute-start.9 = (bf16[2,2,512,128]{3,2,1,0:T(8,128)(2,1)S(1)}, bf16[2,2,512,128]{3,2,1,0:T(8,128)(2,1)S(1)}, u32[]{:S(2)}, u32[]{:S(2)}) collective-permute-start(bf16[2,2,512,128]{3,2,1,0:T(8,128)(2,1)S(1)} %shard_map.108), channel_id=1, source_target_pairs={{0,2},{2,0},{4,6},{6,4},{8,10},{10,8},{12,14},{14,12},{16,18},{18,... | collective-permute-start | bytes 1572872 | tf_op jit(solution)/shard_map/ppermute | solution.py:405
  73.4 22.5 %collective-permute-start.8 = (bf16[2,3,512,128]{3,2,1,0:T(8,128)(2,1)S(1)}, bf16[2,3,512,128]{3,2,1,0:T(8,128)(2,1)S(1)}, u32[]{:S(2)}, u32[]{:S(2)}) collective-permute-start(bf16[2,3,512,128]{3,2,1,0:T(8,128)(2,1)S(1)} %shard_map.107), channel_id=1, source_target_pairs={{4,0},{6,2},{8,4},{10,6},{12,8},{14,10},{16,12},{18,14},{20,16},{2... | collective-permute-start | bytes 2359304 | tf_op jit(solution)/shard_map/ppermute | solution.py:413
  76.3 14.3 %copy-start.1 = (bf16[1,3,512,128]{3,2,1,0:T(8,128)(2,1)S(1)}, bf16[1,3,512,128]{3,2,1,0:T(8,128)(2,1)}, u32[]{:S(2)}) copy-start(bf16[1,3,512,128]{3,2,1,0:T(8,128)(2,1)} %copy-done) | copy-start | bytes 1179652
  87.4 3.9 %collective-permute-start.18 = (bf16[2,512,128]{2,1,0:T(8,128)(2,1)S(1)}, bf16[2,512,128]{2,1,0:T(8,128)(2,1)S(1)}, u32[]{:S(2)}, u32[]{:S(2)}) collective-permute-start(bf16[2,512,128]{2,1,0:T(8,128)(2,1)S(1)} %get-tuple-element.87), channel_id=1, source_target_pairs={{0,2},{2,0},{4,6},{6,4},{8,10},{10,8},{12,14},{14,12},{16,18},{18,... | collective-permute-start | bytes 786440 | tf_op jit(solution)/shard_map/ppermute | solution.py:378
  87.4 4.0 %collective-permute-start.19 = (bf16[2,512,128]{2,1,0:T(8,128)(2,1)S(1)}, bf16[2,512,128]{2,1,0:T(8,128)(2,1)S(1)}, u32[]{:S(2)}, u32[]{:S(2)}) collective-permute-start(bf16[2,512,128]{2,1,0:T(8,128)(2,1)S(1)} %get-tuple-element.88), channel_id=1, source_target_pairs={{0,2},{2,0},{4,6},{6,4},{8,10},{10,8},{12,14},{14,12},{16,18},{18,... | collective-permute-start | bytes 786440 | tf_op jit(solution)/shard_map/ppermute | solution.py:378
  88.0 8.0 %collective-permute-start.11 = (f32[2,128]{1,0:T(2,128)S(1)}, f32[2,128]{1,0:T(2,128)S(1)}, u32[]{:S(2)}, u32[]{:S(2)}) collective-permute-start(f32[2,128]{1,0:T(2,128)S(1)} %add_add_fusion.2.in_ref), channel_id=1, source_target_pairs={{0,4},{1,5},{2,6},{3,7},{4,0},{5,1},{6,2},{7,3},{8,12},{9,13},{10,... | collective-permute-start | bytes 3080 | tf_op jit(solution)/shard_map/ppermute | solution.py:343
  91.6 15.5 %collective-permute-start.20 = (bf16[2,2,512,128]{3,2,1,0:T(8,128)(2,1)S(1)}, bf16[2,2,512,128]{3,2,1,0:T(8,128)(2,1)S(1)}, u32[]{:S(2)}, u32[]{:S(2)}) collective-permute-start(bf16[2,2,512,128]{3,2,1,0:T(8,128)(2,1)S(1)} %shard_map.114), channel_id=1, source_target_pairs={{4,0},{6,2},{8,4},{10,6},{12,8},{14,10},{16,12},{18,14},{20,16},{2... | collective-permute-start | bytes 1572872 | tf_op jit(solution)/shard_map/ppermute | solution.py:434
  95.9 3.0 %collective-permute-start.14 = (f32[2,128]{1,0:T(2,128)S(1)}, f32[2,128]{1,0:T(2,128)S(1)}, u32[]{:S(2)}, u32[]{:S(2)}) collective-permute-start(f32[2,128]{1,0:T(2,128)S(1)} %add.29), channel_id=1, source_target_pairs={{0,3},{1,2},{2,1},{3,0},{4,7},{5,6},{6,5},{7,4},{8,11},{9,10},{10,... | collective-permute-start | bytes 3080 | tf_op jit(solution)/shard_map/ppermute | solution.py:343
  96.8 2.1 %collective-permute-start.13 = (f32[2,128]{1,0:T(2,128)S(1)}, f32[2,128]{1,0:T(2,128)S(1)}, u32[]{:S(2)}, u32[]{:S(2)}) collective-permute-start(f32[2,128]{1,0:T(2,128)S(1)} %add.29), channel_id=1, source_target_pairs={{0,2},{1,3},{2,0},{3,1},{4,6},{5,7},{6,4},{7,5},{8,10},{9,11},{10,... | collective-permute-start | bytes 3080 | tf_op jit(solution)/shard_map/ppermute | solution.py:343
  97.6 3.6 %collective-permute-start.12 = (f32[2,128]{1,0:T(2,128)S(1)}, f32[2,128]{1,0:T(2,128)S(1)}, u32[]{:S(2)}, u32[]{:S(2)}) collective-permute-start(f32[2,128]{1,0:T(2,128)S(1)} %add.29), channel_id=1, source_target_pairs={{0,1},{1,0},{2,3},{3,2},{4,5},{5,4},{6,7},{7,6},{8,9},{9,8},{10,11... | collective-permute-start | bytes 3080 | tf_op jit(solution)/shard_map/ppermute | solution.py:343
  101.1 10.3 %collective-permute-start.17 = (f32[2,128]{1,0:T(2,128)S(1)}, f32[2,128]{1,0:T(2,128)S(1)}, u32[]{:S(2)}, u32[]{:S(2)}) collective-permute-start(f32[2,128]{1,0:T(2,128)S(1)} %add_add_fusion.1), channel_id=1, source_target_pairs={{0,24},{1,25},{2,26},{3,27},{4,28},{5,29},{6,30},{7,31},{8,16},{9,... | collective-permute-start | bytes 3080 | tf_op jit(solution)/shard_map/ppermute | solution.py:343
  106.1 5.4 %collective-permute-start.16 = (f32[2,128]{1,0:T(2,128)S(1)}, f32[2,128]{1,0:T(2,128)S(1)}, u32[]{:S(2)}, u32[]{:S(2)}) collective-permute-start(f32[2,128]{1,0:T(2,128)S(1)} %add_add_fusion.1), channel_id=1, source_target_pairs={{0,16},{1,17},{2,18},{3,19},{4,20},{5,21},{6,22},{7,23},{8,24},{9,... | collective-permute-start | bytes 3080 | tf_op jit(solution)/shard_map/ppermute | solution.py:343
  106.1 5.4 %collective-permute-start.15 = (f32[2,128]{1,0:T(2,128)S(1)}, f32[2,128]{1,0:T(2,128)S(1)}, u32[]{:S(2)}, u32[]{:S(2)}) collective-permute-start(f32[2,128]{1,0:T(2,128)S(1)} %add_add_fusion.1), channel_id=1, source_target_pairs={{0,8},{1,9},{2,10},{3,11},{4,12},{5,13},{6,14},{7,15},{8,0},{9,1},... | collective-permute-start | bytes 3080 | tf_op jit(solution)/shard_map/ppermute | solution.py:343
  (4 other events, 12.2 us)

commit v8 on v7

--- a/solution.py
+++ b/solution.py
@@ -36,13 +36,12 @@
 def heads_kernel(
     shard_ref, q_ref, g_ref, own_ref, near_ref, far_ref, q_gain_ref, k_gain_ref, _,
     dq_ref, d_own_ref, d_near_k_ref, d_near_v_ref, d_far_ref, gains_ref,
-    k_low, k_low_t, k_rms, values, q_low, q_rms, probs_all, d_scores_all,
+    k_low, k_low_t, k_rms, values, q_low, q_rms, key_total, value_total,
 ):
     rows = own_ref.shape[2]
     group = q_ref.shape[1] // rows
     lanes = TILE * group
     blocks = rows // TILE
-    tiles = WINDOW // TILE
     q_gain, k_gain = q_gain_ref[...], k_gain_ref[...]
     far_ok = jnp.where(shard_ref[0] >= 2, 1.0, 0.0)
     near_ok = jnp.where(shard_ref[0] >= 1, 1.0, 0.0)
@@ -77,7 +76,8 @@
     q_gain_sum = jnp.zeros_like(q_gain)
 
     for block in range(blocks):
-        span = slice(block * TILE, block * TILE + WINDOW + TILE)
+        start = block * TILE
+        span = slice(start, start + WINDOW + TILE)
         mine = slice(block * lanes, (block + 1) * lanes)
         scores = lax.dot_general(
             k_low[span, :], q_low[mine, :], NT, preferred_element_type=jnp.float32
@@ -108,48 +108,40 @@
         )
         offset = jnp.sum(probs * d_probs, axis=0, keepdims=True)
         d_scores = probs * (d_probs - offset)
-        for whole, held in ((probs, probs_all), (d_scores, d_scores_all)):
-            start = block * TILE
-            held[start : start + TILE, mine] = jnp.where(late, 0.0, whole[:TILE]).astype(
-                jnp.bfloat16
-            )
-            held[start + TILE : start + WINDOW, mine] = whole[TILE:].astype(jnp.bfloat16)
-            held[start + WINDOW : start + WINDOW + TILE, mine] = jnp.where(
-                late, whole[:TILE], 0.0
+        probs_low, d_scores_low = (
+            jnp.concatenate(
+                [jnp.where(late, 0.0, whole[:TILE]), whole[TILE:], jnp.where(late, whole[:TILE], 0.0)],
+                axis=0,
             ).astype(jnp.bfloat16)
+            for whole in (probs, d_scores)
+        )
         query_grad = score_scale * jnp.dot(
-            k_low_t[:, span], d_scores_all[span, mine], preferred_element_type=jnp.float32
+            k_low_t[:, span], d_scores_low, preferred_element_type=jnp.float32
         ).T
+        for held, left, right in (
+            (value_total, probs_low, g_ref[0, mine, :]),
+            (key_total, d_scores_low, q_low[mine, :]),
+        ):
+            part = jnp.dot(left, right, preferred_element_type=jnp.float32)
+            if block:
+                held[start : start + WINDOW, :] += part[:WINDOW]
+                held[start + WINDOW : start + WINDOW + TILE, :] = part[WINDOW:]
+            else:
+                held[span, :] = part
         raw = q_ref[0, mine, :].astype(jnp.float32)
         inverse_rms = q_rms[mine, :]
         q_gain_sum = q_gain_sum + jnp.sum(query_grad * (raw * inverse_rms), axis=0, keepdims=True)
         query_grad = norm_back(query_grad, raw, inverse_rms, q_gain).astype(dq_ref.dtype)
         dq_ref[start : start + TILE, 0, :, :] = query_grad.reshape(TILE, group, -1)
 
-    pieces = [(tile, tile + 1, 0, tile + 1) for tile in range(blocks - 1)]
-    pieces += [(blocks - 1, tiles + 1, 0, blocks)]
-    pieces += [(tiles + block, tiles + block + 1, block, blocks) for block in range(1, blocks)]
     k_gain_sum = jnp.zeros_like(k_gain)
-    for first, last, low, high in pieces:
-        meets = slice(low * lanes, high * lanes)
-        keys = slice(first * TILE, last * TILE)
-        value_grad = jnp.dot(
-            probs_all[keys, meets], g_ref[0, meets, :], preferred_element_type=jnp.float32
-        )
-        key_grad = score_scale * jnp.dot(
-            d_scores_all[keys, meets], q_low[meets, :], preferred_element_type=jnp.float32
-        )
-        for place, (ref, outs) in enumerate(zip(key_refs, grad_refs, strict=True)):
-            start = max(first * TILE, place * rows)
-            stop = min(last * TILE, (place + 1) * rows)
-            if start >= stop:
-                continue
-            inside = slice(start - place * rows, stop - place * rows)
-            here = slice(start - first * TILE, stop - first * TILE)
-            unit = ref[0, 0, inside, :].astype(jnp.float32) * k_rms[start:stop, :]
-            k_gain_sum = k_gain_sum + jnp.sum(key_grad[here] * unit, axis=0, keepdims=True)
-            outs[0][0, inside, :] = key_grad[here].astype(outs[0].dtype)
-            outs[1][0, inside, :] = value_grad[here].astype(outs[1].dtype)
+    for place, (ref, outs) in enumerate(zip(key_refs, grad_refs, strict=True)):
+        here = slice(place * rows, (place + 1) * rows)
+        key_grad = score_scale * key_total[here, :]
+        unit = ref[0, 0].astype(jnp.float32) * k_rms[here, :]
+        k_gain_sum = k_gain_sum + jnp.sum(key_grad * unit, axis=0, keepdims=True)
+        outs[0][0] = key_grad.astype(outs[0].dtype)
+        outs[1][0] = value_total[here, :].astype(outs[1].dtype)
     gains_ref[0:1, :] += q_gain_sum
     gains_ref[1:2, :] += k_gain_sum
 
@@ -293,8 +285,8 @@
             pltpu.VMEM((span, width), jnp.bfloat16),
             pltpu.VMEM((query_rows, width), jnp.bfloat16),
             pltpu.VMEM((query_rows, width), jnp.float32),
-            pltpu.VMEM((span, query_rows), jnp.bfloat16),
-            pltpu.VMEM((span, query_rows), jnp.bfloat16),
+            pltpu.VMEM((span, width), jnp.float32),
+            pltpu.VMEM((span, width), jnp.float32),
         ],
         input_output_aliases={8: 0},
         compiler_params=pltpu.CompilerParams(vmem_limit_bytes=22 * 1024 * 1024),

time: 112 us -> 112 us (level)
  transfers between devices with their start and end apart: 21 -> 21, of which waited for: 13 -> 12; matrix products, arithmetic and copies ran while one was open for 7% -> 7% of each run, Pallas kernels for 45% -> 44%
where the time goes in v8:
time: 112 us
  Pallas kernels  49.8 us (44%)
  waiting for transfers between devices  25.3 us (23%)
  starting transfers between devices  24.9 us (22%)
  local copies, waits for them, and re-layouts  10.5 us (9%)
    pallas_call x3, Pallas kernels, group_grads(): pl.pallas_call(heads_kernel, grid=(count,), in_specs=[pl.BlockSpec(memory...  41.9 us
    ppermute x2, waiting for transfers between devices, per_device(): fars = [lax.ppermute(own, 'seq', ahead) for own in owns]  12.5 us
    ppermute x7, starting transfers between devices, exchanged(): lax.ppermute(value, ('seq', 'head'), [(source, source ^ mask) for source...  10.4 us
    ppermute x2, starting transfers between devices, per_device(): fars = [lax.ppermute(own, 'seq', ahead) for own in owns]  8.4 us
    reshape x2, local copies, waits for them, and re-layouts, by_head(): split = array.reshape(rows, kv_dev, group, width)  4.62 us
    ppermute x2, waiting for transfers between devices, per_device(): kept.append((stays, lax.ppermute(relayed, 'seq', back)))  4.03 us
    ppermute x7, waiting for transfers between devices, exchanged(): lax.ppermute(value, ('seq', 'head'), [(source, source ^ mask) for source...  3.94 us
    ppermute x3, waiting for transfers between devices, per_device(): near = lax.ppermute(chosen, 'seq', swap)  3.07 us
  transfers between devices with their start and end apart: 21, of which 12 were waited for; matrix products, arithmetic and copies ran while one was open for 7% of the time, Pallas kernels for 44%

profile of v8, /device:TPU:0, one launch (start us, length us, event | category | flops | bytes accessed | tf_op | source)
XLA Modules:
  0.0 111.6 jit_solution(10893593641407617322)
XLA Ops:
  0.6 1.9 %copy_bitcast_fusion = (bf16[8,512,128]{2,1,0:T(8,128)(2,1)S(1)}, bf16[8,512,128]{2,1,0:T(8,128)(2,1)S(1)}) fusion(bf16[512,8,128]{2,1,0:T(8,128)(2,1)} %param.8, bf16[512,8,128]{2,1,0:T(8,128)(2,1)} %param.7), kind=kLoop, calls=%fused_computation.1 | loop fusion | bytes 4194304 | tf_op jit(solution)/shard_map/transpose | solution.py:362
  2.7 5.8 %collective-permute-start = (bf16[2,3,512,128]{3,2,1,0:T(8,128)(2,1)S(1)}, bf16[2,3,512,128]{3,2,1,0:T(8,128)(2,1)}, u32[]{:S(2)}, u32[]{:S(2)}) collective-permute-start(bf16[2,3,512,128]{3,2,1,0:T(8,128)(2,1)S(1)} %pad_maximum_fusion.1.own_ref), channel_id=1, source_target_pairs={{0,4},{2,6},{4,8},{6,10},{8,12},{10,14},{12,16},{14,18},{16,20},{1... | collective-permute-start | bytes 2359304 | tf_op jit(solution)/shard_map/ppermute | solution.py:364
  9.5 2.6 %collective-permute-start.1 = (bf16[2,5,512,128]{3,2,1,0:T(8,128)(2,1)S(1)}, bf16[2,5,512,128]{3,2,1,0:T(8,128)(2,1)S(1)}, u32[]{:S(2)}, u32[]{:S(2)}) collective-permute-start(bf16[2,5,512,128]{3,2,1,0:T(8,128)(2,1)S(1)} %pad_maximum_fusion.own_ref), channel_id=1, source_target_pairs={{0,4},{2,6},{4,8},{6,10},{8,12},{10,14},{12,16},{14,18},{16,20},{1... | collective-permute-start | bytes 3932168 | tf_op jit(solution)/shard_map/ppermute | solution.py:364
  12.2 3.2 %copy.16 = bf16[512,8,2,128]{3,2,0,1:T(2,128)(2,1)S(1)} copy(bf16[512,8,2,128]{3,2,1,0:T(2,128)(2,1)} %bitcast.50) | data formatting | bytes 4194304 | tf_op jit(solution)/shard_map/reshape | solution.py:356
  15.4 1.4 %copy.17 = bf16[512,8,2,128]{3,2,0,1:T(2,128)(2,1)S(1)} copy(bf16[512,8,2,128]{3,2,1,0:T(2,128)(2,1)S(1)} %bitcast.51) | data formatting | bytes 4194304 | tf_op jit(solution)/shard_map/reshape | solution.py:356
  16.8 8.7 %collective-permute-done.far_ref = bf16[2,3,512,128]{3,2,1,0:T(8,128)(2,1)} collective-permute-done((bf16[2,3,512,128]{3,2,1,0:T(8,128)(2,1)S(1)}, bf16[2,3,512,128]{3,2,1,0:T(8,128)(2,1)}, u32[]{:S(2)}, u32[]{:S(2)}) %collective-permute-start) | collective-permute-done | bytes 786464 | tf_op jit(solution)/shard_map/ppermute | solution.py:364
  25.5 2.0 %shard_map.101 = bf16[2,3,512,128]{3,2,1,0:T(8,128)(2,1)S(1)} custom-call(s32[1]{0:T(128)} %bitcast.shard_ref.in_ref, bf16[2,3,512,128]{3,2,1,0:T(8,128)(2,1)} %collective-permute-done.far_ref, bf16[2,3,512,128]{3,2,1,0:T(8,128)(2,1)S(1)} %pad_maximum_fusion.1.own_ref), custom_call_target="tpu_custom_call" | custom-call | flops 1000 | bytes 1000 | tf_op jit(solution)/shard_map/pallas_call | solution.py:204
  27.7 2.3 %collective-permute-done.2.near_ref = bf16[2,3,512,128]{3,2,1,0:T(8,128)(2,1)S(1)} collective-permute-done((bf16[2,3,512,128]{3,2,1,0:T(8,128)(2,1)S(1)}, bf16[2,3,512,128]{3,2,1,0:T(8,128)(2,1)S(1)}, u32[]{:S(2)}, u32[]{:S(2)}) %collective-permute-start.2) | collective-permute-done | bytes 786464 | tf_op jit(solution)/shard_map/ppermute | solution.py:397
  29.9 2.4 %broadcast_in_dim.3._ = bf16[512,8,2,128]{3,2,1,0:T(2,128)(2,1)} broadcast(bf16[]{:T(256)} %constant.7.clone.1), dimensions={} | broadcast | bytes 2097154 | tf_op jit(solution)/shard_map/broadcast_in_dim | solution.py:379
  32.3 15.9 %shard_map.102 = (bf16[512,8,2,128]{3,2,1,0:T(2,128)(2,1)}, bf16[2,3,512,128]{3,2,1,0:T(8,128)(2,1)S(1)}, bf16[3,512,128]{2,1,0:T(8,128)(2,1)S(1)}, bf16[3,512,1...) custom-call(s32[1]{0:T(128)} %bitcast.shard_ref.in_ref, ...), custom_call_target="tpu_custom_call", output_to_operand_aliasing={{0}: (8, {})} | custom-call | flops 1000 | bytes 1000 | tf_op jit(solution)/shard_map/pallas_call | solution.py:258
  48.7 3.7 %collective-permute-done.1.far_ref = bf16[2,5,512,128]{3,2,1,0:T(8,128)(2,1)S(1)} collective-permute-done((bf16[2,5,512,128]{3,2,1,0:T(8,128)(2,1)S(1)}, bf16[2,5,512,128]{3,2,1,0:T(8,128)(2,1)S(1)}, u32[]{:S(2)}, u32[]{:S(2)}) %collective-permute-start.1) | collective-permute-done | bytes 1310752 | tf_op jit(solution)/shard_map/ppermute | solution.py:364
  53.2 1.5 %collective-permute-start.10 = (bf16[2,3,512,128]{3,2,1,0:T(8,128)(2,1)S(1)}, bf16[2,3,512,128]{3,2,1,0:T(8,128)(2,1)S(1)}, u32[]{:S(2)}, u32[]{:S(2)}) collective-permute-start(bf16[2,3,512,128]{3,2,1,0:T(8,128)(2,1)S(1)} %shard_map.104), channel_id=1, source_target_pairs={{4,0},{6,2},{8,4},{10,6},{12,8},{14,10},{16,12},{18,14},{20,16},{2... | collective-permute-start | bytes 2359304 | tf_op jit(solution)/shard_map/ppermute | solution.py:405
  55.4 15.1 %shard_map.106 = (bf16[512,8,2,128]{3,2,1,0:T(2,128)(2,1)}, bf16[2,3,512,128]{3,2,1,0:T(8,128)(2,1)S(1)}, bf16[3,512,128]{2,1,0:T(8,128)(2,1)S(1)}, bf16[3,512,1...) custom-call(s32[1]{0:T(128)} %bitcast.shard_ref.in_ref, ...), custom_call_target="tpu_custom_call", output_to_operand_aliasing={{0}: (8, {})} | custom-call | flops 1000 | bytes 1000 | tf_op jit(solution)/shard_map/pallas_call | solution.py:258
  73.0 1.3 %collective-permute-start.8 = (bf16[2,3,512,128]{3,2,1,0:T(8,128)(2,1)S(1)}, bf16[2,3,512,128]{3,2,1,0:T(8,128)(2,1)S(1)}, u32[]{:S(2)}, u32[]{:S(2)}) collective-permute-start(bf16[2,3,512,128]{3,2,1,0:T(8,128)(2,1)S(1)} %shard_map.107), channel_id=1, source_target_pairs={{4,0},{6,2},{8,4},{10,6},{12,8},{14,10},{16,12},{18,14},{20,16},{2... | collective-permute-start | bytes 2359304 | tf_op jit(solution)/shard_map/ppermute | solution.py:405
  74.3 1.4 %collective-permute-done.10.returned = bf16[2,3,512,128]{3,2,1,0:T(8,128)(2,1)S(1)} collective-permute-done((bf16[2,3,512,128]{3,2,1,0:T(8,128)(2,1)S(1)}, bf16[2,3,512,128]{3,2,1,0:T(8,128)(2,1)S(1)}, u32[]{:S(2)}, u32[]{:S(2)}) %collective-permute-start.10) | collective-permute-done | bytes 786464 | tf_op jit(solution)/shard_map/ppermute | solution.py:405
  76.3 10.9 %shard_map.111 = (bf16[512,8,2,128]{3,2,1,0:T(2,128)(2,1)}, bf16[2,2,512,128]{3,2,1,0:T(8,128)(2,1)S(1)}, bf16[2,512,128]{2,1,0:T(8,128)(2,1)S(1)}, bf16[2,512,1...) custom-call(s32[1]{0:T(128)} %shard_map.110.shard_ref, ...), custom_call_target="tpu_custom_call", output_to_operand_aliasing={{0}: (8, {})} | custom-call | flops 1000 | bytes 1000 | tf_op jit(solution)/shard_map/pallas_call | solution.py:258
  87.7 2.6 %collective-permute-start.11 = (f32[2,128]{1,0:T(2,128)S(1)}, f32[2,128]{1,0:T(2,128)S(1)}, u32[]{:S(2)}, u32[]{:S(2)}) collective-permute-start(f32[2,128]{1,0:T(2,128)S(1)} %add_add_fusion.2.in_ref), channel_id=1, source_target_pairs={{0,4},{1,5},{2,6},{3,7},{4,0},{5,1},{6,2},{7,3},{8,12},{9,13},{10,... | collective-permute-start | bytes 3080 | tf_op jit(solution)/shard_map/ppermute | solution.py:335
  91.3 1.5 %collective-permute-start.20 = (bf16[2,2,512,128]{3,2,1,0:T(8,128)(2,1)S(1)}, bf16[2,2,512,128]{3,2,1,0:T(8,128)(2,1)S(1)}, u32[]{:S(2)}, u32[]{:S(2)}) collective-permute-start(bf16[2,2,512,128]{3,2,1,0:T(8,128)(2,1)S(1)} %shard_map.114), channel_id=1, source_target_pairs={{4,0},{6,2},{8,4},{10,6},{12,8},{14,10},{16,12},{18,14},{20,16},{2... | collective-permute-start | bytes 1572872 | tf_op jit(solution)/shard_map/ppermute | solution.py:426
  92.9 2.6 %collective-permute-done.8.returned = bf16[2,3,512,128]{3,2,1,0:T(8,128)(2,1)S(1)} collective-permute-done((bf16[2,3,512,128]{3,2,1,0:T(8,128)(2,1)S(1)}, bf16[2,3,512,128]{3,2,1,0:T(8,128)(2,1)S(1)}, u32[]{:S(2)}, u32[]{:S(2)}) %collective-permute-start.8) | collective-permute-done | bytes 786464 | tf_op jit(solution)/shard_map/ppermute | solution.py:405
  95.5 0.9 collective-permute-start.14
  98.6 2.2 %collective-permute-done.12 = f32[2,128]{1,0:T(2,128)S(1)} collective-permute-done((f32[2,128]{1,0:T(2,128)S(1)}, f32[2,128]{1,0:T(2,128)S(1)}, u32[]{:S(2)}, u32[]{:S(2)}) %collective-permute-start.12) | collective-permute-done | bytes 1056 | tf_op jit(solution)/shard_map/ppermute | solution.py:335
  100.7 4.9 %collective-permute-start.17 = (f32[2,128]{1,0:T(2,128)S(1)}, f32[2,128]{1,0:T(2,128)S(1)}, u32[]{:S(2)}, u32[]{:S(2)}) collective-permute-start(f32[2,128]{1,0:T(2,128)S(1)} %add_add_fusion.1), channel_id=1, source_target_pairs={{0,24},{1,25},{2,26},{3,27},{4,28},{5,29},{6,30},{7,31},{8,16},{9,... | collective-permute-start | bytes 3080 | tf_op jit(solution)/shard_map/ppermute | solution.py:335
  106.8 2.6 %shard_map.115 = (bf16[512,8,128]{2,1,0:T(8,128)(2,1)}, bf16[512,8,128]{2,1,0:T(8,128)(2,1)}) custom-call(s32[1]{0:T(128)} %bitcast.shard_ref.in_ref, bf16[2,2,512,128]{3,2,1,0:T(8,128)(2,1)S(1)} %get-tuple-element.85.own, bf16[2,2,512,128]{3,2,1,0:T(8,128)(2,1)S(1)} %collective-permute-done.20.returned, ...), custom_call_target="tpu_custom_call" | custom-call | tf_op jit(solution)/shard_map/pallas_call | solution.py:314
  109.4 1.7 %collective-permute-done.17 = f32[2,128]{1,0:T(2,128)S(1)} collective-permute-done((f32[2,128]{1,0:T(2,128)S(1)}, f32[2,128]{1,0:T(2,128)S(1)}, u32[]{:S(2)}, u32[]{:S(2)}) %collective-permute-start.17) | collective-permute-done | bytes 1056 | tf_op jit(solution)/shard_map/ppermute | solution.py:335
  (67 shorter events, 11.5 us)
Async XLA Ops:
  2.7 22.8 %collective-permute-start = (bf16[2,3,512,128]{3,2,1,0:T(8,128)(2,1)S(1)}, bf16[2,3,512,128]{3,2,1,0:T(8,128)(2,1)}, u32[]{:S(2)}, u32[]{:S(2)}) collective-permute-start(bf16[2,3,512,128]{3,2,1,0:T(8,128)(2,1)S(1)} %pad_maximum_fusion.1.own_ref), channel_id=1, source_target_pairs={{0,4},{2,6},{4,8},{6,10},{8,12},{10,14},{12,16},{14,18},{16,20},{1... | collective-permute-start | bytes 2359304 | tf_op jit(solution)/shard_map/ppermute | solution.py:364
  9.5 42.9 %collective-permute-start.1 = (bf16[2,5,512,128]{3,2,1,0:T(8,128)(2,1)S(1)}, bf16[2,5,512,128]{3,2,1,0:T(8,128)(2,1)S(1)}, u32[]{:S(2)}, u32[]{:S(2)}) collective-permute-start(bf16[2,5,512,128]{3,2,1,0:T(8,128)(2,1)S(1)} %pad_maximum_fusion.own_ref), channel_id=1, source_target_pairs={{0,4},{2,6},{4,8},{6,10},{8,12},{10,14},{12,16},{14,18},{16,20},{1... | collective-permute-start | bytes 3932168 | tf_op jit(solution)/shard_map/ppermute | solution.py:364
  25.5 6.8 %copy-start.2 = (f32[128]{0:T(128)S(1)}, f32[128]{0:T(128)}, u32[]{:S(2)}) copy-start(f32[128]{0:T(128)} %param.11) | copy-start | bytes 1540
  25.5 6.8 %copy-start.3 = (f32[128]{0:T(128)S(1)}, f32[128]{0:T(128)}, u32[]{:S(2)}) copy-start(f32[128]{0:T(128)} %param.10) | copy-start | bytes 1540
  27.6 2.4 %collective-permute-start.2 = (bf16[2,3,512,128]{3,2,1,0:T(8,128)(2,1)S(1)}, bf16[2,3,512,128]{3,2,1,0:T(8,128)(2,1)S(1)}, u32[]{:S(2)}, u32[]{:S(2)}) collective-permute-start(bf16[2,3,512,128]{3,2,1,0:T(8,128)(2,1)S(1)} %shard_map.101), channel_id=1, source_target_pairs={{0,2},{2,0},{4,6},{6,4},{8,10},{10,8},{12,14},{14,12},{16,18},{18,... | collective-permute-start | bytes 2359304 | tf_op jit(solution)/shard_map/ppermute | solution.py:397
  48.2 4.3 %collective-permute-start.3 = (bf16[3,512,128]{2,1,0:T(8,128)(2,1)S(1)}, bf16[3,512,128]{2,1,0:T(8,128)(2,1)S(1)}, u32[]{:S(2)}, u32[]{:S(2)}) collective-permute-start(bf16[3,512,128]{2,1,0:T(8,128)(2,1)S(1)} %get-tuple-element.60), channel_id=1, source_target_pairs={{0,2},{2,0},{4,6},{6,4},{8,10},{10,8},{12,14},{14,12},{16,18},{18,... | collective-permute-start | bytes 1179656 | tf_op jit(solution)/shard_map/ppermute | solution.py:370
  48.3 4.1 %collective-permute-start.4 = (bf16[3,512,128]{2,1,0:T(8,128)(2,1)S(1)}, bf16[3,512,128]{2,1,0:T(8,128)(2,1)S(1)}, u32[]{:S(2)}, u32[]{:S(2)}) collective-permute-start(bf16[3,512,128]{2,1,0:T(8,128)(2,1)S(1)} %get-tuple-element.61), channel_id=1, source_target_pairs={{0,2},{2,0},{4,6},{6,4},{8,10},{10,8},{12,14},{14,12},{16,18},{18,... | collective-permute-start | bytes 1179656 | tf_op jit(solution)/shard_map/ppermute | solution.py:370
  53.1 2.4 %collective-permute-start.5 = (bf16[2,3,512,128]{3,2,1,0:T(8,128)(2,1)S(1)}, bf16[2,3,512,128]{3,2,1,0:T(8,128)(2,1)S(1)}, u32[]{:S(2)}, u32[]{:S(2)}) collective-permute-start(bf16[2,3,512,128]{3,2,1,0:T(8,128)(2,1)S(1)} %shard_map.105), channel_id=1, source_target_pairs={{0,2},{2,0},{4,6},{6,4},{8,10},{10,8},{12,14},{14,12},{16,18},{18,... | collective-permute-start | bytes 2359304 | tf_op jit(solution)/shard_map/ppermute | solution.py:397
  53.2 22.6 %collective-permute-start.10 = (bf16[2,3,512,128]{3,2,1,0:T(8,128)(2,1)S(1)}, bf16[2,3,512,128]{3,2,1,0:T(8,128)(2,1)S(1)}, u32[]{:S(2)}, u32[]{:S(2)}) collective-permute-start(bf16[2,3,512,128]{3,2,1,0:T(8,128)(2,1)S(1)} %shard_map.104), channel_id=1, source_target_pairs={{4,0},{6,2},{8,4},{10,6},{12,8},{14,10},{16,12},{18,14},{20,16},{2... | collective-permute-start | bytes 2359304 | tf_op jit(solution)/shard_map/ppermute | solution.py:405
  70.5 1.7 %collective-permute-start.6 = (bf16[3,512,128]{2,1,0:T(8,128)(2,1)S(1)}, bf16[3,512,128]{2,1,0:T(8,128)(2,1)S(1)}, u32[]{:S(2)}, u32[]{:S(2)}) collective-permute-start(bf16[3,512,128]{2,1,0:T(8,128)(2,1)S(1)} %get-tuple-element.65), channel_id=1, source_target_pairs={{0,2},{2,0},{4,6},{6,4},{8,10},{10,8},{12,14},{14,12},{16,18},{18,... | collective-permute-start | bytes 1179656 | tf_op jit(solution)/shard_map/ppermute | solution.py:370
  70.6 2.2 %collective-permute-start.7 = (bf16[3,512,128]{2,1,0:T(8,128)(2,1)S(1)}, bf16[3,512,128]{2,1,0:T(8,128)(2,1)S(1)}, u32[]{:S(2)}, u32[]{:S(2)}) collective-permute-start(bf16[3,512,128]{2,1,0:T(8,128)(2,1)S(1)} %get-tuple-element.66), channel_id=1, source_target_pairs={{0,2},{2,0},{4,6},{6,4},{8,10},{10,8},{12,14},{14,12},{16,18},{18,... | collective-permute-start | bytes 1179656 | tf_op jit(solution)/shard_map/ppermute | solution.py:370
  71.2 4.5 %collective-permute-start.9 = (bf16[2,2,512,128]{3,2,1,0:T(8,128)(2,1)S(1)}, bf16[2,2,512,128]{3,2,1,0:T(8,128)(2,1)S(1)}, u32[]{:S(2)}, u32[]{:S(2)}) collective-permute-start(bf16[2,2,512,128]{3,2,1,0:T(8,128)(2,1)S(1)} %shard_map.108), channel_id=1, source_target_pairs={{0,2},{2,0},{4,6},{6,4},{8,10},{10,8},{12,14},{14,12},{16,18},{18,... | collective-permute-start | bytes 1572872 | tf_op jit(solution)/shard_map/ppermute | solution.py:397
  73.0 22.5 %collective-permute-start.8 = (bf16[2,3,512,128]{3,2,1,0:T(8,128)(2,1)S(1)}, bf16[2,3,512,128]{3,2,1,0:T(8,128)(2,1)S(1)}, u32[]{:S(2)}, u32[]{:S(2)}) collective-permute-start(bf16[2,3,512,128]{3,2,1,0:T(8,128)(2,1)S(1)} %shard_map.107), channel_id=1, source_target_pairs={{4,0},{6,2},{8,4},{10,6},{12,8},{14,10},{16,12},{18,14},{20,16},{2... | collective-permute-start | bytes 2359304 | tf_op jit(solution)/shard_map/ppermute | solution.py:405
  76.3 14.1 %copy-start.1 = (bf16[1,3,512,128]{3,2,1,0:T(8,128)(2,1)S(1)}, bf16[1,3,512,128]{3,2,1,0:T(8,128)(2,1)}, u32[]{:S(2)}) copy-start(bf16[1,3,512,128]{3,2,1,0:T(8,128)(2,1)} %copy-done) | copy-start | bytes 1179652
  87.2 3.9 %collective-permute-start.18 = (bf16[2,512,128]{2,1,0:T(8,128)(2,1)S(1)}, bf16[2,512,128]{2,1,0:T(8,128)(2,1)S(1)}, u32[]{:S(2)}, u32[]{:S(2)}) collective-permute-start(bf16[2,512,128]{2,1,0:T(8,128)(2,1)S(1)} %get-tuple-element.87), channel_id=1, source_target_pairs={{0,2},{2,0},{4,6},{6,4},{8,10},{10,8},{12,14},{14,12},{16,18},{18,... | collective-permute-start | bytes 786440 | tf_op jit(solution)/shard_map/ppermute | solution.py:370
  87.2 3.9 %collective-permute-start.19 = (bf16[2,512,128]{2,1,0:T(8,128)(2,1)S(1)}, bf16[2,512,128]{2,1,0:T(8,128)(2,1)S(1)}, u32[]{:S(2)}, u32[]{:S(2)}) collective-permute-start(bf16[2,512,128]{2,1,0:T(8,128)(2,1)S(1)} %get-tuple-element.88), channel_id=1, source_target_pairs={{0,2},{2,0},{4,6},{6,4},{8,10},{10,8},{12,14},{14,12},{16,18},{18,... | collective-permute-start | bytes 786440 | tf_op jit(solution)/shard_map/ppermute | solution.py:370
  87.7 7.8 %collective-permute-start.11 = (f32[2,128]{1,0:T(2,128)S(1)}, f32[2,128]{1,0:T(2,128)S(1)}, u32[]{:S(2)}, u32[]{:S(2)}) collective-permute-start(f32[2,128]{1,0:T(2,128)S(1)} %add_add_fusion.2.in_ref), channel_id=1, source_target_pairs={{0,4},{1,5},{2,6},{3,7},{4,0},{5,1},{6,2},{7,3},{8,12},{9,13},{10,... | collective-permute-start | bytes 3080 | tf_op jit(solution)/shard_map/ppermute | solution.py:335
  91.3 15.4 %collective-permute-start.20 = (bf16[2,2,512,128]{3,2,1,0:T(8,128)(2,1)S(1)}, bf16[2,2,512,128]{3,2,1,0:T(8,128)(2,1)S(1)}, u32[]{:S(2)}, u32[]{:S(2)}) collective-permute-start(bf16[2,2,512,128]{3,2,1,0:T(8,128)(2,1)S(1)} %shard_map.114), channel_id=1, source_target_pairs={{4,0},{6,2},{8,4},{10,6},{12,8},{14,10},{16,12},{18,14},{20,16},{2... | collective-permute-start | bytes 1572872 | tf_op jit(solution)/shard_map/ppermute | solution.py:426
  95.5 3.0 %collective-permute-start.14 = (f32[2,128]{1,0:T(2,128)S(1)}, f32[2,128]{1,0:T(2,128)S(1)}, u32[]{:S(2)}, u32[]{:S(2)}) collective-permute-start(f32[2,128]{1,0:T(2,128)S(1)} %add.29), channel_id=1, source_target_pairs={{0,3},{1,2},{2,1},{3,0},{4,7},{5,6},{6,5},{7,4},{8,11},{9,10},{10,... | collective-permute-start | bytes 3080 | tf_op jit(solution)/shard_map/ppermute | solution.py:335
  96.4 2.1 %collective-permute-start.13 = (f32[2,128]{1,0:T(2,128)S(1)}, f32[2,128]{1,0:T(2,128)S(1)}, u32[]{:S(2)}, u32[]{:S(2)}) collective-permute-start(f32[2,128]{1,0:T(2,128)S(1)} %add.29), channel_id=1, source_target_pairs={{0,2},{1,3},{2,0},{3,1},{4,6},{5,7},{6,4},{7,5},{8,10},{9,11},{10,... | collective-permute-start | bytes 3080 | tf_op jit(solution)/shard_map/ppermute | solution.py:335
  97.2 3.6 %collective-permute-start.12 = (f32[2,128]{1,0:T(2,128)S(1)}, f32[2,128]{1,0:T(2,128)S(1)}, u32[]{:S(2)}, u32[]{:S(2)}) collective-permute-start(f32[2,128]{1,0:T(2,128)S(1)} %add.29), channel_id=1, source_target_pairs={{0,1},{1,0},{2,3},{3,2},{4,5},{5,4},{6,7},{7,6},{8,9},{9,8},{10,11... | collective-permute-start | bytes 3080 | tf_op jit(solution)/shard_map/ppermute | solution.py:335
  100.7 10.3 %collective-permute-start.17 = (f32[2,128]{1,0:T(2,128)S(1)}, f32[2,128]{1,0:T(2,128)S(1)}, u32[]{:S(2)}, u32[]{:S(2)}) collective-permute-start(f32[2,128]{1,0:T(2,128)S(1)} %add_add_fusion.1), channel_id=1, source_target_pairs={{0,24},{1,25},{2,26},{3,27},{4,28},{5,29},{6,30},{7,31},{8,16},{9,... | collective-permute-start | bytes 3080 | tf_op jit(solution)/shard_map/ppermute | solution.py:335
  105.7 5.4 %collective-permute-start.16 = (f32[2,128]{1,0:T(2,128)S(1)}, f32[2,128]{1,0:T(2,128)S(1)}, u32[]{:S(2)}, u32[]{:S(2)}) collective-permute-start(f32[2,128]{1,0:T(2,128)S(1)} %add_add_fusion.1), channel_id=1, source_target_pairs={{0,16},{1,17},{2,18},{3,19},{4,20},{5,21},{6,22},{7,23},{8,24},{9,... | collective-permute-start | bytes 3080 | tf_op jit(solution)/shard_map/ppermute | solution.py:335
  105.7 5.4 %collective-permute-start.15 = (f32[2,128]{1,0:T(2,128)S(1)}, f32[2,128]{1,0:T(2,128)S(1)}, u32[]{:S(2)}, u32[]{:S(2)}) collective-permute-start(f32[2,128]{1,0:T(2,128)S(1)} %add_add_fusion.1), channel_id=1, source_target_pairs={{0,8},{1,9},{2,10},{3,11},{4,12},{5,13},{6,14},{7,15},{8,0},{9,1},... | collective-permute-start | bytes 3080 | tf_op jit(solution)/shard_map/ppermute | solution.py:335
  (4 other events, 12.2 us)

commit v9 on v8

--- a/solution.py
+++ b/solution.py
@@ -177,6 +177,31 @@
                 grad = norm_back(grad, raw, inverse_rms_of(raw), k_gain_ref[...])
             by_token[pl.ds(len(before) + head, rows, stride=heads), :] = grad
         out[...] = by_token[...].reshape(out.shape).astype(out.dtype)
+
+
+def pack_kernel(first, key_ref, value_ref, out_ref, by_token):
+    tokens, heads, _ = key_ref.shape
+    for kind, ref in enumerate((key_ref, value_ref)):
+        by_token[...] = ref[...].astype(jnp.float32).reshape(by_token.shape)
+        for head in range(out_ref.shape[1]):
+            part = by_token[pl.ds(first + head, tokens, stride=heads), :]
+            out_ref[kind, head] = part.astype(out_ref.dtype)
+
+
+def pack(key, value, first, count):
+    rows, heads, width = key.shape
+    tokens = rows // 2
+    part = pl.BlockSpec((tokens, heads, width), lambda step: (step, 0, 0))
+    return pl.pallas_call(
+        functools.partial(pack_kernel, first),
+        grid=(rows // tokens,),
+        in_specs=[part, part],
+        out_specs=pl.BlockSpec((2, count, tokens, width), lambda step: (0, 0, step, 0)),
+        out_shape=jax.ShapeDtypeStruct((2, count, rows, width), key.dtype),
+        scratch_shapes=[pltpu.VMEM((tokens * heads, width), jnp.float32)],
+        compiler_params=pltpu.CompilerParams(vmem_limit_bytes=12 * 1024 * 1024),
+        cost_estimate=LIGHT,
+    )(key, value)
 
 
 def choose_kernel(shard_ref, far_ref, own_ref, out_ref):
@@ -359,8 +384,7 @@
     sizes = group_sizes(kv_dev)
     starts = [sum(sizes[:place]) for place in range(len(sizes))]
     cuts = [(0, sizes[0])] + ([(sizes[0], kv_dev)] if len(sizes) > 1 else [])
-    by_kind = lax.optimization_barrier([jnp.transpose(kind, (1, 0, 2)) for kind in (key, value)])
-    owns = [jnp.stack([kind[low:high] for kind in by_kind]) for low, high in cuts]
+    owns = [pack(key, value, low, high - low) for low, high in cuts]
     fars = [lax.ppermute(own, "seq", ahead) for own in owns]
     queries, grads = by_head(query), by_head(grad_out)
     scalar = shard.astype(jnp.int32).reshape(1)
@@ -384,8 +408,6 @@
         if place < 2:
             own, far, start = owns[place], fars[place], cuts[place][0]
             if place:
-                far, gains[0] = lax.optimization_barrier((far, gains[0]))
-                gains[0] = later(far, gains[0])
                 far, gains[0], relayed = lax.optimization_barrier((far, gains[0], relayed))
             else:
                 far, queries, grads, *_ = lax.optimization_barrier(

time: 112 us -> 113 us (level)
  Pallas kernels: 49.8 us -> 51.1 us
    transpose x1 -> x0, local copies, waits for them, and re-layouts: 1.92 us -> none  [per_device(): jnp.transpose(kind, (1, 0, 2))]
    ppermute x2, waiting for transfers between devices: 12.5 us -> 10.7 us  [per_device(): fars = [lax.ppermute(own, 'seq', ahead) for own in owns]]
    ppermute x6, waiting for transfers between devices: 1.35 us -> 3.12 us  [split(): swapped = [lax.ppermute(half, 'seq', swap) for half in (d_near_k, d_near_v)]]
    unnamed x14 -> x10, local copies, waits for them, and re-layouts: 0.81 us -> 2.46 us
    pallas_call x0 -> x2, Pallas kernels: none -> 1.4 us  [pack(): pl.pallas_call(functools.partial(pack_kernel, first), grid=(rows // token...]
  transfers between devices with their start and end apart: 21 -> 21, of which waited for: 12 -> 15; matrix products, arithmetic and copies ran while one was open for 7% -> 6% of each run, Pallas kernels for 44% -> 44%
where the time goes in v9:
time: 113 us
  Pallas kernels  51.1 us (45%)
  waiting for transfers between devices  25.7 us (23%)
  starting transfers between devices  25.1 us (22%)
  local copies, waits for them, and re-layouts  10.1 us (9%)
    pallas_call x3, Pallas kernels, group_grads(): pl.pallas_call(heads_kernel, grid=(count,), in_specs=[pl.BlockSpec(memory...  41.8 us
    ppermute x2, waiting for transfers between devices, per_device(): fars = [lax.ppermute(own, 'seq', ahead) for own in owns]  10.7 us
    ppermute x7, starting transfers between devices, exchanged(): lax.ppermute(value, ('seq', 'head'), [(source, source ^ mask) for source...  10.5 us
    ppermute x2, starting transfers between devices, per_device(): fars = [lax.ppermute(own, 'seq', ahead) for own in owns]  8.42 us
    reshape x2, local copies, waits for them, and re-layouts, by_head(): split = array.reshape(rows, kv_dev, group, width)  4.62 us
    ppermute x7, waiting for transfers between devices, exchanged(): lax.ppermute(value, ('seq', 'head'), [(source, source ^ mask) for source...  4.46 us
    ppermute x2, waiting for transfers between devices, per_device(): kept.append((stays, lax.ppermute(relayed, 'seq', back)))  4 us
    ppermute x6, waiting for transfers between devices, split(): swapped = [lax.ppermute(half, 'seq', swap) for half in (d_near_k, d_near_v)]  3.12 us
  transfers between devices with their start and end apart: 21, of which 15 were waited for; matrix products, arithmetic and copies ran while one was open for 6% of the time, Pallas kernels for 44%

profile of v9, /device:TPU:0, one launch (start us, length us, event | category | flops | bytes accessed | tf_op | source)
XLA Modules:
  0.0 112.9 jit_solution(1727110253851421632)
XLA Ops:
  3.7 5.8 %collective-permute-start = (bf16[2,3,512,128]{3,2,1,0:T(8,128)(2,1)S(1)}, bf16[2,3,512,128]{3,2,1,0:T(8,128)(2,1)}, u32[]{:S(2)}, u32[]{:S(2)}) collective-permute-start(bf16[2,3,512,128]{3,2,1,0:T(8,128)(2,1)S(1)} %shard_map.101.own_ref), channel_id=1, source_target_pairs={{0,4},{2,6},{4,8},{6,10},{8,12},{10,14},{12,16},{14,18},{16,20},{1... | collective-permute-start | bytes 2359304 | tf_op jit(solution)/shard_map/ppermute | solution.py:388
  10.3 2.6 %collective-permute-start.1 = (bf16[2,5,512,128]{3,2,1,0:T(8,128)(2,1)S(1)}, bf16[2,5,512,128]{3,2,1,0:T(8,128)(2,1)S(1)}, u32[]{:S(2)}, u32[]{:S(2)}) collective-permute-start(bf16[2,5,512,128]{3,2,1,0:T(8,128)(2,1)S(1)} %shard_map.102.own_ref), channel_id=1, source_target_pairs={{0,4},{2,6},{4,8},{6,10},{8,12},{10,14},{12,16},{14,18},{16,20},{1... | collective-permute-start | bytes 3932168 | tf_op jit(solution)/shard_map/ppermute | solution.py:388
  12.9 3.2 %copy.14 = bf16[512,8,2,128]{3,2,0,1:T(2,128)(2,1)S(1)} copy(bf16[512,8,2,128]{3,2,1,0:T(2,128)(2,1)} %bitcast.36) | data formatting | bytes 4194304 | tf_op jit(solution)/shard_map/reshape | solution.py:381
  16.1 1.4 %copy.15 = bf16[512,8,2,128]{3,2,0,1:T(2,128)(2,1)S(1)} copy(bf16[512,8,2,128]{3,2,1,0:T(2,128)(2,1)S(1)} %bitcast.37) | data formatting | bytes 4194304 | tf_op jit(solution)/shard_map/reshape | solution.py:381
  17.6 8.9 %collective-permute-done.far_ref = bf16[2,3,512,128]{3,2,1,0:T(8,128)(2,1)} collective-permute-done((bf16[2,3,512,128]{3,2,1,0:T(8,128)(2,1)S(1)}, bf16[2,3,512,128]{3,2,1,0:T(8,128)(2,1)}, u32[]{:S(2)}, u32[]{:S(2)}) %collective-permute-start) | collective-permute-done | bytes 786464 | tf_op jit(solution)/shard_map/ppermute | solution.py:388
  26.5 2.0 %shard_map.103 = bf16[2,3,512,128]{3,2,1,0:T(8,128)(2,1)S(1)} custom-call(s32[1]{0:T(128)} %bitcast.shard_ref.in_ref, bf16[2,3,512,128]{3,2,1,0:T(8,128)(2,1)} %collective-permute-done.far_ref, bf16[2,3,512,128]{3,2,1,0:T(8,128)(2,1)S(1)} %shard_map.101.own_ref), custom_call_target="tpu_custom_call" | custom-call | flops 1000 | bytes 1000 | tf_op jit(solution)/shard_map/pallas_call | solution.py:229
  28.6 2.3 %collective-permute-done.2.near_ref = bf16[2,3,512,128]{3,2,1,0:T(8,128)(2,1)S(1)} collective-permute-done((bf16[2,3,512,128]{3,2,1,0:T(8,128)(2,1)S(1)}, bf16[2,3,512,128]{3,2,1,0:T(8,128)(2,1)S(1)}, u32[]{:S(2)}, u32[]{:S(2)}) %collective-permute-start.2) | collective-permute-done | bytes 786464 | tf_op jit(solution)/shard_map/ppermute | solution.py:419
  30.9 2.4 %broadcast_in_dim.3._ = bf16[512,8,2,128]{3,2,1,0:T(2,128)(2,1)} broadcast(bf16[]{:T(256)} %constant.7.clone.1), dimensions={} | broadcast | bytes 2097154 | tf_op jit(solution)/shard_map/broadcast_in_dim | solution.py:403
  33.3 15.9 %shard_map.104 = (bf16[512,8,2,128]{3,2,1,0:T(2,128)(2,1)}, bf16[2,3,512,128]{3,2,1,0:T(8,128)(2,1)S(1)}, bf16[3,512,128]{2,1,0:T(8,128)(2,1)S(1)}, bf16[3,512,1...) custom-call(s32[1]{0:T(128)} %bitcast.shard_ref.in_ref, ...), custom_call_target="tpu_custom_call", output_to_operand_aliasing={{0}: (8, {})} | custom-call | flops 1000 | bytes 1000 | tf_op jit(solution)/shard_map/pallas_call | solution.py:283
  51.7 1.7 %collective-permute-done.1.far_ref = bf16[2,5,512,128]{3,2,1,0:T(8,128)(2,1)S(1)} collective-permute-done((bf16[2,5,512,128]{3,2,1,0:T(8,128)(2,1)S(1)}, bf16[2,5,512,128]{3,2,1,0:T(8,128)(2,1)S(1)}, u32[]{:S(2)}, u32[]{:S(2)}) %collective-permute-start.1) | collective-permute-done | bytes 1310752 | tf_op jit(solution)/shard_map/ppermute | solution.py:388
  53.8 1.5 %collective-permute-start.10 = (bf16[2,3,512,128]{3,2,1,0:T(8,128)(2,1)S(1)}, bf16[2,3,512,128]{3,2,1,0:T(8,128)(2,1)S(1)}, u32[]{:S(2)}, u32[]{:S(2)}) collective-permute-start(bf16[2,3,512,128]{3,2,1,0:T(8,128)(2,1)S(1)} %shard_map.105), channel_id=1, source_target_pairs={{4,0},{6,2},{8,4},{10,6},{12,8},{14,10},{16,12},{18,14},{20,16},{2... | collective-permute-start | bytes 2359304 | tf_op jit(solution)/shard_map/ppermute | solution.py:427
  56.1 15.1 %shard_map.107 = (bf16[512,8,2,128]{3,2,1,0:T(2,128)(2,1)}, bf16[2,3,512,128]{3,2,1,0:T(8,128)(2,1)S(1)}, bf16[3,512,128]{2,1,0:T(8,128)(2,1)S(1)}, bf16[3,512,1...) custom-call(s32[1]{0:T(128)} %bitcast.shard_ref.in_ref, ...), custom_call_target="tpu_custom_call", output_to_operand_aliasing={{0}: (8, {})} | custom-call | flops 1000 | bytes 1000 | tf_op jit(solution)/shard_map/pallas_call | solution.py:283
  73.7 1.3 %collective-permute-start.8 = (bf16[2,3,512,128]{3,2,1,0:T(8,128)(2,1)S(1)}, bf16[2,3,512,128]{3,2,1,0:T(8,128)(2,1)S(1)}, u32[]{:S(2)}, u32[]{:S(2)}) collective-permute-start(bf16[2,3,512,128]{3,2,1,0:T(8,128)(2,1)S(1)} %shard_map.108), channel_id=1, source_target_pairs={{4,0},{6,2},{8,4},{10,6},{12,8},{14,10},{16,12},{18,14},{20,16},{2... | collective-permute-start | bytes 2359304 | tf_op jit(solution)/shard_map/ppermute | solution.py:427
  75.0 1.4 %collective-permute-done.10.returned = bf16[2,3,512,128]{3,2,1,0:T(8,128)(2,1)S(1)} collective-permute-done((bf16[2,3,512,128]{3,2,1,0:T(8,128)(2,1)S(1)}, bf16[2,3,512,128]{3,2,1,0:T(8,128)(2,1)S(1)}, u32[]{:S(2)}, u32[]{:S(2)}) %collective-permute-start.10) | collective-permute-done | bytes 786464 | tf_op jit(solution)/shard_map/ppermute | solution.py:427
  77.0 10.9 %shard_map.112 = (bf16[512,8,2,128]{3,2,1,0:T(2,128)(2,1)}, bf16[2,2,512,128]{3,2,1,0:T(8,128)(2,1)S(1)}, bf16[2,512,128]{2,1,0:T(8,128)(2,1)S(1)}, bf16[2,512,1...) custom-call(s32[1]{0:T(128)} %shard_map.111.shard_ref, ...), custom_call_target="tpu_custom_call", output_to_operand_aliasing={{0}: (8, {})} | custom-call | flops 1000 | bytes 1000 | tf_op jit(solution)/shard_map/pallas_call | solution.py:283
  88.4 2.7 %collective-permute-start.11 = (f32[2,128]{1,0:T(2,128)S(1)}, f32[2,128]{1,0:T(2,128)S(1)}, u32[]{:S(2)}, u32[]{:S(2)}) collective-permute-start(f32[2,128]{1,0:T(2,128)S(1)} %add_add_fusion.2.in_ref), channel_id=1, source_target_pairs={{0,4},{1,5},{2,6},{3,7},{4,0},{5,1},{6,2},{7,3},{8,12},{9,13},{10,... | collective-permute-start | bytes 3080 | tf_op jit(solution)/shard_map/ppermute | solution.py:360
  92.1 1.5 %collective-permute-start.20 = (bf16[2,2,512,128]{3,2,1,0:T(8,128)(2,1)S(1)}, bf16[2,2,512,128]{3,2,1,0:T(8,128)(2,1)S(1)}, u32[]{:S(2)}, u32[]{:S(2)}) collective-permute-start(bf16[2,2,512,128]{3,2,1,0:T(8,128)(2,1)S(1)} %shard_map.115), channel_id=1, source_target_pairs={{4,0},{6,2},{8,4},{10,6},{12,8},{14,10},{16,12},{18,14},{20,16},{2... | collective-permute-start | bytes 1572872 | tf_op jit(solution)/shard_map/ppermute | solution.py:448
  93.6 2.6 %collective-permute-done.8.returned = bf16[2,3,512,128]{3,2,1,0:T(8,128)(2,1)S(1)} collective-permute-done((bf16[2,3,512,128]{3,2,1,0:T(8,128)(2,1)S(1)}, bf16[2,3,512,128]{3,2,1,0:T(8,128)(2,1)S(1)}, u32[]{:S(2)}, u32[]{:S(2)}) %collective-permute-start.8) | collective-permute-done | bytes 786464 | tf_op jit(solution)/shard_map/ppermute | solution.py:427
  96.3 1.6 %collective-permute-start.14 = (f32[2,128]{1,0:T(2,128)S(1)}, f32[2,128]{1,0:T(2,128)S(1)}, u32[]{:S(2)}, u32[]{:S(2)}) collective-permute-start(f32[2,128]{1,0:T(2,128)S(1)} %add.29), channel_id=1, source_target_pairs={{0,3},{1,2},{2,1},{3,0},{4,7},{5,6},{6,5},{7,4},{8,11},{9,10},{10,... | collective-permute-start | bytes 3080 | tf_op jit(solution)/shard_map/ppermute | solution.py:360
  99.3 2.1 %collective-permute-done.12 = f32[2,128]{1,0:T(2,128)S(1)} collective-permute-done((f32[2,128]{1,0:T(2,128)S(1)}, f32[2,128]{1,0:T(2,128)S(1)}, u32[]{:S(2)}, u32[]{:S(2)}) %collective-permute-start.12) | collective-permute-done | bytes 1056 | tf_op jit(solution)/shard_map/ppermute | solution.py:360
  101.4 3.2 %collective-permute-start.15 = (f32[2,128]{1,0:T(2,128)S(1)}, f32[2,128]{1,0:T(2,128)S(1)}, u32[]{:S(2)}, u32[]{:S(2)}) collective-permute-start(f32[2,128]{1,0:T(2,128)S(1)} %add_add_fusion.1), channel_id=1, source_target_pairs={{0,8},{1,9},{2,10},{3,11},{4,12},{5,13},{6,14},{7,15},{8,0},{9,1},... | collective-permute-start | bytes 3080 | tf_op jit(solution)/shard_map/ppermute | solution.py:360
  104.6 2.3 %collective-permute-start.16 = (f32[2,128]{1,0:T(2,128)S(1)}, f32[2,128]{1,0:T(2,128)S(1)}, u32[]{:S(2)}, u32[]{:S(2)}) collective-permute-start(f32[2,128]{1,0:T(2,128)S(1)} %add_add_fusion.1), channel_id=1, source_target_pairs={{0,16},{1,17},{2,18},{3,19},{4,20},{5,21},{6,22},{7,23},{8,24},{9,... | collective-permute-start | bytes 3080 | tf_op jit(solution)/shard_map/ppermute | solution.py:360
  107.5 2.6 %shard_map.116 = (bf16[512,8,128]{2,1,0:T(8,128)(2,1)}, bf16[512,8,128]{2,1,0:T(8,128)(2,1)}) custom-call(s32[1]{0:T(128)} %bitcast.shard_ref.in_ref, bf16[2,2,512,128]{3,2,1,0:T(8,128)(2,1)S(1)} %get-tuple-element.77.own, bf16[2,2,512,128]{3,2,1,0:T(8,128)(2,1)S(1)} %collective-permute-done.20.returned, ...), custom_call_target="tpu_custom_call" | custom-call | tf_op jit(solution)/shard_map/pallas_call | solution.py:339
  110.7 1.6 %collective-permute-done.17 = f32[2,128]{1,0:T(2,128)S(1)} collective-permute-done((f32[2,128]{1,0:T(2,128)S(1)}, f32[2,128]{1,0:T(2,128)S(1)}, u32[]{:S(2)}, u32[]{:S(2)}) %collective-permute-start.17) | collective-permute-done | bytes 1056 | tf_op jit(solution)/shard_map/ppermute | solution.py:360
  (57 shorter events, 15.3 us)
Async XLA Ops:
  3.7 22.8 %collective-permute-start = (bf16[2,3,512,128]{3,2,1,0:T(8,128)(2,1)S(1)}, bf16[2,3,512,128]{3,2,1,0:T(8,128)(2,1)}, u32[]{:S(2)}, u32[]{:S(2)}) collective-permute-start(bf16[2,3,512,128]{3,2,1,0:T(8,128)(2,1)S(1)} %shard_map.101.own_ref), channel_id=1, source_target_pairs={{0,4},{2,6},{4,8},{6,10},{8,12},{10,14},{12,16},{14,18},{16,20},{1... | collective-permute-start | bytes 2359304 | tf_op jit(solution)/shard_map/ppermute | solution.py:388
  10.3 43.2 %collective-permute-start.1 = (bf16[2,5,512,128]{3,2,1,0:T(8,128)(2,1)S(1)}, bf16[2,5,512,128]{3,2,1,0:T(8,128)(2,1)S(1)}, u32[]{:S(2)}, u32[]{:S(2)}) collective-permute-start(bf16[2,5,512,128]{3,2,1,0:T(8,128)(2,1)S(1)} %shard_map.102.own_ref), channel_id=1, source_target_pairs={{0,4},{2,6},{4,8},{6,10},{8,12},{10,14},{12,16},{14,18},{16,20},{1... | collective-permute-start | bytes 3932168 | tf_op jit(solution)/shard_map/ppermute | solution.py:388
  12.9 3.2 %copy-start.4 = (bf16[512,16,128]{2,1,0:T(8,128)(2,1)S(1)}, bf16[512,16,128]{2,1,0:T(8,128)(2,1)}, u32[]{:S(2)}) copy-start(bf16[512,16,128]{2,1,0:T(8,128)(2,1)} %param.9) | copy-start | bytes 6291460
  26.5 6.8 %copy-start.2 = (f32[128]{0:T(128)S(1)}, f32[128]{0:T(128)}, u32[]{:S(2)}) copy-start(f32[128]{0:T(128)} %param.11) | copy-start | bytes 1540
  26.5 6.8 %copy-start.3 = (f32[128]{0:T(128)S(1)}, f32[128]{0:T(128)}, u32[]{:S(2)}) copy-start(f32[128]{0:T(128)} %param.10) | copy-start | bytes 1540
  28.5 2.4 %collective-permute-start.2 = (bf16[2,3,512,128]{3,2,1,0:T(8,128)(2,1)S(1)}, bf16[2,3,512,128]{3,2,1,0:T(8,128)(2,1)S(1)}, u32[]{:S(2)}, u32[]{:S(2)}) collective-permute-start(bf16[2,3,512,128]{3,2,1,0:T(8,128)(2,1)S(1)} %shard_map.103), channel_id=1, source_target_pairs={{0,2},{2,0},{4,6},{6,4},{8,10},{10,8},{12,14},{14,12},{16,18},{18,... | collective-permute-start | bytes 2359304 | tf_op jit(solution)/shard_map/ppermute | solution.py:419
  49.2 1.7 %collective-permute-start.3 = (bf16[3,512,128]{2,1,0:T(8,128)(2,1)S(1)}, bf16[3,512,128]{2,1,0:T(8,128)(2,1)S(1)}, u32[]{:S(2)}, u32[]{:S(2)}) collective-permute-start(bf16[3,512,128]{2,1,0:T(8,128)(2,1)S(1)} %get-tuple-element.52), channel_id=1, source_target_pairs={{0,2},{2,0},{4,6},{6,4},{8,10},{10,8},{12,14},{14,12},{16,18},{18,... | collective-permute-start | bytes 1179656 | tf_op jit(solution)/shard_map/ppermute | solution.py:394
  49.3 2.1 %collective-permute-start.4 = (bf16[3,512,128]{2,1,0:T(8,128)(2,1)S(1)}, bf16[3,512,128]{2,1,0:T(8,128)(2,1)S(1)}, u32[]{:S(2)}, u32[]{:S(2)}) collective-permute-start(bf16[3,512,128]{2,1,0:T(8,128)(2,1)S(1)} %get-tuple-element.53), channel_id=1, source_target_pairs={{0,2},{2,0},{4,6},{6,4},{8,10},{10,8},{12,14},{14,12},{16,18},{18,... | collective-permute-start | bytes 1179656 | tf_op jit(solution)/shard_map/ppermute | solution.py:394
  53.8 2.4 %collective-permute-start.5 = (bf16[2,3,512,128]{3,2,1,0:T(8,128)(2,1)S(1)}, bf16[2,3,512,128]{3,2,1,0:T(8,128)(2,1)S(1)}, u32[]{:S(2)}, u32[]{:S(2)}) collective-permute-start(bf16[2,3,512,128]{3,2,1,0:T(8,128)(2,1)S(1)} %shard_map.106), channel_id=1, source_target_pairs={{0,2},{2,0},{4,6},{6,4},{8,10},{10,8},{12,14},{14,12},{16,18},{18,... | collective-permute-start | bytes 2359304 | tf_op jit(solution)/shard_map/ppermute | solution.py:419
  53.8 22.6 %collective-permute-start.10 = (bf16[2,3,512,128]{3,2,1,0:T(8,128)(2,1)S(1)}, bf16[2,3,512,128]{3,2,1,0:T(8,128)(2,1)S(1)}, u32[]{:S(2)}, u32[]{:S(2)}) collective-permute-start(bf16[2,3,512,128]{3,2,1,0:T(8,128)(2,1)S(1)} %shard_map.105), channel_id=1, source_target_pairs={{4,0},{6,2},{8,4},{10,6},{12,8},{14,10},{16,12},{18,14},{20,16},{2... | collective-permute-start | bytes 2359304 | tf_op jit(solution)/shard_map/ppermute | solution.py:427
  71.2 1.7 %collective-permute-start.6 = (bf16[3,512,128]{2,1,0:T(8,128)(2,1)S(1)}, bf16[3,512,128]{2,1,0:T(8,128)(2,1)S(1)}, u32[]{:S(2)}, u32[]{:S(2)}) collective-permute-start(bf16[3,512,128]{2,1,0:T(8,128)(2,1)S(1)} %get-tuple-element.57), channel_id=1, source_target_pairs={{0,2},{2,0},{4,6},{6,4},{8,10},{10,8},{12,14},{14,12},{16,18},{18,... | collective-permute-start | bytes 1179656 | tf_op jit(solution)/shard_map/ppermute | solution.py:394
  71.3 2.2 %collective-permute-start.7 = (bf16[3,512,128]{2,1,0:T(8,128)(2,1)S(1)}, bf16[3,512,128]{2,1,0:T(8,128)(2,1)S(1)}, u32[]{:S(2)}, u32[]{:S(2)}) collective-permute-start(bf16[3,512,128]{2,1,0:T(8,128)(2,1)S(1)} %get-tuple-element.58), channel_id=1, source_target_pairs={{0,2},{2,0},{4,6},{6,4},{8,10},{10,8},{12,14},{14,12},{16,18},{18,... | collective-permute-start | bytes 1179656 | tf_op jit(solution)/shard_map/ppermute | solution.py:394
  71.9 4.5 %collective-permute-start.9 = (bf16[2,2,512,128]{3,2,1,0:T(8,128)(2,1)S(1)}, bf16[2,2,512,128]{3,2,1,0:T(8,128)(2,1)S(1)}, u32[]{:S(2)}, u32[]{:S(2)}) collective-permute-start(bf16[2,2,512,128]{3,2,1,0:T(8,128)(2,1)S(1)} %shard_map.109), channel_id=1, source_target_pairs={{0,2},{2,0},{4,6},{6,4},{8,10},{10,8},{12,14},{14,12},{16,18},{18,... | collective-permute-start | bytes 1572872 | tf_op jit(solution)/shard_map/ppermute | solution.py:419
  73.7 22.5 %collective-permute-start.8 = (bf16[2,3,512,128]{3,2,1,0:T(8,128)(2,1)S(1)}, bf16[2,3,512,128]{3,2,1,0:T(8,128)(2,1)S(1)}, u32[]{:S(2)}, u32[]{:S(2)}) collective-permute-start(bf16[2,3,512,128]{3,2,1,0:T(8,128)(2,1)S(1)} %shard_map.108), channel_id=1, source_target_pairs={{4,0},{6,2},{8,4},{10,6},{12,8},{14,10},{16,12},{18,14},{20,16},{2... | collective-permute-start | bytes 2359304 | tf_op jit(solution)/shard_map/ppermute | solution.py:427
  87.8 4.0 %collective-permute-start.18 = (bf16[2,512,128]{2,1,0:T(8,128)(2,1)S(1)}, bf16[2,512,128]{2,1,0:T(8,128)(2,1)S(1)}, u32[]{:S(2)}, u32[]{:S(2)}) collective-permute-start(bf16[2,512,128]{2,1,0:T(8,128)(2,1)S(1)} %get-tuple-element.79), channel_id=1, source_target_pairs={{0,2},{2,0},{4,6},{6,4},{8,10},{10,8},{12,14},{14,12},{16,18},{18,... | collective-permute-start | bytes 786440 | tf_op jit(solution)/shard_map/ppermute | solution.py:394
  87.8 4.0 %collective-permute-start.19 = (bf16[2,512,128]{2,1,0:T(8,128)(2,1)S(1)}, bf16[2,512,128]{2,1,0:T(8,128)(2,1)S(1)}, u32[]{:S(2)}, u32[]{:S(2)}) collective-permute-start(bf16[2,512,128]{2,1,0:T(8,128)(2,1)S(1)} %get-tuple-element.80), channel_id=1, source_target_pairs={{0,2},{2,0},{4,6},{6,4},{8,10},{10,8},{12,14},{14,12},{16,18},{18,... | collective-permute-start | bytes 786440 | tf_op jit(solution)/shard_map/ppermute | solution.py:394
  88.4 7.8 %collective-permute-start.11 = (f32[2,128]{1,0:T(2,128)S(1)}, f32[2,128]{1,0:T(2,128)S(1)}, u32[]{:S(2)}, u32[]{:S(2)}) collective-permute-start(f32[2,128]{1,0:T(2,128)S(1)} %add_add_fusion.2.in_ref), channel_id=1, source_target_pairs={{0,4},{1,5},{2,6},{3,7},{4,0},{5,1},{6,2},{7,3},{8,12},{9,13},{10,... | collective-permute-start | bytes 3080 | tf_op jit(solution)/shard_map/ppermute | solution.py:360
  92.1 15.4 %collective-permute-start.20 = (bf16[2,2,512,128]{3,2,1,0:T(8,128)(2,1)S(1)}, bf16[2,2,512,128]{3,2,1,0:T(8,128)(2,1)S(1)}, u32[]{:S(2)}, u32[]{:S(2)}) collective-permute-start(bf16[2,2,512,128]{3,2,1,0:T(8,128)(2,1)S(1)} %shard_map.115), channel_id=1, source_target_pairs={{4,0},{6,2},{8,4},{10,6},{12,8},{14,10},{16,12},{18,14},{20,16},{2... | collective-permute-start | bytes 1572872 | tf_op jit(solution)/shard_map/ppermute | solution.py:448
  96.2 3.0 %collective-permute-start.13 = (f32[2,128]{1,0:T(2,128)S(1)}, f32[2,128]{1,0:T(2,128)S(1)}, u32[]{:S(2)}, u32[]{:S(2)}) collective-permute-start(f32[2,128]{1,0:T(2,128)S(1)} %add.29), channel_id=1, source_target_pairs={{0,2},{1,3},{2,0},{3,1},{4,6},{5,7},{6,4},{7,5},{8,10},{9,11},{10,... | collective-permute-start | bytes 3080 | tf_op jit(solution)/shard_map/ppermute | solution.py:360
  96.3 3.1 %collective-permute-start.14 = (f32[2,128]{1,0:T(2,128)S(1)}, f32[2,128]{1,0:T(2,128)S(1)}, u32[]{:S(2)}, u32[]{:S(2)}) collective-permute-start(f32[2,128]{1,0:T(2,128)S(1)} %add.29), channel_id=1, source_target_pairs={{0,3},{1,2},{2,1},{3,0},{4,7},{5,6},{6,5},{7,4},{8,11},{9,10},{10,... | collective-permute-start | bytes 3080 | tf_op jit(solution)/shard_map/ppermute | solution.py:360
  97.9 3.6 %collective-permute-start.12 = (f32[2,128]{1,0:T(2,128)S(1)}, f32[2,128]{1,0:T(2,128)S(1)}, u32[]{:S(2)}, u32[]{:S(2)}) collective-permute-start(f32[2,128]{1,0:T(2,128)S(1)} %add.29), channel_id=1, source_target_pairs={{0,1},{1,0},{2,3},{3,2},{4,5},{5,4},{6,7},{7,6},{8,9},{9,8},{10,11... | collective-permute-start | bytes 3080 | tf_op jit(solution)/shard_map/ppermute | solution.py:360
  101.4 8.7 %collective-permute-start.15 = (f32[2,128]{1,0:T(2,128)S(1)}, f32[2,128]{1,0:T(2,128)S(1)}, u32[]{:S(2)}, u32[]{:S(2)}) collective-permute-start(f32[2,128]{1,0:T(2,128)S(1)} %add_add_fusion.1), channel_id=1, source_target_pairs={{0,8},{1,9},{2,10},{3,11},{4,12},{5,13},{6,14},{7,15},{8,0},{9,1},... | collective-permute-start | bytes 3080 | tf_op jit(solution)/shard_map/ppermute | solution.py:360
  104.6 6.1 %collective-permute-start.16 = (f32[2,128]{1,0:T(2,128)S(1)}, f32[2,128]{1,0:T(2,128)S(1)}, u32[]{:S(2)}, u32[]{:S(2)}) collective-permute-start(f32[2,128]{1,0:T(2,128)S(1)} %add_add_fusion.1), channel_id=1, source_target_pairs={{0,16},{1,17},{2,18},{3,19},{4,20},{5,21},{6,22},{7,23},{8,24},{9,... | collective-permute-start | bytes 3080 | tf_op jit(solution)/shard_map/ppermute | solution.py:360
  107.0 5.4 %collective-permute-start.17 = (f32[2,128]{1,0:T(2,128)S(1)}, f32[2,128]{1,0:T(2,128)S(1)}, u32[]{:S(2)}, u32[]{:S(2)}) collective-permute-start(f32[2,128]{1,0:T(2,128)S(1)} %add_add_fusion.1), channel_id=1, source_target_pairs={{0,24},{1,25},{2,26},{3,27},{4,28},{5,29},{6,30},{7,31},{8,16},{9,... | collective-permute-start | bytes 3080 | tf_op jit(solution)/shard_map/ppermute | solution.py:360
  (2 other events, 2.5 us)

commit v10 on v8

--- a/solution.py
+++ b/solution.py
@@ -384,8 +384,6 @@
         if place < 2:
             own, far, start = owns[place], fars[place], cuts[place][0]
             if place:
-                far, gains[0] = lax.optimization_barrier((far, gains[0]))
-                gains[0] = later(far, gains[0])
                 far, gains[0], relayed = lax.optimization_barrier((far, gains[0], relayed))
             else:
                 far, queries, grads, *_ = lax.optimization_barrier(

time: 112 us -> 112 us (level)
    ppermute x2, waiting for transfers between devices: 12.5 us -> 10.5 us  [per_device(): fars = [lax.ppermute(own, 'seq', ahead) for own in owns]]
    ppermute x6, waiting for transfers between devices: 1.35 us -> 3.11 us  [split(): swapped = [lax.ppermute(half, 'seq', swap) for half in (d_near_k, d_near_v)]]
  transfers between devices with their start and end apart: 21 -> 21, of which waited for: 12 -> 13; matrix products, arithmetic and copies ran while one was open for 7% -> 7% of each run, Pallas kernels for 44% -> 44%
where the time goes in v10:
time: 112 us; the launch traced here: 111 us
  Pallas kernels  49.8 us (44%)
  waiting for transfers between devices  25 us (22%)
  starting transfers between devices  24.9 us (22%)
  local copies, waits for them, and re-layouts  10.5 us (9%)
    pallas_call x3, Pallas kernels, group_grads(): pl.pallas_call(heads_kernel, grid=(count,), in_specs=[pl.BlockSpec(memory...  41.9 us
    ppermute x2, waiting for transfers between devices, per_device(): fars = [lax.ppermute(own, 'seq', ahead) for own in owns]  10.5 us
    ppermute x7, starting transfers between devices, exchanged(): lax.ppermute(value, ('seq', 'head'), [(source, source ^ mask) for source...  10.4 us
    ppermute x2, starting transfers between devices, per_device(): fars = [lax.ppermute(own, 'seq', ahead) for own in owns]  8.4 us
    reshape x2, local copies, waits for them, and re-layouts, by_head(): split = array.reshape(rows, kv_dev, group, width)  4.62 us
    ppermute x2, waiting for transfers between devices, per_device(): kept.append((stays, lax.ppermute(relayed, 'seq', back)))  4.01 us
    ppermute x7, waiting for transfers between devices, exchanged(): lax.ppermute(value, ('seq', 'head'), [(source, source ^ mask) for source...  3.92 us
    ppermute x6, waiting for transfers between devices, split(): swapped = [lax.ppermute(half, 'seq', swap) for half in (d_near_k, d_near_v)]  3.11 us
  transfers between devices with their start and end apart: 21, of which 13 were waited for; matrix products, arithmetic and copies ran while one was open for 7% of the time, Pallas kernels for 44%

profile of v10, /device:TPU:0, one launch (start us, length us, event | category | flops | bytes accessed | tf_op | source)
XLA Modules:
  0.0 111.3 jit_solution(5229244154170988542)
XLA Ops:
  0.6 1.9 %copy_bitcast_fusion = (bf16[8,512,128]{2,1,0:T(8,128)(2,1)S(1)}, bf16[8,512,128]{2,1,0:T(8,128)(2,1)S(1)}) fusion(bf16[512,8,128]{2,1,0:T(8,128)(2,1)} %param.8, bf16[512,8,128]{2,1,0:T(8,128)(2,1)} %param.7), kind=kLoop, calls=%fused_computation.1 | loop fusion | bytes 4194304 | tf_op jit(solution)/shard_map/transpose | solution.py:362
  2.7 5.8 %collective-permute-start = (bf16[2,3,512,128]{3,2,1,0:T(8,128)(2,1)S(1)}, bf16[2,3,512,128]{3,2,1,0:T(8,128)(2,1)}, u32[]{:S(2)}, u32[]{:S(2)}) collective-permute-start(bf16[2,3,512,128]{3,2,1,0:T(8,128)(2,1)S(1)} %pad_maximum_fusion.1.own_ref), channel_id=1, source_target_pairs={{0,4},{2,6},{4,8},{6,10},{8,12},{10,14},{12,16},{14,18},{16,20},{1... | collective-permute-start | bytes 2359304 | tf_op jit(solution)/shard_map/ppermute | solution.py:364
  9.5 2.6 %collective-permute-start.1 = (bf16[2,5,512,128]{3,2,1,0:T(8,128)(2,1)S(1)}, bf16[2,5,512,128]{3,2,1,0:T(8,128)(2,1)S(1)}, u32[]{:S(2)}, u32[]{:S(2)}) collective-permute-start(bf16[2,5,512,128]{3,2,1,0:T(8,128)(2,1)S(1)} %pad_maximum_fusion.own_ref), channel_id=1, source_target_pairs={{0,4},{2,6},{4,8},{6,10},{8,12},{10,14},{12,16},{14,18},{16,20},{1... | collective-permute-start | bytes 3932168 | tf_op jit(solution)/shard_map/ppermute | solution.py:364
  12.2 3.2 %copy.16 = bf16[512,8,2,128]{3,2,0,1:T(2,128)(2,1)S(1)} copy(bf16[512,8,2,128]{3,2,1,0:T(2,128)(2,1)} %bitcast.48) | data formatting | bytes 4194304 | tf_op jit(solution)/shard_map/reshape | solution.py:356
  15.4 1.4 %copy.17 = bf16[512,8,2,128]{3,2,0,1:T(2,128)(2,1)S(1)} copy(bf16[512,8,2,128]{3,2,1,0:T(2,128)(2,1)S(1)} %bitcast.49) | data formatting | bytes 4194304 | tf_op jit(solution)/shard_map/reshape | solution.py:356
  16.8 8.7 %collective-permute-done.far_ref = bf16[2,3,512,128]{3,2,1,0:T(8,128)(2,1)} collective-permute-done((bf16[2,3,512,128]{3,2,1,0:T(8,128)(2,1)S(1)}, bf16[2,3,512,128]{3,2,1,0:T(8,128)(2,1)}, u32[]{:S(2)}, u32[]{:S(2)}) %collective-permute-start) | collective-permute-done | bytes 786464 | tf_op jit(solution)/shard_map/ppermute | solution.py:364
  25.5 2.0 %shard_map.101 = bf16[2,3,512,128]{3,2,1,0:T(8,128)(2,1)S(1)} custom-call(s32[1]{0:T(128)} %bitcast.shard_ref.in_ref, bf16[2,3,512,128]{3,2,1,0:T(8,128)(2,1)} %collective-permute-done.far_ref, bf16[2,3,512,128]{3,2,1,0:T(8,128)(2,1)S(1)} %pad_maximum_fusion.1.own_ref), custom_call_target="tpu_custom_call" | custom-call | flops 1000 | bytes 1000 | tf_op jit(solution)/shard_map/pallas_call | solution.py:204
  27.7 2.3 %collective-permute-done.2.near_ref = bf16[2,3,512,128]{3,2,1,0:T(8,128)(2,1)S(1)} collective-permute-done((bf16[2,3,512,128]{3,2,1,0:T(8,128)(2,1)S(1)}, bf16[2,3,512,128]{3,2,1,0:T(8,128)(2,1)S(1)}, u32[]{:S(2)}, u32[]{:S(2)}) %collective-permute-start.2) | collective-permute-done | bytes 786464 | tf_op jit(solution)/shard_map/ppermute | solution.py:395
  29.9 2.4 %broadcast_in_dim.3._ = bf16[512,8,2,128]{3,2,1,0:T(2,128)(2,1)} broadcast(bf16[]{:T(256)} %constant.7.clone.1), dimensions={} | broadcast | bytes 2097154 | tf_op jit(solution)/shard_map/broadcast_in_dim | solution.py:379
  32.3 15.9 %shard_map.102 = (bf16[512,8,2,128]{3,2,1,0:T(2,128)(2,1)}, bf16[2,3,512,128]{3,2,1,0:T(8,128)(2,1)S(1)}, bf16[3,512,128]{2,1,0:T(8,128)(2,1)S(1)}, bf16[3,512,1...) custom-call(s32[1]{0:T(128)} %bitcast.shard_ref.in_ref, ...), custom_call_target="tpu_custom_call", output_to_operand_aliasing={{0}: (8, {})} | custom-call | flops 1000 | bytes 1000 | tf_op jit(solution)/shard_map/pallas_call | solution.py:258
  48.7 1.2 %collective-permute-done.3.swapped_k_ref.swapped_k = bf16[3,512,128]{2,1,0:T(8,128)(2,1)S(1)} collective-permute-done((bf16[3,512,128]{2,1,0:T(8,128)(2,1)S(1)}, bf16[3,512,128]{2,1,0:T(8,128)(2,1)S(1)}, u32[]{:S(2)}, u32[]{:S(2)}) %collective-permute-start.3) | collective-permute-done | bytes 393248 | tf_op jit(solution)/shard_map/ppermute | solution.py:370
  50.7 1.7 %collective-permute-done.1.far_ref = bf16[2,5,512,128]{3,2,1,0:T(8,128)(2,1)S(1)} collective-permute-done((bf16[2,5,512,128]{3,2,1,0:T(8,128)(2,1)S(1)}, bf16[2,5,512,128]{3,2,1,0:T(8,128)(2,1)S(1)}, u32[]{:S(2)}, u32[]{:S(2)}) %collective-permute-start.1) | collective-permute-done | bytes 1310752 | tf_op jit(solution)/shard_map/ppermute | solution.py:364
  52.9 1.5 %collective-permute-start.10 = (bf16[2,3,512,128]{3,2,1,0:T(8,128)(2,1)S(1)}, bf16[2,3,512,128]{3,2,1,0:T(8,128)(2,1)S(1)}, u32[]{:S(2)}, u32[]{:S(2)}) collective-permute-start(bf16[2,3,512,128]{3,2,1,0:T(8,128)(2,1)S(1)} %shard_map.103), channel_id=1, source_target_pairs={{4,0},{6,2},{8,4},{10,6},{12,8},{14,10},{16,12},{18,14},{20,16},{2... | collective-permute-start | bytes 2359304 | tf_op jit(solution)/shard_map/ppermute | solution.py:403
  55.2 15.1 %shard_map.105 = (bf16[512,8,2,128]{3,2,1,0:T(2,128)(2,1)}, bf16[2,3,512,128]{3,2,1,0:T(8,128)(2,1)S(1)}, bf16[3,512,128]{2,1,0:T(8,128)(2,1)S(1)}, bf16[3,512,1...) custom-call(s32[1]{0:T(128)} %bitcast.shard_ref.in_ref, ...), custom_call_target="tpu_custom_call", output_to_operand_aliasing={{0}: (8, {})} | custom-call | flops 1000 | bytes 1000 | tf_op jit(solution)/shard_map/pallas_call | solution.py:258
  72.7 1.3 %collective-permute-start.8 = (bf16[2,3,512,128]{3,2,1,0:T(8,128)(2,1)S(1)}, bf16[2,3,512,128]{3,2,1,0:T(8,128)(2,1)S(1)}, u32[]{:S(2)}, u32[]{:S(2)}) collective-permute-start(bf16[2,3,512,128]{3,2,1,0:T(8,128)(2,1)S(1)} %shard_map.106), channel_id=1, source_target_pairs={{4,0},{6,2},{8,4},{10,6},{12,8},{14,10},{16,12},{18,14},{20,16},{2... | collective-permute-start | bytes 2359304 | tf_op jit(solution)/shard_map/ppermute | solution.py:403
  74.0 1.4 %collective-permute-done.10.returned = bf16[2,3,512,128]{3,2,1,0:T(8,128)(2,1)S(1)} collective-permute-done((bf16[2,3,512,128]{3,2,1,0:T(8,128)(2,1)S(1)}, bf16[2,3,512,128]{3,2,1,0:T(8,128)(2,1)S(1)}, u32[]{:S(2)}, u32[]{:S(2)}) %collective-permute-start.10) | collective-permute-done | bytes 786464 | tf_op jit(solution)/shard_map/ppermute | solution.py:403
  76.0 11.0 %shard_map.110 = (bf16[512,8,2,128]{3,2,1,0:T(2,128)(2,1)}, bf16[2,2,512,128]{3,2,1,0:T(8,128)(2,1)S(1)}, bf16[2,512,128]{2,1,0:T(8,128)(2,1)S(1)}, bf16[2,512,1...) custom-call(s32[1]{0:T(128)} %shard_map.109.shard_ref, ...), custom_call_target="tpu_custom_call", output_to_operand_aliasing={{0}: (8, {})} | custom-call | flops 1000 | bytes 1000 | tf_op jit(solution)/shard_map/pallas_call | solution.py:258
  87.5 2.6 %collective-permute-start.11 = (f32[2,128]{1,0:T(2,128)S(1)}, f32[2,128]{1,0:T(2,128)S(1)}, u32[]{:S(2)}, u32[]{:S(2)}) collective-permute-start(f32[2,128]{1,0:T(2,128)S(1)} %add_add_fusion.2.in_ref), channel_id=1, source_target_pairs={{0,4},{1,5},{2,6},{3,7},{4,0},{5,1},{6,2},{7,3},{8,12},{9,13},{10,... | collective-permute-start | bytes 3080 | tf_op jit(solution)/shard_map/ppermute | solution.py:335
  91.1 1.5 %collective-permute-start.20 = (bf16[2,2,512,128]{3,2,1,0:T(8,128)(2,1)S(1)}, bf16[2,2,512,128]{3,2,1,0:T(8,128)(2,1)S(1)}, u32[]{:S(2)}, u32[]{:S(2)}) collective-permute-start(bf16[2,2,512,128]{3,2,1,0:T(8,128)(2,1)S(1)} %shard_map.113), channel_id=1, source_target_pairs={{4,0},{6,2},{8,4},{10,6},{12,8},{14,10},{16,12},{18,14},{20,16},{2... | collective-permute-start | bytes 1572872 | tf_op jit(solution)/shard_map/ppermute | solution.py:424
  92.6 2.6 %collective-permute-done.8.returned = bf16[2,3,512,128]{3,2,1,0:T(8,128)(2,1)S(1)} collective-permute-done((bf16[2,3,512,128]{3,2,1,0:T(8,128)(2,1)S(1)}, bf16[2,3,512,128]{3,2,1,0:T(8,128)(2,1)S(1)}, u32[]{:S(2)}, u32[]{:S(2)}) %collective-permute-start.8) | collective-permute-done | bytes 786464 | tf_op jit(solution)/shard_map/ppermute | solution.py:403
  98.3 2.2 %collective-permute-done.12 = f32[2,128]{1,0:T(2,128)S(1)} collective-permute-done((f32[2,128]{1,0:T(2,128)S(1)}, f32[2,128]{1,0:T(2,128)S(1)}, u32[]{:S(2)}, u32[]{:S(2)}) %collective-permute-start.12) | collective-permute-done | bytes 1056 | tf_op jit(solution)/shard_map/ppermute | solution.py:335
  100.5 4.9 %collective-permute-start.17 = (f32[2,128]{1,0:T(2,128)S(1)}, f32[2,128]{1,0:T(2,128)S(1)}, u32[]{:S(2)}, u32[]{:S(2)}) collective-permute-start(f32[2,128]{1,0:T(2,128)S(1)} %add_add_fusion.1), channel_id=1, source_target_pairs={{0,24},{1,25},{2,26},{3,27},{4,28},{5,29},{6,30},{7,31},{8,16},{9,... | collective-permute-start | bytes 3080 | tf_op jit(solution)/shard_map/ppermute | solution.py:335
  106.5 2.6 %shard_map.114 = (bf16[512,8,128]{2,1,0:T(8,128)(2,1)}, bf16[512,8,128]{2,1,0:T(8,128)(2,1)}) custom-call(s32[1]{0:T(128)} %bitcast.shard_ref.in_ref, bf16[2,2,512,128]{3,2,1,0:T(8,128)(2,1)S(1)} %get-tuple-element.81.own, bf16[2,2,512,128]{3,2,1,0:T(8,128)(2,1)S(1)} %collective-permute-done.20.returned, ...), custom_call_target="tpu_custom_call" | custom-call | tf_op jit(solution)/shard_map/pallas_call | solution.py:314
  109.1 1.7 %collective-permute-done.17 = f32[2,128]{1,0:T(2,128)S(1)} collective-permute-done((f32[2,128]{1,0:T(2,128)S(1)}, f32[2,128]{1,0:T(2,128)S(1)}, u32[]{:S(2)}, u32[]{:S(2)}) %collective-permute-start.17) | collective-permute-done | bytes 1056 | tf_op jit(solution)/shard_map/ppermute | solution.py:335
  (65 shorter events, 12.9 us)
Async XLA Ops:
  2.7 22.8 %collective-permute-start = (bf16[2,3,512,128]{3,2,1,0:T(8,128)(2,1)S(1)}, bf16[2,3,512,128]{3,2,1,0:T(8,128)(2,1)}, u32[]{:S(2)}, u32[]{:S(2)}) collective-permute-start(bf16[2,3,512,128]{3,2,1,0:T(8,128)(2,1)S(1)} %pad_maximum_fusion.1.own_ref), channel_id=1, source_target_pairs={{0,4},{2,6},{4,8},{6,10},{8,12},{10,14},{12,16},{14,18},{16,20},{1... | collective-permute-start | bytes 2359304 | tf_op jit(solution)/shard_map/ppermute | solution.py:364
  9.5 42.9 %collective-permute-start.1 = (bf16[2,5,512,128]{3,2,1,0:T(8,128)(2,1)S(1)}, bf16[2,5,512,128]{3,2,1,0:T(8,128)(2,1)S(1)}, u32[]{:S(2)}, u32[]{:S(2)}) collective-permute-start(bf16[2,5,512,128]{3,2,1,0:T(8,128)(2,1)S(1)} %pad_maximum_fusion.own_ref), channel_id=1, source_target_pairs={{0,4},{2,6},{4,8},{6,10},{8,12},{10,14},{12,16},{14,18},{16,20},{1... | collective-permute-start | bytes 3932168 | tf_op jit(solution)/shard_map/ppermute | solution.py:364
  25.5 6.8 %copy-start.2 = (f32[128]{0:T(128)S(1)}, f32[128]{0:T(128)}, u32[]{:S(2)}) copy-start(f32[128]{0:T(128)} %param.11) | copy-start | bytes 1540
  25.5 6.8 %copy-start.3 = (f32[128]{0:T(128)S(1)}, f32[128]{0:T(128)}, u32[]{:S(2)}) copy-start(f32[128]{0:T(128)} %param.10) | copy-start | bytes 1540
  27.6 2.4 %collective-permute-start.2 = (bf16[2,3,512,128]{3,2,1,0:T(8,128)(2,1)S(1)}, bf16[2,3,512,128]{3,2,1,0:T(8,128)(2,1)S(1)}, u32[]{:S(2)}, u32[]{:S(2)}) collective-permute-start(bf16[2,3,512,128]{3,2,1,0:T(8,128)(2,1)S(1)} %shard_map.101), channel_id=1, source_target_pairs={{0,2},{2,0},{4,6},{6,4},{8,10},{10,8},{12,14},{14,12},{16,18},{18,... | collective-permute-start | bytes 2359304 | tf_op jit(solution)/shard_map/ppermute | solution.py:395
  48.2 1.7 %collective-permute-start.3 = (bf16[3,512,128]{2,1,0:T(8,128)(2,1)S(1)}, bf16[3,512,128]{2,1,0:T(8,128)(2,1)S(1)}, u32[]{:S(2)}, u32[]{:S(2)}) collective-permute-start(bf16[3,512,128]{2,1,0:T(8,128)(2,1)S(1)} %get-tuple-element.56), channel_id=1, source_target_pairs={{0,2},{2,0},{4,6},{6,4},{8,10},{10,8},{12,14},{14,12},{16,18},{18,... | collective-permute-start | bytes 1179656 | tf_op jit(solution)/shard_map/ppermute | solution.py:370
  48.4 2.2 %collective-permute-start.4 = (bf16[3,512,128]{2,1,0:T(8,128)(2,1)S(1)}, bf16[3,512,128]{2,1,0:T(8,128)(2,1)S(1)}, u32[]{:S(2)}, u32[]{:S(2)}) collective-permute-start(bf16[3,512,128]{2,1,0:T(8,128)(2,1)S(1)} %get-tuple-element.57), channel_id=1, source_target_pairs={{0,2},{2,0},{4,6},{6,4},{8,10},{10,8},{12,14},{14,12},{16,18},{18,... | collective-permute-start | bytes 1179656 | tf_op jit(solution)/shard_map/ppermute | solution.py:370
  52.8 2.4 %collective-permute-start.5 = (bf16[2,3,512,128]{3,2,1,0:T(8,128)(2,1)S(1)}, bf16[2,3,512,128]{3,2,1,0:T(8,128)(2,1)S(1)}, u32[]{:S(2)}, u32[]{:S(2)}) collective-permute-start(bf16[2,3,512,128]{3,2,1,0:T(8,128)(2,1)S(1)} %shard_map.104), channel_id=1, source_target_pairs={{0,2},{2,0},{4,6},{6,4},{8,10},{10,8},{12,14},{14,12},{16,18},{18,... | collective-permute-start | bytes 2359304 | tf_op jit(solution)/shard_map/ppermute | solution.py:395
  52.9 22.6 %collective-permute-start.10 = (bf16[2,3,512,128]{3,2,1,0:T(8,128)(2,1)S(1)}, bf16[2,3,512,128]{3,2,1,0:T(8,128)(2,1)S(1)}, u32[]{:S(2)}, u32[]{:S(2)}) collective-permute-start(bf16[2,3,512,128]{3,2,1,0:T(8,128)(2,1)S(1)} %shard_map.103), channel_id=1, source_target_pairs={{4,0},{6,2},{8,4},{10,6},{12,8},{14,10},{16,12},{18,14},{20,16},{2... | collective-permute-start | bytes 2359304 | tf_op jit(solution)/shard_map/ppermute | solution.py:403
  70.2 1.7 %collective-permute-start.6 = (bf16[3,512,128]{2,1,0:T(8,128)(2,1)S(1)}, bf16[3,512,128]{2,1,0:T(8,128)(2,1)S(1)}, u32[]{:S(2)}, u32[]{:S(2)}) collective-permute-start(bf16[3,512,128]{2,1,0:T(8,128)(2,1)S(1)} %get-tuple-element.61), channel_id=1, source_target_pairs={{0,2},{2,0},{4,6},{6,4},{8,10},{10,8},{12,14},{14,12},{16,18},{18,... | collective-permute-start | bytes 1179656 | tf_op jit(solution)/shard_map/ppermute | solution.py:370
  70.4 2.1 %collective-permute-start.7 = (bf16[3,512,128]{2,1,0:T(8,128)(2,1)S(1)}, bf16[3,512,128]{2,1,0:T(8,128)(2,1)S(1)}, u32[]{:S(2)}, u32[]{:S(2)}) collective-permute-start(bf16[3,512,128]{2,1,0:T(8,128)(2,1)S(1)} %get-tuple-element.62), channel_id=1, source_target_pairs={{0,2},{2,0},{4,6},{6,4},{8,10},{10,8},{12,14},{14,12},{16,18},{18,... | collective-permute-start | bytes 1179656 | tf_op jit(solution)/shard_map/ppermute | solution.py:370
  71.0 4.5 %collective-permute-start.9 = (bf16[2,2,512,128]{3,2,1,0:T(8,128)(2,1)S(1)}, bf16[2,2,512,128]{3,2,1,0:T(8,128)(2,1)S(1)}, u32[]{:S(2)}, u32[]{:S(2)}) collective-permute-start(bf16[2,2,512,128]{3,2,1,0:T(8,128)(2,1)S(1)} %shard_map.107), channel_id=1, source_target_pairs={{0,2},{2,0},{4,6},{6,4},{8,10},{10,8},{12,14},{14,12},{16,18},{18,... | collective-permute-start | bytes 1572872 | tf_op jit(solution)/shard_map/ppermute | solution.py:395
  72.7 22.5 %collective-permute-start.8 = (bf16[2,3,512,128]{3,2,1,0:T(8,128)(2,1)S(1)}, bf16[2,3,512,128]{3,2,1,0:T(8,128)(2,1)S(1)}, u32[]{:S(2)}, u32[]{:S(2)}) collective-permute-start(bf16[2,3,512,128]{3,2,1,0:T(8,128)(2,1)S(1)} %shard_map.106), channel_id=1, source_target_pairs={{4,0},{6,2},{8,4},{10,6},{12,8},{14,10},{16,12},{18,14},{20,16},{2... | collective-permute-start | bytes 2359304 | tf_op jit(solution)/shard_map/ppermute | solution.py:403
  76.0 14.1 %copy-start.1 = (bf16[1,3,512,128]{3,2,1,0:T(8,128)(2,1)S(1)}, bf16[1,3,512,128]{3,2,1,0:T(8,128)(2,1)}, u32[]{:S(2)}) copy-start(bf16[1,3,512,128]{3,2,1,0:T(8,128)(2,1)} %copy-done) | copy-start | bytes 1179652
  87.0 3.9 %collective-permute-start.18 = (bf16[2,512,128]{2,1,0:T(8,128)(2,1)S(1)}, bf16[2,512,128]{2,1,0:T(8,128)(2,1)S(1)}, u32[]{:S(2)}, u32[]{:S(2)}) collective-permute-start(bf16[2,512,128]{2,1,0:T(8,128)(2,1)S(1)} %get-tuple-element.83), channel_id=1, source_target_pairs={{0,2},{2,0},{4,6},{6,4},{8,10},{10,8},{12,14},{14,12},{16,18},{18,... | collective-permute-start | bytes 786440 | tf_op jit(solution)/shard_map/ppermute | solution.py:370
  87.0 4.0 %collective-permute-start.19 = (bf16[2,512,128]{2,1,0:T(8,128)(2,1)S(1)}, bf16[2,512,128]{2,1,0:T(8,128)(2,1)S(1)}, u32[]{:S(2)}, u32[]{:S(2)}) collective-permute-start(bf16[2,512,128]{2,1,0:T(8,128)(2,1)S(1)} %get-tuple-element.84), channel_id=1, source_target_pairs={{0,2},{2,0},{4,6},{6,4},{8,10},{10,8},{12,14},{14,12},{16,18},{18,... | collective-permute-start | bytes 786440 | tf_op jit(solution)/shard_map/ppermute | solution.py:370
  87.5 7.8 %collective-permute-start.11 = (f32[2,128]{1,0:T(2,128)S(1)}, f32[2,128]{1,0:T(2,128)S(1)}, u32[]{:S(2)}, u32[]{:S(2)}) collective-permute-start(f32[2,128]{1,0:T(2,128)S(1)} %add_add_fusion.2.in_ref), channel_id=1, source_target_pairs={{0,4},{1,5},{2,6},{3,7},{4,0},{5,1},{6,2},{7,3},{8,12},{9,13},{10,... | collective-permute-start | bytes 3080 | tf_op jit(solution)/shard_map/ppermute | solution.py:335
  91.1 15.4 %collective-permute-start.20 = (bf16[2,2,512,128]{3,2,1,0:T(8,128)(2,1)S(1)}, bf16[2,2,512,128]{3,2,1,0:T(8,128)(2,1)S(1)}, u32[]{:S(2)}, u32[]{:S(2)}) collective-permute-start(bf16[2,2,512,128]{3,2,1,0:T(8,128)(2,1)S(1)} %shard_map.113), channel_id=1, source_target_pairs={{4,0},{6,2},{8,4},{10,6},{12,8},{14,10},{16,12},{18,14},{20,16},{2... | collective-permute-start | bytes 1572872 | tf_op jit(solution)/shard_map/ppermute | solution.py:424
  95.2 3.0 %collective-permute-start.14 = (f32[2,128]{1,0:T(2,128)S(1)}, f32[2,128]{1,0:T(2,128)S(1)}, u32[]{:S(2)}, u32[]{:S(2)}) collective-permute-start(f32[2,128]{1,0:T(2,128)S(1)} %add.29), channel_id=1, source_target_pairs={{0,3},{1,2},{2,1},{3,0},{4,7},{5,6},{6,5},{7,4},{8,11},{9,10},{10,... | collective-permute-start | bytes 3080 | tf_op jit(solution)/shard_map/ppermute | solution.py:335
  96.1 2.1 %collective-permute-start.13 = (f32[2,128]{1,0:T(2,128)S(1)}, f32[2,128]{1,0:T(2,128)S(1)}, u32[]{:S(2)}, u32[]{:S(2)}) collective-permute-start(f32[2,128]{1,0:T(2,128)S(1)} %add.29), channel_id=1, source_target_pairs={{0,2},{1,3},{2,0},{3,1},{4,6},{5,7},{6,4},{7,5},{8,10},{9,11},{10,... | collective-permute-start | bytes 3080 | tf_op jit(solution)/shard_map/ppermute | solution.py:335
  96.9 3.6 %collective-permute-start.12 = (f32[2,128]{1,0:T(2,128)S(1)}, f32[2,128]{1,0:T(2,128)S(1)}, u32[]{:S(2)}, u32[]{:S(2)}) collective-permute-start(f32[2,128]{1,0:T(2,128)S(1)} %add.29), channel_id=1, source_target_pairs={{0,1},{1,0},{2,3},{3,2},{4,5},{5,4},{6,7},{7,6},{8,9},{9,8},{10,11... | collective-permute-start | bytes 3080 | tf_op jit(solution)/shard_map/ppermute | solution.py:335
  100.5 10.3 %collective-permute-start.17 = (f32[2,128]{1,0:T(2,128)S(1)}, f32[2,128]{1,0:T(2,128)S(1)}, u32[]{:S(2)}, u32[]{:S(2)}) collective-permute-start(f32[2,128]{1,0:T(2,128)S(1)} %add_add_fusion.1), channel_id=1, source_target_pairs={{0,24},{1,25},{2,26},{3,27},{4,28},{5,29},{6,30},{7,31},{8,16},{9,... | collective-permute-start | bytes 3080 | tf_op jit(solution)/shard_map/ppermute | solution.py:335
  105.4 5.4 %collective-permute-start.16 = (f32[2,128]{1,0:T(2,128)S(1)}, f32[2,128]{1,0:T(2,128)S(1)}, u32[]{:S(2)}, u32[]{:S(2)}) collective-permute-start(f32[2,128]{1,0:T(2,128)S(1)} %add_add_fusion.1), channel_id=1, source_target_pairs={{0,16},{1,17},{2,18},{3,19},{4,20},{5,21},{6,22},{7,23},{8,24},{9,... | collective-permute-start | bytes 3080 | tf_op jit(solution)/shard_map/ppermute | solution.py:335
  105.4 5.4 %collective-permute-start.15 = (f32[2,128]{1,0:T(2,128)S(1)}, f32[2,128]{1,0:T(2,128)S(1)}, u32[]{:S(2)}, u32[]{:S(2)}) collective-permute-start(f32[2,128]{1,0:T(2,128)S(1)} %add_add_fusion.1), channel_id=1, source_target_pairs={{0,8},{1,9},{2,10},{3,11},{4,12},{5,13},{6,14},{7,15},{8,0},{9,1},... | collective-permute-start | bytes 3080 | tf_op jit(solution)/shard_map/ppermute | solution.py:335
  (4 other events, 12.2 us)

commit v11 on v10

--- a/solution.py
+++ b/solution.py
@@ -424,13 +424,13 @@
     returned = lax.ppermute(relayed, "seq", back)
     grad_query = grad_query.reshape(rows, heads, width)
     exchanges = [(0, head_bits), *((bit,) for bit in range(1, head_bits))]
-    exchanges += [(bit,) for bit in chips[1:-2]]
+    exchanges += [(bit,) for bit in chips[1:-1]]
     for bits in exchanges:
         gain_sum = summed(gain_sum, exchanged(gain_sum, *bits))
     gain_sum, grad_query, done = lax.optimization_barrier((gain_sum, grad_query, done))
     d_own, swapped, raw = stays
     grad_key, grad_value = finish(scalar, d_own, returned, swapped, raw, k_gain_2d, done)
-    others, grad_key = lax.optimization_barrier((exchanged(gain_sum, *chips[-2:]), grad_key))
+    others, grad_key = lax.optimization_barrier((exchanged(gain_sum, chips[-1]), grad_key))
     gain_sum = summed(gain_sum, others)
     return (grad_query, grad_key, grad_value, gain_sum[0], gain_sum[1])
 

time: 112 us -> 115 us (1.027)
  waiting for transfers between devices: 25 us -> 26.8 us
  starting transfers between devices: 24.9 us -> 26.3 us
    ppermute x7 -> x6, waiting for transfers between devices: 3.92 us -> 6.16 us  [exchanged(): lax.ppermute(value, ('seq', 'head'), [(source, source ^ mask) for source...]
    ppermute x7 -> x6, starting transfers between devices: 10.4 us -> 11.7 us  [exchanged(): lax.ppermute(value, ('seq', 'head'), [(source, source ^ mask) for source...]
  transfers between devices with their start and end apart: 21 -> 20, of which waited for: 13 -> 13; matrix products, arithmetic and copies ran while one was open for 7% -> 6% of each run, Pallas kernels for 44% -> 43%
where the time goes in v11:
time: 115 us; the launch traced here: 114 us
  Pallas kernels  49.8 us (43%)
  waiting for transfers between devices  26.8 us (23%)
  starting transfers between devices  26.3 us (23%)
  local copies, waits for them, and re-layouts  10.5 us (9%)
    pallas_call x3, Pallas kernels, group_grads(): pl.pallas_call(heads_kernel, grid=(count,), in_specs=[pl.BlockSpec(memory...  41.9 us
    ppermute x6, starting transfers between devices, exchanged(): lax.ppermute(value, ('seq', 'head'), [(source, source ^ mask) for source...  11.7 us
    ppermute x2, waiting for transfers between devices, per_device(): fars = [lax.ppermute(own, 'seq', ahead) for own in owns]  10.5 us
    ppermute x2, starting transfers between devices, per_device(): fars = [lax.ppermute(own, 'seq', ahead) for own in owns]  8.4 us
    ppermute x6, waiting for transfers between devices, exchanged(): lax.ppermute(value, ('seq', 'head'), [(source, source ^ mask) for source...  6.16 us
    reshape x2, local copies, waits for them, and re-layouts, by_head(): split = array.reshape(rows, kv_dev, group, width)  4.62 us
    ppermute x2, waiting for transfers between devices, per_device(): kept.append((stays, lax.ppermute(relayed, 'seq', back)))  4.01 us
    ppermute x6, waiting for transfers between devices, split(): swapped = [lax.ppermute(half, 'seq', swap) for half in (d_near_k, d_near_v)]  3.11 us
  transfers between devices with their start and end apart: 20, of which 13 were waited for; matrix products, arithmetic and copies ran while one was open for 6% of the time, Pallas kernels for 43%

profile of v11, /device:TPU:0, one launch (start us, length us, event | category | flops | bytes accessed | tf_op | source)
XLA Modules:
  0.0 114.5 jit_solution(2873490680620516217)
XLA Ops:
  0.6 1.9 %copy_bitcast_fusion = (bf16[8,512,128]{2,1,0:T(8,128)(2,1)S(1)}, bf16[8,512,128]{2,1,0:T(8,128)(2,1)S(1)}) fusion(bf16[512,8,128]{2,1,0:T(8,128)(2,1)} %param.8, bf16[512,8,128]{2,1,0:T(8,128)(2,1)} %param.7), kind=kLoop, calls=%fused_computation.1 | loop fusion | bytes 4194304 | tf_op jit(solution)/shard_map/transpose | solution.py:362
  2.7 5.8 %collective-permute-start = (bf16[2,3,512,128]{3,2,1,0:T(8,128)(2,1)S(1)}, bf16[2,3,512,128]{3,2,1,0:T(8,128)(2,1)}, u32[]{:S(2)}, u32[]{:S(2)}) collective-permute-start(bf16[2,3,512,128]{3,2,1,0:T(8,128)(2,1)S(1)} %pad_maximum_fusion.1.own_ref), channel_id=1, source_target_pairs={{0,4},{2,6},{4,8},{6,10},{8,12},{10,14},{12,16},{14,18},{16,20},{1... | collective-permute-start | bytes 2359304 | tf_op jit(solution)/shard_map/ppermute | solution.py:364
  9.5 2.6 %collective-permute-start.1 = (bf16[2,5,512,128]{3,2,1,0:T(8,128)(2,1)S(1)}, bf16[2,5,512,128]{3,2,1,0:T(8,128)(2,1)S(1)}, u32[]{:S(2)}, u32[]{:S(2)}) collective-permute-start(bf16[2,5,512,128]{3,2,1,0:T(8,128)(2,1)S(1)} %pad_maximum_fusion.own_ref), channel_id=1, source_target_pairs={{0,4},{2,6},{4,8},{6,10},{8,12},{10,14},{12,16},{14,18},{16,20},{1... | collective-permute-start | bytes 3932168 | tf_op jit(solution)/shard_map/ppermute | solution.py:364
  12.2 3.2 %copy.16 = bf16[512,8,2,128]{3,2,0,1:T(2,128)(2,1)S(1)} copy(bf16[512,8,2,128]{3,2,1,0:T(2,128)(2,1)} %bitcast.48) | data formatting | bytes 4194304 | tf_op jit(solution)/shard_map/reshape | solution.py:356
  15.4 1.4 %copy.17 = bf16[512,8,2,128]{3,2,0,1:T(2,128)(2,1)S(1)} copy(bf16[512,8,2,128]{3,2,1,0:T(2,128)(2,1)S(1)} %bitcast.49) | data formatting | bytes 4194304 | tf_op jit(solution)/shard_map/reshape | solution.py:356
  16.8 8.7 %collective-permute-done.far_ref = bf16[2,3,512,128]{3,2,1,0:T(8,128)(2,1)} collective-permute-done((bf16[2,3,512,128]{3,2,1,0:T(8,128)(2,1)S(1)}, bf16[2,3,512,128]{3,2,1,0:T(8,128)(2,1)}, u32[]{:S(2)}, u32[]{:S(2)}) %collective-permute-start) | collective-permute-done | bytes 786464 | tf_op jit(solution)/shard_map/ppermute | solution.py:364
  25.5 2.0 %shard_map.101 = bf16[2,3,512,128]{3,2,1,0:T(8,128)(2,1)S(1)} custom-call(s32[1]{0:T(128)} %bitcast.shard_ref.in_ref, bf16[2,3,512,128]{3,2,1,0:T(8,128)(2,1)} %collective-permute-done.far_ref, bf16[2,3,512,128]{3,2,1,0:T(8,128)(2,1)S(1)} %pad_maximum_fusion.1.own_ref), custom_call_target="tpu_custom_call" | custom-call | flops 1000 | bytes 1000 | tf_op jit(solution)/shard_map/pallas_call | solution.py:204
  27.7 2.3 %collective-permute-done.2.near_ref = bf16[2,3,512,128]{3,2,1,0:T(8,128)(2,1)S(1)} collective-permute-done((bf16[2,3,512,128]{3,2,1,0:T(8,128)(2,1)S(1)}, bf16[2,3,512,128]{3,2,1,0:T(8,128)(2,1)S(1)}, u32[]{:S(2)}, u32[]{:S(2)}) %collective-permute-start.2) | collective-permute-done | bytes 786464 | tf_op jit(solution)/shard_map/ppermute | solution.py:395
  29.9 2.4 %broadcast_in_dim.3._ = bf16[512,8,2,128]{3,2,1,0:T(2,128)(2,1)} broadcast(bf16[]{:T(256)} %constant.7.clone.1), dimensions={} | broadcast | bytes 2097154 | tf_op jit(solution)/shard_map/broadcast_in_dim | solution.py:379
  32.3 15.9 %shard_map.102 = (bf16[512,8,2,128]{3,2,1,0:T(2,128)(2,1)}, bf16[2,3,512,128]{3,2,1,0:T(8,128)(2,1)S(1)}, bf16[3,512,128]{2,1,0:T(8,128)(2,1)S(1)}, bf16[3,512,1...) custom-call(s32[1]{0:T(128)} %bitcast.shard_ref.in_ref, ...), custom_call_target="tpu_custom_call", output_to_operand_aliasing={{0}: (8, {})} | custom-call | flops 1000 | bytes 1000 | tf_op jit(solution)/shard_map/pallas_call | solution.py:258
  50.7 1.7 %collective-permute-done.1.far_ref = bf16[2,5,512,128]{3,2,1,0:T(8,128)(2,1)S(1)} collective-permute-done((bf16[2,5,512,128]{3,2,1,0:T(8,128)(2,1)S(1)}, bf16[2,5,512,128]{3,2,1,0:T(8,128)(2,1)S(1)}, u32[]{:S(2)}, u32[]{:S(2)}) %collective-permute-start.1) | collective-permute-done | bytes 1310752 | tf_op jit(solution)/shard_map/ppermute | solution.py:364
  52.9 1.5 %collective-permute-start.10 = (bf16[2,3,512,128]{3,2,1,0:T(8,128)(2,1)S(1)}, bf16[2,3,512,128]{3,2,1,0:T(8,128)(2,1)S(1)}, u32[]{:S(2)}, u32[]{:S(2)}) collective-permute-start(bf16[2,3,512,128]{3,2,1,0:T(8,128)(2,1)S(1)} %shard_map.103), channel_id=1, source_target_pairs={{4,0},{6,2},{8,4},{10,6},{12,8},{14,10},{16,12},{18,14},{20,16},{2... | collective-permute-start | bytes 2359304 | tf_op jit(solution)/shard_map/ppermute | solution.py:403
  55.2 15.1 %shard_map.105 = (bf16[512,8,2,128]{3,2,1,0:T(2,128)(2,1)}, bf16[2,3,512,128]{3,2,1,0:T(8,128)(2,1)S(1)}, bf16[3,512,128]{2,1,0:T(8,128)(2,1)S(1)}, bf16[3,512,1...) custom-call(s32[1]{0:T(128)} %bitcast.shard_ref.in_ref, ...), custom_call_target="tpu_custom_call", output_to_operand_aliasing={{0}: (8, {})} | custom-call | flops 1000 | bytes 1000 | tf_op jit(solution)/shard_map/pallas_call | solution.py:258
  72.7 1.3 %collective-permute-start.8 = (bf16[2,3,512,128]{3,2,1,0:T(8,128)(2,1)S(1)}, bf16[2,3,512,128]{3,2,1,0:T(8,128)(2,1)S(1)}, u32[]{:S(2)}, u32[]{:S(2)}) collective-permute-start(bf16[2,3,512,128]{3,2,1,0:T(8,128)(2,1)S(1)} %shard_map.106), channel_id=1, source_target_pairs={{4,0},{6,2},{8,4},{10,6},{12,8},{14,10},{16,12},{18,14},{20,16},{2... | collective-permute-start | bytes 2359304 | tf_op jit(solution)/shard_map/ppermute | solution.py:403
  74.0 1.4 %collective-permute-done.10.returned = bf16[2,3,512,128]{3,2,1,0:T(8,128)(2,1)S(1)} collective-permute-done((bf16[2,3,512,128]{3,2,1,0:T(8,128)(2,1)S(1)}, bf16[2,3,512,128]{3,2,1,0:T(8,128)(2,1)S(1)}, u32[]{:S(2)}, u32[]{:S(2)}) %collective-permute-start.10) | collective-permute-done | bytes 786464 | tf_op jit(solution)/shard_map/ppermute | solution.py:403
  76.0 11.0 %shard_map.110 = (bf16[512,8,2,128]{3,2,1,0:T(2,128)(2,1)}, bf16[2,2,512,128]{3,2,1,0:T(8,128)(2,1)S(1)}, bf16[2,512,128]{2,1,0:T(8,128)(2,1)S(1)}, bf16[2,512,1...) custom-call(s32[1]{0:T(128)} %shard_map.109.shard_ref, ...), custom_call_target="tpu_custom_call", output_to_operand_aliasing={{0}: (8, {})} | custom-call | flops 1000 | bytes 1000 | tf_op jit(solution)/shard_map/pallas_call | solution.py:258
  87.5 2.6 %collective-permute-start.11 = (f32[2,128]{1,0:T(2,128)S(1)}, f32[2,128]{1,0:T(2,128)S(1)}, u32[]{:S(2)}, u32[]{:S(2)}) collective-permute-start(f32[2,128]{1,0:T(2,128)S(1)} %add_add_fusion.1.in_ref), channel_id=1, source_target_pairs={{0,4},{1,5},{2,6},{3,7},{4,0},{5,1},{6,2},{7,3},{8,12},{9,13},{10,... | collective-permute-start | bytes 3080 | tf_op jit(solution)/shard_map/ppermute | solution.py:335
  91.1 1.5 %collective-permute-start.19 = (bf16[2,2,512,128]{3,2,1,0:T(8,128)(2,1)S(1)}, bf16[2,2,512,128]{3,2,1,0:T(8,128)(2,1)S(1)}, u32[]{:S(2)}, u32[]{:S(2)}) collective-permute-start(bf16[2,2,512,128]{3,2,1,0:T(8,128)(2,1)S(1)} %shard_map.113), channel_id=1, source_target_pairs={{4,0},{6,2},{8,4},{10,6},{12,8},{14,10},{16,12},{18,14},{20,16},{2... | collective-permute-start | bytes 1572872 | tf_op jit(solution)/shard_map/ppermute | solution.py:424
  92.6 2.6 %collective-permute-done.8.returned = bf16[2,3,512,128]{3,2,1,0:T(8,128)(2,1)S(1)} collective-permute-done((bf16[2,3,512,128]{3,2,1,0:T(8,128)(2,1)S(1)}, bf16[2,3,512,128]{3,2,1,0:T(8,128)(2,1)S(1)}, u32[]{:S(2)}, u32[]{:S(2)}) %collective-permute-start.8) | collective-permute-done | bytes 786464 | tf_op jit(solution)/shard_map/ppermute | solution.py:403
  98.3 2.2 %collective-permute-done.12 = f32[2,128]{1,0:T(2,128)S(1)} collective-permute-done((f32[2,128]{1,0:T(2,128)S(1)}, f32[2,128]{1,0:T(2,128)S(1)}, u32[]{:S(2)}, u32[]{:S(2)}) %collective-permute-start.12) | collective-permute-done | bytes 1056 | tf_op jit(solution)/shard_map/ppermute | solution.py:335
  100.5 3.2 %collective-permute-start.15 = (f32[2,128]{1,0:T(2,128)S(1)}, f32[2,128]{1,0:T(2,128)S(1)}, u32[]{:S(2)}, u32[]{:S(2)}) collective-permute-start(f32[2,128]{1,0:T(2,128)S(1)} %add_add_fusion), channel_id=1, source_target_pairs={{0,8},{1,9},{2,10},{3,11},{4,12},{5,13},{6,14},{7,15},{8,0},{9,1},... | collective-permute-start | bytes 3080 | tf_op jit(solution)/shard_map/ppermute | solution.py:335
  104.5 3.1 %collective-permute-done.15 = f32[2,128]{1,0:T(2,128)S(1)} collective-permute-done((f32[2,128]{1,0:T(2,128)S(1)}, f32[2,128]{1,0:T(2,128)S(1)}, u32[]{:S(2)}, u32[]{:S(2)}) %collective-permute-start.15) | collective-permute-done | bytes 1056 | tf_op jit(solution)/shard_map/ppermute | solution.py:335
  107.6 3.7 %collective-permute-start.16 = (f32[2,128]{1,0:T(2,128)S(1)}, f32[2,128]{1,0:T(2,128)S(1)}, u32[]{:S(2)}, u32[]{:S(2)}) collective-permute-start(f32[2,128]{1,0:T(2,128)S(1)} %add.30), channel_id=1, source_target_pairs={{0,16},{1,17},{2,18},{3,19},{4,20},{5,21},{6,22},{7,23},{8,24},{9,... | collective-permute-start | bytes 3080 | tf_op jit(solution)/shard_map/ppermute | solution.py:335
  111.4 2.6 %shard_map.114 = (bf16[512,8,128]{2,1,0:T(8,128)(2,1)}, bf16[512,8,128]{2,1,0:T(8,128)(2,1)}) custom-call(s32[1]{0:T(128)} %bitcast.shard_ref.in_ref, bf16[2,2,512,128]{3,2,1,0:T(8,128)(2,1)S(1)} %get-tuple-element.79.own, bf16[2,2,512,128]{3,2,1,0:T(8,128)(2,1)S(1)} %collective-permute-done.19.returned, ...), custom_call_target="tpu_custom_call" | custom-call | tf_op jit(solution)/shard_map/pallas_call | solution.py:314
  (64 shorter events, 13.9 us)
Async XLA Ops:
  2.7 22.8 %collective-permute-start = (bf16[2,3,512,128]{3,2,1,0:T(8,128)(2,1)S(1)}, bf16[2,3,512,128]{3,2,1,0:T(8,128)(2,1)}, u32[]{:S(2)}, u32[]{:S(2)}) collective-permute-start(bf16[2,3,512,128]{3,2,1,0:T(8,128)(2,1)S(1)} %pad_maximum_fusion.1.own_ref), channel_id=1, source_target_pairs={{0,4},{2,6},{4,8},{6,10},{8,12},{10,14},{12,16},{14,18},{16,20},{1... | collective-permute-start | bytes 2359304 | tf_op jit(solution)/shard_map/ppermute | solution.py:364
  9.5 43.0 %collective-permute-start.1 = (bf16[2,5,512,128]{3,2,1,0:T(8,128)(2,1)S(1)}, bf16[2,5,512,128]{3,2,1,0:T(8,128)(2,1)S(1)}, u32[]{:S(2)}, u32[]{:S(2)}) collective-permute-start(bf16[2,5,512,128]{3,2,1,0:T(8,128)(2,1)S(1)} %pad_maximum_fusion.own_ref), channel_id=1, source_target_pairs={{0,4},{2,6},{4,8},{6,10},{8,12},{10,14},{12,16},{14,18},{16,20},{1... | collective-permute-start | bytes 3932168 | tf_op jit(solution)/shard_map/ppermute | solution.py:364
  25.5 6.8 %copy-start.2 = (f32[128]{0:T(128)S(1)}, f32[128]{0:T(128)}, u32[]{:S(2)}) copy-start(f32[128]{0:T(128)} %param.11) | copy-start | bytes 1540
  25.5 6.8 %copy-start.3 = (f32[128]{0:T(128)S(1)}, f32[128]{0:T(128)}, u32[]{:S(2)}) copy-start(f32[128]{0:T(128)} %param.10) | copy-start | bytes 1540
  27.6 2.4 %collective-permute-start.2 = (bf16[2,3,512,128]{3,2,1,0:T(8,128)(2,1)S(1)}, bf16[2,3,512,128]{3,2,1,0:T(8,128)(2,1)S(1)}, u32[]{:S(2)}, u32[]{:S(2)}) collective-permute-start(bf16[2,3,512,128]{3,2,1,0:T(8,128)(2,1)S(1)} %shard_map.101), channel_id=1, source_target_pairs={{0,2},{2,0},{4,6},{6,4},{8,10},{10,8},{12,14},{14,12},{16,18},{18,... | collective-permute-start | bytes 2359304 | tf_op jit(solution)/shard_map/ppermute | solution.py:395
  48.2 1.7 %collective-permute-start.3 = (bf16[3,512,128]{2,1,0:T(8,128)(2,1)S(1)}, bf16[3,512,128]{2,1,0:T(8,128)(2,1)S(1)}, u32[]{:S(2)}, u32[]{:S(2)}) collective-permute-start(bf16[3,512,128]{2,1,0:T(8,128)(2,1)S(1)} %get-tuple-element.54), channel_id=1, source_target_pairs={{0,2},{2,0},{4,6},{6,4},{8,10},{10,8},{12,14},{14,12},{16,18},{18,... | collective-permute-start | bytes 1179656 | tf_op jit(solution)/shard_map/ppermute | solution.py:370
  48.4 2.2 %collective-permute-start.4 = (bf16[3,512,128]{2,1,0:T(8,128)(2,1)S(1)}, bf16[3,512,128]{2,1,0:T(8,128)(2,1)S(1)}, u32[]{:S(2)}, u32[]{:S(2)}) collective-permute-start(bf16[3,512,128]{2,1,0:T(8,128)(2,1)S(1)} %get-tuple-element.55), channel_id=1, source_target_pairs={{0,2},{2,0},{4,6},{6,4},{8,10},{10,8},{12,14},{14,12},{16,18},{18,... | collective-permute-start | bytes 1179656 | tf_op jit(solution)/shard_map/ppermute | solution.py:370
  52.8 2.4 %collective-permute-start.5 = (bf16[2,3,512,128]{3,2,1,0:T(8,128)(2,1)S(1)}, bf16[2,3,512,128]{3,2,1,0:T(8,128)(2,1)S(1)}, u32[]{:S(2)}, u32[]{:S(2)}) collective-permute-start(bf16[2,3,512,128]{3,2,1,0:T(8,128)(2,1)S(1)} %shard_map.104), channel_id=1, source_target_pairs={{0,2},{2,0},{4,6},{6,4},{8,10},{10,8},{12,14},{14,12},{16,18},{18,... | collective-permute-start | bytes 2359304 | tf_op jit(solution)/shard_map/ppermute | solution.py:395
  52.9 22.6 %collective-permute-start.10 = (bf16[2,3,512,128]{3,2,1,0:T(8,128)(2,1)S(1)}, bf16[2,3,512,128]{3,2,1,0:T(8,128)(2,1)S(1)}, u32[]{:S(2)}, u32[]{:S(2)}) collective-permute-start(bf16[2,3,512,128]{3,2,1,0:T(8,128)(2,1)S(1)} %shard_map.103), channel_id=1, source_target_pairs={{4,0},{6,2},{8,4},{10,6},{12,8},{14,10},{16,12},{18,14},{20,16},{2... | collective-permute-start | bytes 2359304 | tf_op jit(solution)/shard_map/ppermute | solution.py:403
  70.2 1.7 %collective-permute-start.6 = (bf16[3,512,128]{2,1,0:T(8,128)(2,1)S(1)}, bf16[3,512,128]{2,1,0:T(8,128)(2,1)S(1)}, u32[]{:S(2)}, u32[]{:S(2)}) collective-permute-start(bf16[3,512,128]{2,1,0:T(8,128)(2,1)S(1)} %get-tuple-element.59), channel_id=1, source_target_pairs={{0,2},{2,0},{4,6},{6,4},{8,10},{10,8},{12,14},{14,12},{16,18},{18,... | collective-permute-start | bytes 1179656 | tf_op jit(solution)/shard_map/ppermute | solution.py:370
  70.4 2.1 %collective-permute-start.7 = (bf16[3,512,128]{2,1,0:T(8,128)(2,1)S(1)}, bf16[3,512,128]{2,1,0:T(8,128)(2,1)S(1)}, u32[]{:S(2)}, u32[]{:S(2)}) collective-permute-start(bf16[3,512,128]{2,1,0:T(8,128)(2,1)S(1)} %get-tuple-element.60), channel_id=1, source_target_pairs={{0,2},{2,0},{4,6},{6,4},{8,10},{10,8},{12,14},{14,12},{16,18},{18,... | collective-permute-start | bytes 1179656 | tf_op jit(solution)/shard_map/ppermute | solution.py:370
  71.0 4.5 %collective-permute-start.9 = (bf16[2,2,512,128]{3,2,1,0:T(8,128)(2,1)S(1)}, bf16[2,2,512,128]{3,2,1,0:T(8,128)(2,1)S(1)}, u32[]{:S(2)}, u32[]{:S(2)}) collective-permute-start(bf16[2,2,512,128]{3,2,1,0:T(8,128)(2,1)S(1)} %shard_map.107), channel_id=1, source_target_pairs={{0,2},{2,0},{4,6},{6,4},{8,10},{10,8},{12,14},{14,12},{16,18},{18,... | collective-permute-start | bytes 1572872 | tf_op jit(solution)/shard_map/ppermute | solution.py:395
  72.7 22.5 %collective-permute-start.8 = (bf16[2,3,512,128]{3,2,1,0:T(8,128)(2,1)S(1)}, bf16[2,3,512,128]{3,2,1,0:T(8,128)(2,1)S(1)}, u32[]{:S(2)}, u32[]{:S(2)}) collective-permute-start(bf16[2,3,512,128]{3,2,1,0:T(8,128)(2,1)S(1)} %shard_map.106), channel_id=1, source_target_pairs={{4,0},{6,2},{8,4},{10,6},{12,8},{14,10},{16,12},{18,14},{20,16},{2... | collective-permute-start | bytes 2359304 | tf_op jit(solution)/shard_map/ppermute | solution.py:403
  76.0 14.1 %copy-start.1 = (bf16[1,3,512,128]{3,2,1,0:T(8,128)(2,1)S(1)}, bf16[1,3,512,128]{3,2,1,0:T(8,128)(2,1)}, u32[]{:S(2)}) copy-start(bf16[1,3,512,128]{3,2,1,0:T(8,128)(2,1)} %copy-done) | copy-start | bytes 1179652
  87.0 3.9 %collective-permute-start.17 = (bf16[2,512,128]{2,1,0:T(8,128)(2,1)S(1)}, bf16[2,512,128]{2,1,0:T(8,128)(2,1)S(1)}, u32[]{:S(2)}, u32[]{:S(2)}) collective-permute-start(bf16[2,512,128]{2,1,0:T(8,128)(2,1)S(1)} %get-tuple-element.81), channel_id=1, source_target_pairs={{0,2},{2,0},{4,6},{6,4},{8,10},{10,8},{12,14},{14,12},{16,18},{18,... | collective-permute-start | bytes 786440 | tf_op jit(solution)/shard_map/ppermute | solution.py:370
  87.0 4.0 %collective-permute-start.18 = (bf16[2,512,128]{2,1,0:T(8,128)(2,1)S(1)}, bf16[2,512,128]{2,1,0:T(8,128)(2,1)S(1)}, u32[]{:S(2)}, u32[]{:S(2)}) collective-permute-start(bf16[2,512,128]{2,1,0:T(8,128)(2,1)S(1)} %get-tuple-element.82), channel_id=1, source_target_pairs={{0,2},{2,0},{4,6},{6,4},{8,10},{10,8},{12,14},{14,12},{16,18},{18,... | collective-permute-start | bytes 786440 | tf_op jit(solution)/shard_map/ppermute | solution.py:370
  87.5 7.8 %collective-permute-start.11 = (f32[2,128]{1,0:T(2,128)S(1)}, f32[2,128]{1,0:T(2,128)S(1)}, u32[]{:S(2)}, u32[]{:S(2)}) collective-permute-start(f32[2,128]{1,0:T(2,128)S(1)} %add_add_fusion.1.in_ref), channel_id=1, source_target_pairs={{0,4},{1,5},{2,6},{3,7},{4,0},{5,1},{6,2},{7,3},{8,12},{9,13},{10,... | collective-permute-start | bytes 3080 | tf_op jit(solution)/shard_map/ppermute | solution.py:335
  91.1 20.3 %collective-permute-start.19 = (bf16[2,2,512,128]{3,2,1,0:T(8,128)(2,1)S(1)}, bf16[2,2,512,128]{3,2,1,0:T(8,128)(2,1)S(1)}, u32[]{:S(2)}, u32[]{:S(2)}) collective-permute-start(bf16[2,2,512,128]{3,2,1,0:T(8,128)(2,1)S(1)} %shard_map.113), channel_id=1, source_target_pairs={{4,0},{6,2},{8,4},{10,6},{12,8},{14,10},{16,12},{18,14},{20,16},{2... | collective-permute-start | bytes 1572872 | tf_op jit(solution)/shard_map/ppermute | solution.py:424
  95.2 8.5 %copy-start.5 = (bf16[1,5,512,128]{3,2,1,0:T(8,128)(2,1)S(1)}, bf16[1,5,512,128]{3,2,1,0:T(8,128)(2,1)}, u32[]{:S(2)}) copy-start(bf16[1,5,512,128]{3,2,1,0:T(8,128)(2,1)} %copy-done.4) | copy-start | bytes 1966084
  95.2 3.0 %collective-permute-start.14 = (f32[2,128]{1,0:T(2,128)S(1)}, f32[2,128]{1,0:T(2,128)S(1)}, u32[]{:S(2)}, u32[]{:S(2)}) collective-permute-start(f32[2,128]{1,0:T(2,128)S(1)} %add.26), channel_id=1, source_target_pairs={{0,3},{1,2},{2,1},{3,0},{4,7},{5,6},{6,5},{7,4},{8,11},{9,10},{10,... | collective-permute-start | bytes 3080 | tf_op jit(solution)/shard_map/ppermute | solution.py:335
  96.1 2.1 %collective-permute-start.13 = (f32[2,128]{1,0:T(2,128)S(1)}, f32[2,128]{1,0:T(2,128)S(1)}, u32[]{:S(2)}, u32[]{:S(2)}) collective-permute-start(f32[2,128]{1,0:T(2,128)S(1)} %add.26), channel_id=1, source_target_pairs={{0,2},{1,3},{2,0},{3,1},{4,6},{5,7},{6,4},{7,5},{8,10},{9,11},{10,... | collective-permute-start | bytes 3080 | tf_op jit(solution)/shard_map/ppermute | solution.py:335
  96.9 3.6 %collective-permute-start.12 = (f32[2,128]{1,0:T(2,128)S(1)}, f32[2,128]{1,0:T(2,128)S(1)}, u32[]{:S(2)}, u32[]{:S(2)}) collective-permute-start(f32[2,128]{1,0:T(2,128)S(1)} %add.26), channel_id=1, source_target_pairs={{0,1},{1,0},{2,3},{3,2},{4,5},{5,4},{6,7},{7,6},{8,9},{9,8},{10,11... | collective-permute-start | bytes 3080 | tf_op jit(solution)/shard_map/ppermute | solution.py:335
  100.5 7.1 %collective-permute-start.15 = (f32[2,128]{1,0:T(2,128)S(1)}, f32[2,128]{1,0:T(2,128)S(1)}, u32[]{:S(2)}, u32[]{:S(2)}) collective-permute-start(f32[2,128]{1,0:T(2,128)S(1)} %add_add_fusion), channel_id=1, source_target_pairs={{0,8},{1,9},{2,10},{3,11},{4,12},{5,13},{6,14},{7,15},{8,0},{9,1},... | collective-permute-start | bytes 3080 | tf_op jit(solution)/shard_map/ppermute | solution.py:335
  107.6 6.3 %collective-permute-start.16 = (f32[2,128]{1,0:T(2,128)S(1)}, f32[2,128]{1,0:T(2,128)S(1)}, u32[]{:S(2)}, u32[]{:S(2)}) collective-permute-start(f32[2,128]{1,0:T(2,128)S(1)} %add.30), channel_id=1, source_target_pairs={{0,16},{1,17},{2,18},{3,19},{4,20},{5,21},{6,22},{7,23},{8,24},{9,... | collective-permute-start | bytes 3080 | tf_op jit(solution)/shard_map/ppermute | solution.py:335
  (3 other events, 10.0 us)

commit v12 on v9

--- a/solution.py
+++ b/solution.py
@@ -199,7 +199,7 @@
         out_specs=pl.BlockSpec((2, count, tokens, width), lambda step: (0, 0, step, 0)),
         out_shape=jax.ShapeDtypeStruct((2, count, rows, width), key.dtype),
         scratch_shapes=[pltpu.VMEM((tokens * heads, width), jnp.float32)],
-        compiler_params=pltpu.CompilerParams(vmem_limit_bytes=12 * 1024 * 1024),
+        compiler_params=pltpu.CompilerParams(vmem_limit_bytes=56 * 1024 * 1024),
         cost_estimate=LIGHT,
     )(key, value)
 

time: 113 us -> 113 us (level)
  local copies, waits for them, and re-layouts: 10.1 us -> 7.64 us
  Pallas kernels: 51.1 us -> 52.3 us
    pallas_call x2, Pallas kernels: 1.4 us -> 5.35 us  [pack(): pl.pallas_call(functools.partial(pack_kernel, first), grid=(rows // token...]
    unnamed x10, local copies, waits for them, and re-layouts: 2.46 us -> 0.02 us
    pallas_call x3, Pallas kernels: 2.58 us -> 0.87 us  [choose(): pl.pallas_call(choose_kernel, grid=(count,), in_specs=[pl.BlockSpec(memor...]
where the time goes in v12:
time: 113 us
  Pallas kernels  52.3 us (46%)
  waiting for transfers between devices  26.6 us (24%)
  starting transfers between devices  25 us (22%)
  local copies, waits for them, and re-layouts  7.64 us (7%)
    pallas_call x3, Pallas kernels, group_grads(): pl.pallas_call(heads_kernel, grid=(count,), in_specs=[pl.BlockSpec(memory...  41 us
    ppermute x2, waiting for transfers between devices, per_device(): fars = [lax.ppermute(own, 'seq', ahead) for own in owns]  11.5 us
    ppermute x7, starting transfers between devices, exchanged(): lax.ppermute(value, ('seq', 'head'), [(source, source ^ mask) for source...  10.5 us
    ppermute x2, starting transfers between devices, per_device(): fars = [lax.ppermute(own, 'seq', ahead) for own in owns]  8.36 us
    pallas_call x2, Pallas kernels, pack(): pl.pallas_call(functools.partial(pack_kernel, first), grid=(rows // token...  5.35 us
    ppermute x7, waiting for transfers between devices, exchanged(): lax.ppermute(value, ('seq', 'head'), [(source, source ^ mask) for source...  4.62 us
    reshape x2, local copies, waits for them, and re-layouts, by_head(): split = array.reshape(rows, kv_dev, group, width)  4.62 us
    ppermute x2, waiting for transfers between devices, per_device(): kept.append((stays, lax.ppermute(relayed, 'seq', back)))  3.92 us
  transfers between devices with their start and end apart: 21, of which 15 were waited for; matrix products, arithmetic and copies ran while one was open for 6% of the time, Pallas kernels for 44%

profile of v12, /device:TPU:0, one launch (start us, length us, event | category | flops | bytes accessed | tf_op | source)
XLA Modules:
  0.0 112.5 jit_solution(5367118560909690958)
XLA Ops:
  0.6 2.5 %shard_map.101.own_ref = bf16[2,3,512,128]{3,2,1,0:T(8,128)(2,1)} custom-call(bf16[512,8,128]{2,1,0:T(8,128)(2,1)} %key_ref.3, bf16[512,8,128]{2,1,0:T(8,128)(2,1)} %value_ref.3), custom_call_target="tpu_custom_call" | custom-call | flops 1000 | bytes 1000 | tf_op jit(solution)/shard_map/pallas_call | solution.py:195
  3.2 4.9 %collective-permute-start = (bf16[2,3,512,128]{3,2,1,0:T(8,128)(2,1)}, bf16[2,3,512,128]{3,2,1,0:T(8,128)(2,1)S(1)}, u32[]{:S(2)}, u32[]{:S(2)}) collective-permute-start(bf16[2,3,512,128]{3,2,1,0:T(8,128)(2,1)} %shard_map.101.own_ref), channel_id=1, source_target_pairs={{0,4},{2,6},{4,8},{6,10},{8,12},{10,14},{12,16},{14,18},{16,20},{1... | collective-permute-start | bytes 2359304 | tf_op jit(solution)/shard_map/ppermute | solution.py:388
  8.1 2.8 %shard_map.102.own_ref = bf16[2,5,512,128]{3,2,1,0:T(8,128)(2,1)} custom-call(bf16[512,8,128]{2,1,0:T(8,128)(2,1)} %key_ref.3, bf16[512,8,128]{2,1,0:T(8,128)(2,1)} %value_ref.3), custom_call_target="tpu_custom_call" | custom-call | flops 1000 | bytes 1000 | tf_op jit(solution)/shard_map/pallas_call | solution.py:195
  10.9 3.4 %collective-permute-start.1 = (bf16[2,5,512,128]{3,2,1,0:T(8,128)(2,1)}, bf16[2,5,512,128]{3,2,1,0:T(8,128)(2,1)S(1)}, u32[]{:S(2)}, u32[]{:S(2)}) collective-permute-start(bf16[2,5,512,128]{3,2,1,0:T(8,128)(2,1)} %shard_map.102.own_ref), channel_id=1, source_target_pairs={{0,4},{2,6},{4,8},{6,10},{8,12},{10,14},{12,16},{14,18},{16,20},{1... | collective-permute-start | bytes 3932168 | tf_op jit(solution)/shard_map/ppermute | solution.py:388
  14.4 3.2 %copy.14 = bf16[512,8,2,128]{3,2,0,1:T(2,128)(2,1)S(1)} copy(bf16[512,8,2,128]{3,2,1,0:T(2,128)(2,1)} %bitcast.36) | data formatting | bytes 4194304 | tf_op jit(solution)/shard_map/reshape | solution.py:381
  17.6 1.4 %copy.15 = bf16[512,8,2,128]{3,2,0,1:T(2,128)(2,1)S(1)} copy(bf16[512,8,2,128]{3,2,1,0:T(2,128)(2,1)S(1)} %bitcast.37) | data formatting | bytes 4194304 | tf_op jit(solution)/shard_map/reshape | solution.py:381
  19.0 7.3 %collective-permute-done.far_ref = bf16[2,3,512,128]{3,2,1,0:T(8,128)(2,1)S(1)} collective-permute-done((bf16[2,3,512,128]{3,2,1,0:T(8,128)(2,1)}, bf16[2,3,512,128]{3,2,1,0:T(8,128)(2,1)S(1)}, u32[]{:S(2)}, u32[]{:S(2)}) %collective-permute-start) | collective-permute-done | bytes 786464 | tf_op jit(solution)/shard_map/ppermute | solution.py:388
  26.7 2.3 %collective-permute-done.2.near_ref = bf16[2,3,512,128]{3,2,1,0:T(8,128)(2,1)S(1)} collective-permute-done((bf16[2,3,512,128]{3,2,1,0:T(8,128)(2,1)S(1)}, bf16[2,3,512,128]{3,2,1,0:T(8,128)(2,1)S(1)}, u32[]{:S(2)}, u32[]{:S(2)}) %collective-permute-start.2) | collective-permute-done | bytes 786464 | tf_op jit(solution)/shard_map/ppermute | solution.py:419
  29.0 2.4 %broadcast_in_dim.3._ = bf16[512,8,2,128]{3,2,1,0:T(2,128)(2,1)} broadcast(bf16[]{:T(256)} %constant.7.clone.1), dimensions={} | broadcast | bytes 2097154 | tf_op jit(solution)/shard_map/broadcast_in_dim | solution.py:403
  31.4 15.0 %shard_map.104 = (bf16[512,8,2,128]{3,2,1,0:T(2,128)(2,1)}, bf16[2,3,512,128]{3,2,1,0:T(8,128)(2,1)S(1)}, bf16[3,512,128]{2,1,0:T(8,128)(2,1)S(1)}, bf16[3,512,1...) custom-call(s32[1]{0:T(128)} %bitcast.shard_ref.in_ref, ...), custom_call_target="tpu_custom_call", output_to_operand_aliasing={{0}: (8, {})} | custom-call | flops 1000 | bytes 1000 | tf_op jit(solution)/shard_map/pallas_call | solution.py:283
  48.9 4.3 %collective-permute-done.1.far_ref = bf16[2,5,512,128]{3,2,1,0:T(8,128)(2,1)S(1)} collective-permute-done((bf16[2,5,512,128]{3,2,1,0:T(8,128)(2,1)}, bf16[2,5,512,128]{3,2,1,0:T(8,128)(2,1)S(1)}, u32[]{:S(2)}, u32[]{:S(2)}) %collective-permute-start.1) | collective-permute-done | bytes 1310752 | tf_op jit(solution)/shard_map/ppermute | solution.py:388
  53.6 1.5 %collective-permute-start.10 = (bf16[2,3,512,128]{3,2,1,0:T(8,128)(2,1)S(1)}, bf16[2,3,512,128]{3,2,1,0:T(8,128)(2,1)S(1)}, u32[]{:S(2)}, u32[]{:S(2)}) collective-permute-start(bf16[2,3,512,128]{3,2,1,0:T(8,128)(2,1)S(1)} %shard_map.105), channel_id=1, source_target_pairs={{4,0},{6,2},{8,4},{10,6},{12,8},{14,10},{16,12},{18,14},{20,16},{2... | collective-permute-start | bytes 2359304 | tf_op jit(solution)/shard_map/ppermute | solution.py:427
  55.9 15.1 %shard_map.107 = (bf16[512,8,2,128]{3,2,1,0:T(2,128)(2,1)}, bf16[2,3,512,128]{3,2,1,0:T(8,128)(2,1)S(1)}, bf16[3,512,128]{2,1,0:T(8,128)(2,1)S(1)}, bf16[3,512,1...) custom-call(s32[1]{0:T(128)} %bitcast.shard_ref.in_ref, ...), custom_call_target="tpu_custom_call", output_to_operand_aliasing={{0}: (8, {})} | custom-call | flops 1000 | bytes 1000 | tf_op jit(solution)/shard_map/pallas_call | solution.py:283
  74.8 1.3 %collective-permute-done.10.returned = bf16[2,3,512,128]{3,2,1,0:T(8,128)(2,1)S(1)} collective-permute-done((bf16[2,3,512,128]{3,2,1,0:T(8,128)(2,1)S(1)}, bf16[2,3,512,128]{3,2,1,0:T(8,128)(2,1)S(1)}, u32[]{:S(2)}, u32[]{:S(2)}) %collective-permute-start.10) | collective-permute-done | bytes 786464 | tf_op jit(solution)/shard_map/ppermute | solution.py:427
  76.6 10.9 %shard_map.112 = (bf16[512,8,2,128]{3,2,1,0:T(2,128)(2,1)}, bf16[2,2,512,128]{3,2,1,0:T(8,128)(2,1)S(1)}, bf16[2,512,128]{2,1,0:T(8,128)(2,1)S(1)}, bf16[2,512,1...) custom-call(s32[1]{0:T(128)} %shard_map.111.shard_ref, ...), custom_call_target="tpu_custom_call", output_to_operand_aliasing={{0}: (8, {})} | custom-call | flops 1000 | bytes 1000 | tf_op jit(solution)/shard_map/pallas_call | solution.py:283
  88.1 2.7 %collective-permute-start.11 = (f32[2,128]{1,0:T(2,128)S(1)}, f32[2,128]{1,0:T(2,128)S(1)}, u32[]{:S(2)}, u32[]{:S(2)}) collective-permute-start(f32[2,128]{1,0:T(2,128)S(1)} %add_add_fusion.2.in_ref), channel_id=1, source_target_pairs={{0,4},{1,5},{2,6},{3,7},{4,0},{5,1},{6,2},{7,3},{8,12},{9,13},{10,... | collective-permute-start | bytes 3080 | tf_op jit(solution)/shard_map/ppermute | solution.py:360
  91.7 1.5 %collective-permute-start.20 = (bf16[2,2,512,128]{3,2,1,0:T(8,128)(2,1)S(1)}, bf16[2,2,512,128]{3,2,1,0:T(8,128)(2,1)S(1)}, u32[]{:S(2)}, u32[]{:S(2)}) collective-permute-start(bf16[2,2,512,128]{3,2,1,0:T(8,128)(2,1)S(1)} %shard_map.115), channel_id=1, source_target_pairs={{4,0},{6,2},{8,4},{10,6},{12,8},{14,10},{16,12},{18,14},{20,16},{2... | collective-permute-start | bytes 1572872 | tf_op jit(solution)/shard_map/ppermute | solution.py:448
  93.2 2.6 %collective-permute-done.8.returned = bf16[2,3,512,128]{3,2,1,0:T(8,128)(2,1)S(1)} collective-permute-done((bf16[2,3,512,128]{3,2,1,0:T(8,128)(2,1)S(1)}, bf16[2,3,512,128]{3,2,1,0:T(8,128)(2,1)S(1)}, u32[]{:S(2)}, u32[]{:S(2)}) %collective-permute-start.8) | collective-permute-done | bytes 786464 | tf_op jit(solution)/shard_map/ppermute | solution.py:427
  95.9 1.6 %collective-permute-start.14 = (f32[2,128]{1,0:T(2,128)S(1)}, f32[2,128]{1,0:T(2,128)S(1)}, u32[]{:S(2)}, u32[]{:S(2)}) collective-permute-start(f32[2,128]{1,0:T(2,128)S(1)} %add.29), channel_id=1, source_target_pairs={{0,3},{1,2},{2,1},{3,0},{4,7},{5,6},{6,5},{7,4},{8,11},{9,10},{10,... | collective-permute-start | bytes 3080 | tf_op jit(solution)/shard_map/ppermute | solution.py:360
  99.0 2.1 %collective-permute-done.12 = f32[2,128]{1,0:T(2,128)S(1)} collective-permute-done((f32[2,128]{1,0:T(2,128)S(1)}, f32[2,128]{1,0:T(2,128)S(1)}, u32[]{:S(2)}, u32[]{:S(2)}) %collective-permute-start.12) | collective-permute-done | bytes 1056 | tf_op jit(solution)/shard_map/ppermute | solution.py:360
  101.1 3.2 %collective-permute-start.15 = (f32[2,128]{1,0:T(2,128)S(1)}, f32[2,128]{1,0:T(2,128)S(1)}, u32[]{:S(2)}, u32[]{:S(2)}) collective-permute-start(f32[2,128]{1,0:T(2,128)S(1)} %add_add_fusion.1), channel_id=1, source_target_pairs={{0,8},{1,9},{2,10},{3,11},{4,12},{5,13},{6,14},{7,15},{8,0},{9,1},... | collective-permute-start | bytes 3080 | tf_op jit(solution)/shard_map/ppermute | solution.py:360
  104.3 2.3 %collective-permute-start.16 = (f32[2,128]{1,0:T(2,128)S(1)}, f32[2,128]{1,0:T(2,128)S(1)}, u32[]{:S(2)}, u32[]{:S(2)}) collective-permute-start(f32[2,128]{1,0:T(2,128)S(1)} %add_add_fusion.1), channel_id=1, source_target_pairs={{0,16},{1,17},{2,18},{3,19},{4,20},{5,21},{6,22},{7,23},{8,24},{9,... | collective-permute-start | bytes 3080 | tf_op jit(solution)/shard_map/ppermute | solution.py:360
  107.2 2.5 %shard_map.116 = (bf16[512,8,128]{2,1,0:T(8,128)(2,1)}, bf16[512,8,128]{2,1,0:T(8,128)(2,1)}) custom-call(s32[1]{0:T(128)} %bitcast.shard_ref.in_ref, bf16[2,2,512,128]{3,2,1,0:T(8,128)(2,1)S(1)} %get-tuple-element.77.own, bf16[2,2,512,128]{3,2,1,0:T(8,128)(2,1)S(1)} %collective-permute-done.20.returned, ...), custom_call_target="tpu_custom_call" | custom-call | tf_op jit(solution)/shard_map/pallas_call | solution.py:339
  110.4 1.6 %collective-permute-done.17 = f32[2,128]{1,0:T(2,128)S(1)} collective-permute-done((f32[2,128]{1,0:T(2,128)S(1)}, f32[2,128]{1,0:T(2,128)S(1)}, u32[]{:S(2)}, u32[]{:S(2)}) %collective-permute-start.17) | collective-permute-done | bytes 1056 | tf_op jit(solution)/shard_map/ppermute | solution.py:360
  (57 shorter events, 13.2 us)
Async XLA Ops:
  3.2 23.1 %collective-permute-start = (bf16[2,3,512,128]{3,2,1,0:T(8,128)(2,1)}, bf16[2,3,512,128]{3,2,1,0:T(8,128)(2,1)S(1)}, u32[]{:S(2)}, u32[]{:S(2)}) collective-permute-start(bf16[2,3,512,128]{3,2,1,0:T(8,128)(2,1)} %shard_map.101.own_ref), channel_id=1, source_target_pairs={{0,4},{2,6},{4,8},{6,10},{8,12},{10,14},{12,16},{14,18},{16,20},{1... | collective-permute-start | bytes 2359304 | tf_op jit(solution)/shard_map/ppermute | solution.py:388
  10.9 42.3 %collective-permute-start.1 = (bf16[2,5,512,128]{3,2,1,0:T(8,128)(2,1)}, bf16[2,5,512,128]{3,2,1,0:T(8,128)(2,1)S(1)}, u32[]{:S(2)}, u32[]{:S(2)}) collective-permute-start(bf16[2,5,512,128]{3,2,1,0:T(8,128)(2,1)} %shard_map.102.own_ref), channel_id=1, source_target_pairs={{0,4},{2,6},{4,8},{6,10},{8,12},{10,14},{12,16},{14,18},{16,20},{1... | collective-permute-start | bytes 3932168 | tf_op jit(solution)/shard_map/ppermute | solution.py:388
  17.6 8.7 %copy-start.1 = (bf16[2,3,512,128]{3,2,1,0:T(8,128)(2,1)S(1)}, bf16[2,3,512,128]{3,2,1,0:T(8,128)(2,1)}, u32[]{:S(2)}) copy-start(bf16[2,3,512,128]{3,2,1,0:T(8,128)(2,1)} %shard_map.101.own_ref) | copy-start | bytes 2359300
  26.3 5.1 %copy-start.3 = (f32[128]{0:T(128)S(1)}, f32[128]{0:T(128)}, u32[]{:S(2)}) copy-start(f32[128]{0:T(128)} %param.10) | copy-start | bytes 1540
  26.6 2.4 %collective-permute-start.2 = (bf16[2,3,512,128]{3,2,1,0:T(8,128)(2,1)S(1)}, bf16[2,3,512,128]{3,2,1,0:T(8,128)(2,1)S(1)}, u32[]{:S(2)}, u32[]{:S(2)}) collective-permute-start(bf16[2,3,512,128]{3,2,1,0:T(8,128)(2,1)S(1)} %shard_map.103), channel_id=1, source_target_pairs={{0,2},{2,0},{4,6},{6,4},{8,10},{10,8},{12,14},{14,12},{16,18},{18,... | collective-permute-start | bytes 2359304 | tf_op jit(solution)/shard_map/ppermute | solution.py:419
  46.4 6.8 %copy-start = (bf16[2,5,512,128]{3,2,1,0:T(8,128)(2,1)S(1)}, bf16[2,5,512,128]{3,2,1,0:T(8,128)(2,1)}, u32[]{:S(2)}) copy-start(bf16[2,5,512,128]{3,2,1,0:T(8,128)(2,1)} %shard_map.102.own_ref) | copy-start | bytes 3932164
  46.4 1.7 %collective-permute-start.3 = (bf16[3,512,128]{2,1,0:T(8,128)(2,1)S(1)}, bf16[3,512,128]{2,1,0:T(8,128)(2,1)S(1)}, u32[]{:S(2)}, u32[]{:S(2)}) collective-permute-start(bf16[3,512,128]{2,1,0:T(8,128)(2,1)S(1)} %get-tuple-element.52), channel_id=1, source_target_pairs={{0,2},{2,0},{4,6},{6,4},{8,10},{10,8},{12,14},{14,12},{16,18},{18,... | collective-permute-start | bytes 1179656 | tf_op jit(solution)/shard_map/ppermute | solution.py:394
  46.5 2.2 %collective-permute-start.4 = (bf16[3,512,128]{2,1,0:T(8,128)(2,1)S(1)}, bf16[3,512,128]{2,1,0:T(8,128)(2,1)S(1)}, u32[]{:S(2)}, u32[]{:S(2)}) collective-permute-start(bf16[3,512,128]{2,1,0:T(8,128)(2,1)S(1)} %get-tuple-element.53), channel_id=1, source_target_pairs={{0,2},{2,0},{4,6},{6,4},{8,10},{10,8},{12,14},{14,12},{16,18},{18,... | collective-permute-start | bytes 1179656 | tf_op jit(solution)/shard_map/ppermute | solution.py:394
  53.6 2.4 %collective-permute-start.5 = (bf16[2,3,512,128]{3,2,1,0:T(8,128)(2,1)S(1)}, bf16[2,3,512,128]{3,2,1,0:T(8,128)(2,1)S(1)}, u32[]{:S(2)}, u32[]{:S(2)}) collective-permute-start(bf16[2,3,512,128]{3,2,1,0:T(8,128)(2,1)S(1)} %shard_map.106), channel_id=1, source_target_pairs={{0,2},{2,0},{4,6},{6,4},{8,10},{10,8},{12,14},{14,12},{16,18},{18,... | collective-permute-start | bytes 2359304 | tf_op jit(solution)/shard_map/ppermute | solution.py:419
  53.6 22.5 %collective-permute-start.10 = (bf16[2,3,512,128]{3,2,1,0:T(8,128)(2,1)S(1)}, bf16[2,3,512,128]{3,2,1,0:T(8,128)(2,1)S(1)}, u32[]{:S(2)}, u32[]{:S(2)}) collective-permute-start(bf16[2,3,512,128]{3,2,1,0:T(8,128)(2,1)S(1)} %shard_map.105), channel_id=1, source_target_pairs={{4,0},{6,2},{8,4},{10,6},{12,8},{14,10},{16,12},{18,14},{20,16},{2... | collective-permute-start | bytes 2359304 | tf_op jit(solution)/shard_map/ppermute | solution.py:427
  71.0 1.7 %collective-permute-start.6 = (bf16[3,512,128]{2,1,0:T(8,128)(2,1)S(1)}, bf16[3,512,128]{2,1,0:T(8,128)(2,1)S(1)}, u32[]{:S(2)}, u32[]{:S(2)}) collective-permute-start(bf16[3,512,128]{2,1,0:T(8,128)(2,1)S(1)} %get-tuple-element.57), channel_id=1, source_target_pairs={{0,2},{2,0},{4,6},{6,4},{8,10},{10,8},{12,14},{14,12},{16,18},{18,... | collective-permute-start | bytes 1179656 | tf_op jit(solution)/shard_map/ppermute | solution.py:394
  71.1 2.1 %collective-permute-start.7 = (bf16[3,512,128]{2,1,0:T(8,128)(2,1)S(1)}, bf16[3,512,128]{2,1,0:T(8,128)(2,1)S(1)}, u32[]{:S(2)}, u32[]{:S(2)}) collective-permute-start(bf16[3,512,128]{2,1,0:T(8,128)(2,1)S(1)} %get-tuple-element.58), channel_id=1, source_target_pairs={{0,2},{2,0},{4,6},{6,4},{8,10},{10,8},{12,14},{14,12},{16,18},{18,... | collective-permute-start | bytes 1179656 | tf_op jit(solution)/shard_map/ppermute | solution.py:394
  71.7 4.4 %collective-permute-start.9 = (bf16[2,2,512,128]{3,2,1,0:T(8,128)(2,1)S(1)}, bf16[2,2,512,128]{3,2,1,0:T(8,128)(2,1)S(1)}, u32[]{:S(2)}, u32[]{:S(2)}) collective-permute-start(bf16[2,2,512,128]{3,2,1,0:T(8,128)(2,1)S(1)} %shard_map.109), channel_id=1, source_target_pairs={{0,2},{2,0},{4,6},{6,4},{8,10},{10,8},{12,14},{14,12},{16,18},{18,... | collective-permute-start | bytes 1572872 | tf_op jit(solution)/shard_map/ppermute | solution.py:419
  73.5 22.4 %collective-permute-start.8 = (bf16[2,3,512,128]{3,2,1,0:T(8,128)(2,1)S(1)}, bf16[2,3,512,128]{3,2,1,0:T(8,128)(2,1)S(1)}, u32[]{:S(2)}, u32[]{:S(2)}) collective-permute-start(bf16[2,3,512,128]{3,2,1,0:T(8,128)(2,1)S(1)} %shard_map.108), channel_id=1, source_target_pairs={{4,0},{6,2},{8,4},{10,6},{12,8},{14,10},{16,12},{18,14},{20,16},{2... | collective-permute-start | bytes 2359304 | tf_op jit(solution)/shard_map/ppermute | solution.py:427
  87.5 4.0 %collective-permute-start.18 = (bf16[2,512,128]{2,1,0:T(8,128)(2,1)S(1)}, bf16[2,512,128]{2,1,0:T(8,128)(2,1)S(1)}, u32[]{:S(2)}, u32[]{:S(2)}) collective-permute-start(bf16[2,512,128]{2,1,0:T(8,128)(2,1)S(1)} %get-tuple-element.79), channel_id=1, source_target_pairs={{0,2},{2,0},{4,6},{6,4},{8,10},{10,8},{12,14},{14,12},{16,18},{18,... | collective-permute-start | bytes 786440 | tf_op jit(solution)/shard_map/ppermute | solution.py:394
  87.5 4.0 %collective-permute-start.19 = (bf16[2,512,128]{2,1,0:T(8,128)(2,1)S(1)}, bf16[2,512,128]{2,1,0:T(8,128)(2,1)S(1)}, u32[]{:S(2)}, u32[]{:S(2)}) collective-permute-start(bf16[2,512,128]{2,1,0:T(8,128)(2,1)S(1)} %get-tuple-element.80), channel_id=1, source_target_pairs={{0,2},{2,0},{4,6},{6,4},{8,10},{10,8},{12,14},{14,12},{16,18},{18,... | collective-permute-start | bytes 786440 | tf_op jit(solution)/shard_map/ppermute | solution.py:394
  88.1 7.8 %collective-permute-start.11 = (f32[2,128]{1,0:T(2,128)S(1)}, f32[2,128]{1,0:T(2,128)S(1)}, u32[]{:S(2)}, u32[]{:S(2)}) collective-permute-start(f32[2,128]{1,0:T(2,128)S(1)} %add_add_fusion.2.in_ref), channel_id=1, source_target_pairs={{0,4},{1,5},{2,6},{3,7},{4,0},{5,1},{6,2},{7,3},{8,12},{9,13},{10,... | collective-permute-start | bytes 3080 | tf_op jit(solution)/shard_map/ppermute | solution.py:360
  91.7 15.4 %collective-permute-start.20 = (bf16[2,2,512,128]{3,2,1,0:T(8,128)(2,1)S(1)}, bf16[2,2,512,128]{3,2,1,0:T(8,128)(2,1)S(1)}, u32[]{:S(2)}, u32[]{:S(2)}) collective-permute-start(bf16[2,2,512,128]{3,2,1,0:T(8,128)(2,1)S(1)} %shard_map.115), channel_id=1, source_target_pairs={{4,0},{6,2},{8,4},{10,6},{12,8},{14,10},{16,12},{18,14},{20,16},{2... | collective-permute-start | bytes 1572872 | tf_op jit(solution)/shard_map/ppermute | solution.py:448
  95.9 3.0 %collective-permute-start.13 = (f32[2,128]{1,0:T(2,128)S(1)}, f32[2,128]{1,0:T(2,128)S(1)}, u32[]{:S(2)}, u32[]{:S(2)}) collective-permute-start(f32[2,128]{1,0:T(2,128)S(1)} %add.29), channel_id=1, source_target_pairs={{0,2},{1,3},{2,0},{3,1},{4,6},{5,7},{6,4},{7,5},{8,10},{9,11},{10,... | collective-permute-start | bytes 3080 | tf_op jit(solution)/shard_map/ppermute | solution.py:360
  95.9 3.1 %collective-permute-start.14 = (f32[2,128]{1,0:T(2,128)S(1)}, f32[2,128]{1,0:T(2,128)S(1)}, u32[]{:S(2)}, u32[]{:S(2)}) collective-permute-start(f32[2,128]{1,0:T(2,128)S(1)} %add.29), channel_id=1, source_target_pairs={{0,3},{1,2},{2,1},{3,0},{4,7},{5,6},{6,5},{7,4},{8,11},{9,10},{10,... | collective-permute-start | bytes 3080 | tf_op jit(solution)/shard_map/ppermute | solution.py:360
  97.5 3.6 %collective-permute-start.12 = (f32[2,128]{1,0:T(2,128)S(1)}, f32[2,128]{1,0:T(2,128)S(1)}, u32[]{:S(2)}, u32[]{:S(2)}) collective-permute-start(f32[2,128]{1,0:T(2,128)S(1)} %add.29), channel_id=1, source_target_pairs={{0,1},{1,0},{2,3},{3,2},{4,5},{5,4},{6,7},{7,6},{8,9},{9,8},{10,11... | collective-permute-start | bytes 3080 | tf_op jit(solution)/shard_map/ppermute | solution.py:360
  101.1 8.5 %collective-permute-start.15 = (f32[2,128]{1,0:T(2,128)S(1)}, f32[2,128]{1,0:T(2,128)S(1)}, u32[]{:S(2)}, u32[]{:S(2)}) collective-permute-start(f32[2,128]{1,0:T(2,128)S(1)} %add_add_fusion.1), channel_id=1, source_target_pairs={{0,8},{1,9},{2,10},{3,11},{4,12},{5,13},{6,14},{7,15},{8,0},{9,1},... | collective-permute-start | bytes 3080 | tf_op jit(solution)/shard_map/ppermute | solution.py:360
  104.3 6.0 %collective-permute-start.16 = (f32[2,128]{1,0:T(2,128)S(1)}, f32[2,128]{1,0:T(2,128)S(1)}, u32[]{:S(2)}, u32[]{:S(2)}) collective-permute-start(f32[2,128]{1,0:T(2,128)S(1)} %add_add_fusion.1), channel_id=1, source_target_pairs={{0,16},{1,17},{2,18},{3,19},{4,20},{5,21},{6,22},{7,23},{8,24},{9,... | collective-permute-start | bytes 3080 | tf_op jit(solution)/shard_map/ppermute | solution.py:360
  106.6 5.4 %collective-permute-start.17 = (f32[2,128]{1,0:T(2,128)S(1)}, f32[2,128]{1,0:T(2,128)S(1)}, u32[]{:S(2)}, u32[]{:S(2)}) collective-permute-start(f32[2,128]{1,0:T(2,128)S(1)} %add_add_fusion.1), channel_id=1, source_target_pairs={{0,24},{1,25},{2,26},{3,27},{4,28},{5,29},{6,30},{7,31},{8,16},{9,... | collective-permute-start | bytes 3080 | tf_op jit(solution)/shard_map/ppermute | solution.py:360
  (2 other events, 8.3 us)
